TPU v7x, 32 devices: a whole 2x2x4 slice. The times are simulated.
32 devices in a mesh: seq: 4 (over y, core), ctx: 2 (over x), exp: 4 (over z).
Axes of the slice: x: 2, y: 2, z: 4, core: 2. Of those that a mesh axis runs over, the one named last changes fastest.
Arguments:
- residual_in: bfloat16 [16, 1024, 2048], P(('seq', 'exp'), 'ctx'), may hold values from -24 to 24
- segments: int32 [16, 1024], P(('seq', 'exp')), may hold values from 0 to 515, as said below
- routes: int32 [16, 1024, 8], P(('seq', 'exp'), 'ctx'), may hold values from 0 to 15, all different within a row; in each aligned block of 512 rows (0 to 511, 512 to 1023, ..., all dimensions but the last counted through in order) at most 288 rows name the same one
- gates: float32 [16, 1024, 8], P(('seq', 'exp'), 'ctx'), may hold values from 0.005 to 0.7
- attn_gain: bfloat16 [2048], P(('seq', 'ctx', 'exp')), may hold values from 0.5 to 1.5
- q_proj: bfloat16 [2048, 4096], P(('seq', 'ctx', 'exp')), may hold values from -0.125 to 0.125
- key_projection: bfloat16 [2048, 512], P(('seq', 'ctx', 'exp')), may hold values from -0.125 to 0.125
- value_projection: bfloat16 [2048, 512], P(('seq', 'ctx', 'exp')), may hold values from -0.125 to 0.125
- q_gain: bfloat16 [128], P(('seq', 'ctx', 'exp')), may hold values from 0.5 to 1.5
- k_gain: bfloat16 [128], P(('seq', 'ctx', 'exp')), may hold values from 0.5 to 1.5
- o_proj: bfloat16 [4096, 2048], P(('seq', 'ctx', 'exp')), may hold values from -0.5 to 0.5
- mlp_gain: bfloat16 [2048], P(('seq', 'ctx', 'exp')), may hold values from 0.5 to 1.5
- gate_proj: bfloat16 [16, 2048, 768], P('exp', ('seq', 'ctx')), may hold values from -0.125 to 0.125
- up_proj: bfloat16 [16, 2048, 768], P('exp', ('seq', 'ctx')), may hold values from -0.125 to 0.125
- down_proj: bfloat16 [16, 768, 2048], P('exp', ('seq', 'ctx')), may hold values from -0.875 to 0.875
- out_grad: bfloat16 [16, 1024, 2048], P(('seq', 'exp'), 'ctx'), may hold values from -6 to 6
Outputs:
- residual_out: bfloat16 [16, 1024, 2048], P(('seq', 'exp'), 'ctx')
- residual_grad: bfloat16 [16, 1024, 2048], P(('seq', 'exp'), 'ctx')
- attn_gain_grad: float32 [2048], P(('seq', 'ctx', 'exp'))
- q_proj_grad: float32 [2048, 4096], P(('seq', 'ctx', 'exp'))
- k_proj_grad: float32 [2048, 512], P(('seq', 'ctx', 'exp'))
- v_proj_grad: float32 [2048, 512], P(('seq', 'ctx', 'exp'))
- q_gain_grad: float32 [128], P(('seq', 'ctx', 'exp'))
- k_gain_grad: float32 [128], P(('seq', 'ctx', 'exp'))
- o_proj_grad: float32 [4096, 2048], P(('seq', 'ctx', 'exp'))
- mlp_gain_grad: float32 [2048], P(('seq', 'ctx', 'exp'))
- gate_proj_grad: float32 [16, 2048, 768], P('exp', ('seq', 'ctx'))
- up_proj_grad: float32 [16, 2048, 768], P('exp', ('seq', 'ctx'))
- down_proj_grad: float32 [16, 768, 2048], P('exp', ('seq', 'ctx'))
- rms_stats: float32 [3], replicated
Inputs may be any that keep to these rules, and one draw needn't show every extreme that they name: `segments`: along a sequence the numbers never fall; 0 marks unused slots, which come only at the end, one or more in every sequence; the last used document of every sequence has the number 512 + 3; in every sequence one document begins among the first 512 positions and ends among the last 512. `routes`: A token names 8 different experts. In the tokens of one device (aligned blocks of 512 tokens) no expert is named more than 288 times, a bound that some block reaches.
All inputs are finite; a program needn't handle non-finite values.
Results may differ from a plain program's by a relative error of at most 0.015.
Values may be sent and summed in bfloat16 or wider, within the bound.
A program may use at most 576 MiB of HBM per device.

v0:
```python
import jax
import jax.numpy as jnp
from jax import lax
from jax.sharding import PartitionSpec as P

QUERY_HEADS = 32
KEY_VALUE_HEADS = 4
HEAD_DIM = 128


EPS = 1e-06
ROPE_BASE = 1000000.0
MASKED = -1e30


def contract_rows(first_op, second_op):
    return lax.dot_general(
        first_op, second_op, (((0,), (0,)), ((), ())), preferred_element_type=jnp.float32
    )


def contract_cols(first_op, second_op):
    return lax.dot_general(
        first_op, second_op, (((1,), (1,)), ((), ())), preferred_element_type=jnp.float32
    )


def rope_tables(positions):
    half_dim = HEAD_DIM // 2
    inverse = ROPE_BASE ** (-jnp.arange(half_dim, dtype=jnp.float32) * 2.0 / HEAD_DIM)
    angles = positions.astype(jnp.float32)[:, None] * inverse[None, :]
    cosine_table = jnp.cos(angles)
    sine_values = jnp.sin(angles)
    return (
        jnp.concatenate([cosine_table, cosine_table], -1),
        jnp.concatenate([sine_values, sine_values], -1),
    )


def rotate(vectors, cosine_table, sine_values):
    half_dim = vectors.shape[-1] // 2
    turned = jnp.concatenate([-vectors[..., half_dim:], vectors[..., :half_dim]], -1)
    return vectors * cosine_table[:, None, :] + turned * sine_values[:, None, :]


def inverse_rotation(gradient, cosine_table, sine_values):
    half_dim = gradient.shape[-1] // 2
    scaled = gradient * sine_values[:, None, :]
    return gradient * cosine_table[:, None, :] + jnp.concatenate(
        [scaled[..., half_dim:], -scaled[..., :half_dim]], -1
    )


def norm_back(gradient, source, inverse, gain_vec):
    scaled = gradient * gain_vec
    return inverse * scaled - source * inverse**3 * jnp.mean(
        scaled * source, axis=-1, keepdims=True
    )


def on_device(
    residual_in,
    segments,
    routes,
    gates,
    attn_gain,
    q_proj,
    key_projection,
    value_projection,
    q_gain,
    k_gain,
    o_proj,
    mlp_gain,
    gate_proj,
    up_proj,
    down_proj,
    out_grad,
):
    token_count = residual_in.shape[1]
    model_width = residual_in.shape[2]
    sequence_length = segments.shape[1]
    span_index = lax.axis_index("ctx")
    route_count = routes.shape[2]
    local_experts = gate_proj.shape[0]
    owner_count = lax.axis_size("exp")
    expert_count = local_experts * owner_count
    capacity = token_count * route_count * 9 // (expert_count * 8)
    heads_per_group = QUERY_HEADS // KEY_VALUE_HEADS
    score_scale = HEAD_DIM ** (-0.5)
    dense_full = (
        lax.all_gather(attn_gain, ("seq", "ctx", "exp"), axis=0, tiled=True),
        lax.all_gather(q_proj, ("seq", "ctx", "exp"), axis=0, tiled=True),
        lax.all_gather(key_projection, ("seq", "ctx", "exp"), axis=0, tiled=True),
        lax.all_gather(value_projection, ("seq", "ctx", "exp"), axis=0, tiled=True),
        lax.all_gather(q_gain, ("seq", "ctx", "exp"), axis=0, tiled=True),
        lax.all_gather(k_gain, ("seq", "ctx", "exp"), axis=0, tiled=True),
        lax.all_gather(o_proj, ("seq", "ctx", "exp"), axis=0, tiled=True),
        lax.all_gather(mlp_gain, ("seq", "ctx", "exp"), axis=0, tiled=True),
    )
    gain_attn, w_query, key_weight, value_weight, gain_query, gain_key, w_out, gain_mlp = dense_full
    w_gate, w_up, w_down = (
        lax.all_gather(gate_proj, ("seq", "ctx"), axis=1, tiled=True),
        lax.all_gather(up_proj, ("seq", "ctx"), axis=1, tiled=True),
        lax.all_gather(down_proj, ("seq", "ctx"), axis=1, tiled=True),
    )
    hidden = residual_in[0].astype(jnp.float32)
    seg_all = segments[0]
    seg_mine = lax.dynamic_slice_in_dim(seg_all, span_index * token_count, token_count)
    valid_rows = (seg_mine > 0).astype(jnp.float32)[:, None]
    positions = span_index * token_count + jnp.arange(token_count, dtype=jnp.int32)
    cosine_table, sine_values = rope_tables(positions)
    inv_attn = lax.rsqrt(jnp.mean(hidden * hidden, axis=-1, keepdims=True) + EPS)
    normalized_input = (hidden * inv_attn * gain_attn.astype(jnp.float32)).astype(jnp.bfloat16)
    q_raw = jnp.dot(normalized_input, w_query, preferred_element_type=jnp.float32).reshape(
        token_count, QUERY_HEADS, HEAD_DIM
    )
    unrotated_keys = jnp.dot(
        normalized_input, key_weight, preferred_element_type=jnp.float32
    ).reshape(token_count, KEY_VALUE_HEADS, HEAD_DIM)
    value_rows = jnp.dot(normalized_input, value_weight, preferred_element_type=jnp.float32).astype(
        jnp.bfloat16
    )
    inv_query = lax.rsqrt(jnp.mean(q_raw * q_raw, axis=-1, keepdims=True) + EPS)
    inv_key = lax.rsqrt(jnp.mean(unrotated_keys * unrotated_keys, axis=-1, keepdims=True) + EPS)
    gain_query_f = gain_query.astype(jnp.float32)
    gain_key_f = gain_key.astype(jnp.float32)
    query_rows = rotate(q_raw * inv_query * gain_query_f, cosine_table, sine_values).astype(
        jnp.bfloat16
    )
    key_rows = (
        rotate(unrotated_keys * inv_key * gain_key_f, cosine_table, sine_values)
        .astype(jnp.bfloat16)
        .reshape(token_count, KEY_VALUE_HEADS * HEAD_DIM)
    )
    full_keys, full_values = (
        lax.all_gather(key_rows, "ctx", axis=0, tiled=True),
        lax.all_gather(value_rows, "ctx", axis=0, tiled=True),
    )
    key_pos = jnp.arange(sequence_length, dtype=jnp.int32)
    allowed = (seg_mine[:, None] == seg_all[None, :]) & (positions[:, None] >= key_pos[None, :])
    grouped_queries = query_rows.reshape(token_count, KEY_VALUE_HEADS, heads_per_group, HEAD_DIM)
    key_head_rows = full_keys.reshape(sequence_length, KEY_VALUE_HEADS, HEAD_DIM)
    value_head_rows = full_values.reshape(sequence_length, KEY_VALUE_HEADS, HEAD_DIM)

    def head_scores(shared_head):
        raw_scores = (
            jnp.einsum(
                "qgd,kd->gqk",
                grouped_queries[:, shared_head],
                key_head_rows[:, shared_head],
                preferred_element_type=jnp.float32,
            )
            * score_scale
        )
        return jnp.where(allowed[None], raw_scores, MASKED)

    mixed_parts = []
    log_totals = []
    for shared_head in range(KEY_VALUE_HEADS):
        scores = head_scores(shared_head)
        row_peak = jnp.max(scores, axis=-1, keepdims=True)
        exp_scores = jnp.exp(scores - row_peak)
        row_total = jnp.sum(exp_scores, axis=-1, keepdims=True)
        probs_low = (exp_scores / row_total).astype(jnp.bfloat16)
        mixed_parts.append(
            jnp.einsum(
                "gqk,kd->qgd",
                probs_low,
                value_head_rows[:, shared_head],
                preferred_element_type=jnp.float32,
            )
        )
        log_totals.append(row_peak + jnp.log(row_total))
    mixed_heads = jnp.stack(mixed_parts, 1).reshape(token_count, QUERY_HEADS * HEAD_DIM)
    mixed_low = (mixed_heads * valid_rows).astype(jnp.bfloat16)
    attn_out = jnp.dot(mixed_low, w_out, preferred_element_type=jnp.float32)
    middle = hidden + attn_out
    gain_mlp_f = gain_mlp.astype(jnp.float32)
    inv_mlp = lax.rsqrt(jnp.mean(middle * middle, axis=-1, keepdims=True) + EPS)
    normed_mlp = (middle * inv_mlp * gain_mlp_f).astype(jnp.bfloat16)
    route_ids = routes[0]
    hit_counts = (
        (route_ids[:, :, None] == jnp.arange(expert_count, dtype=jnp.int32)[None, None, :])
        .astype(jnp.int32)
        .sum(1)
    )
    earlier = jnp.cumsum(hit_counts, axis=0) - hit_counts
    slot_ids = jnp.take_along_axis(earlier, route_ids, axis=1)
    targets = (route_ids * capacity + slot_ids).reshape(-1)
    token_ids = jnp.broadcast_to(
        jnp.arange(token_count, dtype=jnp.int32)[:, None], route_ids.shape
    ).reshape(-1)
    slot_token = (
        jnp.full((expert_count * capacity,), token_count, jnp.int32).at[targets].set(token_ids)
    )
    gate_rows = gates[0]
    slot_gate = (
        jnp.zeros((expert_count * capacity,), jnp.float32).at[targets].set(gate_rows.reshape(-1))
    )
    padded = jnp.concatenate([normed_mlp, jnp.zeros((1, model_width), jnp.bfloat16)], 0)
    outgoing = padded[slot_token].reshape(owner_count, local_experts, capacity, model_width)
    incoming = lax.all_to_all(outgoing, "exp", split_axis=0, concat_axis=0, tiled=True)
    gate_part = jnp.einsum("serd,edf->serf", incoming, w_gate, preferred_element_type=jnp.float32)
    up_part = jnp.einsum("serd,edf->serf", incoming, w_up, preferred_element_type=jnp.float32)
    product = (jax.nn.silu(gate_part) * up_part).astype(jnp.bfloat16)
    result = jnp.einsum(
        "serf,efd->serd", product, w_down, preferred_element_type=jnp.float32
    ).astype(jnp.bfloat16)
    returned_rows = lax.all_to_all(result, "exp", split_axis=0, concat_axis=0, tiled=True)
    picked = returned_rows.reshape(expert_count * capacity, model_width)[targets].reshape(
        token_count, route_count, model_width
    )
    expert_out = jnp.sum(picked.astype(jnp.float32) * gate_rows[:, :, None], axis=1)
    final_out = middle + expert_out
    stat_sums = lax.psum(
        (
            jnp.sum(hidden * hidden * valid_rows),
            jnp.sum(attn_out * attn_out * valid_rows),
            jnp.sum(expert_out * expert_out * valid_rows),
            jnp.sum(valid_rows),
        ),
        ("seq", "ctx", "exp"),
    )
    rms_stats = jnp.sqrt(
        jnp.stack([stat_sums[0], stat_sums[1], stat_sums[2]]) / (stat_sums[3] * model_width)
    )
    cotangent = out_grad[0].astype(jnp.float32)
    expert_shards, anchor_one = lax.optimization_barrier(
        ((gate_proj, up_proj, down_proj), expert_out)
    )
    w_gate, w_up, w_down = (
        lax.all_gather(expert_shards[0], ("seq", "ctx"), axis=1, tiled=True),
        lax.all_gather(expert_shards[1], ("seq", "ctx"), axis=1, tiled=True),
        lax.all_gather(expert_shards[2], ("seq", "ctx"), axis=1, tiled=True),
    )
    cot_padded = jnp.concatenate([cotangent, jnp.zeros((1, model_width), jnp.float32)], 0)
    grad_out = (
        (cot_padded[slot_token] * slot_gate[:, None])
        .astype(jnp.bfloat16)
        .reshape(owner_count, local_experts, capacity, model_width)
    )
    grad_in = lax.all_to_all(grad_out, "exp", split_axis=0, concat_axis=0, tiled=True)
    sigmoid_gate = jax.nn.sigmoid(gate_part)
    silu_gate = gate_part * sigmoid_gate
    product_low = (silu_gate * up_part).astype(jnp.bfloat16)
    grad_product = jnp.einsum("serd,efd->serf", grad_in, w_down, preferred_element_type=jnp.float32)
    grad_gate = (
        grad_product * up_part * sigmoid_gate * (1.0 + gate_part * (1.0 - sigmoid_gate))
    ).astype(jnp.bfloat16)
    grad_up = (grad_product * silu_gate).astype(jnp.bfloat16)
    down_grad = jnp.einsum(
        "serf,serd->efd", product_low, grad_in, preferred_element_type=jnp.float32
    )
    gate_grad = jnp.einsum(
        "serd,serf->edf", incoming, grad_gate, preferred_element_type=jnp.float32
    )
    up_grad = jnp.einsum("serd,serf->edf", incoming, grad_up, preferred_element_type=jnp.float32)
    grad_rows = (
        jnp.einsum("serf,edf->serd", grad_gate, w_gate, preferred_element_type=jnp.float32)
        + jnp.einsum("serf,edf->serd", grad_up, w_up, preferred_element_type=jnp.float32)
    ).astype(jnp.bfloat16)
    grad_back = lax.all_to_all(grad_rows, "exp", split_axis=0, concat_axis=0, tiled=True)
    gate_grad, up_grad, down_grad = (
        lax.psum_scatter(
            gate_grad.astype(jnp.bfloat16), ("seq", "ctx"), scatter_dimension=1, tiled=True
        ).astype(jnp.float32),
        lax.psum_scatter(
            up_grad.astype(jnp.bfloat16), ("seq", "ctx"), scatter_dimension=1, tiled=True
        ).astype(jnp.float32),
        lax.psum_scatter(
            down_grad.astype(jnp.bfloat16), ("seq", "ctx"), scatter_dimension=1, tiled=True
        ).astype(jnp.float32),
    )
    grad_normed_mlp = jnp.sum(
        grad_back.reshape(expert_count * capacity, model_width)[targets]
        .reshape(token_count, route_count, model_width)
        .astype(jnp.float32),
        axis=1,
    )
    mlp_gain_grad = jnp.sum(grad_normed_mlp * middle * inv_mlp, axis=0)
    grad_middle = cotangent + norm_back(grad_normed_mlp, middle, inv_mlp, gain_mlp_f)
    dense_shards, anchor_two = lax.optimization_barrier(
        (
            (attn_gain, q_proj, key_projection, value_projection, q_gain, k_gain, o_proj, mlp_gain),
            grad_middle,
        )
    )
    dense_back = (
        lax.all_gather(dense_shards[0], ("seq", "ctx", "exp"), axis=0, tiled=True),
        lax.all_gather(dense_shards[1], ("seq", "ctx", "exp"), axis=0, tiled=True),
        lax.all_gather(dense_shards[2], ("seq", "ctx", "exp"), axis=0, tiled=True),
        lax.all_gather(dense_shards[3], ("seq", "ctx", "exp"), axis=0, tiled=True),
        lax.all_gather(dense_shards[4], ("seq", "ctx", "exp"), axis=0, tiled=True),
        lax.all_gather(dense_shards[5], ("seq", "ctx", "exp"), axis=0, tiled=True),
        lax.all_gather(dense_shards[6], ("seq", "ctx", "exp"), axis=0, tiled=True),
        lax.all_gather(dense_shards[7], ("seq", "ctx", "exp"), axis=0, tiled=True),
    )
    gain_attn, w_query, key_weight, value_weight, gain_query, gain_key, w_out, gain_mlp = dense_back
    gain_query_f = gain_query.astype(jnp.float32)
    gain_key_f = gain_key.astype(jnp.float32)
    grad_attn = grad_middle.astype(jnp.bfloat16)
    o_proj_grad = contract_rows(mixed_low, grad_attn)
    mixture_gradient = contract_cols(grad_attn, w_out).astype(jnp.bfloat16) * valid_rows.astype(
        jnp.bfloat16
    )
    group_gradient = mixture_gradient.reshape(
        token_count, KEY_VALUE_HEADS, heads_per_group, HEAD_DIM
    )
    grad_q_parts = []
    key_part_gradient = []
    value_part_gradient = []
    for shared_head in range(KEY_VALUE_HEADS):
        scores = head_scores(shared_head)
        probs = jnp.exp(scores - log_totals[shared_head])
        grad_head = group_gradient[:, shared_head]
        grad_probs = jnp.einsum(
            "qgd,kd->gqk",
            grad_head,
            value_head_rows[:, shared_head],
            preferred_element_type=jnp.float32,
        )
        inner_sum = jnp.sum(probs * grad_probs, axis=-1, keepdims=True)
        grad_scores = (probs * (grad_probs - inner_sum)).astype(jnp.bfloat16)
        grad_q_parts.append(
            jnp.einsum(
                "gqk,kd->qgd",
                grad_scores,
                key_head_rows[:, shared_head],
                preferred_element_type=jnp.float32,
            )
            * score_scale
        )
        key_part_gradient.append(
            jnp.einsum(
                "gqk,qgd->kd",
                grad_scores,
                grouped_queries[:, shared_head],
                preferred_element_type=jnp.float32,
            )
            * score_scale
        )
        value_part_gradient.append(
            jnp.einsum(
                "gqk,qgd->kd",
                probs.astype(jnp.bfloat16),
                grad_head,
                preferred_element_type=jnp.float32,
            )
        )
    grad_queries = jnp.stack(grad_q_parts, 1).reshape(token_count, QUERY_HEADS, HEAD_DIM)
    full_key_gradient = jnp.stack(key_part_gradient, 1).reshape(
        sequence_length, KEY_VALUE_HEADS * HEAD_DIM
    )
    full_value_gradient = jnp.stack(value_part_gradient, 1).reshape(
        sequence_length, KEY_VALUE_HEADS * HEAD_DIM
    )
    key_gradient, grad_values = (
        lax.psum_scatter(
            full_key_gradient.astype(jnp.bfloat16), "ctx", scatter_dimension=0, tiled=True
        ).astype(jnp.float32),
        lax.psum_scatter(
            full_value_gradient.astype(jnp.bfloat16), "ctx", scatter_dimension=0, tiled=True
        ).astype(jnp.float32),
    )
    grad_qn = inverse_rotation(grad_queries, cosine_table, sine_values)
    q_gain_grad = jnp.sum(grad_qn * q_raw * inv_query, axis=(0, 1))
    grad_q_raw = (
        norm_back(grad_qn, q_raw, inv_query, gain_query_f)
        .astype(jnp.bfloat16)
        .reshape(token_count, QUERY_HEADS * HEAD_DIM)
    )
    normed_key_gradient = inverse_rotation(
        key_gradient.reshape(token_count, KEY_VALUE_HEADS, HEAD_DIM), cosine_table, sine_values
    )
    k_gain_grad = jnp.sum(normed_key_gradient * unrotated_keys * inv_key, axis=(0, 1))
    grad_k_raw = (
        norm_back(normed_key_gradient, unrotated_keys, inv_key, gain_key_f)
        .astype(jnp.bfloat16)
        .reshape(token_count, KEY_VALUE_HEADS * HEAD_DIM)
    )
    grad_v_low = grad_values.astype(jnp.bfloat16)
    grad_normed = (
        contract_cols(grad_q_raw, w_query)
        + contract_cols(grad_k_raw, key_weight)
        + contract_cols(grad_v_low, value_weight)
    )
    q_proj_grad = contract_rows(normalized_input, grad_q_raw)
    k_proj_grad = contract_rows(normalized_input, grad_k_raw)
    v_proj_grad = contract_rows(normalized_input, grad_v_low)
    attn_gain_grad = jnp.sum(grad_normed * hidden * inv_attn, axis=0)
    grad_hidden = grad_middle + norm_back(
        grad_normed, hidden, inv_attn, gain_attn.astype(jnp.float32)
    )
    reduced = (
        lax.psum_scatter(attn_gain_grad, ("seq", "ctx", "exp"), scatter_dimension=0, tiled=True),
        lax.psum_scatter(q_proj_grad, ("seq", "ctx", "exp"), scatter_dimension=0, tiled=True),
        lax.psum_scatter(k_proj_grad, ("seq", "ctx", "exp"), scatter_dimension=0, tiled=True),
        lax.psum_scatter(v_proj_grad, ("seq", "ctx", "exp"), scatter_dimension=0, tiled=True),
        lax.psum_scatter(q_gain_grad, ("seq", "ctx", "exp"), scatter_dimension=0, tiled=True),
        lax.psum_scatter(k_gain_grad, ("seq", "ctx", "exp"), scatter_dimension=0, tiled=True),
        lax.psum_scatter(o_proj_grad, ("seq", "ctx", "exp"), scatter_dimension=0, tiled=True),
        lax.psum_scatter(mlp_gain_grad, ("seq", "ctx", "exp"), scatter_dimension=0, tiled=True),
    )
    return (
        final_out.astype(jnp.bfloat16)[None],
        grad_hidden.astype(jnp.bfloat16)[None],
        reduced[0],
        reduced[1],
        reduced[2],
        reduced[3],
        reduced[4],
        reduced[5],
        reduced[6],
        reduced[7],
        gate_grad,
        up_grad,
        down_grad,
        rms_stats,
    )


def solution(mesh):
    in_specs = (
        P(("seq", "exp"), "ctx", None),
        P(("seq", "exp"), None),
        P(("seq", "exp"), "ctx", None),
        P(("seq", "exp"), "ctx", None),
        P(("seq", "ctx", "exp")),
        P(("seq", "ctx", "exp"), None),
        P(("seq", "ctx", "exp"), None),
        P(("seq", "ctx", "exp"), None),
        P(("seq", "ctx", "exp")),
        P(("seq", "ctx", "exp")),
        P(("seq", "ctx", "exp"), None),
        P(("seq", "ctx", "exp")),
        P("exp", ("seq", "ctx"), None),
        P("exp", ("seq", "ctx"), None),
        P("exp", ("seq", "ctx"), None),
        P(("seq", "exp"), "ctx", None),
    )
    out_specs = (
        P(("seq", "exp"), "ctx", None),
        P(("seq", "exp"), "ctx", None),
        P(("seq", "ctx", "exp")),
        P(("seq", "ctx", "exp"), None),
        P(("seq", "ctx", "exp"), None),
        P(("seq", "ctx", "exp"), None),
        P(("seq", "ctx", "exp")),
        P(("seq", "ctx", "exp")),
        P(("seq", "ctx", "exp"), None),
        P(("seq", "ctx", "exp")),
        P("exp", ("seq", "ctx"), None),
        P("exp", ("seq", "ctx"), None),
        P("exp", ("seq", "ctx"), None),
        P(),
    )
    return jax.shard_map(
        on_device, mesh=mesh, in_specs=in_specs, out_specs=out_specs, check_vma=False
    )
```

profile of v0, /device:TPU:0, one launch (start us, length us, event | category | flops | bytes accessed | tf_op | source)
XLA Modules:
  0.0 5059.1 jit_solution(4075278602574568390)
XLA Ops:
  12.1 42.3 all-reduce.15
  57.3 12.8 all-gather.17.cloned.1.call-done
  75.8 52.6 %all-gather.21.cloned.1.call-done = bf16[2048,512]{1,0:T(8,128)(2,1)} async-done(((bf16[64,512]{1,0:T(8,128)(2,1)}), bf16[2048,512]{1,0:T(8,128)(2,1)}) %all-gather.21.cloned.1.call-update) | async-done | bytes 2097168 | tf_op jit(solution)/shard_map/all_gather | solution.py:93
  145.7 26.7 gather_fusion.4
  172.5 15.5 scatter_custom_fusion
  191.6 76.9 %all-gather.25.cloned.1.call-done = bf16[2048,4096]{1,0:T(8,128)(2,1)} async-done(((bf16[64,4096]{1,0:T(8,128)(2,1)}), bf16[2048,4096]{1,0:T(8,128)(2,1)}) %all-gather.25.cloned.1.call-update) | async-done | bytes 16777232 | tf_op jit(solution)/shard_map/all_gather | solution.py:92
  268.5 22.7 copy.212
  291.2 12.1 multiply_reduce_fusion.2
  314.9 10.4 fusion.190
  356.0 8.9 fusion.105
  373.1 9.2 fusion.106
  390.5 8.4 fusion.22
  420.1 15.3 multiply_reduce_fusion.7
  438.0 18.2 gather_fusion
  464.4 15.6 all-gather.29.cloned.1.call-done
  480.0 392.3 %all-to-all-done = bf16[4,4,288,2048]{3,2,1,0:T(8,128)(2,1)} async-done(((bf16[4,4,288,2048]{3,2,1,0:T(8,128)(2,1)}), bf16[4,4,288,2048]{3,2,1,0:T(8,128)(2,1)}, u32[]{:S(2)}, u32[]{:S(2)}) %all-to-all-start) | async-done | bytes 18874400 | tf_op jit(solution)/shard_map/all_to_all | solution.py:202
  872.3 23.6 fusion.20
  896.0 28.8 fusion.30
  924.7 23.6 convert_bitcast_fusion
  948.3 16.9 copy.235
  973.0 407.6 %all-to-all-done.1 = bf16[4,4,288,2048]{3,2,1,0:T(8,128)(2,1)} async-done(((bf16[4,4,288,2048]{3,2,1,0:T(8,128)(2,1)}), bf16[4,4,288,2048]{3,2,1,0:T(8,128)(2,1)}, u32[]{:S(2)}, u32[]{:S(2)}) %all-to-all-start.1) | async-done | bytes 18874400 | tf_op jit(solution)/shard_map/all_to_all | solution.py:209
  1380.6 40.1 gather_fusion.1
  1420.8 17.0 fusion
  1441.5 36.6 gather_fusion.2
  1478.3 15.5 scatter_custom_fusion.1
  1493.9 21.1 multiply_convert_fusion
  1523.6 405.6 %all-to-all-done.2 = bf16[4,4,288,2048]{3,2,1,0:T(8,128)(2,1)} async-done(((bf16[4,4,288,2048]{3,2,1,0:T(8,128)(2,1)}), bf16[4,4,288,2048]{3,2,1,0:T(8,128)(2,1)}, u32[]{:S(2)}, u32[]{:S(2)}) %all-to-all-start.2) | async-done | bytes 18874400 | tf_op jit(solution)/shard_map/all_to_all | solution.py:242
  1929.2 29.4 fusion.29
  1958.7 23.8 fusion.41
  1982.5 28.8 fusion.1
  2011.3 9.3 copy.239
  2020.5 412.7 %all_to_all.20 = bf16[4,4,288,2048]{3,2,1,0:T(8,128)(2,1)} all-to-all(bf16[4,4,288,2048]{3,2,1,0:T(8,128)(2,1)S(1)} %copy.239), channel_id=1, replica_groups=mesh['seq'=4,'ctx'=2,'exp'=4] {'exp'}, dimensions={0} | all-to-all | bytes 37748736 | tf_op jit(solution)/shard_map/all_to_all | solution.py:262
  2433.3 40.1 gather_fusion.3
  2473.4 13.9 convert_reduce_fusion
  2496.3 113.3 %all-gather.41.cloned.1.call-done = bf16[4096,2048]{1,0:T(8,128)(2,1)} async-done(((bf16[128,2048]{1,0:T(8,128)(2,1)}), bf16[4096,2048]{1,0:T(8,128)(2,1)}) %all-gather.41.cloned.1.call-update) | async-done | bytes 16777232 | tf_op jit(solution)/shard_map/all_gather | solution.py:295
  2609.6 14.1 fusion.93
  2626.9 9.1 fusion.154
  2637.8 10.7 fusion.2
  2648.5 12.4 fusion.4
  2670.7 10.7 fusion.5
  2681.4 12.2 fusion.7
  2703.3 8.8 fusion.8
  2712.1 12.2 fusion.10
  2734.1 9.0 fusion.11
  2759.4 9.4 fusion.151
  2768.9 9.6 fusion.148
  2782.6 24.0 bitcast_convert_fusion
  2806.7 24.6 bitcast_convert_fusion.2
  2831.4 24.6 bitcast_convert_fusion.1
  2858.9 37.3 all-reduce.14
  2910.1 21.2 fusion.160
  2954.6 8.8 fusion.187
  2963.4 9.2 multiply_reduce_fusion
  2980.1 18.2 fusion.102
  3005.8 84.2 %reduce-scatter.24.cloned.1.call-done = bf16[4,256,768]{2,1,0:T(8,128)(2,1)} async-done(((bf16[4,2048,768]{2,1,0:T(8,128)(2,1)}), bf16[4,256,768]{2,1,0:T(8,128)(2,1)}) %reduce-scatter.24.cloned.1.call-update) | async-done | bytes 1572880 | tf_op jit(solution)/shard_map/reduce_scatter | solution.py:267
  3093.3 56.1 %all-gather.47.cloned.1.call-done = bf16[2048,512]{1,0:T(8,128)(2,1)} async-done(((bf16[64,512]{1,0:T(8,128)(2,1)}), bf16[2048,512]{1,0:T(8,128)(2,1)}) %all-gather.47.cloned.1.call-update) | async-done | bytes 2097168 | tf_op jit(solution)/shard_map/all_gather | solution.py:292
  3154.2 53.3 %all-gather.45.cloned.1.call-done = bf16[2048,512]{1,0:T(8,128)(2,1)} async-done(((bf16[64,512]{1,0:T(8,128)(2,1)}), bf16[2048,512]{1,0:T(8,128)(2,1)}) %all-gather.45.cloned.1.call-update) | async-done | bytes 2097168 | tf_op jit(solution)/shard_map/all_gather | solution.py:291
  3212.3 111.9 %all-gather.43.cloned.1.call-done = bf16[2048,4096]{1,0:T(8,128)(2,1)} async-done(((bf16[64,4096]{1,0:T(8,128)(2,1)}), bf16[2048,4096]{1,0:T(8,128)(2,1)}) %all-gather.43.cloned.1.call-update) | async-done | bytes 16777232 | tf_op jit(solution)/shard_map/all_gather | solution.py:290
  3324.2 18.6 fusion.90
  3342.8 40.0 all-reduce.13
  3394.2 80.8 %reduce-scatter.16.cloned.1.call-done = f32[64,512]{1,0:T(8,128)} async-done(((f32[2048,512]{1,0:T(8,128)}), f32[64,512]{1,0:T(8,128)}) %reduce-scatter.16.cloned.1.call-update) | async-done | bytes 131088 | tf_op jit(solution)/shard_map/reduce_scatter | solution.py:397
  3475.0 151.6 %reduce-scatter.18.cloned.1.call-done = f32[64,512]{1,0:T(8,128)} async-done(((f32[2048,512]{1,0:T(8,128)}), f32[64,512]{1,0:T(8,128)}) %reduce-scatter.18.cloned.1.call-update) | async-done | bytes 131088 | tf_op jit(solution)/shard_map/reduce_scatter | solution.py:398
  3626.6 711.5 %reduce-scatter.20.cloned.1.call-done = f32[128,2048]{1,0:T(8,128)} async-done(((f32[4096,2048]{1,0:T(8,128)}), f32[128,2048]{1,0:T(8,128)}) %reduce-scatter.20.cloned.1.call-update) | async-done | bytes 1048592 | tf_op jit(solution)/shard_map/reduce_scatter | solution.py:401
  4338.2 714.2 %reduce-scatter.14.cloned.1.call-done = f32[64,4096]{1,0:T(8,128)} async-done(((f32[2048,4096]{1,0:T(8,128)}), f32[64,4096]{1,0:T(8,128)}) %reduce-scatter.14.cloned.1.call-update) | async-done | bytes 1048592 | tf_op jit(solution)/shard_map/reduce_scatter | solution.py:396
  (433 shorter events, 286.6 us)
Async XLA Ops:
  7.2 63.0 %all-gather.17.cloned.1.call-start = ((), (), s32[]{:S(2)}) async-start(), calls=%async_computation.13 | async-start | bytes 2162688 | tf_op jit(solution)/shard_map/all_gather | solution.py:94
  7.9 120.5 %all-gather.21.cloned.1.call-start = ((), (), s32[]{:S(2)}) async-start(), calls=%async_computation.15 | async-start | bytes 2162688 | tf_op jit(solution)/shard_map/all_gather | solution.py:93
  8.7 180.5 %all-gather.19.cloned.1.call-start = ((), (), s32[]{:S(2)}) async-start(), calls=%async_computation.14 | async-start | bytes 1572864 | tf_op jit(solution)/shard_map/all_gather | solution.py:137
  54.4 236.7 %copy-start.36 = (f32[2048]{0:T(1024)}, f32[2048]{0:T(1024)S(1)}, u32[]{:S(2)}) copy-start(f32[2048]{0:T(1024)S(1)} %convert_element_type.223) | copy-start | bytes 24580
  54.4 77.9 %copy-start.1 = (bf16[1,512,2048]{2,1,0:T(8,128)(2,1)S(1)}, bf16[1,512,2048]{2,1,0:T(8,128)(2,1)}, u32[]{:S(2)}) copy-start(bf16[1,512,2048]{2,1,0:T(8,128)(2,1)} %param.16) | copy-start | bytes 6291460
  57.3 233.9 %copy-start.59 = (f32[512]{0:T(512)}, f32[512]{0:T(512)S(1)}, u32[]{:S(2)}) copy-start(f32[512]{0:T(512)S(1)} %get-tuple-element.88) | copy-start | bytes 6148
  74.5 194.0 %all-gather.25.cloned.1.call-start = ((), (), s32[]{:S(2)}) async-start(), calls=%async_computation.17 | async-start | bytes 17301504 | tf_op jit(solution)/shard_map/all_gather | solution.py:92
  75.1 239.8 %all-gather.23.cloned.1.call-start = ((), (), s32[]{:S(2)}) async-start(), calls=%async_computation.16 | async-start | bytes 1572864 | tf_op jit(solution)/shard_map/all_gather | solution.py:136
  75.8 233.4 %copy-start.15 = (f32[512,128]{0,1:T(8,128)}, f32[512,128]{0,1:T(8,128)S(1)}, u32[]{:S(2)}) copy-start(f32[512,128]{0,1:T(8,128)S(1)} %get-tuple-element.117) | copy-start | bytes 786436
  75.8 233.4 %copy-start.19 = (f32[512,128]{0,1:T(8,128)}, f32[512,128]{0,1:T(8,128)S(1)}, u32[]{:S(2)}) copy-start(f32[512,128]{0,1:T(8,128)S(1)} %get-tuple-element.118) | copy-start | bytes 786436
  137.5 282.6 %all-gather.27.cloned.1.call-start = ((), (), s32[]{:S(2)}) async-start(), calls=%async_computation.18 | async-start | bytes 17301504 | tf_op jit(solution)/shard_map/all_gather | solution.py:97
  138.1 341.9 %all-gather.29.cloned.1.call-start = ((), (), s32[]{:S(2)}) async-start(), calls=%async_computation.19 | async-start | bytes 14155776 | tf_op jit(solution)/shard_map/all_gather | solution.py:102
  138.8 757.1 %all-gather.31.cloned.1.call-start = ((), (), s32[]{:S(2)}) async-start(), calls=%async_computation.20 | async-start | bytes 14155776 | tf_op jit(solution)/shard_map/all_gather | solution.py:103
  172.5 118.7 %copy-start.62 = (s32[4096,1]{0,1:T(1,128)}, s32[4096,1]{0,1:T(1,128)S(1)}, u32[]{:S(2)}) copy-start(s32[4096,1]{0,1:T(1,128)S(1)} %compare_select_fusion) | copy-start | bytes 49156
  325.2 30.8 copy-start.46
  332.8 40.3 copy-start.48
  340.2 58.6 %copy-start.50 = (f32[8,512]{1,0:T(8,128)}, f32[8,512]{1,0:T(8,128)S(1)}, u32[]{:S(2)}) copy-start(f32[8,512]{1,0:T(8,128)S(1)} %get-tuple-element.101) | copy-start | bytes 49156
  347.9 59.2 %copy-start.52 = (f32[8,512]{1,0:T(8,128)}, f32[8,512]{1,0:T(8,128)S(1)}, u32[]{:S(2)}) copy-start(f32[8,512]{1,0:T(8,128)S(1)} %get-tuple-element.103) | copy-start | bytes 49156
  456.3 416.0 %all-to-all-start = ((bf16[4,4,288,2048]{3,2,1,0:T(8,128)(2,1)}), bf16[4,4,288,2048]{3,2,1,0:T(8,128)(2,1)}, u32[]{:S(2)}, u32[]{:S(2)}) async-start(bf16[4,4,288,2048]{3,2,1,0:T(8,128)(2,1)} %bitcast.545), calls=%async_computation | async-start | bytes 37748736 | tf_op jit(solution)/shard_map/all_to_all | solution.py:202
  463.6 461.1 %all-gather.33.cloned.1.call-start = ((), (), s32[]{:S(2)}) async-start(), calls=%async_computation.21 | async-start | bytes 14155776 | tf_op jit(solution)/shard_map/all_gather | solution.py:104
  965.2 415.4 %all-to-all-start.1 = ((bf16[4,4,288,2048]{3,2,1,0:T(8,128)(2,1)}), bf16[4,4,288,2048]{3,2,1,0:T(8,128)(2,1)}, u32[]{:S(2)}, u32[]{:S(2)}) async-start(bf16[4,4,288,2048]{3,2,1,0:T(8,128)(2,1)} %copy.235), calls=%async_computation.1 | async-start | bytes 37748736 | tf_op jit(solution)/shard_map/all_to_all | solution.py:209
  972.7 956.5 %all-gather.37.cloned.1.call-start = ((), (), s32[]{:S(2)}) async-start(), calls=%async_computation.23 | async-start | bytes 14155776 | tf_op jit(solution)/shard_map/all_gather | solution.py:234
  973.0 407.7 %copy-start.54 = (s32[4096]{0:T(1024)}, s32[4096]{0:T(1024)S(1)}, u32[]{:S(2)}) copy-start(s32[4096]{0:T(1024)S(1)} %broadcast_clamp_fusion) | copy-start | bytes 49156
  1437.8 520.9 %all-gather.35.cloned.1.call-start = ((), (), s32[]{:S(2)}) async-start(), calls=%async_computation.22 | async-start | bytes 14155776 | tf_op jit(solution)/shard_map/all_gather | solution.py:232
  1515.0 414.3 %all-to-all-start.2 = ((bf16[4,4,288,2048]{3,2,1,0:T(8,128)(2,1)}), bf16[4,4,288,2048]{3,2,1,0:T(8,128)(2,1)}, u32[]{:S(2)}, u32[]{:S(2)}) async-start(bf16[4,4,288,2048]{3,2,1,0:T(8,128)(2,1)} %multiply_convert_fusion), calls=%async_computation.2 | async-start | bytes 37748736 | tf_op jit(solution)/shard_map/all_to_all | solution.py:242
  1523.0 459.5 %all-gather.39.cloned.1.call-start = ((), (), s32[]{:S(2)}) async-start(), calls=%async_computation.24 | async-start | bytes 14155776 | tf_op jit(solution)/shard_map/all_gather | solution.py:233
  1523.6 1086.0 %all-gather.41.cloned.1.call-start = ((), (), s32[]{:S(2)}) async-start(), calls=%async_computation.25 | async-start | bytes 17301504 | tf_op jit(solution)/shard_map/all_gather | solution.py:295
  2020.5 412.7 %copy-start.55 = (s32[4096]{0:T(1024)S(1)}, s32[4096]{0:T(1024)}, u32[]{:S(2)}) copy-start(s32[4096]{0:T(1024)} %copy-done.54) | copy-start | bytes 49156
  2490.3 119.2 %copy-start.82 = (bf16[512]{0:T(512)(128)(2,1)S(1)}, bf16[512]{0:T(512)(128)(2,1)}, u32[]{:S(2)}) copy-start(bf16[512]{0:T(512)(128)(2,1)} %get-tuple-element.89) | copy-start | bytes 3076
  2496.0 400.3 %reduce-scatter.10.cloned.1.call-start = ((), (), s32[]{:S(2)}) async-start(), calls=%async_computation.27 | async-start | bytes 1572864 | tf_op jit(solution)/shard_map/reduce_scatter | solution.py:358
  2496.2 185.2 %copy-start.34 = (f32[8,512]{1,0:T(8,128)}, f32[8,512]{1,0:T(8,128)S(1)}, u32[]{:S(2)}) copy-start(f32[8,512]{1,0:T(8,128)S(1)} %log_add_fusion.1) | copy-start | bytes 49156
  2496.2 215.9 %copy-start.33 = (f32[8,512]{1,0:T(8,128)}, f32[8,512]{1,0:T(8,128)S(1)}, u32[]{:S(2)}) copy-start(f32[8,512]{1,0:T(8,128)S(1)} %log_add_fusion.2) | copy-start | bytes 49156
  2648.5 22.1 slice-start.16
  2648.5 22.1 slice-start.17
  2648.5 22.1 slice-start.18
  2648.5 22.1 slice-start.19
  2681.3 22.0 slice-start.12
  2681.3 22.0 slice-start.13
  2681.3 22.0 slice-start.14
  2681.3 22.0 slice-start.15
  2712.1 21.9 slice-start.4
  2759.3 146.1 %reduce-scatter.12.cloned.1.call-start = ((), (), s32[]{:S(2)}) async-start(), calls=%async_computation.29 | async-start | bytes 1572864 | tf_op jit(solution)/shard_map/reduce_scatter | solution.py:361
  2782.6 215.8 %reduce-scatter.26.cloned.1.call-start = ((), (), s32[]{:S(2)}) async-start(), calls=%async_computation.37 | async-start | bytes 14155776 | tf_op jit(solution)/shard_map/reduce_scatter | solution.py:270
  2806.6 195.3 %reduce-scatter.22.cloned.1.call-start = ((), (), s32[]{:S(2)}) async-start(), calls=%async_computation.35 | async-start | bytes 14155776 | tf_op jit(solution)/shard_map/reduce_scatter | solution.py:264
  2831.3 258.6 %reduce-scatter.24.cloned.1.call-start = ((), (), s32[]{:S(2)}) async-start(), calls=%async_computation.36 | async-start | bytes 14155776 | tf_op jit(solution)/shard_map/reduce_scatter | solution.py:267
  2856.0 41.7 copy-start.13
  2856.0 41.7 copy-start.16
  2856.0 41.7 copy-start.43
  2856.0 43.6 copy-start.72
  2856.0 45.9 copy-start.3
  2856.0 45.8 copy-start.37
  2856.0 45.8 copy-start.60
  2856.1 293.3 %all-gather.47.cloned.1.call-start = ((), (), s32[]{:S(2)}) async-start(), calls=%async_computation.30 | async-start | bytes 2162688 | tf_op jit(solution)/shard_map/all_gather | solution.py:292
  2856.8 350.6 %all-gather.45.cloned.1.call-start = ((), (), s32[]{:S(2)}) async-start(), calls=%async_computation.28 | async-start | bytes 2162688 | tf_op jit(solution)/shard_map/all_gather | solution.py:291
  2857.4 466.8 %all-gather.43.cloned.1.call-start = ((), (), s32[]{:S(2)}) async-start(), calls=%async_computation.26 | async-start | bytes 17301504 | tf_op jit(solution)/shard_map/all_gather | solution.py:290
  2858.1 616.9 %reduce-scatter.16.cloned.1.call-start = ((), (), s32[]{:S(2)}) async-start(), calls=%async_computation.32 | async-start | bytes 4325376 | tf_op jit(solution)/shard_map/reduce_scatter | solution.py:397
  2905.4 721.2 %reduce-scatter.18.cloned.1.call-start = ((), (), s32[]{:S(2)}) async-start(), calls=%async_computation.33 | async-start | bytes 4325376 | tf_op jit(solution)/shard_map/reduce_scatter | solution.py:398
  2910.0 1428.2 %reduce-scatter.20.cloned.1.call-start = ((), (), s32[]{:S(2)}) async-start(), calls=%async_computation.34 | async-start | bytes 34603008 | tf_op jit(solution)/shard_map/reduce_scatter | solution.py:401
  2931.2 2121.1 %reduce-scatter.14.cloned.1.call-start = ((), (), s32[]{:S(2)}) async-start(), calls=%async_computation.31 | async-start | bytes 34603008 | tf_op jit(solution)/shard_map/reduce_scatter | solution.py:396
  2998.4 151.0 %copy-start.27 = (bf16[512,512]{0,1:T(8,128)(2,1)S(1)}, bf16[512,512]{0,1:T(8,128)(2,1)}, u32[]{:S(2)}) copy-start(bf16[512,512]{0,1:T(8,128)(2,1)} %reduce-scatter.12.cloned.1.call-done) | copy-start | bytes 1572868
  3001.9 205.6 %copy-start.22 = (bf16[512,4,128]{0,2,1:T(8,128)(2,1)S(1)}, bf16[512,4,128]{0,2,1:T(8,128)(2,1)}, u32[]{:S(2)}) copy-start(bf16[512,4,128]{0,2,1:T(8,128)(2,1)} %copy-done.21) | copy-start | bytes 1572868
  3093.3 231.0 %copy-start.78 = (f32[512]{0:T(512)S(1)}, f32[512]{0:T(512)}, u32[]{:S(2)}) copy-start(f32[512]{0:T(512)} %get-tuple-element.90) | copy-start | bytes 6148
  3212.3 130.6 %copy-start.73 = (f32[2048]{0:T(1024)S(1)}, f32[2048]{0:T(1024)}, u32[]{:S(2)}) copy-start(f32[2048]{0:T(1024)} %get-tuple-element.36) | copy-start | bytes 24580
  3212.3 176.0 %copy-start.81 = (f32[512]{0:T(512)S(1)}, f32[512]{0:T(512)}, u32[]{:S(2)}) copy-start(f32[512]{0:T(512)} %get-tuple-element.87) | copy-start | bytes 6148
  (80 other events, 616.0 us)
Sparse Core Ops, SparseCore 0:
  10.9 59.1 all-gather.16
  73.1 55.2 all-gather.20
  130.5 20.1 all-gather.18
  153.6 114.8 all-gather.24
  270.5 19.4 all-gather.22
  292.8 114.8 all-gather.26
  409.7 70.2 all-gather.28
  481.9 72.1 all-gather.30
  556.0 72.1 all-gather.32
  1437.9 70.9 all-gather.36
  1510.8 72.1 all-gather.34
  1584.7 72.1 all-gather.38
  2496.2 113.3 all-gather.40
  2759.5 18.4 reduce-scatter.9
  2782.7 18.4 reduce-scatter.11
  2806.7 91.5 reduce-scatter.25
  2901.7 92.3 reduce-scatter.21
  2997.5 92.3 reduce-scatter.23
  3092.8 56.4 all-gather.46
  3152.1 55.2 all-gather.44
  3210.4 113.7 all-gather.42
  3327.1 147.9 reduce-scatter.15
  3477.9 148.6 reduce-scatter.17
  3629.4 708.7 reduce-scatter.19
  4341.0 711.2 reduce-scatter.13
where the time goes:
time: 5070 us; the launch traced here: 5060 us
  waiting for transfers between devices  3450 us (68%)
  blocking collectives  532 us (10%)
  matrix products  522 us (10%)
  local copies, waits for them, and re-layouts  290 us (6%)
  other arithmetic  225 us (4%)
    reduce_scatter x1, waiting for transfers between devices, on_device(): lax.psum_scatter(q_proj_grad, ('seq', 'ctx', 'exp'), scatter_dimension=0,...  714 us
    reduce_scatter x1, waiting for transfers between devices, on_device(): lax.psum_scatter(o_proj_grad, ('seq', 'ctx', 'exp'), scatter_dimension=0,...  712 us
    all_to_all x1, blocking collectives, on_device(): lax.all_to_all(grad_rows, 'exp', split_axis=0, concat_axis=0, tiled=True)  413 us
    all_to_all x1, waiting for transfers between devices, on_device(): lax.all_to_all(result, 'exp', split_axis=0, concat_axis=0, tiled=True)  408 us
    all_to_all x1, waiting for transfers between devices, on_device(): lax.all_to_all(grad_out, 'exp', split_axis=0, concat_axis=0, tiled=True)  406 us
    all_to_all x1, waiting for transfers between devices, on_device(): lax.all_to_all(outgoing, 'exp', split_axis=0, concat_axis=0, tiled=True)  392 us
    reduce_scatter x1, waiting for transfers between devices, on_device(): lax.psum_scatter(v_proj_grad, ('seq', 'ctx', 'exp'), scatter_dimension=0,...  152 us
    unnamed x3, blocking collectives  120 us
  transfers between devices with their start and end apart: 28, of which 16 were waited for; matrix products, arithmetic and copies ran while one was open for 13% of the time, Pallas kernels for 0%

commit v1 on v0

v1 whole, which is shorter than its diff:
```python
import jax
import jax.numpy as jnp
from jax import lax
from jax.sharding import PartitionSpec as P

QUERY_HEADS = 32
KEY_VALUE_HEADS = 4
HEAD_DIM = 128


EPS = 1e-06
ROPE_BASE = 1000000.0
MASKED = -1e30


def contract_rows(first_op, second_op):
    return lax.dot_general(
        first_op, second_op, (((0,), (0,)), ((), ())), preferred_element_type=jnp.float32
    )


def contract_cols(first_op, second_op):
    return lax.dot_general(
        first_op, second_op, (((1,), (1,)), ((), ())), preferred_element_type=jnp.float32
    )


def rope_tables(positions):
    half_dim = HEAD_DIM // 2
    inverse = ROPE_BASE ** (-jnp.arange(half_dim, dtype=jnp.float32) * 2.0 / HEAD_DIM)
    angles = positions.astype(jnp.float32)[:, None] * inverse[None, :]
    cosine_table = jnp.cos(angles)
    sine_values = jnp.sin(angles)
    return (
        jnp.concatenate([cosine_table, cosine_table], -1),
        jnp.concatenate([sine_values, sine_values], -1),
    )


def rotate(vectors, cosine_table, sine_values):
    half_dim = vectors.shape[-1] // 2
    turned = jnp.concatenate([-vectors[..., half_dim:], vectors[..., :half_dim]], -1)
    return vectors * cosine_table[:, None, :] + turned * sine_values[:, None, :]


def inverse_rotation(gradient, cosine_table, sine_values):
    half_dim = gradient.shape[-1] // 2
    scaled = gradient * sine_values[:, None, :]
    return gradient * cosine_table[:, None, :] + jnp.concatenate(
        [scaled[..., half_dim:], -scaled[..., :half_dim]], -1
    )


def norm_back(gradient, source, inverse, gain_vec):
    scaled = gradient * gain_vec
    return inverse * scaled - source * inverse**3 * jnp.mean(
        scaled * source, axis=-1, keepdims=True
    )


def pick(core, first, second):
    return jnp.where(core == 0, first, second)


def column_halves(weight, core):
    width = weight.shape[1] // KEY_VALUE_HEADS
    parts = [weight[:, i * width : (i + 1) * width] for i in range(KEY_VALUE_HEADS)]
    mine = [pick(core, parts[i], parts[i + 1]) for i in range(0, KEY_VALUE_HEADS, 2)]
    other = [pick(core, parts[i + 1], parts[i]) for i in range(0, KEY_VALUE_HEADS, 2)]
    return mine, other


def on_device(
    residual_in,
    segments,
    routes,
    gates,
    attn_gain,
    q_proj,
    key_projection,
    value_projection,
    q_gain,
    k_gain,
    o_proj,
    mlp_gain,
    gate_proj,
    up_proj,
    down_proj,
    out_grad,
):
    bf16, f32 = jnp.bfloat16, jnp.float32
    n_seq, n_ctx, n_exp = lax.axis_size("seq"), lax.axis_size("ctx"), lax.axis_size("exp")
    n_y = n_seq // 2
    devices = n_seq * n_ctx * n_exp
    core = lax.axis_index("seq") % 2
    span_index = lax.axis_index("ctx")
    z_index = lax.axis_index("exp")
    group_all = [
        [(s * n_ctx + x) * n_exp + z for s in range(c, n_seq, 2) for x in range(n_ctx) for z in range(n_exp)]
        for c in range(2)
    ]
    group_plane = [[s * n_ctx + x for s in range(c, n_seq, 2) for x in range(n_ctx)] for c in range(2)]

    def swap(value):
        return lax.ppermute(value, "seq", [(i, i ^ 1) for i in range(n_seq)])

    def across(value, step):
        return lax.ppermute(value, "exp", [(i, i ^ step) for i in range(n_exp)])

    token_count = residual_in.shape[1]
    model_width = residual_in.shape[2]
    sequence_length = segments.shape[1]
    route_count = routes.shape[2]
    local_experts = gate_proj.shape[0]
    expert_count = local_experts * n_exp
    half_experts = local_experts // 2
    capacity = token_count * route_count * 9 // (expert_count * 8)
    slots = -(-capacity // 16) * 16
    groups = KEY_VALUE_HEADS // 2
    heads = QUERY_HEADS // 2
    heads_per_group = QUERY_HEADS // KEY_VALUE_HEADS
    score_scale = HEAD_DIM ** (-0.5)
    rows = q_proj.shape[0]
    gain_rows = q_gain.shape[0]
    q_width, kv_width = heads * HEAD_DIM, groups * HEAD_DIM
    width = q_width + 2 * kv_width

    extra = jnp.zeros((rows, 128), bf16)
    extra = extra.at[0, :rows].set(attn_gain).at[0, rows : 2 * rows].set(mlp_gain)
    extra = extra.at[1, :gain_rows].set(q_gain).at[1, gain_rows : 2 * gain_rows].set(k_gain)
    mine_cols, other_cols = [], []
    for weight in (q_proj, key_projection, value_projection):
        mine, other = column_halves(weight, core)
        mine_cols += mine
        other_cols += other
    mine_block = jnp.concatenate(mine_cols + [extra], 1)
    theirs = swap(jnp.concatenate(other_cols + [extra], 1))
    pair = jnp.stack([pick(core, mine_block, theirs), pick(core, theirs, mine_block)])
    w_gathered = lax.all_gather(
        pair, ("seq", "ctx", "exp"), axis=0, tiled=False, axis_index_groups=group_all
    )
    w_rows = w_gathered.reshape(n_y, n_ctx * n_exp, 2, rows, width + 128).transpose(0, 2, 1, 3, 4)
    w_qkv = w_rows[..., :width].reshape(model_width, width)
    w_extra = w_rows[..., width:].reshape(devices, rows, 128)[:, :2]
    gain_attn = w_extra[:, 0, :rows].reshape(model_width).astype(f32)
    gain_mlp_f = w_extra[:, 0, rows : 2 * rows].reshape(model_width).astype(f32)
    gain_query_f = w_extra[:, 1, :gain_rows].reshape(HEAD_DIM).astype(f32)
    gain_key_f = w_extra[:, 1, gain_rows : 2 * gain_rows].reshape(HEAD_DIM).astype(f32)
    w_out = lax.all_gather(
        o_proj, ("seq", "ctx", "exp"), axis=0, tiled=True, axis_index_groups=group_all
    )

    def gather_expert(weight):
        mine = pick(core, weight[:half_experts], weight[half_experts:])
        theirs = swap(pick(core, weight[half_experts:], weight[:half_experts]))
        both = jnp.stack([pick(core, mine, theirs), pick(core, theirs, mine)])
        full = lax.all_gather(
            both, ("seq", "ctx"), axis=0, tiled=False, axis_index_groups=group_plane
        )
        full = full.reshape((n_y, n_ctx, 2) + mine.shape).transpose(3, 0, 2, 1, 4, 5)
        return full.reshape(half_experts, -1, weight.shape[2])

    w_gate, w_up, w_down = gather_expert(gate_proj), gather_expert(up_proj), gather_expert(down_proj)

    route_ids = routes[0]
    route_hit = route_ids[:, :, None] == jnp.arange(expert_count, dtype=jnp.int32)[None, None, :]
    hit_counts = route_hit.astype(jnp.int32).sum(1)
    earlier = jnp.cumsum(hit_counts, axis=0) - hit_counts
    slot_of = jnp.where(hit_counts > 0, earlier, -1).astype(f32)
    gate_of = jnp.sum(jnp.where(route_hit, gates[0][:, :, None], 0.0), axis=1)
    table = jnp.concatenate([slot_of.T, gate_of.T], 0)
    table_own = lax.all_gather(table, "exp", axis=0, tiled=False)
    table_sib = swap(table_own)
    tables = jnp.stack([table_own, table_sib], 1).reshape(
        n_exp, 2, 2, n_exp, 2, half_experts, token_count
    )
    tables = lax.dynamic_index_in_dim(tables, z_index, 3, keepdims=False)
    tables = lax.dynamic_index_in_dim(tables, core, 3, keepdims=False)

    cot_chunks = []
    for step in range(n_exp):
        own = out_grad[0] if step == 0 else across(out_grad[0], step)
        cot_chunks.append(jnp.stack([own, swap(own)]))

    hidden = residual_in[0].astype(f32)
    seg_two = jnp.stack([segments[0], swap(segments)[0]])
    seg_here = lax.dynamic_slice_in_dim(seg_two, span_index * token_count, token_count, 1)
    valid_two = (seg_here > 0).astype(f32).reshape(2 * token_count, 1)
    valid_rows = valid_two[:token_count]
    positions = span_index * token_count + jnp.arange(token_count, dtype=jnp.int32)
    cos_one, sin_one = rope_tables(positions)
    cosine_table, sine_values = jnp.concatenate([cos_one] * 2, 0), jnp.concatenate([sin_one] * 2, 0)
    inv_attn = lax.rsqrt(jnp.mean(hidden * hidden, axis=-1, keepdims=True) + EPS)
    normed_own = (hidden * inv_attn * gain_attn).astype(bf16)
    normed_two = jnp.concatenate([normed_own, swap(normed_own)], 0)
    kv_raw = jnp.dot(normed_two, w_qkv[:, q_width:], preferred_element_type=f32)
    k_raw = kv_raw[:, :kv_width].reshape(-1, groups, HEAD_DIM)
    value_rows = kv_raw[:, kv_width:].astype(bf16)
    inv_key = lax.rsqrt(jnp.mean(k_raw * k_raw, axis=-1, keepdims=True) + EPS)
    key_rows = rotate(k_raw * inv_key * gain_key_f, cosine_table, sine_values).astype(bf16)
    kv_here = jnp.concatenate([key_rows.reshape(-1, kv_width), value_rows], 1).reshape(
        2, token_count, 2 * kv_width
    )
    if n_ctx == 2:
        kv_there = lax.ppermute(kv_here, "ctx", [(0, 1), (1, 0)])
        kv_full = jnp.concatenate(
            [pick(span_index, kv_here, kv_there), pick(span_index, kv_there, kv_here)], 1
        )
    else:
        kv_full = lax.all_gather(kv_here, "ctx", axis=1, tiled=True)
    q_raw = jnp.dot(normed_two, w_qkv[:, :q_width], preferred_element_type=f32).reshape(
        -1, heads, HEAD_DIM
    )
    inv_query = lax.rsqrt(jnp.mean(q_raw * q_raw, axis=-1, keepdims=True) + EPS)
    query_rows = rotate(q_raw * inv_query * gain_query_f, cosine_table, sine_values).astype(bf16)
    grouped_queries = query_rows.reshape(2, token_count, groups, heads_per_group, HEAD_DIM)
    key_heads = kv_full[..., :kv_width].reshape(2, sequence_length, groups, HEAD_DIM)
    value_heads = kv_full[..., kv_width:].reshape(2, sequence_length, groups, HEAD_DIM)
    key_pos = jnp.arange(sequence_length, dtype=jnp.int32)
    allowed = (seg_here[:, :, None] == seg_two[:, None, :]) & (
        positions[None, :, None] >= key_pos[None, None, :]
    )

    def head_scores(s, g):
        raw_scores = (
            jnp.einsum(
                "qgd,kd->gqk", grouped_queries[s, :, g], key_heads[s, :, g], preferred_element_type=f32
            )
            * score_scale
        )
        return jnp.where(allowed[s][None], raw_scores, MASKED)

    mixed_parts, log_totals = [], {}
    for s in range(2):
        for g in range(groups):
            scores = head_scores(s, g)
            row_peak = jnp.max(scores, axis=-1, keepdims=True)
            exp_scores = jnp.exp(scores - row_peak)
            row_total = jnp.sum(exp_scores, axis=-1, keepdims=True)
            probs_low = (exp_scores / row_total).astype(bf16)
            mixed_parts.append(
                jnp.einsum("gqk,kd->qgd", probs_low, value_heads[s, :, g], preferred_element_type=f32)
            )
            log_totals[s, g] = row_peak + jnp.log(row_total)
    mixed_heads = jnp.stack(mixed_parts).reshape(2, groups, token_count, heads_per_group * HEAD_DIM)
    mixed_heads = mixed_heads.transpose(0, 2, 1, 3).reshape(2 * token_count, q_width)
    mixed_low = (mixed_heads * valid_two).astype(bf16)
    attn_partial = jnp.dot(mixed_low, w_out, preferred_element_type=f32)
    attn_out = attn_partial[:token_count] + swap(attn_partial[token_count:])
    middle = hidden + attn_out
    inv_mlp = lax.rsqrt(jnp.mean(middle * middle, axis=-1, keepdims=True) + EPS)
    normed_mlp = (middle * inv_mlp * gain_mlp_f).astype(bf16)

    row_chunks, val_chunks, product_chunks, gg_chunks, gu_chunks = [], [], [], [], []
    grad_total, out_total = None, None
    for step in range(n_exp):
        own = normed_mlp if step == 0 else across(normed_mlp, step)
        tokens = jnp.stack([own, swap(own)])
        table_here = lax.dynamic_index_in_dim(tables, z_index ^ step, 0, keepdims=False)
        slot_here, gate_here = table_here[:, 0], table_here[:, 1]
        hits = slot_here[:, :, None, :] == jnp.arange(slots, dtype=f32)[None, None, :, None]
        one_hot = hits.astype(bf16)
        gate_row = jnp.sum(jnp.where(hits, gate_here[:, :, None, :], 0.0), -1, keepdims=True)
        x_rows = jnp.einsum("sert,std->serd", one_hot, tokens, preferred_element_type=f32).astype(bf16)
        cot_rows = jnp.einsum("sert,std->serd", one_hot, cot_chunks[step], preferred_element_type=f32)
        grad_val = (gate_row * cot_rows).astype(bf16)
        gate_part = jnp.einsum("serd,edf->serf", x_rows, w_gate, preferred_element_type=f32)
        up_part = jnp.einsum("serd,edf->serf", x_rows, w_up, preferred_element_type=f32)
        sigmoid_gate = jax.nn.sigmoid(gate_part)
        silu_gate = gate_part * sigmoid_gate
        product = (silu_gate * up_part).astype(bf16)
        expert_val = jnp.einsum("serf,efd->serd", product, w_down, preferred_element_type=f32)
        weighted = (gate_row * expert_val).astype(bf16)
        grad_product = jnp.einsum("serd,efd->serf", grad_val, w_down, preferred_element_type=f32)
        grad_gate = (
            grad_product * up_part * sigmoid_gate * (1.0 + gate_part * (1.0 - sigmoid_gate))
        ).astype(bf16)
        grad_up = (grad_product * silu_gate).astype(bf16)
        grad_rows = (
            jnp.einsum("serf,edf->serd", grad_gate, w_gate, preferred_element_type=f32)
            + jnp.einsum("serf,edf->serd", grad_up, w_up, preferred_element_type=f32)
        ).astype(bf16)
        grad_part = jnp.einsum("sert,serd->std", one_hot, grad_rows, preferred_element_type=f32)
        out_part = jnp.einsum("sert,serd->std", one_hot, weighted, preferred_element_type=f32)
        grad_part = grad_part[0] + swap(grad_part[1].astype(bf16)).astype(f32)
        out_part = out_part[0] + swap(out_part[1].astype(bf16)).astype(f32)
        if step:
            grad_part = across(grad_part.astype(bf16), step).astype(f32)
            out_part = across(out_part.astype(bf16), step).astype(f32)
        grad_total = grad_part if grad_total is None else grad_total + grad_part
        out_total = out_part if out_total is None else out_total + out_part
        row_chunks.append(x_rows)
        val_chunks.append(grad_val)
        product_chunks.append(product)
        gg_chunks.append(grad_gate)
        gu_chunks.append(grad_up)
    grad_normed_mlp, expert_out = grad_total, out_total
    final_out = middle + expert_out

    stats = jnp.zeros((8, 128), f32)
    for index, value in enumerate(
        (
            jnp.sum(hidden * hidden * valid_rows),
            jnp.sum(attn_out * attn_out * valid_rows),
            jnp.sum(expert_out * expert_out * valid_rows),
            jnp.sum(valid_rows),
        )
    ):
        stats = stats.at[0, index].set(value)
    for axis, count in (("seq", n_seq), ("ctx", n_ctx), ("exp", n_exp)):
        hop = 1
        while hop < count:
            stats = stats + lax.ppermute(stats, axis, [(i, i ^ hop) for i in range(count)])
            hop *= 2
    rms_stats = jnp.sqrt(stats[0, :3] / (stats[0, 3] * model_width))

    x_all, val_all, product_all, gg_all, gu_all = (
        jnp.stack(chunks) for chunks in (row_chunks, val_chunks, product_chunks, gg_chunks, gu_chunks)
    )

    def scatter_expert(grad):
        depth = grad.shape[1] // (n_seq * n_ctx)
        blocks = grad.astype(bf16).reshape(half_experts, n_y, 2, n_ctx, depth, grad.shape[2])
        blocks = blocks.transpose(1, 3, 2, 0, 4, 5).reshape(
            n_y * n_ctx, 2, half_experts, depth, grad.shape[2]
        )
        part = lax.psum_scatter(
            blocks,
            ("seq", "ctx"),
            scatter_dimension=0,
            tiled=True,
            axis_index_groups=group_plane,
        )[0]
        mine = pick(core, part[0], part[1])
        theirs = swap(pick(core, part[1], part[0]))
        return jnp.concatenate([pick(core, mine, theirs), pick(core, theirs, mine)], 0).astype(f32)

    down_grad = scatter_expert(
        jnp.einsum("cserf,cserd->efd", product_all, val_all, preferred_element_type=f32)
    )
    gate_grad = scatter_expert(
        jnp.einsum("cserd,cserf->edf", x_all, gg_all, preferred_element_type=f32)
    )
    up_grad = scatter_expert(
        jnp.einsum("cserd,cserf->edf", x_all, gu_all, preferred_element_type=f32)
    )

    cotangent = out_grad[0].astype(f32)
    mlp_gain_grad = jnp.sum(grad_normed_mlp * middle * inv_mlp, axis=0)
    grad_middle = cotangent + norm_back(grad_normed_mlp, middle, inv_mlp, gain_mlp_f)
    grad_attn_own = grad_middle.astype(bf16)
    grad_attn = jnp.concatenate([grad_attn_own, swap(grad_attn_own)], 0)
    o_grad_part = contract_rows(mixed_low, grad_attn).astype(bf16)
    o_proj_grad = lax.psum_scatter(
        o_grad_part,
        ("seq", "ctx", "exp"),
        scatter_dimension=0,
        tiled=True,
        axis_index_groups=group_all,
    ).astype(f32)
    mixture_gradient = contract_cols(grad_attn, w_out).astype(bf16) * valid_two.astype(bf16)
    group_gradient = mixture_gradient.reshape(
        2, token_count, groups, heads_per_group, HEAD_DIM
    )
    grad_q_parts, key_parts, value_parts = [], [], []
    for s in range(2):
        for g in range(groups):
            probs = jnp.exp(head_scores(s, g) - log_totals[s, g])
            grad_head = group_gradient[s, :, g]
            grad_probs = jnp.einsum(
                "qgd,kd->gqk", grad_head, value_heads[s, :, g], preferred_element_type=f32
            )
            inner_sum = jnp.sum(probs * grad_probs, axis=-1, keepdims=True)
            grad_scores = (probs * (grad_probs - inner_sum)).astype(bf16)
            grad_q_parts.append(
                jnp.einsum(
                    "gqk,kd->qgd", grad_scores, key_heads[s, :, g], preferred_element_type=f32
                )
                * score_scale
            )
            key_parts.append(
                jnp.einsum(
                    "gqk,qgd->kd", grad_scores, grouped_queries[s, :, g], preferred_element_type=f32
                )
                * score_scale
            )
            value_parts.append(
                jnp.einsum("gqk,qgd->kd", probs.astype(bf16), grad_head, preferred_element_type=f32)
            )
    grad_queries = (
        jnp.stack(grad_q_parts)
        .reshape(2, groups, token_count, heads_per_group, HEAD_DIM)
        .transpose(0, 2, 1, 3, 4)
        .reshape(2 * token_count, heads, HEAD_DIM)
    )
    kv_grad = jnp.concatenate(
        [
            jnp.stack([jnp.concatenate(parts[s * groups : (s + 1) * groups], 1) for s in range(2)])
            for parts in (key_parts, value_parts)
        ],
        2,
    )
    if n_ctx == 2:
        first, second = kv_grad[:, :token_count], kv_grad[:, token_count:]
        received = lax.ppermute(
            pick(span_index, second, first).astype(bf16), "ctx", [(0, 1), (1, 0)]
        )
        kv_grad_here = pick(span_index, first, second) + received.astype(f32)
    else:
        kv_grad_here = lax.psum_scatter(
            kv_grad.astype(bf16), "ctx", scatter_dimension=1, tiled=True
        ).astype(f32)
    kv_grad_here = kv_grad_here.reshape(2 * token_count, 2 * kv_width)
    grad_qn = inverse_rotation(grad_queries, cosine_table, sine_values)
    q_gain_grad = jnp.sum(grad_qn * q_raw * inv_query, axis=(0, 1))
    grad_q_raw = norm_back(grad_qn, q_raw, inv_query, gain_query_f).astype(bf16)
    grad_kn = inverse_rotation(
        kv_grad_here[:, :kv_width].reshape(-1, groups, HEAD_DIM), cosine_table, sine_values
    )
    k_gain_grad = jnp.sum(grad_kn * k_raw * inv_key, axis=(0, 1))
    grad_k_raw = norm_back(grad_kn, k_raw, inv_key, gain_key_f).astype(bf16)
    grad_qkv = jnp.concatenate(
        [
            grad_q_raw.reshape(-1, q_width),
            grad_k_raw.reshape(-1, kv_width),
            kv_grad_here[:, kv_width:].astype(bf16),
        ],
        1,
    )
    normed_partial = contract_cols(grad_qkv, w_qkv)
    grad_normed = normed_partial[:token_count] + swap(normed_partial[token_count:])
    attn_gain_grad = jnp.sum(grad_normed * hidden * inv_attn, axis=0)
    grad_hidden = grad_middle + norm_back(grad_normed, hidden, inv_attn, gain_attn)

    extra_grad = jnp.zeros((devices, rows, 128), f32)
    extra_grad = extra_grad.at[:, 0, :rows].set(attn_gain_grad.reshape(devices, rows))
    extra_grad = extra_grad.at[:, 0, rows : 2 * rows].set(mlp_gain_grad.reshape(devices, rows))
    extra_grad = extra_grad.at[:, 1, :gain_rows].set(q_gain_grad.reshape(devices, gain_rows))
    extra_grad = extra_grad.at[:, 1, gain_rows : 2 * gain_rows].set(
        k_gain_grad.reshape(devices, gain_rows)
    )
    w_grad = jnp.concatenate(
        [
            contract_rows(normed_two, grad_qkv).astype(bf16),
            extra_grad.reshape(model_width, 128).astype(bf16),
        ],
        1,
    )
    w_grad = (
        w_grad.reshape(n_y, 2, n_ctx * n_exp, rows, width + 128)
        .transpose(0, 2, 1, 3, 4)
        .reshape(devices // 2, 2, rows, width + 128)
    )
    w_grad = lax.psum_scatter(
        w_grad,
        ("seq", "ctx", "exp"),
        scatter_dimension=0,
        tiled=True,
        axis_index_groups=group_all,
    )[0]
    grad_mine = pick(core, w_grad[0], w_grad[1])
    grad_theirs = swap(pick(core, w_grad[1], w_grad[0]))
    even = pick(core, grad_mine, grad_theirs).astype(f32)
    odd = pick(core, grad_theirs, grad_mine).astype(f32)

    def columns(start, size):
        step = size // groups
        parts = []
        for g in range(groups):
            parts += [half[:, start + g * step : start + (g + 1) * step] for half in (even, odd)]
        return jnp.concatenate(parts, 1)

    extra_total = even[:, width:] + odd[:, width:]
    return (
        final_out.astype(bf16)[None],
        grad_hidden.astype(bf16)[None],
        extra_total[0, :rows],
        columns(0, q_width),
        columns(q_width, kv_width),
        columns(q_width + kv_width, kv_width),
        extra_total[1, :gain_rows],
        extra_total[1, gain_rows : 2 * gain_rows],
        o_proj_grad,
        extra_total[0, rows : 2 * rows],
        gate_grad,
        up_grad,
        down_grad,
        rms_stats,
    )


def solution(mesh):
    in_specs = (
        P(("seq", "exp"), "ctx", None),
        P(("seq", "exp"), None),
        P(("seq", "exp"), "ctx", None),
        P(("seq", "exp"), "ctx", None),
        P(("seq", "ctx", "exp")),
        P(("seq", "ctx", "exp"), None),
        P(("seq", "ctx", "exp"), None),
        P(("seq", "ctx", "exp"), None),
        P(("seq", "ctx", "exp")),
        P(("seq", "ctx", "exp")),
        P(("seq", "ctx", "exp"), None),
        P(("seq", "ctx", "exp")),
        P("exp", ("seq", "ctx"), None),
        P("exp", ("seq", "ctx"), None),
        P("exp", ("seq", "ctx"), None),
        P(("seq", "exp"), "ctx", None),
    )
    out_specs = (
        P(("seq", "exp"), "ctx", None),
        P(("seq", "exp"), "ctx", None),
        P(("seq", "ctx", "exp")),
        P(("seq", "ctx", "exp"), None),
        P(("seq", "ctx", "exp"), None),
        P(("seq", "ctx", "exp"), None),
        P(("seq", "ctx", "exp")),
        P(("seq", "ctx", "exp")),
        P(("seq", "ctx", "exp"), None),
        P(("seq", "ctx", "exp")),
        P("exp", ("seq", "ctx"), None),
        P("exp", ("seq", "ctx"), None),
        P("exp", ("seq", "ctx"), None),
        P(),
    )
    return jax.shard_map(
        on_device, mesh=mesh, in_specs=in_specs, out_specs=out_specs, check_vma=False
    )
```

time: 5070 us -> 2460 us (0.49)
  waiting for transfers between devices: 3450 us -> 893 us
  blocking collectives: 532 us -> 13.9 us
  starting transfers between devices: 24 us -> 210 us
  matrix products: 522 us -> 653 us
  other arithmetic: 225 us -> 326 us
    reduce_scatter x9 -> x2, waiting for transfers between devices: 1740 us -> 300 us  [the longest x1 179 us: on_device(): lax.psum_scatter(o_grad_part, ('seq', 'ctx', 'exp'), scatter_dimension=0,...]
    all_to_all x3 -> x0, waiting for transfers between devices: 1210 us -> none  [the longest x1 408 us: on_device(): lax.all_to_all(result, 'exp', split_axis=0, concat_axis=0, tiled=True)]
    all_to_all x1 -> x0, blocking collectives: 413 us -> none  [on_device(): lax.all_to_all(grad_rows, 'exp', split_axis=0, concat_axis=0, tiled=True)]
    ppermute x0 -> x49, waiting for transfers between devices: none -> 337 us  [the longest x12 324 us: across(): return lax.ppermute(value, 'exp', [(i, i ^ step) for i in range(n_exp)])]
    all_gather x16 -> x5, waiting for transfers between devices: 493 us -> 255 us  [the longest x1 255 us: on_device(): lax.all_gather(pair, ('seq', 'ctx', 'exp'), axis=0, tiled=False, axis_ind...]
    ppermute x0 -> x49, starting transfers between devices: none -> 209 us  [the longest x12 193 us: across(): return lax.ppermute(value, 'exp', [(i, i ^ step) for i in range(n_exp)])]
    gather x7 -> x0, local copies, waits for them, and re-layouts: 164 us -> none  [the longest x1 40.1 us: on_device(): returned_rows.reshape(expert_count * capacity, model_width)[targets]]
    dot_general x37 -> x62, matrix products: 433 us -> 590 us  [the longest x4 53.2 us: on_device(): jnp.einsum('serd,efd->serf', grad_val, w_down, preferred_element_type=f32)]
  transfers between devices with their start and end apart: 28 -> 57, of which waited for: 16 -> 15; matrix products, arithmetic and copies ran while one was open for 13% -> 51% of each run, Pallas kernels for 0% -> 0%
where the time goes in v1:
time: 2460 us; the launch traced here: 2450 us
  waiting for transfers between devices  893 us (36%)
  matrix products  653 us (27%)
  local copies, waits for them, and re-layouts  329 us (13%)
  other arithmetic  326 us (13%)
  starting transfers between devices  210 us (9%)
    ppermute x12, waiting for transfers between devices, across(): return lax.ppermute(value, 'exp', [(i, i ^ step) for i in range(n_exp)])  324 us
    all_gather x1, waiting for transfers between devices, on_device(): lax.all_gather(pair, ('seq', 'ctx', 'exp'), axis=0, tiled=False, axis_ind...  255 us
    ppermute x12, starting transfers between devices, across(): return lax.ppermute(value, 'exp', [(i, i ^ step) for i in range(n_exp)])  193 us
    reduce_scatter x1, waiting for transfers between devices, on_device(): lax.psum_scatter(o_grad_part, ('seq', 'ctx', 'exp'), scatter_dimension=0,...  179 us
    reduce_scatter x1, waiting for transfers between devices, on_device(): lax.psum_scatter(w_grad, ('seq', 'ctx', 'exp'), scatter_dimension=0, tile...  121 us
    convert_element_type x4, other arithmetic, on_device(): grad_scores = (probs * (grad_probs - inner_sum)).astype(bf16)  59.1 us
    dot_general x4, matrix products, on_device(): jnp.einsum('serd,efd->serf', grad_val, w_down, preferred_element_type=f32)  53.2 us
    dot_general x4, matrix products, on_device(): jnp.einsum('qgd,kd->gqk', grad_head, value_heads[s, :, g], preferred_elem...  51.9 us
  transfers between devices with their start and end apart: 57, of which 15 were waited for; matrix products, arithmetic and copies ran while one was open for 51% of the time, Pallas kernels for 0%

profile of v1, /device:TPU:0, one launch (start us, length us, event | category | flops | bytes accessed | tf_op | source)
XLA Modules:
  0.0 2446.2 jit_solution(5262728581671601043)
XLA Ops:
  46.9 255.5 %all-gather.13.cloned.1.call-done = bf16[32,64,2688]{2,1,0:T(8,128)(2,1)} async-done(((bf16[2,64,2688]{2,1,0:T(8,128)(2,1)}), bf16[32,64,2688]{2,1,0:T(8,128)(2,1)}) %all-gather.13.cloned.1.call-update) | async-done | bytes 11010064 | tf_op jit(solution)/shard_map/all_gather | solution.py:139
  315.2 8.9 slice.810
  324.1 9.0 copy.831
  334.4 12.7 fusion.36
  353.1 8.8 copy.843
  412.0 8.4 copy.845
  426.9 8.3 copy.844
  435.3 11.6 fusion.39
  511.0 8.7 fusion.15
  519.8 8.8 fusion.280
  536.7 8.4 fusion.281
  549.0 13.8 copy.854
  562.8 10.9 copy.1020
  573.6 13.7 fusion.368
  593.4 13.9 all-gather.1
  612.6 9.2 copy.1002
  626.4 29.1 %collective-permute-done.25 = bf16[512,2048]{1,0:T(8,128)(2,1)} collective-permute-done((bf16[512,2048]{1,0:T(8,128)(2,1)S(1)}, bf16[512,2048]{1,0:T(8,128)(2,1)}, u32[]{:S(2)}, u32[]{:S(2)}) %collective-permute-start.25) | collective-permute-done | bytes 2097184 | tf_op jit(solution)/shard_map/ppermute | solution.py:108
  713.4 9.6 copy.993
  757.6 13.4 fusion.212
  771.0 11.4 fusion.268
  782.4 12.6 fusion.124
  799.2 110.1 %collective-permute-done.15 = bf16[512,2048]{1,0:T(8,128)(2,1)} collective-permute-done((bf16[512,2048]{1,0:T(8,128)(2,1)}, bf16[512,2048]{1,0:T(8,128)(2,1)}, u32[]{:S(2)}, u32[]{:S(2)}) %collective-permute-start.15) | collective-permute-done | bytes 2097184 | tf_op jit(solution)/shard_map/ppermute | solution.py:108
  909.8 12.0 fusion.112
  995.3 13.1 fusion.200
  1008.3 12.3 fusion.103
  1024.5 13.0 fusion.204
  1037.6 12.5 fusion.106
  1054.4 13.7 fusion.208
  1068.1 11.7 fusion.109
  1079.8 10.7 fusion.256
  1090.5 12.9 fusion.115
  1107.3 10.8 fusion.260
  1118.1 12.7 fusion.118
  1133.8 10.8 fusion.264
  1144.6 22.1 bitcast_convert_fusion
  1166.8 13.3 fusion.121
  1219.1 29.7 %collective-permute-done.36 = bf16[512,2048]{1,0:T(8,128)(2,1)} collective-permute-done((bf16[512,2048]{1,0:T(8,128)(2,1)}, bf16[512,2048]{1,0:T(8,128)(2,1)}, u32[]{:S(2)}, u32[]{:S(2)}) %collective-permute-start.36) | collective-permute-done | bytes 2097184 | tf_op jit(solution)/shard_map/ppermute | solution.py:108
  1248.8 177.2 %collective-permute-start.14 = (bf16[512,2048]{1,0:T(8,128)(2,1)}, bf16[512,2048]{1,0:T(8,128)(2,1)}, u32[]{:S(2)}, u32[]{:S(2)}) collective-permute-start(bf16[512,2048]{1,0:T(8,128)(2,1)} %fusion.152), channel_id=1, source_target_pairs={{0,1},{1,0},{2,3},{3,2},{4,5},{5,4},{6,7},{7,6},{8,9},{9,8},{10,11... | collective-permute-start | bytes 6291464 | tf_op jit(solution)/shard_map/ppermute | solution.py:108
  1426.0 44.4 %collective-permute-done.32 = bf16[512,2048]{1,0:T(8,128)(2,1)} collective-permute-done((bf16[512,2048]{1,0:T(8,128)(2,1)}, bf16[512,2048]{1,0:T(8,128)(2,1)}, u32[]{:S(2)}, u32[]{:S(2)}) %collective-permute-start.32) | collective-permute-done | bytes 2097184 | tf_op jit(solution)/shard_map/ppermute | solution.py:108
  1470.4 22.8 bitcast_convert_fusion.2
  1493.2 110.9 %collective-permute-done.28 = bf16[512,2048]{1,0:T(8,128)(2,1)S(1)} collective-permute-done((bf16[512,2048]{1,0:T(8,128)(2,1)}, bf16[512,2048]{1,0:T(8,128)(2,1)S(1)}, u32[]{:S(2)}, u32[]{:S(2)}) %collective-permute-start.28) | collective-permute-done | bytes 2097184 | tf_op jit(solution)/shard_map/ppermute | solution.py:108
  1611.5 11.9 multiply_reduce_fusion.3
  1623.4 23.8 bitcast_convert_fusion.1
  1661.4 12.0 multiply_bitcast_fusion
  1685.6 16.6 fusion.2
  1707.1 11.4 fusion.5
  1718.6 10.1 fusion.301
  1728.7 14.4 fusion.8
  1746.9 9.4 fusion.11
  1756.3 15.7 fusion.4
  1778.3 16.2 fusion.7
  1800.9 16.7 fusion.10
  1824.8 10.5 fusion.13
  1870.8 12.0 reshape.866
  1893.6 10.5 pad_maximum_fusion.5
  1904.1 9.2 copy.1004
  1913.3 10.4 copy.903
  1923.7 9.6 reshape.865
  1945.4 23.0 multiply_reduce_fusion
  1990.2 17.8 fusion.233
  2013.9 17.3 convolution_convert_fusion
  2062.4 15.8 convolution_convert_fusion.1
  2127.3 120.9 %reduce-scatter.3.cloned.1.call-done = bf16[1,2,64,2688]{3,2,1,0:T(8,128)(2,1)} async-done(((bf16[16,2,64,2688]{3,2,1,0:T(8,128)(2,1)}), bf16[1,2,64,2688]{3,2,1,0:T(8,128)(2,1)}) %reduce-scatter.3.cloned.1.call-update) | async-done | bytes 688144 | tf_op jit(solution)/shard_map/reduce_scatter | solution.py:454
  2253.2 179.1 %reduce-scatter.5.cloned.1.call-done = bf16[128,2048]{1,0:T(8,128)(2,1)} async-done(((bf16[2048,2048]{1,0:T(8,128)(2,1)}), bf16[128,2048]{1,0:T(8,128)(2,1)}) %reduce-scatter.5.cloned.1.call-update) | async-done | bytes 524304 | tf_op jit(solution)/shard_map/reduce_scatter | solution.py:354
  (713 shorter events, 666.8 us)
Async XLA Ops:
  7.2 295.2 %all-gather.13.cloned.1.call-start = ((), (), s32[]{:S(2)}) async-start(), calls=%async_computation.5 | async-start | bytes 11698176 | tf_op jit(solution)/shard_map/all_gather | solution.py:139
  22.3 1.8 collective-permute-start
  25.2 548.5 %all-gather.11.cloned.1.call-start = ((), (), s32[]{:S(2)}) async-start(), calls=%async_computation.2 | async-start | bytes 8912896 | tf_op jit(solution)/shard_map/all_gather | solution.py:149
  25.9 662.8 %all-gather.15.cloned.1.call-start = ((), (), s32[]{:S(2)}) async-start(), calls=%async_computation.6 | async-start | bytes 7864320 | tf_op jit(solution)/shard_map/all_gather | solution.py:157
  26.1 2.4 collective-permute-start.6
  29.9 665.4 %all-gather.17.cloned.1.call-start = ((), (), s32[]{:S(2)}) async-start(), calls=%async_computation.7 | async-start | bytes 7864320 | tf_op jit(solution)/shard_map/all_gather | solution.py:157
  30.0 2.4 collective-permute-start.7
  33.9 667.5 %all-gather.19.cloned.1.call-start = ((), (), s32[]{:S(2)}) async-start(), calls=%async_computation.8 | async-start | bytes 7864320 | tf_op jit(solution)/shard_map/all_gather | solution.py:157
  33.9 590.3 %collective-permute-start.33 = (bf16[512,2048]{1,0:T(8,128)(2,1)}, bf16[512,2048]{1,0:T(8,128)(2,1)}, u32[]{:S(2)}, u32[]{:S(2)}) collective-permute-start(bf16[512,2048]{1,0:T(8,128)(2,1)} %bitcast.1088), channel_id=1, source_target_pairs={{0,3},{1,2},{2,1},{3,0},{4,7},{5,6},{6,5},{7,4},{8,11},{9,10},{10,... | collective-permute-start | bytes 6291464 | tf_op jit(solution)/shard_map/ppermute | solution.py:108
  38.9 585.6 %collective-permute-start.29 = (bf16[512,2048]{1,0:T(8,128)(2,1)}, bf16[512,2048]{1,0:T(8,128)(2,1)}, u32[]{:S(2)}, u32[]{:S(2)}) collective-permute-start(bf16[512,2048]{1,0:T(8,128)(2,1)} %bitcast.1089), channel_id=1, source_target_pairs={{0,2},{1,3},{2,0},{3,1},{4,6},{5,7},{6,4},{7,5},{8,10},{9,11},{10,... | collective-permute-start | bytes 6291464 | tf_op jit(solution)/shard_map/ppermute | solution.py:108
  38.9 269.3 %collective-permute-start.3 = (s32[1,1024]{1,0:T(1,128)S(1)}, s32[1,1024]{1,0:T(1,128)S(1)}, u32[]{:S(2)}, u32[]{:S(2)}) collective-permute-start(s32[1,1024]{1,0:T(1,128)S(1)} %copy-done.97), channel_id=1, source_target_pairs={{0,8},{8,0},{16,24},{24,16},{1,9},{9,1},{17,25},{25,17},{2,10},{10... | collective-permute-start | bytes 12296 | tf_op jit(solution)/shard_map/ppermute | solution.py:105
  41.3 270.6 %collective-permute-start.9 = (bf16[2,256,768]{2,1,0:T(8,128)(2,1)}, bf16[2,256,768]{2,1,0:T(8,128)(2,1)}, u32[]{:S(2)}, u32[]{:S(2)}) collective-permute-start(bf16[2,256,768]{2,1,0:T(8,128)(2,1)} %broadcast_select_fusion.5), channel_id=1, source_target_pairs={{0,8},{8,0},{16,24},{24,16},{1,9},{9,1},{17,25},{25,17},{2,10},{10... | collective-permute-start | bytes 2359304 | tf_op jit(solution)/shard_map/ppermute | solution.py:105
  43.9 263.9 %copy-start.34 = (f32[1024,128]{0,1:T(8,128)}, f32[1024,128]{0,1:T(8,128)S(1)}, u32[]{:S(2)}) copy-start(f32[1024,128]{0,1:T(8,128)S(1)} %maximum_maximum_fusion.2) | copy-start | bytes 1572868
  43.9 263.1 %copy-start.96 = (f32[1,512,8]{1,2,0:T(8,128)S(1)}, f32[1,512,8]{1,2,0:T(8,128)}, u32[]{:S(2)}) copy-start(f32[1,512,8]{1,2,0:T(8,128)} %param.43) | copy-start | bytes 49156
  45.0 262.8 %copy-start.87 = (f32[512]{0:T(512)}, f32[512]{0:T(512)S(1)}, u32[]{:S(2)}) copy-start(f32[512]{0:T(512)S(1)} %get-tuple-element.286) | copy-start | bytes 6148
  306.9 27.5 %collective-permute-start.1 = (bf16[512,2048]{1,0:T(8,128)(2,1)}, bf16[512,2048]{1,0:T(8,128)(2,1)}, u32[]{:S(2)}, u32[]{:S(2)}) collective-permute-start(bf16[512,2048]{1,0:T(8,128)(2,1)} %fusion.129), channel_id=1, source_target_pairs={{0,8},{8,0},{16,24},{24,16},{1,9},{9,1},{17,25},{25,17},{2,10},{10... | collective-permute-start | bytes 6291464 | tf_op jit(solution)/shard_map/ppermute | solution.py:105
  315.1 1792.6 %all-reduce.9.cloned.1.call-start = ((), (), s32[]{:S(2)}) async-start(), calls=%async_computation.9 | async-start | bytes 37748736
  394.7 52.2 %collective-permute-start.2 = (bf16[2,512,512]{1,2,0:T(8,128)(2,1)}, bf16[2,512,512]{1,2,0:T(8,128)(2,1)}, u32[]{:S(2)}, u32[]{:S(2)}) collective-permute-start(bf16[2,512,512]{1,2,0:T(8,128)(2,1)} %pad_maximum_fusion.24), channel_id=1, source_target_pairs={{0,4},{4,0},{1,5},{5,1},{2,6},{6,2},{3,7},{7,3},{8,12},{12,8},{9,1... | collective-permute-start | bytes 3145736 | tf_op jit(solution)/shard_map/ppermute | solution.py:205
  593.2 80.0 %collective-permute-start.4 = (f32[512,2048]{1,0:T(8,128)}, f32[512,2048]{1,0:T(8,128)}, u32[]{:S(2)}, u32[]{:S(2)}) collective-permute-start(f32[512,2048]{1,0:T(8,128)} %slice.838), channel_id=1, source_target_pairs={{0,8},{8,0},{16,24},{24,16},{1,9},{9,1},{17,25},{25,17},{2,10},{10... | collective-permute-start | bytes 12582920 | tf_op jit(solution)/shard_map/ppermute | solution.py:105
  607.3 15.1 collective-permute-start.5
  607.3 48.1 %collective-permute-start.25 = (bf16[512,2048]{1,0:T(8,128)(2,1)S(1)}, bf16[512,2048]{1,0:T(8,128)(2,1)}, u32[]{:S(2)}, u32[]{:S(2)}) collective-permute-start(bf16[512,2048]{1,0:T(8,128)(2,1)S(1)} %bitcast.1090), channel_id=1, source_target_pairs={{0,1},{1,0},{2,3},{3,2},{4,5},{5,4},{6,7},{7,6},{8,9},{9,8},{10,11... | collective-permute-start | bytes 6291464 | tf_op jit(solution)/shard_map/ppermute | solution.py:108
  622.4 33.0 %collective-permute-start.23 = (bf16[512,2048]{1,0:T(8,128)(2,1)S(1)}, bf16[512,2048]{1,0:T(8,128)(2,1)S(1)}, u32[]{:S(2)}, u32[]{:S(2)}) collective-permute-start(bf16[512,2048]{1,0:T(8,128)(2,1)S(1)} %bitcast.1091), channel_id=1, source_target_pairs={{0,8},{8,0},{16,24},{24,16},{1,9},{9,1},{17,25},{25,17},{2,10},{10... | collective-permute-start | bytes 6291464 | tf_op jit(solution)/shard_map/ppermute | solution.py:105
  624.2 36.0 %collective-permute-start.34 = (bf16[512,2048]{1,0:T(8,128)(2,1)}, bf16[512,2048]{1,0:T(8,128)(2,1)S(1)}, u32[]{:S(2)}, u32[]{:S(2)}) collective-permute-start(bf16[512,2048]{1,0:T(8,128)(2,1)} %collective-permute-done.33), channel_id=1, source_target_pairs={{0,8},{8,0},{16,24},{24,16},{1,9},{9,1},{17,25},{25,17},{2,10},{10... | collective-permute-start | bytes 6291464 | tf_op jit(solution)/shard_map/ppermute | solution.py:105
  624.5 383.8 %copy-start.65 = (f32[2,2,512]{2,1,0:T(2,128)}, f32[2,2,512]{2,1,0:T(2,128)S(1)}, u32[]{:S(2)}) copy-start(f32[2,2,512]{2,1,0:T(2,128)S(1)} %get-tuple-element.275) | copy-start | bytes 24580
  624.6 42.1 %collective-permute-start.30 = (bf16[512,2048]{1,0:T(8,128)(2,1)}, bf16[512,2048]{1,0:T(8,128)(2,1)S(1)}, u32[]{:S(2)}, u32[]{:S(2)}) collective-permute-start(bf16[512,2048]{1,0:T(8,128)(2,1)} %collective-permute-done.29), channel_id=1, source_target_pairs={{0,8},{8,0},{16,24},{24,16},{1,9},{9,1},{17,25},{25,17},{2,10},{10... | collective-permute-start | bytes 6291464 | tf_op jit(solution)/shard_map/ppermute | solution.py:105
  655.4 26.3 %collective-permute-start.26 = (bf16[512,2048]{1,0:T(8,128)(2,1)}, bf16[512,2048]{1,0:T(8,128)(2,1)}, u32[]{:S(2)}, u32[]{:S(2)}) collective-permute-start(bf16[512,2048]{1,0:T(8,128)(2,1)} %collective-permute-done.25), channel_id=1, source_target_pairs={{0,8},{8,0},{16,24},{24,16},{1,9},{9,1},{17,25},{25,17},{2,10},{10... | collective-permute-start | bytes 6291464 | tf_op jit(solution)/shard_map/ppermute | solution.py:105
  681.2 52.4 %collective-permute-start.8 = (bf16[512,2048]{1,0:T(8,128)(2,1)}, bf16[512,2048]{1,0:T(8,128)(2,1)S(1)}, u32[]{:S(2)}, u32[]{:S(2)}) collective-permute-start(bf16[512,2048]{1,0:T(8,128)(2,1)} %multiply_convert_fusion.5), channel_id=1, source_target_pairs={{0,8},{8,0},{16,24},{24,16},{1,9},{9,1},{17,25},{25,17},{2,10},{10... | collective-permute-start | bytes 6291464 | tf_op jit(solution)/shard_map/ppermute | solution.py:105
  726.5 55.9 %collective-permute-start.19 = (bf16[512,2048]{1,0:T(8,128)(2,1)}, bf16[512,2048]{1,0:T(8,128)(2,1)}, u32[]{:S(2)}, u32[]{:S(2)}) collective-permute-start(bf16[512,2048]{1,0:T(8,128)(2,1)} %multiply_convert_fusion.5), channel_id=1, source_target_pairs={{0,3},{1,2},{2,1},{3,0},{4,7},{5,6},{6,5},{7,4},{8,11},{9,10},{10,... | collective-permute-start | bytes 6291464 | tf_op jit(solution)/shard_map/ppermute | solution.py:108
  729.1 180.3 %collective-permute-start.15 = (bf16[512,2048]{1,0:T(8,128)(2,1)}, bf16[512,2048]{1,0:T(8,128)(2,1)}, u32[]{:S(2)}, u32[]{:S(2)}) collective-permute-start(bf16[512,2048]{1,0:T(8,128)(2,1)} %multiply_convert_fusion.5), channel_id=1, source_target_pairs={{0,2},{1,3},{2,0},{3,1},{4,6},{5,7},{6,4},{7,5},{8,10},{9,11},{10,... | collective-permute-start | bytes 6291464 | tf_op jit(solution)/shard_map/ppermute | solution.py:108
  729.1 180.3 %collective-permute-start.11 = (bf16[512,2048]{1,0:T(8,128)(2,1)}, bf16[512,2048]{1,0:T(8,128)(2,1)}, u32[]{:S(2)}, u32[]{:S(2)}) collective-permute-start(bf16[512,2048]{1,0:T(8,128)(2,1)} %multiply_convert_fusion.5), channel_id=1, source_target_pairs={{0,1},{1,0},{2,3},{3,2},{4,5},{5,4},{6,7},{7,6},{8,9},{9,8},{10,11... | collective-permute-start | bytes 6291464 | tf_op jit(solution)/shard_map/ppermute | solution.py:108
  782.3 143.5 %collective-permute-start.20 = (bf16[512,2048]{1,0:T(8,128)(2,1)}, bf16[512,2048]{1,0:T(8,128)(2,1)}, u32[]{:S(2)}, u32[]{:S(2)}) collective-permute-start(bf16[512,2048]{1,0:T(8,128)(2,1)} %collective-permute-done.19), channel_id=1, source_target_pairs={{0,8},{8,0},{16,24},{24,16},{1,9},{9,1},{17,25},{25,17},{2,10},{10... | collective-permute-start | bytes 6291464 | tf_op jit(solution)/shard_map/ppermute | solution.py:105
  798.7 419.0 %collective-permute-start.24 = (bf16[512,2048]{1,0:T(8,128)(2,1)}, bf16[512,2048]{1,0:T(8,128)(2,1)}, u32[]{:S(2)}, u32[]{:S(2)}) collective-permute-start(bf16[512,2048]{1,0:T(8,128)(2,1)} %fusion.239), channel_id=1, source_target_pairs={{0,8},{8,0},{16,24},{24,16},{1,9},{9,1},{17,25},{25,17},{2,10},{10... | collective-permute-start | bytes 6291464 | tf_op jit(solution)/shard_map/ppermute | solution.py:105
  909.3 39.7 %collective-permute-start.16 = (bf16[512,2048]{1,0:T(8,128)(2,1)}, bf16[512,2048]{1,0:T(8,128)(2,1)}, u32[]{:S(2)}, u32[]{:S(2)}) collective-permute-start(bf16[512,2048]{1,0:T(8,128)(2,1)} %collective-permute-done.15), channel_id=1, source_target_pairs={{0,8},{8,0},{16,24},{24,16},{1,9},{9,1},{17,25},{25,17},{2,10},{10... | collective-permute-start | bytes 6291464 | tf_op jit(solution)/shard_map/ppermute | solution.py:105
  909.3 62.8 %collective-permute-start.12 = (bf16[512,2048]{1,0:T(8,128)(2,1)}, bf16[512,2048]{1,0:T(8,128)(2,1)}, u32[]{:S(2)}, u32[]{:S(2)}) collective-permute-start(bf16[512,2048]{1,0:T(8,128)(2,1)} %collective-permute-done.11), channel_id=1, source_target_pairs={{0,8},{8,0},{16,24},{24,16},{1,9},{9,1},{17,25},{25,17},{2,10},{10... | collective-permute-start | bytes 6291464 | tf_op jit(solution)/shard_map/ppermute | solution.py:105
  1024.5 173.5 %collective-permute-start.21 = (bf16[512,2048]{1,0:T(8,128)(2,1)}, bf16[512,2048]{1,0:T(8,128)(2,1)}, u32[]{:S(2)}, u32[]{:S(2)}) collective-permute-start(bf16[512,2048]{1,0:T(8,128)(2,1)} %fusion.238), channel_id=1, source_target_pairs={{0,8},{8,0},{16,24},{24,16},{1,9},{9,1},{17,25},{25,17},{2,10},{10... | collective-permute-start | bytes 6291464 | tf_op jit(solution)/shard_map/ppermute | solution.py:105
  1054.0 146.3 %collective-permute-start.17 = (bf16[512,2048]{1,0:T(8,128)(2,1)}, bf16[512,2048]{1,0:T(8,128)(2,1)}, u32[]{:S(2)}, u32[]{:S(2)}) collective-permute-start(bf16[512,2048]{1,0:T(8,128)(2,1)} %fusion.237), channel_id=1, source_target_pairs={{0,8},{8,0},{16,24},{24,16},{1,9},{9,1},{17,25},{25,17},{2,10},{10... | collective-permute-start | bytes 6291464 | tf_op jit(solution)/shard_map/ppermute | solution.py:105
  1107.3 81.1 %collective-permute-start.35 = (bf16[512,2048]{1,0:T(8,128)(2,1)}, bf16[512,2048]{1,0:T(8,128)(2,1)}, u32[]{:S(2)}, u32[]{:S(2)}) collective-permute-start(bf16[512,2048]{1,0:T(8,128)(2,1)} %fusion.242), channel_id=1, source_target_pairs={{0,8},{8,0},{16,24},{24,16},{1,9},{9,1},{17,25},{25,17},{2,10},{10... | collective-permute-start | bytes 6291464 | tf_op jit(solution)/shard_map/ppermute | solution.py:105
  1133.3 60.2 %collective-permute-start.31 = (bf16[512,2048]{1,0:T(8,128)(2,1)S(1)}, bf16[512,2048]{1,0:T(8,128)(2,1)}, u32[]{:S(2)}, u32[]{:S(2)}) collective-permute-start(bf16[512,2048]{1,0:T(8,128)(2,1)S(1)} %fusion.241), channel_id=1, source_target_pairs={{0,8},{8,0},{16,24},{24,16},{1,9},{9,1},{17,25},{25,17},{2,10},{10... | collective-permute-start | bytes 6291464 | tf_op jit(solution)/shard_map/ppermute | solution.py:105
  1188.4 19.5 collective-permute-start.13
  1193.5 18.3 collective-permute-start.27
  1198.0 50.8 %collective-permute-start.36 = (bf16[512,2048]{1,0:T(8,128)(2,1)}, bf16[512,2048]{1,0:T(8,128)(2,1)}, u32[]{:S(2)}, u32[]{:S(2)}) collective-permute-start(bf16[512,2048]{1,0:T(8,128)(2,1)} %fusion.138), channel_id=1, source_target_pairs={{0,3},{1,2},{2,1},{3,0},{4,7},{5,6},{6,5},{7,4},{8,11},{9,10},{10,... | collective-permute-start | bytes 6291464 | tf_op jit(solution)/shard_map/ppermute | solution.py:108
  1200.2 270.2 %collective-permute-start.32 = (bf16[512,2048]{1,0:T(8,128)(2,1)}, bf16[512,2048]{1,0:T(8,128)(2,1)}, u32[]{:S(2)}, u32[]{:S(2)}) collective-permute-start(bf16[512,2048]{1,0:T(8,128)(2,1)} %fusion.140), channel_id=1, source_target_pairs={{0,2},{1,3},{2,0},{3,1},{4,6},{5,7},{6,4},{7,5},{8,10},{9,11},{10,... | collective-permute-start | bytes 6291464 | tf_op jit(solution)/shard_map/ppermute | solution.py:108
  1207.9 403.5 %collective-permute-start.10 = (bf16[512,2048]{1,0:T(8,128)(2,1)}, bf16[512,2048]{1,0:T(8,128)(2,1)}, u32[]{:S(2)}, u32[]{:S(2)}) collective-permute-start(bf16[512,2048]{1,0:T(8,128)(2,1)} %fusion.235), channel_id=1, source_target_pairs={{0,8},{8,0},{16,24},{24,16},{1,9},{9,1},{17,25},{25,17},{2,10},{10... | collective-permute-start | bytes 6291464 | tf_op jit(solution)/shard_map/ppermute | solution.py:105
  1211.8 399.6 %collective-permute-start.22 = (bf16[512,2048]{1,0:T(8,128)(2,1)}, bf16[512,2048]{1,0:T(8,128)(2,1)}, u32[]{:S(2)}, u32[]{:S(2)}) collective-permute-start(bf16[512,2048]{1,0:T(8,128)(2,1)} %fusion.148), channel_id=1, source_target_pairs={{0,3},{1,2},{2,1},{3,0},{4,7},{5,6},{6,5},{7,4},{8,11},{9,10},{10,... | collective-permute-start | bytes 6291464 | tf_op jit(solution)/shard_map/ppermute | solution.py:108
  1217.7 393.7 %collective-permute-start.18 = (bf16[512,2048]{1,0:T(8,128)(2,1)}, bf16[512,2048]{1,0:T(8,128)(2,1)}, u32[]{:S(2)}, u32[]{:S(2)}) collective-permute-start(bf16[512,2048]{1,0:T(8,128)(2,1)} %fusion.150), channel_id=1, source_target_pairs={{0,2},{1,3},{2,0},{3,1},{4,6},{5,7},{6,4},{7,5},{8,10},{9,11},{10,... | collective-permute-start | bytes 6291464 | tf_op jit(solution)/shard_map/ppermute | solution.py:108
  1248.8 362.7 %collective-permute-start.14 = (bf16[512,2048]{1,0:T(8,128)(2,1)}, bf16[512,2048]{1,0:T(8,128)(2,1)}, u32[]{:S(2)}, u32[]{:S(2)}) collective-permute-start(bf16[512,2048]{1,0:T(8,128)(2,1)} %fusion.152), channel_id=1, source_target_pairs={{0,1},{1,0},{2,3},{3,2},{4,5},{5,4},{6,7},{7,6},{8,9},{9,8},{10,11... | collective-permute-start | bytes 6291464 | tf_op jit(solution)/shard_map/ppermute | solution.py:108
  1470.4 133.7 %collective-permute-start.28 = (bf16[512,2048]{1,0:T(8,128)(2,1)}, bf16[512,2048]{1,0:T(8,128)(2,1)S(1)}, u32[]{:S(2)}, u32[]{:S(2)}) collective-permute-start(bf16[512,2048]{1,0:T(8,128)(2,1)} %fusion.142), channel_id=1, source_target_pairs={{0,1},{1,0},{2,3},{3,2},{4,5},{5,4},{6,7},{7,6},{8,9},{9,8},{10,11... | collective-permute-start | bytes 6291464 | tf_op jit(solution)/shard_map/ppermute | solution.py:108
  1470.4 133.7 %copy-start.68 = (f32[2048]{0:T(1024)S(1)}, f32[2048]{0:T(1024)}, u32[]{:S(2)}) copy-start(f32[2048]{0:T(1024)} %copy-done.67) | copy-start | bytes 24580
  1470.4 133.7 %copy-start.86 = (f32[512]{0:T(512)S(1)}, f32[512]{0:T(512)}, u32[]{:S(2)}) copy-start(f32[512]{0:T(512)} %copy-done.85) | copy-start | bytes 6148
  1623.4 37.3 %collective-permute-start.37 = (bf16[512,2048]{1,0:T(8,128)(2,1)S(1)}, bf16[512,2048]{1,0:T(8,128)(2,1)}, u32[]{:S(2)}, u32[]{:S(2)}) collective-permute-start(bf16[512,2048]{1,0:T(8,128)(2,1)S(1)} %get-tuple-element.212), channel_id=1, source_target_pairs={{0,8},{8,0},{16,24},{24,16},{1,9},{9,1},{17,25},{25,17},{2,10},{10... | collective-permute-start | bytes 6291464 | tf_op jit(solution)/shard_map/ppermute | solution.py:105
  1660.7 587.5 %reduce-scatter.3.cloned.1.call-start = ((), (), s32[]{:S(2)}) async-start(), calls=%async_computation.3 | async-start | bytes 11698176 | tf_op jit(solution)/shard_map/reduce_scatter | solution.py:454
  1845.4 123.0 %collective-permute-start.38 = (bf16[2,512,512]{1,2,0:T(8,128)(2,1)}, bf16[2,512,512]{1,2,0:T(8,128)(2,1)}, u32[]{:S(2)}, u32[]{:S(2)}) collective-permute-start(bf16[2,512,512]{1,2,0:T(8,128)(2,1)} %select_convert_fusion), channel_id=1, source_target_pairs={{0,4},{4,0},{1,5},{5,1},{2,6},{6,2},{3,7},{7,3},{8,12},{12,8},{9,1... | collective-permute-start | bytes 3145736 | tf_op jit(solution)/shard_map/ppermute | solution.py:405
  2012.8 18.4 collective-permute-start.39
  2061.7 370.6 %reduce-scatter.5.cloned.1.call-start = ((), (), s32[]{:S(2)}) async-start(), calls=%async_computation.4 | async-start | bytes 8912896 | tf_op jit(solution)/shard_map/reduce_scatter | solution.py:354
  2093.3 1.4 collective-permute-start.44
  2094.7 3.6 collective-permute-start.45
  2098.3 3.6 collective-permute-start.46
  2101.9 3.7 collective-permute-start.47
  2105.6 12.2 collective-permute-start.48
  2110.5 11.2 collective-permute-start.41
  2119.8 6.0 collective-permute-start.42
  2121.0 5.5 collective-permute-start.43
  2249.4 185.0 %collective-permute-start.40 = (bf16[64,2688]{1,0:T(8,128)(2,1)S(1)}, bf16[64,2688]{1,0:T(8,128)(2,1)}, u32[]{:S(2)}, u32[]{:S(2)}) collective-permute-start(bf16[64,2688]{1,0:T(8,128)(2,1)S(1)} %select_bitcast_fusion.9), channel_id=1, source_target_pairs={{0,8},{8,0},{16,24},{24,16},{1,9},{9,1},{17,25},{25,17},{2,10},{10... | collective-permute-start | bytes 1032200 | tf_op jit(solution)/shard_map/ppermute | solution.py:105
  2251.3 183.1 %copy-start.39 = (bf16[1,2,64,2688]{3,2,1,0:T(8,128)(2,1)S(1)}, bf16[1,2,64,2688]{3,2,1,0:T(8,128)(2,1)}, u32[]{:S(2)}) copy-start(bf16[1,2,64,2688]{3,2,1,0:T(8,128)(2,1)} %reduce-scatter.3.cloned.1.call-done) | copy-start | bytes 2064388
  (151 other events, 2719.2 us)
Sparse Core Ops, SparseCore 0:
  25.3 277.0 all-gather.12
  305.2 124.6 all-gather.10
  432.2 68.4 all-gather.14
  503.0 70.1 all-gather.16
  574.9 70.1 all-gather.18
  1660.8 364.8 all-reduce.8
  2061.8 186.3 reduce-scatter.2
  2250.6 181.6 reduce-scatter.4

commit v2 on v1

v2 whole, which is shorter than its diff:
```python
import functools

import jax
import jax.numpy as jnp
from jax import lax
from jax.experimental import pallas as pl
from jax.experimental.pallas import tpu as pltpu
from jax.sharding import PartitionSpec as P

QUERY_HEADS = 32
KEY_VALUE_HEADS = 4
HEAD_DIM = 128


EPS = 1e-06
ROPE_BASE = 1000000.0
MASKED = -1e30


def contract_rows(first_op, second_op):
    return lax.dot_general(
        first_op, second_op, (((0,), (0,)), ((), ())), preferred_element_type=jnp.float32
    )


def contract_cols(first_op, second_op):
    return lax.dot_general(
        first_op, second_op, (((1,), (1,)), ((), ())), preferred_element_type=jnp.float32
    )


def rope_tables(positions):
    half_dim = HEAD_DIM // 2
    inverse = ROPE_BASE ** (-jnp.arange(half_dim, dtype=jnp.float32) * 2.0 / HEAD_DIM)
    angles = positions.astype(jnp.float32)[:, None] * inverse[None, :]
    cosine_table = jnp.cos(angles)
    sine_values = jnp.sin(angles)
    return (
        jnp.concatenate([cosine_table, cosine_table], -1),
        jnp.concatenate([sine_values, sine_values], -1),
    )


def inverse_rotation(gradient, cosine_table, sine_values):
    half_dim = gradient.shape[-1] // 2
    scaled = gradient * sine_values[:, None, :]
    return gradient * cosine_table[:, None, :] + jnp.concatenate(
        [scaled[..., half_dim:], -scaled[..., :half_dim]], -1
    )


def norm_back(gradient, source, inverse, gain_vec):
    scaled = gradient * gain_vec
    return inverse * scaled - source * inverse**3 * jnp.mean(
        scaled * source, axis=-1, keepdims=True
    )


def neighbours(n_exp):
    seq, x, z = lax.axis_index("seq"), lax.axis_index("ctx"), lax.axis_index("exp")
    y, core = seq // 2, seq % 2
    ids = {
        "core": {"seq": 2 * y + 1 - core},
        "x": {"ctx": 1 - x},
        "y": {"seq": 2 * (1 - y) + core},
        "up": {"exp": z + 1},
        "down": {"exp": z - 1},
    }
    return x, y, z, core, ids


def greet(z, n_exp, ids, names):
    barrier = pltpu.get_barrier_semaphore()
    count = 0
    for name in names:
        if name in ("up", "down"):
            there = (z < n_exp - 1) if name == "up" else (z > 0)

            @pl.when(there)
            def _():
                pl.semaphore_signal(
                    barrier, inc=1, device_id=ids[name], device_id_type=pl.DeviceIdType.MESH
                )

            count = count + there.astype(jnp.int32)
        else:
            pl.semaphore_signal(
                barrier, inc=1, device_id=ids[name], device_id_type=pl.DeviceIdType.MESH
            )
            count = count + 1
    pl.semaphore_wait(barrier, count)


def gather_kernel(n_exp, mine_ref, other_ref, full_ref, local_sem, core_sems, z_sems, x_sems, y_sems, xf_sems, yf_sems):
    x, y, z, core, ids = neighbours(n_exp)
    greet(z, n_exp, ids, ("core", "x", "y", "up", "down"))
    here, beside, across = 2 * y + x, 2 * y + 1 - x, 2 * (1 - y) + x

    def remote(part, sems, slot, name):
        return pltpu.make_async_remote_copy(
            src_ref=part,
            dst_ref=part,
            send_sem=sems.at[0, slot],
            recv_sem=sems.at[1, slot],
            device_id=ids[name],
            device_id_type=pl.DeviceIdType.MESH,
        )

    local = pltpu.make_async_copy(mine_ref, full_ref.at[here, z, core], local_sem)
    local.start()
    to_core = pltpu.make_async_remote_copy(
        src_ref=other_ref,
        dst_ref=full_ref.at[here, z, core],
        send_sem=core_sems.at[0],
        recv_sem=core_sems.at[1],
        device_id=ids["core"],
        device_id_type=pl.DeviceIdType.MESH,
    )
    to_core.start()
    to_core.wait()
    local.wait()

    def source(label):
        hop = (label + 1) // 2
        if label == 0:
            return z, None
        return (z - hop, z >= hop) if label % 2 else (z + hop, z + hop < n_exp)

    labels = range(2 * n_exp - 1)

    def guarded(condition, action):
        if condition is None:
            action()
        else:
            pl.when(condition)(action)

    def z_copy(label, name):
        part, _ = source(label)
        slot = label + 1 if label % 2 else label + 1
        if label == 0:
            slot = 0 if name == "up" else 1
        else:
            slot = label + 1
        return remote(full_ref.at[here, part], z_sems, slot, name)

    def z_sends(label):
        part, there = source(label)
        for name in ("up", "down") if label == 0 else (("up",) if label % 2 else ("down",)):
            room = (z < n_exp - 1) if name == "up" else (z > 0)
            yield name, room if there is None else there & room

    def z_arrival(label):
        hop = (label + 1) // 2
        name = "up" if label % 2 else "down"
        slot = (label - 1) if hop > 1 else (0 if name == "up" else 1)
        part, _ = source(label)
        remote(full_ref.at[here, part], z_sems, slot, name).wait_recv()

    def spread(label):
        part, there = source(label)

        def action():
            remote(full_ref.at[here, part], x_sems, label, "x").start()
            remote(full_ref.at[here, part], y_sems, label, "y").start()

        guarded(there, action)
        for name, condition in z_sends(label):
            pl.when(condition)(lambda name=name: z_copy(label, name).start())

    def turn(label):
        part, there = source(label)

        def action():
            remote(full_ref.at[beside, part], x_sems, label, "x").wait_recv()
            remote(full_ref.at[beside, part, 0], xf_sems, label, "y").start()
            remote(full_ref.at[across, part], y_sems, label, "y").wait_recv()
            remote(full_ref.at[across, part, 1], yf_sems, label, "x").start()

        guarded(there, action)

    spread(0)
    for hop in range(1, n_exp):
        for label in (2 * hop - 1, 2 * hop):
            part, there = source(label)

            def action(label=label):
                z_arrival(label)

            pl.when(there)(action)
            spread(label)
        for label in (0,) if hop == 1 else (2 * hop - 3, 2 * hop - 2):
            turn(label)
    for label in (2 * n_exp - 3, 2 * n_exp - 2):
        turn(label)
    opposite = 2 * (1 - y) + 1 - x
    for label in labels:
        part, there = source(label)

        def action(label=label, part=part):
            remote(full_ref.at[here, part], x_sems, label, "x").wait_send()
            remote(full_ref.at[here, part], y_sems, label, "y").wait_send()
            remote(full_ref.at[beside, part, 0], xf_sems, label, "y").wait_send()
            remote(full_ref.at[across, part, 1], yf_sems, label, "x").wait_send()
            remote(full_ref.at[opposite, part, 0], xf_sems, label, "y").wait_recv()
            remote(full_ref.at[opposite, part, 1], yf_sems, label, "x").wait_recv()

        guarded(there, action)
        for name, condition in z_sends(label):
            pl.when(condition)(lambda label=label, name=name: z_copy(label, name).wait_send())


def gather_chips(mine, other, n_exp):
    labels = 2 * n_exp - 1
    any_spec = pl.BlockSpec(memory_space=pl.ANY)
    vmem_spec = pl.BlockSpec(memory_space=pltpu.VMEM)
    pair = lambda count: pltpu.SemaphoreType.DMA((2, count))
    return pl.pallas_call(
        functools.partial(gather_kernel, n_exp),
        in_specs=[vmem_spec, vmem_spec],
        out_specs=any_spec,
        out_shape=jax.ShapeDtypeStruct((4, n_exp, 2) + mine.shape, mine.dtype),
        scratch_shapes=[
            pltpu.SemaphoreType.DMA,
            pltpu.SemaphoreType.DMA((2,)),
            pair(2 * n_exp),
            pair(labels),
            pair(labels),
            pair(labels),
            pair(labels),
        ],
        compiler_params=pltpu.CompilerParams(collective_id=1, has_side_effects=True),
        name="gather_chips",
    )(mine, other)


def exchange_kernel(n_exp, token_ref, table_ref, tokens_ref, tables_ref, z_sems, core_sems):
    x, y, z, core, ids = neighbours(n_exp)
    greet(z, n_exp, ids, ("core", "up", "down"))
    sources, results = (token_ref, table_ref), (tokens_ref, tables_ref)

    def remote(which, label, sems, slot, name):
        there = results[which].at[source(label)[0], core]
        return pltpu.make_async_remote_copy(
            src_ref=sources[which] if label == 0 else there,
            dst_ref=there,
            send_sem=sems.at[0, which, slot],
            recv_sem=sems.at[1, which, slot],
            device_id=ids[name],
            device_id_type=pl.DeviceIdType.MESH,
        )

    def source(label):
        hop = (label + 1) // 2
        if label == 0:
            return z, None
        return (z - hop, z >= hop) if label % 2 else (z + hop, z + hop < n_exp)

    def guarded(condition, action):
        if condition is None:
            action()
        else:
            pl.when(condition)(action)

    def each(label, sems, slot, name, method):
        for which in range(2):
            getattr(remote(which, label, sems, slot, name), method)()

    def z_sends(label, method):
        part, there = source(label)
        for name in ("up", "down") if label == 0 else (("up",) if label % 2 else ("down",)):
            room = (z < n_exp - 1) if name == "up" else (z > 0)
            slot = (0 if name == "up" else 1) if label == 0 else label + 1
            condition = room if there is None else there & room
            pl.when(condition)(lambda name=name, slot=slot: each(label, z_sems, slot, name, method))

    z_sends(0, "start")
    each(0, core_sems, 0, "core", "start")
    for hop in range(1, n_exp):
        for label in (2 * hop - 1, 2 * hop):
            part, there = source(label)
            name = "up" if label % 2 else "down"
            slot = (label - 1) if hop > 1 else (0 if name == "up" else 1)
            guarded(there, lambda: each(label, z_sems, slot, name, "wait_recv"))
            z_sends(label, "start")
            guarded(there, lambda: each(label, core_sems, label, "core", "start"))
    for label in range(2 * n_exp - 1):
        part, there = source(label)
        z_sends(label, "wait_send")
        guarded(there, lambda: each(label, core_sems, label, "core", "wait"))


def exchange_column(tokens, table, n_exp):
    any_spec = pl.BlockSpec(memory_space=pl.ANY)
    labels = 2 * n_exp - 1
    return pl.pallas_call(
        functools.partial(exchange_kernel, n_exp),
        in_specs=[any_spec] * 2,
        out_specs=[any_spec] * 2,
        out_shape=[
            jax.ShapeDtypeStruct((n_exp, 2) + a.shape, a.dtype) for a in (tokens, table)
        ],
        scratch_shapes=[
            pltpu.SemaphoreType.DMA((2, 2, 2 * n_exp)),
            pltpu.SemaphoreType.DMA((2, 2, labels)),
        ],
        compiler_params=pltpu.CompilerParams(collective_id=3, has_side_effects=True),
        cost_estimate=pl.CostEstimate(
            flops=0, bytes_accessed=16 * n_exp * tokens.size, transcendentals=0
        ),
        name="exchange_column",
    )(tokens, table)


def scatter_kernel(
    n_exp,
    normed_ref,
    grad_ref,
    kv_grad_ref,
    extra_ref,
    after_ref,
    mine_ref,
    theirs_ref,
    turned,
    part,
    from_x,
    from_y,
    second_x,
    second_y,
    total,
    from_z,
    from_core,
    x_sems,
    y_sems,
    x2_sems,
    y2_sems,
    z_sems,
    core_sems,
):
    bf16, f32 = jnp.bfloat16, jnp.float32
    x, y, z, core, ids = neighbours(n_exp)
    barrier = pltpu.get_barrier_semaphore()
    columns = [{"exp": (z + k) % n_exp} for k in range(1, n_exp)]
    for there in [ids["core"], ids["x"], ids["y"]] + columns:
        pl.semaphore_signal(barrier, inc=1, device_id=there, device_id_type=pl.DeviceIdType.MESH)
    pl.semaphore_wait(barrier, 2 + n_exp)

    def remote(source, target, sems, slot, there):
        return pltpu.make_async_remote_copy(
            src_ref=source,
            dst_ref=target,
            send_sem=sems.at[0, slot],
            recv_sem=sems.at[1, slot],
            device_id=there,
            device_id_type=pl.DeviceIdType.MESH,
        )

    rows = mine_ref.shape[0]
    q_width, width = grad_ref.shape[1], grad_ref.shape[1] + kv_grad_ref.shape[1]
    turned[...] = normed_ref[...].T
    steps = range(n_exp)

    def first_copies(k):
        return [
            remote(part.at[k, 1 - x, :, 0], from_x.at[k], x_sems, k, ids["x"]),
            remote(part.at[k, :, 1 - y, 1], from_y.at[k], y_sems, k, ids["y"]),
        ]

    def second_copies(k):
        return [
            remote(part.at[k, x, 1 - y, 0], second_x.at[k], x2_sems, k, ids["y"]),
            remote(part.at[k, 1 - x, y, 1], second_y.at[k], y2_sems, k, ids["x"]),
        ]

    def z_copy(k):
        return remote(
            total.at[k], from_z.at[k], z_sems, k, {"exp": (z + k + 1) % n_exp}
        )

    for k in steps:
        place = (z + k + 1) % n_exp
        blocks = []
        for px in range(2):
            for py in range(2):
                for c in range(2):
                    start = (((py * 2 + c) * 2 + px) * n_exp + place) * rows
                    blocks.append(turned[pl.ds(pl.multiple_of(start, rows), rows), :])
        block = jnp.concatenate(blocks, 0)
        grad = dot_plain(block, grad_ref[...]).astype(bf16)
        kv_grad = dot_plain(block, kv_grad_ref[...]).astype(bf16)
        i = 0
        for px in range(2):
            for py in range(2):
                for c in range(2):
                    part[k, px, py, c, :, :q_width] = grad[i * rows : (i + 1) * rows]
                    part[k, px, py, c, :, q_width:width] = kv_grad[i * rows : (i + 1) * rows]
                    part[k, px, py, c, :, width:] = extra_ref[py, c, px, place]
                    i += 1
        for copy in first_copies(k):
            copy.start()

    def second(k):
        along_x, along_y = first_copies(k)
        along_x.wait_recv()
        for py in range(2):
            part[k, x, py, 0] = (part[k, x, py, 0].astype(f32) + from_x[k, py].astype(f32)).astype(bf16)
        along_y.wait_recv()
        for px in range(2):
            part[k, px, y, 1] = (part[k, px, y, 1].astype(f32) + from_y[k, px].astype(f32)).astype(bf16)
        for copy in second_copies(k):
            copy.start()

    def third(k):
        along_y, along_x = second_copies(k)
        along_y.wait_recv()
        total[k, 0] = (part[k, x, y, 0].astype(f32) + second_x[k].astype(f32)).astype(bf16)
        along_x.wait_recv()
        total[k, 1] = (part[k, x, y, 1].astype(f32) + second_y[k].astype(f32)).astype(bf16)
        if k < n_exp - 1:
            z_copy(k).start()

    second(0)
    for k in range(1, n_exp):
        second(k)
        third(k - 1)
    third(n_exp - 1)
    result = total[n_exp - 1].astype(f32)
    for k in range(n_exp - 1):
        z_copy(k).wait_recv()
        result = result + from_z[k].astype(f32)
    total[n_exp - 1] = result.astype(bf16)
    to_core = remote(total.at[n_exp - 1, 1 - core], from_core, core_sems, 0, ids["core"])
    to_core.start()
    for k in steps:
        for copy in first_copies(k) + second_copies(k) + ([z_copy(k)] if k < n_exp - 1 else []):
            copy.wait_send()
    to_core.wait()
    mine_ref[...] = total[n_exp - 1, core].astype(f32)
    theirs_ref[...] = from_core[...].astype(f32)


def dense_grad_scatter(normed, grad, kv_grad, extra, after, n_exp):
    bf16 = jnp.bfloat16
    rows, model = extra.shape[4], normed.shape[1]
    width = grad.shape[1] + kv_grad.shape[1] + extra.shape[5]
    block = (rows, width)
    vmem = lambda *lead: pltpu.VMEM(lead + block, bf16)
    pair = lambda count: pltpu.SemaphoreType.DMA((2, count))
    spec = pl.BlockSpec(memory_space=pltpu.VMEM)
    return pl.pallas_call(
        functools.partial(scatter_kernel, n_exp),
        in_specs=[spec] * 4 + [pl.BlockSpec(memory_space=pl.ANY)],
        out_specs=[spec] * 2,
        out_shape=[jax.ShapeDtypeStruct(block, jnp.float32)] * 2,
        scratch_shapes=[
            pltpu.VMEM((model, normed.shape[0]), bf16),
            vmem(n_exp, 2, 2, 2),
            vmem(n_exp, 2),
            vmem(n_exp, 2),
            vmem(n_exp),
            vmem(n_exp),
            vmem(n_exp, 2),
            vmem(n_exp, 2),
            vmem(),
            pair(n_exp),
            pair(n_exp),
            pair(n_exp),
            pair(n_exp),
            pair(n_exp),
            pair(1),
        ],
        compiler_params=pltpu.CompilerParams(
            collective_id=2, has_side_effects=True, vmem_limit_bytes=60 * MIB
        ),
        cost_estimate=pl.CostEstimate(
            flops=2 * normed.shape[0] * model * width, bytes_accessed=16 * MIB, transcendentals=0
        ),
        name="dense_grad_scatter",
    )(normed, grad, kv_grad, extra, after)


def pick(core, first, second):
    return jnp.where(core == 0, first, second)


def column_halves(weight, core):
    width = weight.shape[1] // KEY_VALUE_HEADS
    parts = [weight[:, i * width : (i + 1) * width] for i in range(KEY_VALUE_HEADS)]
    mine = [pick(core, parts[i], parts[i + 1]) for i in range(0, KEY_VALUE_HEADS, 2)]
    other = [pick(core, parts[i + 1], parts[i]) for i in range(0, KEY_VALUE_HEADS, 2)]
    return mine, other


LOG2E = 1.4426950408889634
MIB = 1 << 20


def rotate_rows(vectors, cosine_table, signed_sine):
    return vectors * cosine_table + pltpu.roll(vectors, HEAD_DIM // 2, 1) * signed_sine


def rotate_rows_back(gradient, cosine_table, signed_sine):
    return gradient * cosine_table - pltpu.roll(gradient, HEAD_DIM // 2, 1) * signed_sine


def dot_cols(first, second):
    return lax.dot_general(
        first, second, (((1,), (1,)), ((), ())), preferred_element_type=jnp.float32
    )


def dot_plain(first, second):
    return jnp.dot(first, second, preferred_element_type=jnp.float32)


def projection_kernel(
    n_y, n_xz, normed_ref, weight_ref, gain_ref, cos_ref, sin_ref, raw_ref, low_ref, ordered_ref, *, plain
):
    pieces = [
        weight_ref[y * n_xz + i, c] for y in range(n_y) for c in range(2) for i in range(n_xz)
    ]
    weight = jnp.concatenate(pieces, 0)
    ordered_ref[...] = weight
    raw = dot_plain(normed_ref[...], weight)
    raw_ref[...] = raw
    tokens = cos_ref.shape[0]

    def normed_store():
        for h in range(2):
            columns = slice(h * HEAD_DIM, (h + 1) * HEAD_DIM)
            head = raw[:, columns]
            inverse = lax.rsqrt(jnp.mean(head * head, axis=-1, keepdims=True) + EPS)
            scaled = head * inverse * gain_ref[...]
            for s in range(2):
                part = slice(s * tokens, (s + 1) * tokens)
                low_ref[part, columns] = rotate_rows(
                    scaled[part], cos_ref[...], sin_ref[...]
                ).astype(jnp.bfloat16)

    if plain is None:
        normed_store()
    else:
        pl.when(pl.program_id(0) != plain)(normed_store)

        @pl.when(pl.program_id(0) == plain)
        def _():
            low_ref[...] = raw.astype(jnp.bfloat16)


def project(normed, gathered, first_block, blocks, gain, cos, sin, n_y, plain=None):
    total, model = normed.shape
    n_yxz, _, rows, _ = gathered.shape
    width = 2 * HEAD_DIM
    fixed = lambda j: (0, 0)
    moving = lambda j: (0, j)
    return pl.pallas_call(
        functools.partial(projection_kernel, n_y, n_yxz // n_y, plain=plain),
        grid=(blocks,),
        in_specs=[
            pl.BlockSpec((total, model), fixed),
            pl.BlockSpec((n_yxz, 2, rows, width), lambda j: (0, 0, 0, j + first_block)),
            pl.BlockSpec((1, HEAD_DIM), fixed),
            pl.BlockSpec(cos.shape, fixed),
            pl.BlockSpec(sin.shape, fixed),
        ],
        out_specs=[
            pl.BlockSpec((total, width), moving),
            pl.BlockSpec((total, width), moving),
            pl.BlockSpec((model, width), moving),
        ],
        out_shape=[
            jax.ShapeDtypeStruct((total, blocks * width), jnp.float32),
            jax.ShapeDtypeStruct((total, blocks * width), jnp.bfloat16),
            jax.ShapeDtypeStruct((model, blocks * width), jnp.bfloat16),
        ],
        compiler_params=pltpu.CompilerParams(vmem_limit_bytes=56 * MIB),
        cost_estimate=pl.CostEstimate(
            flops=2 * total * model * blocks * width,
            bytes_accessed=total * model * 2 + blocks * width * (model * 4 + total * 6),
            transcendentals=0,
        ),
        name="project",
    )(normed, gathered, gain, cos, sin)


def mask_bias(seg_key, info):
    keys, tokens = seg_key.shape[0], info.shape[1]
    key_pos = lax.broadcasted_iota(jnp.int32, (keys, tokens), 0)
    allowed = (seg_key == info[0:1]) & (key_pos <= info[1:2])
    return jnp.where(allowed, 0.0, MASKED)


def key_tile(keys):
    return min(keys, 256)


def attention_kernel(info_ref, seg_ref, q_ref, k_ref, v_ref, mixed_ref, recip_ref, bias_ref, vt_ref):
    keys = k_ref.shape[1]
    tile = key_tile(keys)

    @pl.when((pl.program_id(1) == 0) & (pl.program_id(2) == 0))
    def _():
        bias_ref[...] = mask_bias(seg_ref[0], info_ref[0])

    @pl.when(pl.program_id(2) == 0)
    def _():
        vt_ref[...] = v_ref[0].astype(jnp.float32).T.astype(jnp.bfloat16)

    queries = q_ref[...]
    total, mixed = None, None
    for start in range(0, keys, tile):
        part = slice(start, start + tile)
        scores = dot_cols(k_ref[0, part], queries) * (HEAD_DIM**-0.5 * LOG2E) + bias_ref[part]
        weights = jnp.exp2(scores)
        tile_total = jnp.sum(weights, axis=0, keepdims=True)
        tile_mixed = dot_plain(vt_ref[:, part], weights.astype(jnp.bfloat16))
        total = tile_total if total is None else total + tile_total
        mixed = tile_mixed if mixed is None else mixed + tile_mixed
    recip = 1.0 / total
    recip_ref[0] = recip
    valid = (info_ref[0, 0:1] > 0).astype(jnp.float32)
    mixed_ref[...] = (mixed * (recip * valid)).T.astype(jnp.bfloat16)


def attention_specs(tokens, keys, groups, per_group):
    head = pl.BlockSpec((tokens, HEAD_DIM), lambda s, g, h: (s, g * per_group + h))
    return dict(
        info=pl.BlockSpec((1, 8, tokens), lambda s, g, h: (s, 0, 0)),
        seg=pl.BlockSpec((1, keys, 1), lambda s, g, h: (s, 0, 0)),
        head=head,
        key=pl.BlockSpec((1, keys, HEAD_DIM), lambda s, g, h: (s, 0, g)),
        value=pl.BlockSpec((1, keys, HEAD_DIM), lambda s, g, h: (s, 0, groups + g)),
        recip=pl.BlockSpec((1, 1, tokens), lambda s, g, h: ((s * groups + g) * per_group + h, 0, 0)),
    )


def attend(info, seg_keys, queries, kv_full, groups, per_group):
    tokens, keys = info.shape[2], seg_keys.shape[1]
    specs = attention_specs(tokens, keys, groups, per_group)
    steps = 2 * groups * per_group
    return pl.pallas_call(
        attention_kernel,
        grid=(2, groups, per_group),
        in_specs=[specs["info"], specs["seg"], specs["head"], specs["key"], specs["value"]],
        out_specs=[specs["head"], specs["recip"]],
        out_shape=[
            jax.ShapeDtypeStruct(queries.shape, jnp.bfloat16),
            jax.ShapeDtypeStruct((steps, 1, tokens), jnp.float32),
        ],
        scratch_shapes=[
            pltpu.VMEM((keys, tokens), jnp.float32),
            pltpu.VMEM((HEAD_DIM, keys), jnp.bfloat16),
        ],
        compiler_params=pltpu.CompilerParams(vmem_limit_bytes=48 * MIB),
        cost_estimate=pl.CostEstimate(
            flops=steps * 8 * tokens * keys * HEAD_DIM,
            bytes_accessed=queries.size * 4 + kv_full.size * 2,
            transcendentals=steps * tokens * keys,
        ),
        name="attend",
    )(info, seg_keys, queries, kv_full, kv_full)


def attention_back_kernel(
    info_ref,
    seg_ref,
    q_ref,
    k_ref,
    v_ref,
    mixed_ref,
    grad_ref,
    recip_ref,
    raw_ref,
    gain_ref,
    cos_ref,
    sin_ref,
    raw_grad_ref,
    key_grad_ref,
    value_grad_ref,
    gain_grad_ref,
    bias_ref,
    kt_ref,
):
    keys = k_ref.shape[1]
    tile = key_tile(keys)
    scale = HEAD_DIM**-0.5
    first = (pl.program_id(1) == 0) & (pl.program_id(2) == 0)

    @pl.when(first)
    def _():
        bias_ref[...] = mask_bias(seg_ref[0], info_ref[0])

    @pl.when(first & (pl.program_id(0) == 0))
    def _():
        gain_grad_ref[...] = jnp.zeros_like(gain_grad_ref)

    @pl.when(pl.program_id(2) == 0)
    def _():
        kt_ref[...] = k_ref[0].astype(jnp.float32).T.astype(jnp.bfloat16)
        key_grad_ref[...] = jnp.zeros_like(key_grad_ref)
        value_grad_ref[...] = jnp.zeros_like(value_grad_ref)

    queries, grad = q_ref[...], grad_ref[...]
    recip = recip_ref[0]
    overlap = grad.astype(jnp.float32) * mixed_ref[...].astype(jnp.float32)
    inner = jnp.sum(overlap.T, axis=0, keepdims=True)
    query_grad = None
    for start in range(0, keys, tile):
        part = slice(start, start + tile)
        scores = dot_cols(k_ref[0, part], queries) * (scale * LOG2E) + bias_ref[part]
        probs = jnp.exp2(scores) * recip
        grad_probs = dot_cols(v_ref[0, part], grad)
        grad_scores = (probs * (grad_probs - inner)).astype(jnp.bfloat16)
        value_grad_ref[0, part] += dot_plain(probs.astype(jnp.bfloat16), grad)
        key_grad_ref[0, part] += dot_plain(grad_scores, queries) * scale
        tile_grad = dot_plain(kt_ref[:, part], grad_scores)
        query_grad = tile_grad if query_grad is None else query_grad + tile_grad
    turned = rotate_rows_back((query_grad * scale).T, cos_ref[...], sin_ref[...])
    raw = raw_ref[...]
    inverse = lax.rsqrt(jnp.mean(raw * raw, axis=-1, keepdims=True) + EPS)
    unit = raw * inverse
    gain_grad_ref[0:1] += jnp.sum(turned * unit, axis=0, keepdims=True)
    scaled = turned * gain_ref[...]
    raw_grad_ref[...] = (
        inverse * (scaled - unit * jnp.mean(scaled * unit, axis=-1, keepdims=True))
    ).astype(jnp.bfloat16)


def attend_back(
    info, seg_keys, queries, kv_full, mixed, grad_mixed, recip, raw, gain, cos, sin, groups, per_group
):
    tokens, keys = info.shape[2], seg_keys.shape[1]
    specs = attention_specs(tokens, keys, groups, per_group)
    steps = 2 * groups * per_group
    fixed = lambda s, g, h: (0, 0)
    key_grad = jax.ShapeDtypeStruct((2, keys, groups * HEAD_DIM), jnp.float32)
    return pl.pallas_call(
        attention_back_kernel,
        grid=(2, groups, per_group),
        in_specs=[specs["info"], specs["seg"], specs["head"], specs["key"], specs["value"]]
        + [specs["head"], specs["head"], specs["recip"], specs["head"]]
        + [pl.BlockSpec(a.shape, fixed) for a in (gain, cos, sin)],
        out_specs=[specs["head"], specs["key"], specs["key"], pl.BlockSpec((8, HEAD_DIM), fixed)],
        out_shape=[
            jax.ShapeDtypeStruct(queries.shape, jnp.bfloat16),
            key_grad,
            key_grad,
            jax.ShapeDtypeStruct((8, HEAD_DIM), jnp.float32),
        ],
        scratch_shapes=[
            pltpu.VMEM((keys, tokens), jnp.float32),
            pltpu.VMEM((HEAD_DIM, keys), jnp.bfloat16),
        ],
        compiler_params=pltpu.CompilerParams(vmem_limit_bytes=48 * MIB),
        cost_estimate=pl.CostEstimate(
            flops=steps * 20 * tokens * keys * HEAD_DIM,
            bytes_accessed=queries.size * 12 + kv_full.size * 6,
            transcendentals=steps * tokens * keys,
        ),
        name="attend_back",
    )(
        info, seg_keys, queries, kv_full, kv_full, mixed, grad_mixed, recip, raw, gain, cos, sin
    )


def expert_kernel(
    here,
    place_ref,
    table_ref,
    own_ref,
    tokens_ref,
    own_cot_ref,
    sib_cot_ref,
    gate_w_ref,
    up_w_ref,
    down_w_ref,
    *refs,
):
    (x_ref, val_ref, product_ref, gate_grad_ref, up_grad_ref, out_ref, grad_ref) = refs[-12:-5]
    token_scr, cot_scr, out_scr, grad_scr, sems = refs[-5:]
    bf16 = jnp.bfloat16
    e, s = pl.program_id(0), pl.program_id(1)
    slots, tokens = x_ref.shape[1], token_scr.shape[1]
    chip, core = place_ref[0], place_ref[1]
    owner = jnp.where(s == 0, core, 1 - core)

    def copies(which):
        held_by = core if which == 0 else 1 - core
        tokens_from = own_ref if here and which == 0 else tokens_ref.at[chip, held_by]
        sources = (tokens_from, (own_cot_ref, sib_cot_ref)[which])
        return [
            pltpu.make_async_copy(source, scratch.at[which], sems.at[which, i])
            for i, (source, scratch) in enumerate(zip(sources, (token_scr, cot_scr)))
        ]

    @pl.when((e == 0) & (s == 0))
    def _():
        for which in range(2):
            for copy in copies(which):
                copy.start()
        for copy in copies(0):
            copy.wait()

    @pl.when((e == 0) & (s == 1))
    def _():
        for copy in copies(1):
            copy.wait()

    slot_ids = lax.broadcasted_iota(jnp.int32, (slots, tokens), 0).astype(jnp.float32)

    def hits_of(expert):
        return table_ref[chip, owner, pl.ds(place_ref[2] + expert, 1)] == slot_ids

    hits = hits_of(e)
    one_hot = hits.astype(jnp.float32).astype(bf16)
    gate_row = jnp.sum(jnp.where(hits, table_ref[chip, owner, pl.ds(place_ref[3] + e, 1)], 0.0), axis=1, keepdims=True)
    x_rows = dot_plain(one_hot, token_scr[s]).astype(bf16)
    x_ref[0] = x_rows
    grad_val = (gate_row * dot_plain(one_hot, cot_scr[s])).astype(bf16)
    val_ref[0] = grad_val
    gate_act = dot_plain(x_rows, gate_w_ref[0])
    up_act = dot_plain(x_rows, up_w_ref[0])
    sigmoid = 1.0 / (1.0 + jnp.exp(-gate_act))
    silu = gate_act * sigmoid
    product = (silu * up_act).astype(bf16)
    product_ref[0] = product
    grad_product = dot_cols(grad_val, down_w_ref[0])
    grad_gate = (grad_product * up_act * (sigmoid * (1.0 + gate_act * (1.0 - sigmoid)))).astype(bf16)
    grad_up = (grad_product * silu).astype(bf16)
    gate_grad_ref[0] = grad_gate
    up_grad_ref[0] = grad_up
    grad_rows = (dot_cols(grad_gate, gate_w_ref[0]) + dot_cols(grad_up, up_w_ref[0])).astype(bf16)
    weighted = (gate_row * dot_plain(product, down_w_ref[0])).astype(bf16)

    @pl.when(e == 0)
    def _():
        out_scr[s] = weighted
        grad_scr[s] = grad_rows

    @pl.when(e == 1)
    def _():
        before = hits_of(0).astype(jnp.float32).astype(bf16)
        for result, held, rows in ((grad_ref, grad_scr, grad_rows), (out_ref, out_scr, weighted)):
            combined = lax.dot_general(
                jnp.concatenate([before, one_hot], 0),
                jnp.concatenate([held[s], rows], 0),
                (((0,), (0,)), ((), ())),
                preferred_element_type=jnp.float32,
            )
            result[0] = combined.astype(bf16)


def run_experts(step, chips, place, tables, tokens, cots, weights, held):
    bf16 = jnp.bfloat16
    token_count, model = cots[0].shape
    w_gate, w_up, w_down = weights
    slots, ff = held["slots"], w_gate.shape[2]
    at_expert = lambda e, s: (e, 0, 0)
    row_spec = lambda width: pl.BlockSpec((1, slots, width), lambda e, s: (e, 2 * step + s, 0))
    any_spec = pl.BlockSpec(memory_space=pl.ANY)
    widths = (model, model, ff, ff, ff)
    earlier = held.get("rows", [])
    part_spec = pl.BlockSpec((1, token_count, model), lambda e, s: (e * s, 0, 0))
    part_shape = jax.ShapeDtypeStruct((2, token_count, model), bf16)
    results = pl.pallas_call(
        functools.partial(expert_kernel, tokens[0] is not None),
        grid=(2, 2),
        in_specs=[
            pl.BlockSpec(memory_space=pltpu.SMEM),
            pl.BlockSpec(tables.shape, lambda e, s: (0, 0, 0, 0)),
        ]
        + [any_spec] * 4
        + [
            pl.BlockSpec((1, model, ff), at_expert),
            pl.BlockSpec((1, model, ff), at_expert),
            pl.BlockSpec((1, ff, model), at_expert),
        ]
        + [any_spec] * len(earlier),
        out_specs=[row_spec(width) for width in widths] + [part_spec, part_spec],
        out_shape=[
            jax.ShapeDtypeStruct((2, 2 * chips * slots, width), bf16) for width in widths
        ]
        + [part_shape, part_shape],
        scratch_shapes=[
            pltpu.VMEM((2, token_count, model), bf16),
            pltpu.VMEM((2, token_count, model), bf16),
            pltpu.VMEM((2, slots, model), bf16),
            pltpu.VMEM((2, slots, model), bf16),
            pltpu.SemaphoreType.DMA((2, 2)),
        ],
        input_output_aliases={9 + i: i for i in range(len(earlier))},
        compiler_params=pltpu.CompilerParams(vmem_limit_bytes=62 * MIB),
        cost_estimate=pl.CostEstimate(
            flops=4 * (12 * slots * model * ff + 8 * slots * token_count * model),
            bytes_accessed=3 * w_gate.size * 2 + 4 * slots * (2 * model + 3 * ff) * 2 + 16 * token_count * model,
            transcendentals=4 * slots * ff,
        ),
        name="experts",
    )(place, tables, tokens[1] if tokens[0] is None else tokens[0], tokens[1], *cots, w_gate, w_up, w_down, *earlier)
    held["rows"] = results[:5]
    return results[5], results[6]


def weight_grad_kernel(
    n_y, n_ctx, after_ref, x_ref, val_ref, product_ref, gg_ref, gu_ref, gate_ref, up_ref, down_ref, pt_ref, ggt_ref, gut_ref
):
    bf16 = jnp.bfloat16

    @pl.when(pl.program_id(1) == 0)
    def _():
        for source, turned in ((product_ref, pt_ref), (gg_ref, ggt_ref), (gu_ref, gut_ref)):
            turned[...] = source[0].T

    for turned, result in ((ggt_ref, gate_ref), (gut_ref, up_ref)):
        grad = dot_plain(turned[...], x_ref[0]).astype(bf16)
        depth = result.shape[-1]
        for i in range(result.shape[1]):
            result[0, i, 0, 0] = grad[:, i * depth : (i + 1) * depth]
    grad = dot_plain(pt_ref[...], val_ref[0]).astype(bf16)
    depth = down_ref.shape[4]
    for y in range(n_y):
        for c in range(2):
            for x in range(n_ctx):
                start = ((y * 2 + c) * n_ctx + x) * depth
                down_ref[y, x, c, 0] = grad[start : start + depth]


def expert_weight_grads(rows, after, n_y, n_ctx):
    bf16 = jnp.bfloat16
    x_all, val_all, product_all, gg_all, gu_all = rows
    _, total, model = x_all.shape
    ff = gg_all.shape[2]
    shards = 2 * n_y * n_ctx
    col, depth, down_depth = 256, model // shards, ff // shards
    k = max(1, col // depth)
    wide = pl.BlockSpec((1, total, col), lambda e, n: (e, 0, n))
    whole = pl.BlockSpec((1, total, ff), lambda e, n: (e, 0, 0))

    def place(e, n):
        shard = n * k
        return (shard // (2 * n_ctx), shard % n_ctx // k, shard // n_ctx % 2, e, 0, 0)

    up_spec = pl.BlockSpec((1, k, 1, 1, ff, depth), place)
    up_shape = jax.ShapeDtypeStruct((n_y, n_ctx, 2, 2, ff, depth), bf16)
    return pl.pallas_call(
        functools.partial(weight_grad_kernel, n_y, n_ctx),
        grid=(2, model // col),
        in_specs=[pl.BlockSpec(memory_space=pl.ANY), wide, wide, whole, whole, whole],
        out_specs=[
            up_spec,
            up_spec,
            pl.BlockSpec((n_y, n_ctx, 2, 1, down_depth, col), lambda e, n: (0, 0, 0, e, 0, n)),
        ],
        out_shape=[
            up_shape,
            up_shape,
            jax.ShapeDtypeStruct((n_y, n_ctx, 2, 2, down_depth, model), bf16),
        ],
        scratch_shapes=[pltpu.VMEM((ff, total), bf16)] * 3,
        compiler_params=pltpu.CompilerParams(vmem_limit_bytes=60 * MIB),
        cost_estimate=pl.CostEstimate(
            flops=2 * 6 * total * model * ff,
            bytes_accessed=2 * (2 * total * (2 * model + 3 * ff) + 6 * model * ff),
            transcendentals=0,
        ),
        name="expert_weight_grads",
    )(after, x_all, val_all, product_all, gg_all, gu_all)


def on_device(
    residual_in,
    segments,
    routes,
    gates,
    attn_gain,
    q_proj,
    key_projection,
    value_projection,
    q_gain,
    k_gain,
    o_proj,
    mlp_gain,
    gate_proj,
    up_proj,
    down_proj,
    out_grad,
):
    bf16, f32 = jnp.bfloat16, jnp.float32
    n_seq, n_ctx, n_exp = lax.axis_size("seq"), lax.axis_size("ctx"), lax.axis_size("exp")
    n_y = n_seq // 2
    devices = n_seq * n_ctx * n_exp
    core = lax.axis_index("seq") % 2
    span_index = lax.axis_index("ctx")
    z_index = lax.axis_index("exp")
    group_all = [
        [(s * n_ctx + x) * n_exp + z for s in range(c, n_seq, 2) for x in range(n_ctx) for z in range(n_exp)]
        for c in range(2)
    ]
    group_plane = [[s * n_ctx + x for s in range(c, n_seq, 2) for x in range(n_ctx)] for c in range(2)]

    def swap(value):
        return lax.ppermute(value, "seq", [(i, i ^ 1) for i in range(n_seq)])

    def across(value, step):
        return lax.ppermute(value, "exp", [(i, i ^ step) for i in range(n_exp)])

    token_count = residual_in.shape[1]
    model_width = residual_in.shape[2]
    sequence_length = segments.shape[1]
    route_count = routes.shape[2]
    local_experts = gate_proj.shape[0]
    expert_count = local_experts * n_exp
    half_experts = local_experts // 2
    capacity = token_count * route_count * 9 // (expert_count * 8)
    slots = -(-capacity // 16) * 16
    groups = KEY_VALUE_HEADS // 2
    heads = QUERY_HEADS // 2
    heads_per_group = QUERY_HEADS // KEY_VALUE_HEADS
    score_scale = HEAD_DIM ** (-0.5)
    rows = q_proj.shape[0]
    gain_rows = q_gain.shape[0]
    q_width, kv_width = heads * HEAD_DIM, groups * HEAD_DIM
    width = q_width + 2 * kv_width

    extra = jnp.zeros((rows, 128), bf16)
    extra = extra.at[0, :rows].set(attn_gain).at[0, rows : 2 * rows].set(mlp_gain)
    extra = extra.at[1, :gain_rows].set(q_gain).at[1, gain_rows : 2 * gain_rows].set(k_gain)
    mine_cols, other_cols = [], []
    for weight in (q_proj, key_projection, value_projection):
        mine, other = column_halves(weight, core)
        mine_cols += mine
        other_cols += other
    mine_block = jnp.concatenate(mine_cols + [extra], 1)
    other_block = jnp.concatenate(other_cols + [extra], 1)
    chips = n_y * n_ctx
    own_links = n_y == 2 and n_ctx == 2
    if own_links:
        w_gathered = gather_chips(mine_block, other_block, n_exp)
        w_gathered = w_gathered.reshape(chips * n_exp, 2, rows, width + 128)
    else:
        theirs = swap(other_block)
        pair = jnp.stack([pick(core, mine_block, theirs), pick(core, theirs, mine_block)])
        w_gathered = lax.all_gather(
            pair, ("seq", "ctx", "exp"), axis=0, tiled=False, axis_index_groups=group_all
        )
    w_extra = w_gathered[:, :, :2, width:].reshape(n_y, n_ctx * n_exp, 2, 2, 128)
    w_extra = w_extra.transpose(0, 2, 1, 3, 4).reshape(devices, 2, 128).astype(f32)
    gain_attn = w_extra[:, 0, :rows].reshape(model_width)
    gain_mlp_f = w_extra[:, 0, rows : 2 * rows].reshape(model_width)
    gain_query_f = w_extra[:, 1, :gain_rows].reshape(1, HEAD_DIM)
    gain_key_f = w_extra[:, 1, gain_rows : 2 * gain_rows].reshape(1, HEAD_DIM)
    w_out = lax.all_gather(
        o_proj, ("seq", "ctx", "exp"), axis=0, tiled=True, axis_index_groups=group_all
    )

    def gather_expert(weight):
        mine = pick(core, weight[:half_experts], weight[half_experts:])
        theirs = swap(pick(core, weight[half_experts:], weight[:half_experts]))
        both = jnp.stack([pick(core, mine, theirs), pick(core, theirs, mine)])
        both = lax.optimization_barrier((both, normed_own))[0]
        full = lax.all_gather(
            both, ("seq", "ctx"), axis=0, tiled=False, axis_index_groups=group_plane
        )
        full = full.reshape((n_y, n_ctx, 2) + mine.shape).transpose(3, 0, 2, 1, 4, 5)
        return full.reshape(half_experts, -1, weight.shape[2])

    route_ids = routes[0]
    route_hit = route_ids[:, :, None] == jnp.arange(expert_count, dtype=jnp.int32)[None, None, :]
    hit_counts = route_hit.astype(jnp.int32).sum(1)
    earlier = jnp.cumsum(hit_counts, axis=0) - hit_counts
    slot_of = jnp.where(hit_counts > 0, earlier, -1).astype(f32)
    gate_of = jnp.sum(jnp.where(route_hit, gates[0][:, :, None], 0.0), axis=1)
    table = jnp.concatenate([slot_of.T, gate_of.T], 0)
    hidden = residual_in[0].astype(f32)
    seg_two = jnp.stack([segments[0], swap(segments)[0]])
    seg_here = lax.dynamic_slice_in_dim(seg_two, span_index * token_count, token_count, 1)
    valid_two = (seg_here > 0).astype(f32).reshape(2 * token_count, 1)
    valid_rows = valid_two[:token_count]
    positions = span_index * token_count + jnp.arange(token_count, dtype=jnp.int32)
    cos_one, sin_one = rope_tables(positions)
    half_dim = HEAD_DIM // 2
    signed_sine = jnp.concatenate([-sin_one[:, :half_dim], sin_one[:, half_dim:]], 1)
    info = jnp.zeros((2, 8, token_count), jnp.int32)
    info = info.at[:, 0].set(seg_here).at[:, 1].set(positions[None])
    seg_keys = seg_two[:, :, None]
    inv_attn = lax.rsqrt(jnp.mean(hidden * hidden, axis=-1, keepdims=True) + EPS)
    normed_own = (hidden * inv_attn * gain_attn).astype(bf16)
    w_gate, w_up, w_down = gather_expert(gate_proj), gather_expert(up_proj), gather_expert(down_proj)

    ring_up = [(i, i + 1) for i in range(n_exp - 1)]
    ring_down = [(i + 1, i) for i in range(n_exp - 1)]
    cot_up = cot_down = lax.optimization_barrier((out_grad[0], normed_own))[0]
    cot_from = {0: cot_up}
    cot_steps = []
    for hop in range(1, n_exp):
        cot_up = lax.ppermute(cot_up, "exp", ring_up)
        cot_down = lax.ppermute(cot_down, "exp", ring_down)
        cot_from[-hop], cot_from[hop] = cot_up, cot_down
        cot_steps.append(cot_up[:8, :128].astype(f32) + cot_down[:8, :128].astype(f32))
    normed_two = jnp.concatenate([normed_own, swap(normed_own)], 0)
    q_blocks = q_width // (2 * HEAD_DIM)
    kv_raw, kv_low, w_kv = project(
        normed_two, w_gathered, q_blocks, 2, gain_key_f, cos_one, signed_sine, n_y, plain=1
    )
    kv_here = kv_low.reshape(2, token_count, 2 * kv_width)
    if n_ctx == 2:
        kv_there = lax.ppermute(kv_here, "ctx", [(0, 1), (1, 0)])
        kv_full = jnp.concatenate(
            [pick(span_index, kv_here, kv_there), pick(span_index, kv_there, kv_here)], 1
        )
    else:
        kv_full = lax.all_gather(kv_here, "ctx", axis=1, tiled=True)
    q_raw, query_rows, w_query = project(
        normed_two, w_gathered, 0, q_blocks, gain_query_f, cos_one, signed_sine, n_y
    )
    info = lax.optimization_barrier((info, cot_steps[0]))[0]
    mixed_low, recip = attend(info, seg_keys, query_rows, kv_full, groups, heads_per_group)
    mixed_low = lax.optimization_barrier((mixed_low, cot_steps[1]))[0]
    attn_partial = jnp.dot(mixed_low, w_out, preferred_element_type=f32)
    attn_out = attn_partial[:token_count] + swap(attn_partial[token_count:])
    middle = hidden + attn_out
    inv_mlp = lax.rsqrt(jnp.mean(middle * middle, axis=-1, keepdims=True) + EPS)
    normed_mlp = (middle * inv_mlp * gain_mlp_f).astype(bf16)

    tokens_all, tables_all = exchange_column(normed_mlp, table, n_exp)
    tables_all = lax.dynamic_update_slice(
        tables_all, table[None, None], (z_index, core, jnp.int32(0), jnp.int32(0))
    )
    grad_parts, out_parts = [], []
    held = {"slots": slots}
    first_row = z_index * local_experts + core * half_experts
    for step in range(n_exp):
        there = z_index ^ step
        own_cot = cot_from[0]
        if step:
            offsets = sorted({(i ^ step) - i for i in range(n_exp)})
            own_cot = cot_from[offsets[0]]
            for offset in offsets[1:]:
                own_cot = jnp.where(there - z_index == offset, cot_from[offset], own_cot)
        place = jnp.stack([there, core, first_row, expert_count + first_row]).astype(jnp.int32)
        if step == 3:
            place = lax.optimization_barrier((place, grad_parts[1]))[0]
        out_part, grad_part = run_experts(
            step,
            n_exp,
            place,
            tables_all,
            (normed_mlp if step == 0 else None, tokens_all),
            (own_cot, swap(own_cot)),
            (w_gate, w_up, w_down),
            held,
        )
        grad_part = grad_part[0].astype(f32) + swap(grad_part[1]).astype(f32)
        if step:
            grad_part = across(grad_part.astype(bf16), step)
        grad_parts.append(grad_part)
        out_parts.append(out_part)
    grad_total = grad_parts[0]
    for part in grad_parts[1:]:
        grad_total = grad_total + part.astype(f32)
    out_total = None
    for step, part in enumerate(out_parts):
        part = part[0].astype(f32) + swap(part[1]).astype(f32)
        if step:
            part = lax.optimization_barrier((part.astype(bf16), grad_parts[-1]))[0]
            part = across(part, step).astype(f32)
        out_total = part if out_total is None else out_total + part
    grad_normed_mlp, expert_out = grad_total, out_total
    final_out = middle + expert_out

    stats = jnp.zeros((8, 128), f32)
    for index, value in enumerate(
        (
            jnp.sum(hidden * hidden * valid_rows),
            jnp.sum(attn_out * attn_out * valid_rows),
            jnp.sum(expert_out * expert_out * valid_rows),
            jnp.sum(valid_rows),
        )
    ):
        stats = stats.at[0, index].set(value)
    for axis, count in (("seq", n_seq), ("ctx", n_ctx), ("exp", n_exp)):
        hop = 1
        while hop < count:
            stats = stats + lax.ppermute(stats, axis, [(i, i ^ hop) for i in range(count)])
            hop *= 2
    rms_stats = jnp.sqrt(stats[0, :3] / (stats[0, 3] * model_width))

    gate_blocks, up_blocks, down_blocks = expert_weight_grads(
        held["rows"], lax.optimization_barrier((place, grad_parts[2]))[0], n_y, n_ctx
    )

    def scatter_plane(blocks):
        return lax.psum_scatter(
            blocks.reshape((n_y * n_ctx,) + blocks.shape[2:]),
            ("seq", "ctx"),
            scatter_dimension=0,
            tiled=True,
            axis_index_groups=group_plane,
        )[0]

    def all_experts(part):
        mine = pick(core, part[0], part[1])
        theirs = swap(pick(core, part[1], part[0]))
        return jnp.concatenate([pick(core, mine, theirs), pick(core, theirs, mine)], 0).astype(f32)

    gate_part = scatter_plane(gate_blocks)
    up_blocks, gate_part = lax.optimization_barrier((up_blocks, gate_part))
    up_part = scatter_plane(up_blocks)
    down_blocks, up_part = lax.optimization_barrier((down_blocks, up_part))
    down_part = scatter_plane(down_blocks)

    cotangent = out_grad[0].astype(f32)
    mlp_gain_grad = jnp.sum(grad_normed_mlp * middle * inv_mlp, axis=0)
    grad_middle = cotangent + norm_back(grad_normed_mlp, middle, inv_mlp, gain_mlp_f)
    grad_attn_own = grad_middle.astype(bf16)
    grad_attn = jnp.concatenate([grad_attn_own, swap(grad_attn_own)], 0)
    o_grad_part = contract_rows(mixed_low, grad_attn).astype(bf16)
    o_grad_part, down_part = lax.optimization_barrier((o_grad_part, down_part))
    o_proj_grad = lax.psum_scatter(
        scatter_plane(o_grad_part.reshape(n_y, n_ctx, n_exp, -1, model_width)),
        "exp",
        scatter_dimension=0,
        tiled=True,
    )[0].astype(f32)
    mixture_gradient = contract_cols(grad_attn, w_out).astype(bf16) * valid_two.astype(bf16)
    grad_q_raw, key_grad, value_grad, q_gain_rows = attend_back(
        info,
        seg_keys,
        query_rows,
        kv_full,
        mixed_low,
        mixture_gradient,
        recip,
        q_raw,
        gain_query_f,
        cos_one,
        signed_sine,
        groups,
        heads_per_group,
    )
    q_gain_grad = q_gain_rows[0]
    kv_grad = jnp.concatenate([key_grad, value_grad], 2)
    if n_ctx == 2:
        first, second = kv_grad[:, :token_count], kv_grad[:, token_count:]
        received = lax.ppermute(
            pick(span_index, second, first).astype(bf16), "ctx", [(0, 1), (1, 0)]
        )
        kv_grad_here = pick(span_index, first, second) + received.astype(f32)
    else:
        kv_grad_here = lax.psum_scatter(
            kv_grad.astype(bf16), "ctx", scatter_dimension=1, tiled=True
        ).astype(f32)
    kv_grad_here = kv_grad_here.reshape(2 * token_count, 2 * kv_width)
    cosine_table, sine_values = jnp.concatenate([cos_one] * 2, 0), jnp.concatenate([sin_one] * 2, 0)
    k_raw = kv_raw[:, :kv_width].reshape(-1, groups, HEAD_DIM)
    inv_key = lax.rsqrt(jnp.mean(k_raw * k_raw, axis=-1, keepdims=True) + EPS)
    grad_kn = inverse_rotation(
        kv_grad_here[:, :kv_width].reshape(-1, groups, HEAD_DIM), cosine_table, sine_values
    )
    k_gain_grad = jnp.sum(grad_kn * k_raw * inv_key, axis=(0, 1))
    grad_k_raw = norm_back(grad_kn, k_raw, inv_key, gain_key_f).astype(bf16)
    grad_kv = jnp.concatenate(
        [grad_k_raw.reshape(-1, kv_width), kv_grad_here[:, kv_width:].astype(bf16)], 1
    )
    normed_partial = contract_cols(grad_q_raw, w_query) + contract_cols(grad_kv, w_kv)
    grad_normed = normed_partial[:token_count] + swap(normed_partial[token_count:])
    attn_gain_grad = jnp.sum(grad_normed * hidden * inv_attn, axis=0)
    grad_hidden = grad_middle + norm_back(grad_normed, hidden, inv_attn, gain_attn)

    extra_grad = jnp.zeros((devices, rows, 128), f32)
    extra_grad = extra_grad.at[:, 0, :rows].set(attn_gain_grad.reshape(devices, rows))
    extra_grad = extra_grad.at[:, 0, rows : 2 * rows].set(mlp_gain_grad.reshape(devices, rows))
    extra_grad = extra_grad.at[:, 1, :gain_rows].set(q_gain_grad.reshape(devices, gain_rows))
    extra_grad = extra_grad.at[:, 1, gain_rows : 2 * gain_rows].set(
        k_gain_grad.reshape(devices, gain_rows)
    )
    extra_grad = extra_grad.astype(bf16)
    if own_links:
        grad_mine, grad_theirs = dense_grad_scatter(
            normed_two,
            grad_q_raw,
            grad_kv,
            extra_grad.reshape(n_y, 2, n_ctx, n_exp, rows, 128),
            stats,
            n_exp,
        )
    else:
        w_grad = jnp.concatenate(
            [
                contract_rows(normed_two, grad_q_raw).astype(bf16),
                contract_rows(normed_two, grad_kv).astype(bf16),
                extra_grad.reshape(model_width, 128),
            ],
            1,
        )
        w_grad = w_grad.reshape(n_y, 2, n_ctx, n_exp, rows, width + 128).transpose(0, 2, 3, 1, 4, 5)
        w_grad, o_proj_grad = lax.optimization_barrier((w_grad, o_proj_grad))
        w_grad = lax.psum_scatter(
            scatter_plane(w_grad), "exp", scatter_dimension=0, tiled=True
        )[0]
        grad_mine = pick(core, w_grad[0], w_grad[1])
        grad_theirs = swap(pick(core, w_grad[1], w_grad[0]))
    gate_grad = all_experts(gate_part).transpose(0, 2, 1)
    up_grad = all_experts(up_part).transpose(0, 2, 1)
    down_grad = all_experts(down_part)
    even = pick(core, grad_mine, grad_theirs).astype(f32)
    odd = pick(core, grad_theirs, grad_mine).astype(f32)

    def columns(start, size):
        step = size // groups
        parts = []
        for g in range(groups):
            parts += [half[:, start + g * step : start + (g + 1) * step] for half in (even, odd)]
        return jnp.concatenate(parts, 1)

    extra_total = even[:, width:] + odd[:, width:]
    return (
        final_out.astype(bf16)[None],
        grad_hidden.astype(bf16)[None],
        extra_total[0, :rows],
        columns(0, q_width),
        columns(q_width, kv_width),
        columns(q_width + kv_width, kv_width),
        extra_total[1, :gain_rows],
        extra_total[1, gain_rows : 2 * gain_rows],
        o_proj_grad,
        extra_total[0, rows : 2 * rows],
        gate_grad,
        up_grad,
        down_grad,
        rms_stats,
    )


def solution(mesh):
    in_specs = (
        P(("seq", "exp"), "ctx", None),
        P(("seq", "exp"), None),
        P(("seq", "exp"), "ctx", None),
        P(("seq", "exp"), "ctx", None),
        P(("seq", "ctx", "exp")),
        P(("seq", "ctx", "exp"), None),
        P(("seq", "ctx", "exp"), None),
        P(("seq", "ctx", "exp"), None),
        P(("seq", "ctx", "exp")),
        P(("seq", "ctx", "exp")),
        P(("seq", "ctx", "exp"), None),
        P(("seq", "ctx", "exp")),
        P("exp", ("seq", "ctx"), None),
        P("exp", ("seq", "ctx"), None),
        P("exp", ("seq", "ctx"), None),
        P(("seq", "exp"), "ctx", None),
    )
    out_specs = (
        P(("seq", "exp"), "ctx", None),
        P(("seq", "exp"), "ctx", None),
        P(("seq", "ctx", "exp")),
        P(("seq", "ctx", "exp"), None),
        P(("seq", "ctx", "exp"), None),
        P(("seq", "ctx", "exp"), None),
        P(("seq", "ctx", "exp")),
        P(("seq", "ctx", "exp")),
        P(("seq", "ctx", "exp"), None),
        P(("seq", "ctx", "exp")),
        P("exp", ("seq", "ctx"), None),
        P("exp", ("seq", "ctx"), None),
        P("exp", ("seq", "ctx"), None),
        P(),
    )
    return jax.shard_map(
        on_device, mesh=mesh, in_specs=in_specs, out_specs=out_specs, check_vma=False
    )
```

time: 2460 us -> 1820 us (0.74)
  Pallas kernels: 0 us -> 821 us
  matrix products: 653 us -> 55.3 us
  waiting for transfers between devices: 893 us -> 547 us
  local copies, waits for them, and re-layouts: 329 us -> 120 us
  other arithmetic: 326 us -> 136 us
  starting transfers between devices: 210 us -> 113 us
    pallas_call x0 -> x12, Pallas kernels: none -> 821 us  [the longest x4 185 us: run_experts(): pl.pallas_call(functools.partial(expert_kernel, tokens[0] is not None), g...]
    dot_general x61 -> x0, matrix products: 577 us -> none  [the longest x4 53.2 us: on_device(): jnp.einsum('serd,efd->serf', grad_val, w_down, preferred_element_type=f32)]
    reduce_scatter x2 -> x1, waiting for transfers between devices: 300 us -> 42.3 us  [on_device(): lax.psum_scatter(scatter_plane(o_grad_part.reshape(n_y, n_ctx, n_exp, -1,...]
    all_gather x1 -> x0, waiting for transfers between devices: 255 us -> none  [on_device(): lax.all_gather(pair, ('seq', 'ctx', 'exp'), axis=0, tiled=False, axis_ind...]
    ppermute x12 -> x6, starting transfers between devices: 193 us -> 50.5 us  [across(): return lax.ppermute(value, 'exp', [(i, i ^ step) for i in range(n_exp)])]
    unnamed x9 -> x13, waiting for transfers between devices: 0.81 us -> 127 us
    convert_element_type x21 -> x9, other arithmetic: 107 us -> 19.3 us  [the longest x3 8.6 us: on_device(): part = lax.optimization_barrier((part.astype(bf16), grad_parts[-1]))[0]]
    reduce_sum x12 -> x0, other arithmetic: 66.5 us -> none  [the longest x4 32.9 us: on_device(): row_total = jnp.sum(exp_scores, axis=-1, keepdims=True)]
  transfers between devices with their start and end apart: 57 -> 51, of which waited for: 15 -> 21; matrix products, arithmetic and copies ran while one was open for 51% -> 15% of each run, Pallas kernels for 0% -> 39%
where the time goes in v2:
time: 1820 us; the launch traced here: 1810 us
  Pallas kernels  821 us (45%)
  waiting for transfers between devices  547 us (30%)
  other arithmetic  136 us (7%)
  local copies, waits for them, and re-layouts  120 us (7%)
  starting transfers between devices  113 us (6%)
  matrix products  55.3 us (3%)
  between operations  20.1 us (1%)
    ppermute x6, waiting for transfers between devices, across(): return lax.ppermute(value, 'exp', [(i, i ^ step) for i in range(n_exp)])  259 us
    pallas_call x4, Pallas kernels, run_experts(): pl.pallas_call(functools.partial(expert_kernel, tokens[0] is not None), g...  185 us
    pallas_call x1, Pallas kernels, exchange_column(): pl.pallas_call(functools.partial(exchange_kernel, n_exp), in_specs=[any_s...  151 us
    pallas_call x1, Pallas kernels, gather_chips(): pl.pallas_call(functools.partial(gather_kernel, n_exp), in_specs=[vmem_sp...  151 us
    pallas_call x1, Pallas kernels, dense_grad_scatter(): pl.pallas_call(functools.partial(scatter_kernel, n_exp), in_specs=[spec]...  129 us
    unnamed x13, waiting for transfers between devices  127 us
    pallas_call x1, Pallas kernels, attend_back(): pl.pallas_call(attention_back_kernel, grid=(2, groups, per_group), in_spe...  63 us
    pallas_call x1, Pallas kernels, expert_weight_grads(): pl.pallas_call(functools.partial(weight_grad_kernel, n_y, n_ctx), grid=(2...  62.1 us
  transfers between devices with their start and end apart: 51, of which 21 were waited for; matrix products, arithmetic and copies ran while one was open for 15% of the time, Pallas kernels for 39%

profile of v2, /device:TPU:0, one launch (start us, length us, event | category | flops | bytes accessed | tf_op | source)
XLA Modules:
  0.0 1812.6 jit_solution(16389482757505577670)
XLA Ops:
  12.7 2.7 broadcast_select_fusion.16
  23.8 150.5 %gather_chips.1 = bf16[4,4,2,64,2688]{4,3,2,1,0:T(8,128)(2,1)} custom-call(bf16[64,2688]{1,0:T(8,128)(2,1)} %copy-done.52, bf16[64,2688]{1,0:T(8,128)(2,1)} %copy-done.51), custom_call_target="tpu_custom_call" | custom-call | tf_op jit(solution)/shard_map/gather_chips/pallas_call | solution.py:217
  187.9 5.9 collective-permute-start.10
  201.9 4.1 pad_maximum_fusion.normed_ref
  206.0 7.4 project.3
  217.0 19.7 %collective-permute-done.9 = bf16[512,2048]{1,0:T(8,128)(2,1)} collective-permute-done((bf16[512,2048]{1,0:T(8,128)(2,1)}, bf16[512,2048]{1,0:T(8,128)(2,1)}, u32[]{:S(2)}, u32[]{:S(2)}) %collective-permute-start.9) | collective-permute-done | bytes 2097184 | tf_op jit(solution)/shard_map/ppermute | solution.py:1096
  238.0 6.0 collective-permute-start.17
  244.0 33.4 %project.2 = (f32[1024,2048]{1,0:T(8,128)}, bf16[1024,2048]{1,0:T(8,128)(2,1)}, bf16[2048,2048]{1,0:T(8,128)(2,1)}) custom-call(bf16[1024,2048]{1,0:T(8,128)(2,1)} %pad_maximum_fusion.normed_ref, bf16[16,2,64,2688]{3,2,1,0:T(8,128)(2,1)} %bitcast.254, f32[1,128]{1,0:T(1,128)} %reshape_squeeze.7.gain_ref, f32[512,128]{1,0:T(8,128)} %pad_maximum_fusion.11.cos_ref, ...), custom_call_target="tpu_custom_call" | custom-call | flops 8589934592 | bytes 33554432 | tf_op jit(solution)/shard_map/project/pallas_call | solution.py:555
  277.7 40.3 %attend.1 = (bf16[1024,2048]{1,0:T(8,128)(2,1)}, f32[32,1,512]{2,1,0:T(1,128)S(1)}) custom-call(s32[2,8,512]{2,1,0:T(8,128)S(1)} %scatter.49.info_ref, s32[2,1024,1]{2,1,0:T(8,128)S(1)} %copy.113.seg_ref, bf16[1024,2048]{1,0:T(8,128)(2,1)} %get-tuple-element.244.q_ref, bf16[2,1024,512]{2,1,0:T(8,128)(2,1)S(1)} %pad_maximum_fusion.4.k_ref.v_ref, ...), custom_call_target="tpu_custom_call" | custom-call | flops 17179869184 | bytes 10485760 | tf_op jit(solution)/shard_map/attend/pallas_call | solution.py:640
  318.0 12.5 fusion.51
  330.5 2.5 slice.650
  336.4 5.9 collective-permute-start.18
  346.4 3.1 broadcast_select_fusion.own_cot_ref
  350.1 35.2 %collective-permute-done.16 = bf16[512,2048]{1,0:T(8,128)(2,1)} collective-permute-done((bf16[512,2048]{1,0:T(8,128)(2,1)}, bf16[512,2048]{1,0:T(8,128)(2,1)}, u32[]{:S(2)}, u32[]{:S(2)}) %collective-permute-start.16) | collective-permute-done | bytes 2097184 | tf_op jit(solution)/shard_map/ppermute | solution.py:1096
  386.5 5.9 select_select_fusion
  392.4 5.9 copy.116
  398.3 5.9 copy.117
  404.2 9.4 all-gather.14.cloned.1.call-done
  413.7 6.6 copy.118
  420.3 4.3 multiply_reduce_fusion.4
  428.3 150.5 %exchange_column.1 = (bf16[4,2,512,2048]{3,2,1,0:T(8,128)(2,1)}, f32[4,2,32,512]{3,2,1,0:T(8,128)}) custom-call(bf16[512,2048]{1,0:T(8,128)(2,1)} %multiply_convert_fusion.token_ref.own_ref, f32[32,512]{1,0:T(8,128)} %pad_maximum_fusion.15.table_ref), custom_call_target="tpu_custom_call" | custom-call | bytes 67108864 | tf_op jit(solution)/shard_map/exchange_column/pallas_call | solution.py:295
  579.4 46.1 %experts.4 = (bf16[2,2304,2048]{2,1,0:T(8,128)(2,1)}, bf16[2,2304,2048]{2,1,0:T(8,128)(2,1)}, bf16[2,2304,768]{2,1,0:T(8,128)(2,1)}, bf16[2,2304,768]{2,1,0:T(8,...) custom-call(s32[4]{0:T(128)} %add_add_fusion.place_ref, ...), custom_call_target="tpu_custom_call" | custom-call | flops 31406948352 | bytes 50397184 | tf_op jit(solution)/shard_map/experts/pallas_call | solution.py:864
  625.5 46.5 %experts.5 = (bf16[2,2304,2048]{2,1,0:T(8,128)(2,1)}, bf16[2,2304,2048]{2,1,0:T(8,128)(2,1)}, bf16[2,2304,768]{2,1,0:T(8,128)(2,1)}, bf16[2,2304,768]{2,1,0:T(8,...) custom-call(s32[4]{0:T(128)} %add_add_fusion.1.place_ref, ...), custom_call_target="tpu_custom_call", output_to_operand_aliasing={{0}: (9, {}), {1}: (10, {}), {2}: (11, {}), {3}: (12, {}), ... | custom-call | flops 31406948352 | bytes 50397184 | tf_op jit(solution)/shard_map/experts/pallas_call | solution.py:864
  672.1 3.2 slice_bitcast_fusion.5
  675.6 46.3 %experts.6 = (bf16[2,2304,2048]{2,1,0:T(8,128)(2,1)}, bf16[2,2304,2048]{2,1,0:T(8,128)(2,1)}, bf16[2,2304,768]{2,1,0:T(8,128)(2,1)}, bf16[2,2304,768]{2,1,0:T(8,...) custom-call(s32[4]{0:T(128)} %add_add_fusion.3.place_ref, ...), custom_call_target="tpu_custom_call", output_to_operand_aliasing={{0}: (9, {}), {1}: (10, {}), {2}: (11, {}), {3}: (12, {}), ... | custom-call | flops 31406948352 | bytes 50397184 | tf_op jit(solution)/shard_map/experts/pallas_call | solution.py:864
  724.7 2.6 fusion.19
  729.8 86.1 %collective-permute-done.14 = bf16[512,2048]{1,0:T(8,128)(2,1)S(1)} collective-permute-done((bf16[512,2048]{1,0:T(8,128)(2,1)S(1)}, bf16[512,2048]{1,0:T(8,128)(2,1)S(1)}, u32[]{:S(2)}, u32[]{:S(2)}) %collective-permute-start.14) | collective-permute-done | bytes 2097184 | tf_op jit(solution)/shard_map/ppermute | solution.py:1004
  815.9 6.6 collective-permute-done.30
  824.5 46.3 %experts.7 = (bf16[2,2304,2048]{2,1,0:T(8,128)(2,1)}, bf16[2,2304,2048]{2,1,0:T(8,128)(2,1)}, bf16[2,2304,768]{2,1,0:T(8,128)(2,1)}, bf16[2,2304,768]{2,1,0:T(8,...) custom-call(s32[4]{0:T(128)} %add_add_fusion.2.place_ref.after_ref, ...), custom_call_target="tpu_custom_call", output_to_operand_aliasing={{0}: (9, {}), {1}: (10, {}), {2}: (11, {}), {3}: (12, {}), ... | custom-call | flops 31406948352 | bytes 50397184 | tf_op jit(solution)/shard_map/experts/pallas_call | solution.py:864
  870.8 62.1 %expert_weight_grads.1 = (bf16[2,2,2,2,768,256]{5,4,3,2,1,0:T(8,128)(2,1)}, bf16[2,2,2,2,768,256]{5,4,3,2,1,0:T(8,128)(2,1)}, bf16[2,2,2,2,96,2048]{5,4,3,2,1,0:T(8,128)(2,1)}) custom-call(s32[4]{0:T(128)} %add_add_fusion.2.place_ref.after_ref, bf16[2,2304,2048]{2,1,0:T(8,128)(2,1)} %get-tuple-element.292.x_ref, ...), custom_call_target="tpu_custom_call" | custom-call | flops 43486543872 | bytes 77856768 | tf_op jit(solution)/shard_map/expert_weight_grads/pallas_call | solution.py:944
  932.9 8.7 copy.127
  941.7 67.9 %reduce-scatter.16.cloned.1.call-done = bf16[1,2,2,768,256]{3,4,2,1,0:T(8,128)(2,1)} async-done(((bf16[4,2,2,768,256]{3,4,2,1,0:T(8,128)(2,1)}), bf16[1,2,2,768,256]{3,4,2,1,0:T(8,128)(2,1)}) %reduce-scatter.16.cloned.1.call-update) | async-done | bytes 1572880
  1009.5 8.6 copy.128
  1018.2 3.3 slice_bitcast_fusion.4
  1030.0 58.5 %reduce-scatter.18.cloned.1.call-done = bf16[1,2,2,768,256]{3,4,2,1,0:T(8,128)(2,1)} async-done(((bf16[4,2,2,768,256]{3,4,2,1,0:T(8,128)(2,1)}), bf16[1,2,2,768,256]{3,4,2,1,0:T(8,128)(2,1)}) %reduce-scatter.18.cloned.1.call-update) | async-done | bytes 1572880
  1088.7 3.2 fusion.18
  1091.8 3.4 collective-permute-start.22
  1095.6 2.6 fusion.20
  1098.8 3.4 fusion.17
  1102.4 2.7 fusion.16
  1105.1 36.1 %collective-permute-done.22 = bf16[512,2048]{1,0:T(8,128)(2,1)S(1)} collective-permute-done((bf16[512,2048]{1,0:T(8,128)(2,1)S(1)}, bf16[512,2048]{1,0:T(8,128)(2,1)S(1)}, u32[]{:S(2)}, u32[]{:S(2)}) %collective-permute-start.22) | collective-permute-done | bytes 2097184 | tf_op jit(solution)/shard_map/ppermute | solution.py:1004
  1141.2 44.5 %collective-permute-start.23 = (bf16[512,2048]{1,0:T(8,128)(2,1)S(1)}, bf16[512,2048]{1,0:T(8,128)(2,1)}, u32[]{:S(2)}, u32[]{:S(2)}) collective-permute-start(bf16[512,2048]{1,0:T(8,128)(2,1)S(1)} %fusion.20), channel_id=1, source_target_pairs={{0,1},{1,0},{2,3},{3,2},{4,5},{5,4},{6,7},{7,6},{8,9},{9,8},{10,11... | collective-permute-start | bytes 6291464 | tf_op jit(solution)/shard_map/ppermute | solution.py:1004
  1188.8 6.3 multiply_reduce_fusion.2
  1195.1 79.4 %collective-permute-done.23 = bf16[512,2048]{1,0:T(8,128)(2,1)} collective-permute-done((bf16[512,2048]{1,0:T(8,128)(2,1)S(1)}, bf16[512,2048]{1,0:T(8,128)(2,1)}, u32[]{:S(2)}, u32[]{:S(2)}) %collective-permute-start.23) | collective-permute-done | bytes 2097184 | tf_op jit(solution)/shard_map/ppermute | solution.py:1004
  1274.4 50.7 %collective-permute-done.25 = bf16[512,2048]{1,0:T(8,128)(2,1)} collective-permute-done((bf16[512,2048]{1,0:T(8,128)(2,1)S(1)}, bf16[512,2048]{1,0:T(8,128)(2,1)}, u32[]{:S(2)}, u32[]{:S(2)}) %collective-permute-start.25) | collective-permute-done | bytes 2097184 | tf_op jit(solution)/shard_map/ppermute | solution.py:1004
  1325.2 11.9 multiply_reduce_fusion
  1337.2 4.3 collective-permute-done.31
  1341.5 13.8 convolution_convert_fusion
  1355.4 10.5 convert_multiply_fusion.5.grad_ref
  1367.2 63.0 %attend_back.1 = (bf16[1024,2048]{1,0:T(8,128)(2,1)}, f32[2,1024,256]{2,1,0:T(8,128)S(1)}, f32[2,1024,256]{2,1,0:T(8,128)S(1)}, f32[8,128]{1,0:T(8,128)S(1)}) custom-call(s32[2,8,512]{2,1,0:T(8,128)S(1)} %copy-done.6, s32[2,1024,1]{2,1,0:T(8,128)S(1)} %copy-done.4, bf16[1024,2048]{1,0:T(8,128)(2,1)} %get-tuple-element.244.q_ref, ...), custom_call_target="tpu_custom_call" | custom-call | flops 42949672960 | bytes 31457280 | tf_op jit(solution)/shard_map/attend_back/pallas_call | solution.py:736
  1439.4 41.9 %collective-permute-done.32 = bf16[2,512,512]{2,1,0:T(8,128)(2,1)S(1)} collective-permute-done((bf16[2,512,512]{2,1,0:T(8,128)(2,1)S(1)}, bf16[2,512,512]{2,1,0:T(8,128)(2,1)S(1)}, u32[]{:S(2)}, u32[]{:S(2)}) %collective-permute-start.32) | collective-permute-done | bytes 1048608 | tf_op jit(solution)/shard_map/ppermute | solution.py:1244
  1481.3 2.9 convert_add_fusion.9
  1491.2 7.7 multiply_reduce_fusion.6
  1509.8 5.7 fusion.37
  1515.4 12.8 convolution_add_fusion
  1528.3 2.5 slice.660
  1535.7 2.3 select_bitcast_fusion.2
  1540.3 5.4 fusion.11
  1568.3 29.7 %collective-permute-start.37 = (f32[8,128]{1,0:T(8,128)S(1)}, f32[8,128]{1,0:T(8,128)S(1)}, u32[]{:S(2)}, u32[]{:S(2)}) collective-permute-start(f32[8,128]{1,0:T(8,128)S(1)} %add.249), channel_id=1, source_target_pairs={{0,1},{1,0},{2,3},{3,2},{4,5},{5,4},{6,7},{7,6},{8,9},{9,8},{10,11... | collective-permute-start | bytes 12296 | tf_op jit(solution)/shard_map/ppermute | solution.py:1183
  1598.0 5.2 fusion.25
  1606.2 6.2 scatter.59
  1613.0 5.1 scatter.61
  1618.9 128.8 %dense_grad_scatter.1 = (f32[64,2688]{1,0:T(8,128)}, f32[64,2688]{1,0:T(8,128)}) custom-call(bf16[1024,2048]{1,0:T(8,128)(2,1)} %pad_maximum_fusion.normed_ref, bf16[1024,2048]{1,0:T(8,128)(2,1)} %get-tuple-element.282.grad_ref, bf16[1024,512]{1,0:T(8,128)(2,1)} %pad_maximum_fusion.9.kv_grad_ref, bf16[2,2,2,4,64,128]{5,4,3,2,1,0:T(8,128)(2,1)} %bitcast.293, ...), custom_call_target="tpu_custom_call" | custom-call | flops 11274289152 | bytes 16777216 | tf_op jit(solution)/shard_map/dense_grad_scatter/pallas_call | solution.py:449
  1761.4 42.3 %reduce-scatter.14.cloned.1.call-done = bf16[1,128,2048]{2,1,0:T(8,128)(2,1)} async-done(((bf16[4,128,2048]{2,1,0:T(8,128)(2,1)}), bf16[1,128,2048]{2,1,0:T(8,128)(2,1)}) %reduce-scatter.14.cloned.1.call-update) | async-done | bytes 524304 | tf_op jit(solution)/shard_map/reduce_scatter | solution.py:1218
  (410 shorter events, 148.1 us)
Async XLA Ops:
  7.2 310.8 %all-gather.8.cloned.1.call-start = ((), (), s32[]{:S(2)}) async-start(), calls=%async_computation.5 | async-start | bytes 8912896 | tf_op jit(solution)/shard_map/all_gather | solution.py:1051
  7.9 384.5 %all-gather.10.cloned.1.call-start = ((), (), s32[]{:S(2)}) async-start(), calls=%async_computation.7 | async-start | bytes 7864320 | tf_op jit(solution)/shard_map/all_gather | solution.py:1060
  9.4 168.8 %collective-permute-start.5 = (bf16[2,256,768]{2,1,0:T(8,128)(2,1)S(1)}, bf16[2,256,768]{2,1,0:T(8,128)(2,1)}, u32[]{:S(2)}, u32[]{:S(2)}) collective-permute-start(bf16[2,256,768]{2,1,0:T(8,128)(2,1)S(1)} %broadcast_select_fusion.11), channel_id=1, source_target_pairs={{0,8},{8,0},{16,24},{24,16},{1,9},{9,1},{17,25},{25,17},{2,10},{10... | collective-permute-start | bytes 2359304 | tf_op jit(solution)/shard_map/ppermute | solution.py:1001
  23.8 151.4 %copy-start.10 = (bf16[1,512,2048]{2,1,0:T(8,128)(2,1)S(1)}, bf16[1,512,2048]{2,1,0:T(8,128)(2,1)}, u32[]{:S(2)}) copy-start(bf16[1,512,2048]{2,1,0:T(8,128)(2,1)} %param.44) | copy-start | bytes 6291460
  181.0 217.3 %all-gather.12.cloned.1.call-start = ((), (), s32[]{:S(2)}) async-start(), calls=%async_computation.8 | async-start | bytes 7864320 | tf_op jit(solution)/shard_map/all_gather | solution.py:1060
  181.1 2.4 collective-permute-start.6
  186.3 227.3 %all-gather.14.cloned.1.call-start = ((), (), s32[]{:S(2)}) async-start(), calls=%async_computation.9 | async-start | bytes 7864320 | tf_op jit(solution)/shard_map/all_gather | solution.py:1060
  186.4 15.5 collective-permute-start.1
  186.6 50.1 %collective-permute-start.9 = (bf16[512,2048]{1,0:T(8,128)(2,1)}, bf16[512,2048]{1,0:T(8,128)(2,1)}, u32[]{:S(2)}, u32[]{:S(2)}) collective-permute-start(bf16[512,2048]{1,0:T(8,128)(2,1)} %bitcast.23.own_cot_ref), channel_id=1, source_target_pairs={{1,0},{2,1},{3,2},{5,4},{6,5},{7,6},{9,8},{10,9},{11,10},{13,12},{... | collective-permute-start | bytes 6291464 | tf_op jit(solution)/shard_map/ppermute | solution.py:1096
  187.9 50.1 %collective-permute-start.10 = (bf16[512,2048]{1,0:T(8,128)(2,1)}, bf16[512,2048]{1,0:T(8,128)(2,1)}, u32[]{:S(2)}, u32[]{:S(2)}) collective-permute-start(bf16[512,2048]{1,0:T(8,128)(2,1)} %bitcast.23.own_cot_ref), channel_id=1, source_target_pairs={{0,1},{1,2},{2,3},{4,5},{5,6},{6,7},{8,9},{9,10},{10,11},{12,13},{... | collective-permute-start | bytes 6291464 | tf_op jit(solution)/shard_map/ppermute | solution.py:1095
  195.2 3.6 collective-permute-start.7
  201.9 807.6 %reduce-scatter.16.cloned.1.call-start = ((), (), s32[]{:S(2)}) async-start(), calls=%async_computation.10 | async-start | bytes 7864320
  213.4 64.0 %collective-permute-start.2 = (bf16[2,512,512]{2,1,0:T(8,128)(2,1)}, bf16[2,512,512]{2,1,0:T(8,128)(2,1)S(1)}, u32[]{:S(2)}, u32[]{:S(2)}) collective-permute-start(bf16[2,512,512]{2,1,0:T(8,128)(2,1)} %bitcast.291), channel_id=1, source_target_pairs={{0,4},{4,0},{1,5},{5,1},{2,6},{6,2},{3,7},{7,3},{8,12},{12,8},{9,1... | collective-permute-start | bytes 3145736 | tf_op jit(solution)/shard_map/ppermute | solution.py:1106
  214.6 1.2 collective-permute-start
  236.7 98.4 %collective-permute-start.15 = (bf16[512,2048]{1,0:T(8,128)(2,1)}, bf16[512,2048]{1,0:T(8,128)(2,1)}, u32[]{:S(2)}, u32[]{:S(2)}) collective-permute-start(bf16[512,2048]{1,0:T(8,128)(2,1)} %collective-permute-done.9), channel_id=1, source_target_pairs={{1,0},{2,1},{3,2},{5,4},{6,5},{7,6},{9,8},{10,9},{11,10},{13,12},{... | collective-permute-start | bytes 6291464 | tf_op jit(solution)/shard_map/ppermute | solution.py:1096
  238.0 98.4 %collective-permute-start.17 = (bf16[512,2048]{1,0:T(8,128)(2,1)}, bf16[512,2048]{1,0:T(8,128)(2,1)}, u32[]{:S(2)}, u32[]{:S(2)}) collective-permute-start(bf16[512,2048]{1,0:T(8,128)(2,1)} %collective-permute-done.10), channel_id=1, source_target_pairs={{0,1},{1,2},{2,3},{4,5},{5,6},{6,7},{8,9},{9,10},{10,11},{12,13},{... | collective-permute-start | bytes 6291464 | tf_op jit(solution)/shard_map/ppermute | solution.py:1095
  335.0 85.2 %collective-permute-start.3 = (f32[512,2048]{1,0:T(8,128)}, f32[512,2048]{1,0:T(8,128)}, u32[]{:S(2)}, u32[]{:S(2)}) collective-permute-start(f32[512,2048]{1,0:T(8,128)} %slice.650), channel_id=1, source_target_pairs={{0,8},{8,0},{16,24},{24,16},{1,9},{9,1},{17,25},{25,17},{2,10},{10... | collective-permute-start | bytes 12582920 | tf_op jit(solution)/shard_map/ppermute | solution.py:1001
  335.1 50.2 %collective-permute-start.16 = (bf16[512,2048]{1,0:T(8,128)(2,1)}, bf16[512,2048]{1,0:T(8,128)(2,1)}, u32[]{:S(2)}, u32[]{:S(2)}) collective-permute-start(bf16[512,2048]{1,0:T(8,128)(2,1)} %collective-permute-done.15), channel_id=1, source_target_pairs={{1,0},{2,1},{3,2},{5,4},{6,5},{7,6},{9,8},{10,9},{11,10},{13,12},{... | collective-permute-start | bytes 6291464 | tf_op jit(solution)/shard_map/ppermute | solution.py:1096
  336.4 50.1 %collective-permute-start.18 = (bf16[512,2048]{1,0:T(8,128)(2,1)}, bf16[512,2048]{1,0:T(8,128)(2,1)}, u32[]{:S(2)}, u32[]{:S(2)}) collective-permute-start(bf16[512,2048]{1,0:T(8,128)(2,1)} %collective-permute-done.17), channel_id=1, source_target_pairs={{0,1},{1,2},{2,3},{4,5},{5,6},{6,7},{8,9},{9,10},{10,11},{12,13},{... | collective-permute-start | bytes 6291464 | tf_op jit(solution)/shard_map/ppermute | solution.py:1095
  342.2 237.2 %collective-permute-start.4 = (bf16[512,2048]{1,0:T(8,128)(2,1)}, bf16[512,2048]{1,0:T(8,128)(2,1)}, u32[]{:S(2)}, u32[]{:S(2)}) collective-permute-start(bf16[512,2048]{1,0:T(8,128)(2,1)} %bitcast.23.own_cot_ref), channel_id=1, source_target_pairs={{0,8},{8,0},{16,24},{24,16},{1,9},{9,1},{17,25},{25,17},{2,10},{10... | collective-permute-start | bytes 6291464 | tf_op jit(solution)/shard_map/ppermute | solution.py:1001
  342.3 83.0 %copy-start.57 = (f32[2048]{0:T(1024)}, f32[2048]{0:T(1024)S(1)}, u32[]{:S(2)}) copy-start(f32[2048]{0:T(1024)S(1)} %mul.297) | copy-start | bytes 24580
  349.6 326.0 %collective-permute-start.20 = (bf16[512,2048]{1,0:T(8,128)(2,1)}, bf16[512,2048]{1,0:T(8,128)(2,1)}, u32[]{:S(2)}, u32[]{:S(2)}) collective-permute-start(bf16[512,2048]{1,0:T(8,128)(2,1)} %broadcast_select_fusion.own_cot_ref), channel_id=1, source_target_pairs={{0,8},{8,0},{16,24},{24,16},{1,9},{9,1},{17,25},{25,17},{2,10},{10... | collective-permute-start | bytes 6291464 | tf_op jit(solution)/shard_map/ppermute | solution.py:1001
  392.4 233.1 %collective-permute-start.11 = (bf16[512,2048]{1,0:T(8,128)(2,1)}, bf16[512,2048]{1,0:T(8,128)(2,1)}, u32[]{:S(2)}, u32[]{:S(2)}) collective-permute-start(bf16[512,2048]{1,0:T(8,128)(2,1)} %get-tuple-element.331.own_cot_ref), channel_id=1, source_target_pairs={{0,8},{8,0},{16,24},{24,16},{1,9},{9,1},{17,25},{25,17},{2,10},{10... | collective-permute-start | bytes 6291464 | tf_op jit(solution)/shard_map/ppermute | solution.py:1001
  425.3 153.5 %copy-start.66 = (f32[512]{0:T(512)}, f32[512]{0:T(512)S(1)}, u32[]{:S(2)}) copy-start(f32[512]{0:T(512)S(1)} %get-tuple-element.393) | copy-start | bytes 6148
  675.2 48.8 %collective-permute-start.13 = (bf16[512,2048]{1,0:T(8,128)(2,1)}, bf16[512,2048]{1,0:T(8,128)(2,1)}, u32[]{:S(2)}, u32[]{:S(2)}) collective-permute-start(bf16[512,2048]{1,0:T(8,128)(2,1)} %slice_bitcast_fusion.5), channel_id=1, source_target_pairs={{0,8},{8,0},{16,24},{24,16},{1,9},{9,1},{17,25},{25,17},{2,10},{10... | collective-permute-start | bytes 6291464 | tf_op jit(solution)/shard_map/ppermute | solution.py:1001
  723.8 4.2 collective-permute-start.29
  727.3 88.6 %collective-permute-start.14 = (bf16[512,2048]{1,0:T(8,128)(2,1)S(1)}, bf16[512,2048]{1,0:T(8,128)(2,1)S(1)}, u32[]{:S(2)}, u32[]{:S(2)}) collective-permute-start(bf16[512,2048]{1,0:T(8,128)(2,1)S(1)} %fusion.19), channel_id=1, source_target_pairs={{0,1},{1,0},{2,3},{3,2},{4,5},{5,4},{6,7},{7,6},{8,9},{9,8},{10,11... | collective-permute-start | bytes 6291464 | tf_op jit(solution)/shard_map/ppermute | solution.py:1004
  728.9 93.6 %collective-permute-start.30 = (bf16[512,2048]{1,0:T(8,128)(2,1)S(1)}, bf16[512,2048]{1,0:T(8,128)(2,1)S(1)}, u32[]{:S(2)}, u32[]{:S(2)}) collective-permute-start(bf16[512,2048]{1,0:T(8,128)(2,1)S(1)} %fusion.12), channel_id=1, source_target_pairs={{0,2},{1,3},{2,0},{3,1},{4,6},{5,7},{6,4},{7,5},{8,10},{9,11},{10,... | collective-permute-start | bytes 6291464 | tf_op jit(solution)/shard_map/ppermute | solution.py:1004
  729.0 93.5 %collective-permute-start.19 = (bf16[512,2048]{1,0:T(8,128)(2,1)S(1)}, bf16[512,2048]{1,0:T(8,128)(2,1)S(1)}, u32[]{:S(2)}, u32[]{:S(2)}) collective-permute-start(bf16[512,2048]{1,0:T(8,128)(2,1)S(1)} %copy-done.44), channel_id=1, source_target_pairs={{0,8},{8,0},{16,24},{24,16},{1,9},{9,1},{17,25},{25,17},{2,10},{10... | collective-permute-start | bytes 6291464 | tf_op jit(solution)/shard_map/ppermute | solution.py:1001
  941.6 146.9 %reduce-scatter.18.cloned.1.call-start = ((), (), s32[]{:S(2)}) async-start(), calls=%async_computation.11 | async-start | bytes 7864320
  1018.2 347.7 %reduce-scatter.20.cloned.1.call-start = ((), (), s32[]{:S(2)}) async-start(), calls=%async_computation.12 | async-start | bytes 7864320
  1021.5 67.1 %collective-permute-start.21 = (bf16[512,2048]{1,0:T(8,128)(2,1)}, bf16[512,2048]{1,0:T(8,128)(2,1)}, u32[]{:S(2)}, u32[]{:S(2)}) collective-permute-start(bf16[512,2048]{1,0:T(8,128)(2,1)} %slice_bitcast_fusion.4), channel_id=1, source_target_pairs={{0,8},{8,0},{16,24},{24,16},{1,9},{9,1},{17,25},{25,17},{2,10},{10... | collective-permute-start | bytes 6291464 | tf_op jit(solution)/shard_map/ppermute | solution.py:1001
  1023.0 165.7 %collective-permute-start.28 = (bf16[512,2048]{1,0:T(8,128)(2,1)}, bf16[512,2048]{1,0:T(8,128)(2,1)}, u32[]{:S(2)}, u32[]{:S(2)}) collective-permute-start(bf16[512,2048]{1,0:T(8,128)(2,1)} %slice_bitcast_fusion.1), channel_id=1, source_target_pairs={{0,8},{8,0},{16,24},{24,16},{1,9},{9,1},{17,25},{25,17},{2,10},{10... | collective-permute-start | bytes 6291464 | tf_op jit(solution)/shard_map/ppermute | solution.py:1001
  1025.3 70.2 %collective-permute-start.12 = (bf16[512,2048]{1,0:T(8,128)(2,1)}, bf16[512,2048]{1,0:T(8,128)(2,1)}, u32[]{:S(2)}, u32[]{:S(2)}) collective-permute-start(bf16[512,2048]{1,0:T(8,128)(2,1)} %slice_bitcast_fusion.6), channel_id=1, source_target_pairs={{0,8},{8,0},{16,24},{24,16},{1,9},{9,1},{17,25},{25,17},{2,10},{10... | collective-permute-start | bytes 6291464 | tf_op jit(solution)/shard_map/ppermute | solution.py:1001
  1027.0 71.2 %collective-permute-start.24 = (bf16[512,2048]{1,0:T(8,128)(2,1)}, bf16[512,2048]{1,0:T(8,128)(2,1)}, u32[]{:S(2)}, u32[]{:S(2)}) collective-permute-start(bf16[512,2048]{1,0:T(8,128)(2,1)} %slice_bitcast_fusion.3), channel_id=1, source_target_pairs={{0,8},{8,0},{16,24},{24,16},{1,9},{9,1},{17,25},{25,17},{2,10},{10... | collective-permute-start | bytes 6291464 | tf_op jit(solution)/shard_map/ppermute | solution.py:1001
  1029.8 72.4 %collective-permute-start.26 = (bf16[512,2048]{1,0:T(8,128)(2,1)}, bf16[512,2048]{1,0:T(8,128)(2,1)}, u32[]{:S(2)}, u32[]{:S(2)}) collective-permute-start(bf16[512,2048]{1,0:T(8,128)(2,1)} %slice_bitcast_fusion.2), channel_id=1, source_target_pairs={{0,8},{8,0},{16,24},{24,16},{1,9},{9,1},{17,25},{25,17},{2,10},{10... | collective-permute-start | bytes 6291464 | tf_op jit(solution)/shard_map/ppermute | solution.py:1001
  1088.5 99.5 %copy-start.70 = (f32[2,512]{1,0:T(2,128)S(1)}, f32[2,512]{1,0:T(2,128)}, u32[]{:S(2)}) copy-start(f32[2,512]{1,0:T(2,128)} %get-tuple-element.317) | copy-start | bytes 12292
  1088.5 100.2 %copy-start.67 = (f32[512]{0:T(512)S(1)}, f32[512]{0:T(512)}, u32[]{:S(2)}) copy-start(f32[512]{0:T(512)} %copy-done.66) | copy-start | bytes 6148
  1088.6 659.1 %reduce-scatter.22.cloned.1.call-start = ((), (), s32[]{:S(2)}) async-start(), calls=%async_computation.13 | async-start | bytes 10485760
  1088.7 100.1 %copy-start.58 = (f32[2048]{0:T(1024)S(1)}, f32[2048]{0:T(1024)}, u32[]{:S(2)}) copy-start(f32[2048]{0:T(1024)} %copy-done.57) | copy-start | bytes 24580
  1091.8 49.3 %collective-permute-start.22 = (bf16[512,2048]{1,0:T(8,128)(2,1)S(1)}, bf16[512,2048]{1,0:T(8,128)(2,1)S(1)}, u32[]{:S(2)}, u32[]{:S(2)}) collective-permute-start(bf16[512,2048]{1,0:T(8,128)(2,1)S(1)} %fusion.18), channel_id=1, source_target_pairs={{0,3},{1,2},{2,1},{3,0},{4,7},{5,6},{6,5},{7,4},{8,11},{9,10},{10,... | collective-permute-start | bytes 6291464 | tf_op jit(solution)/shard_map/ppermute | solution.py:1004
  1095.2 93.5 %copy-start.48 = (bf16[512,2048]{1,0:T(8,128)(2,1)S(1)}, bf16[512,2048]{1,0:T(8,128)(2,1)}, u32[]{:S(2)}) copy-start(bf16[512,2048]{1,0:T(8,128)(2,1)} %copy-done.47) | copy-start | bytes 6291460
  1095.5 99.5 %collective-permute-start.8 = (bf16[512,2048]{1,0:T(8,128)(2,1)S(1)}, bf16[512,2048]{1,0:T(8,128)(2,1)S(1)}, u32[]{:S(2)}, u32[]{:S(2)}) collective-permute-start(bf16[512,2048]{1,0:T(8,128)(2,1)S(1)} %slice_bitcast_fusion.7), channel_id=1, source_target_pairs={{0,8},{8,0},{16,24},{24,16},{1,9},{9,1},{17,25},{25,17},{2,10},{10... | collective-permute-start | bytes 6291464 | tf_op jit(solution)/shard_map/ppermute | solution.py:1001
  1095.6 93.1 %copy-start.46 = (bf16[512,2048]{1,0:T(8,128)(2,1)S(1)}, bf16[512,2048]{1,0:T(8,128)(2,1)}, u32[]{:S(2)}) copy-start(bf16[512,2048]{1,0:T(8,128)(2,1)} %copy-done.45) | copy-start | bytes 6291460
  1098.8 89.9 %copy-start.36 = (bf16[2,512,2048]{2,1,0:T(8,128)(2,1)S(1)}, bf16[2,512,2048]{2,1,0:T(8,128)(2,1)}, u32[]{:S(2)}) copy-start(bf16[2,512,2048]{2,1,0:T(8,128)(2,1)} %get-tuple-element.278) | copy-start | bytes 12582916
  1102.2 86.5 %copy-start.9 = (f32[512,2048]{1,0:T(8,128)S(1)}, f32[512,2048]{1,0:T(8,128)}, u32[]{:S(2)}) copy-start(f32[512,2048]{1,0:T(8,128)} %copy-done.8) | copy-start | bytes 12582916
  1141.2 133.2 %collective-permute-start.23 = (bf16[512,2048]{1,0:T(8,128)(2,1)S(1)}, bf16[512,2048]{1,0:T(8,128)(2,1)}, u32[]{:S(2)}, u32[]{:S(2)}) collective-permute-start(bf16[512,2048]{1,0:T(8,128)(2,1)S(1)} %fusion.20), channel_id=1, source_target_pairs={{0,1},{1,0},{2,3},{3,2},{4,5},{5,4},{6,7},{7,6},{8,9},{9,8},{10,11... | collective-permute-start | bytes 6291464 | tf_op jit(solution)/shard_map/ppermute | solution.py:1004
  1185.7 139.5 %collective-permute-start.25 = (bf16[512,2048]{1,0:T(8,128)(2,1)S(1)}, bf16[512,2048]{1,0:T(8,128)(2,1)}, u32[]{:S(2)}, u32[]{:S(2)}) collective-permute-start(bf16[512,2048]{1,0:T(8,128)(2,1)S(1)} %fusion.17), channel_id=1, source_target_pairs={{0,2},{1,3},{2,0},{3,1},{4,6},{5,7},{6,4},{7,5},{8,10},{9,11},{10,... | collective-permute-start | bytes 6291464 | tf_op jit(solution)/shard_map/ppermute | solution.py:1004
  1186.6 138.5 %collective-permute-start.27 = (bf16[512,2048]{1,0:T(8,128)(2,1)S(1)}, bf16[512,2048]{1,0:T(8,128)(2,1)}, u32[]{:S(2)}, u32[]{:S(2)}) collective-permute-start(bf16[512,2048]{1,0:T(8,128)(2,1)S(1)} %fusion.16), channel_id=1, source_target_pairs={{0,3},{1,2},{2,1},{3,0},{4,7},{5,6},{6,5},{7,4},{8,11},{9,10},{10,... | collective-permute-start | bytes 6291464 | tf_op jit(solution)/shard_map/ppermute | solution.py:1004
  1188.1 137.1 %slice-start = ((s8[8388608]{0:T(1024)(128)(4,1)}), s8[4194304]{0:T(1024)(128)(4,1)S(1)}, s32[]{:S(2)}) async-start(s8[8388608]{0:T(1024)(128)(4,1)} %bitcast.255), calls=%async_computation.14 | async-start | bytes 8388608
  1188.7 136.5 %slice-start.1 = ((s8[8388608]{0:T(1024)(128)(4,1)}), s8[4194304]{0:T(1024)(128)(4,1)S(1)}, s32[]{:S(2)}) async-start(s8[8388608]{0:T(1024)(128)(4,1)} %bitcast.255), calls=%async_computation.15 | async-start | bytes 8388608
  1188.7 136.5 %copy-start.72 = (f32[512]{0:T(512)S(1)}, f32[512]{0:T(512)}, u32[]{:S(2)}) copy-start(f32[512]{0:T(512)} %get-tuple-element.392) | copy-start | bytes 6148
  1337.1 4.4 collective-permute-start.31
  1365.9 437.9 %reduce-scatter.14.cloned.1.call-start = ((), (), s32[]{:S(2)}) async-start(), calls=%async_computation.6 | async-start | bytes 2621440 | tf_op jit(solution)/shard_map/reduce_scatter | solution.py:1218
  1433.1 48.2 %collective-permute-start.32 = (bf16[2,512,512]{2,1,0:T(8,128)(2,1)S(1)}, bf16[2,512,512]{2,1,0:T(8,128)(2,1)S(1)}, u32[]{:S(2)}, u32[]{:S(2)}) collective-permute-start(bf16[2,512,512]{2,1,0:T(8,128)(2,1)S(1)} %select_convert_fusion), channel_id=1, source_target_pairs={{0,4},{4,0},{1,5},{5,1},{2,6},{6,2},{3,7},{7,3},{8,12},{12,8},{9,1... | collective-permute-start | bytes 3145736 | tf_op jit(solution)/shard_map/ppermute | solution.py:1244
  1532.8 7.5 collective-permute-start.33
  1538.0 21.1 %collective-permute-start.39 = (bf16[2,768,256]{1,2,0:T(8,128)(2,1)}, bf16[2,768,256]{1,2,0:T(8,128)(2,1)}, u32[]{:S(2)}, u32[]{:S(2)}) collective-permute-start(bf16[2,768,256]{1,2,0:T(8,128)(2,1)} %select_bitcast_fusion.2), channel_id=1, source_target_pairs={{0,8},{8,0},{16,24},{24,16},{1,9},{9,1},{17,25},{25,17},{2,10},{10... | collective-permute-start | bytes 2359304 | tf_op jit(solution)/shard_map/ppermute | solution.py:1001
  1558.9 2.1 collective-permute-start.34
  1561.0 3.7 collective-permute-start.35
  1564.7 3.6 collective-permute-start.36
  1568.3 35.0 %collective-permute-start.37 = (f32[8,128]{1,0:T(8,128)S(1)}, f32[8,128]{1,0:T(8,128)S(1)}, u32[]{:S(2)}, u32[]{:S(2)}) collective-permute-start(f32[8,128]{1,0:T(8,128)S(1)} %add.249), channel_id=1, source_target_pairs={{0,1},{1,0},{2,3},{3,2},{4,5},{5,4},{6,7},{7,6},{8,9},{9,8},{10,11... | collective-permute-start | bytes 12296 | tf_op jit(solution)/shard_map/ppermute | solution.py:1183
  1603.3 14.8 collective-permute-start.38
  1755.1 2.4 collective-permute-start.40
  1755.6 3.8 collective-permute-start.41
  (70 other events, 752.7 us)
Sparse Core Ops, SparseCore 0:
  10.8 162.6 all-gather.7
  181.1 91.0 all-gather.9
  274.0 67.6 all-gather.11
  343.4 70.2 all-gather.13
  941.7 67.7 reduce-scatter.15
  1018.3 70.2 reduce-scatter.17
  1091.5 70.2 reduce-scatter.19
  1366.0 149.5 reduce-scatter.21
  1747.8 55.8 reduce-scatter.13

commit v3 on v2

v3 whole, which is shorter than its diff:
```python
import functools

import jax
import jax.numpy as jnp
from jax import lax
from jax.experimental import pallas as pl
from jax.experimental.pallas import tpu as pltpu
from jax.sharding import PartitionSpec as P

QUERY_HEADS = 32
KEY_VALUE_HEADS = 4
HEAD_DIM = 128


EPS = 1e-06
ROPE_BASE = 1000000.0
MASKED = -1e30
MESH = pl.DeviceIdType.MESH
SEQ = "seq"
CTX = "ctx"
EXP = "exp"
CORE = "core"
X = "x"
Y = "y"
UP = "up"
DOWN = "down"
START = "start"
WAIT = "wait"
WAIT_SEND = "wait_send"
WAIT_RECV = "wait_recv"
INFO = "info"
SEG = "seg"
HEAD = "head"
KEY = "key"
VALUE = "value"
RECIP = "recip"


def contract_rows(first_op, second_op):
    return lax.dot_general(
        first_op, second_op, (((0,), (0,)), ((), ())), preferred_element_type=jnp.float32
    )


def contract_cols(first_op, second_op):
    return lax.dot_general(
        first_op, second_op, (((1,), (1,)), ((), ())), preferred_element_type=jnp.float32
    )


def rope_tables(positions):
    half_dim = HEAD_DIM // 2
    inverse = ROPE_BASE ** (-jnp.arange(half_dim, dtype=jnp.float32) * 2.0 / HEAD_DIM)
    angles = positions.astype(jnp.float32)[:, None] * inverse[None, :]
    cosine_table = jnp.cos(angles)
    sine_values = jnp.sin(angles)
    return (
        jnp.concatenate([cosine_table, cosine_table], -1),
        jnp.concatenate([sine_values, sine_values], -1),
    )


def inverse_rotation(gradient, cosine_table, sine_values):
    half_dim = gradient.shape[-1] // 2
    scaled = gradient * sine_values[:, None, :]
    return gradient * cosine_table[:, None, :] + jnp.concatenate(
        [scaled[..., half_dim:], -scaled[..., :half_dim]], -1
    )


def norm_back(gradient, source, inverse, gain_vec):
    scaled = gradient * gain_vec
    return inverse * scaled - source * inverse**3 * jnp.mean(
        scaled * source, axis=-1, keepdims=True
    )


def neighbours(n_exp):
    seq, x, z = lax.axis_index(SEQ), lax.axis_index(CTX), lax.axis_index(EXP)
    y, core = seq // 2, seq % 2
    ids = {
        CORE: {SEQ: 2 * y + 1 - core},
        X: {CTX: 1 - x},
        Y: {SEQ: 2 * (1 - y) + core},
        UP: {EXP: z + 1},
        DOWN: {EXP: z - 1},
    }
    return x, y, z, core, ids


def greet(z, n_exp, ids, names):
    barrier = pltpu.get_barrier_semaphore()
    count = 0
    for name in names:
        if name in (UP, DOWN):
            there = (z < n_exp - 1) if name == UP else (z > 0)

            @pl.when(there)
            def _():
                pl.semaphore_signal(
                    barrier, inc=1, device_id=ids[name], device_id_type=MESH
                )

            count = count + there.astype(jnp.int32)
        else:
            pl.semaphore_signal(
                barrier, inc=1, device_id=ids[name], device_id_type=MESH
            )
            count = count + 1
    pl.semaphore_wait(barrier, count)


def xor_chip(z, step, n_exp):
    result, bit = 0, 1
    while bit < n_exp:
        result = result + bit * ((z // bit % 2 + step // bit % 2) % 2)
        bit *= 2
    return result


class Plane:
    def __init__(self, n_exp, fulls, sems):
        x, y, _, _, self.ids = neighbours(n_exp)
        self.here, self.beside, self.across = 2 * y + x, 2 * y + 1 - x, 2 * (1 - y) + x
        self.fulls, self.sems = fulls, sems

    def each(self, method, far):
        near = ((self.here,), X), ((self.here,), Y)
        cases = (((self.beside, 0), Y), ((self.across, 1), X)) if far else near
        for which, full in enumerate(self.fulls):
            for lane, (place, name) in enumerate(cases):
                part = full.at[place]
                copy = pltpu.make_async_remote_copy(
                    src_ref=part,
                    dst_ref=part,
                    send_sem=self.sems.at[0, which, lane],
                    recv_sem=self.sems.at[1, which, lane],
                    device_id=self.ids[name],
                    device_id_type=MESH,
                )
                getattr(copy, method)()


def plane_sems(arrays):
    return pltpu.SemaphoreType.DMA((2, arrays, 2))


class Column:
    def __init__(self, n_exp, everyone, sems, own=None):
        self.x, self.y, self.z, self.core, self.ids = neighbours(n_exp)
        self.n_exp, self.everyone, self.sems, self.own = n_exp, everyone, sems, own

    def copies(self, lane, part, first):
        for which, result in enumerate(self.everyone):
            there = result.at[part, self.core]
            yield pltpu.make_async_remote_copy(
                src_ref=self.own[which] if first else there,
                dst_ref=there,
                send_sem=self.sems.at[0, which, lane, part],
                recv_sem=self.sems.at[1, which, lane, part],
                device_id=self.ids[(UP, DOWN, CORE)[lane]],
                device_id_type=MESH,
            )

    def each(self, method, cases, first=False):
        for lane, part, there in cases:

            @pl.when(there)
            def _(lane=lane, part=part):
                for copy in self.copies(lane, part, first):
                    getattr(copy, method)()

    def sends(self, hop, method):
        z, n = self.z, self.n_exp
        cases = (
            (0, z - hop + 1, (z >= hop - 1) & (z < n - 1)),
            (1, z + hop - 1, (z + hop - 1 < n) & (z > 0)),
        )
        self.each(method, cases, first=isinstance(hop, int) and hop == 1)

    def arrivals(self, hop):
        z, n = self.z, self.n_exp
        self.each(WAIT_RECV, ((0, z - hop, z >= hop), (1, z + hop, z + hop < n)))

    def passes(self, hop, method):
        z, n = self.z, self.n_exp
        self.each(method, ((2, z - hop, z >= hop), (2, z + hop, z + hop < n)))

    def pass_own(self, method):
        for copy in self.copies(2, self.z, True):
            getattr(copy, method)()


def column_sems(arrays, n_exp):
    return pltpu.SemaphoreType.DMA((2, arrays, 3, n_exp))


def sent_rows(chip_ref, into_ref, job, sems, i, n_exp):
    slot, into, step, start, stop = job
    rows = pl.ds(start, stop - start)
    return pltpu.make_async_remote_copy(
        src_ref=chip_ref.at[slot, rows],
        dst_ref=into_ref.at[into, rows],
        send_sem=sems.at[0, i],
        recv_sem=sems.at[1, i],
        device_id={EXP: xor_chip(lax.axis_index(EXP), step, n_exp)},
        device_id_type=MESH,
    )


def greet_slots(slots, n_exp):
    barrier = pltpu.get_barrier_semaphore()
    for slot in slots:
        pl.semaphore_signal(
            barrier,
            inc=1,
            device_id={EXP: xor_chip(lax.axis_index(EXP), slot, n_exp)},
            device_id_type=MESH,
        )
    pl.semaphore_wait(barrier, len(slots))


def gather_kernel(
    n_exp,
    mine_ref,
    other_ref,
    gate_ref,
    other_gate_ref,
    up_ref,
    other_up_ref,
    down_ref,
    other_down_ref,
    out_ref,
    cot_ref,
    table_ref,
    full_ref,
    out_full_ref,
    gate_full_ref,
    up_full_ref,
    down_pair_ref,
    cots_ref,
    tables_ref,
    local_sems,
    core_sems,
    z_sems,
    x_sems,
    y_sems,
    xf_sems,
    yf_sems,
    column_sem,
):
    column = Column(n_exp, (cots_ref, tables_ref), column_sem, (cot_ref, table_ref))
    x, y, z, core, ids = neighbours(n_exp)
    greet(z, n_exp, ids, (CORE, X, Y, UP, DOWN))
    here, beside, across = 2 * y + x, 2 * y + 1 - x, 2 * (1 - y) + x

    fulls = (full_ref, out_full_ref)

    def act(method, place, sems, slot, name):
        for which, full in enumerate(fulls):
            part = full.at[place]
            copy = pltpu.make_async_remote_copy(
                src_ref=part,
                dst_ref=part,
                send_sem=sems.at[0, which, slot],
                recv_sem=sems.at[1, which, slot],
                device_id=ids[name],
                device_id_type=MESH,
            )
            getattr(copy, method)()

    places = (
        full_ref.at[here, z, core],
        gate_full_ref.at[here, core],
        up_full_ref.at[here, core],
        down_pair_ref.at[core],
    )
    kept = [
        pltpu.make_async_copy(source, place, local_sems.at[i])
        for i, (source, place) in enumerate(zip((mine_ref, gate_ref, up_ref, down_ref), places))
    ]
    kept.insert(1, pltpu.make_async_copy(out_ref, out_full_ref.at[here, z], local_sems.at[4]))
    to_core = [
        pltpu.make_async_remote_copy(
            src_ref=source,
            dst_ref=place,
            send_sem=core_sems.at[0, i],
            recv_sem=core_sems.at[1, i],
            device_id=ids[CORE],
            device_id_type=MESH,
        )
        for i, (source, place) in enumerate(zip((other_ref, other_gate_ref, other_up_ref, other_down_ref), places))
    ]
    for copy in kept + to_core:
        copy.start()
    to_core[0].wait()
    kept[0].wait()
    kept[1].wait()
    column.pass_own(START)

    def source(label):
        hop = (label + 1) // 2
        if label == 0:
            return z, None
        return (z - hop, z >= hop) if label % 2 else (z + hop, z + hop < n_exp)

    labels = range(2 * n_exp - 1)

    def guarded(condition, action):
        if condition is None:
            action()
        else:
            pl.when(condition)(action)

    def z_slot(label, name):
        return label + 1 if label else (0 if name == UP else 1)

    def z_sends(label, method):
        part, there = source(label)
        for name in (UP, DOWN) if label == 0 else ((UP,) if label % 2 else (DOWN,)):
            room = (z < n_exp - 1) if name == UP else (z > 0)
            condition = room if there is None else there & room
            pl.when(condition)(
                lambda name=name: act(method, (here, part), z_sems, z_slot(label, name), name)
            )

    def z_arrival(label):
        hop = (label + 1) // 2
        name = UP if label % 2 else DOWN
        part, there = source(label)
        slot = z_slot(label - 2 if hop > 1 else 0, name)
        pl.when(there)(lambda: act(WAIT_RECV, (here, part), z_sems, slot, name))

    def spread(label):
        part, there = source(label)
        z_sends(label, START)

        def action():
            act(START, (here, part), x_sems, label, X)
            act(START, (here, part), y_sems, label, Y)

        guarded(there, action)

    def turn(label):
        part, there = source(label)

        def action():
            act(WAIT_RECV, (beside, part), x_sems, label, X)
            act(START, (beside, part, 0), xf_sems, label, Y)
            act(WAIT_RECV, (across, part), y_sems, label, Y)
            act(START, (across, part, 1), yf_sems, label, X)

        guarded(there, action)

    spread(0)
    for hop in range(1, n_exp):
        for label in (2 * hop - 1, 2 * hop):
            z_arrival(label)
            spread(label)
        if hop == n_exp - 1:
            column.sends(1, START)
        for label in (0,) if hop == 1 else (2 * hop - 3, 2 * hop - 2):
            turn(label)
    for label in (2 * n_exp - 3, 2 * n_exp - 2):
        turn(label)
    opposite = 2 * (1 - y) + 1 - x
    for label in labels:
        part, there = source(label)

        def action(label=label, part=part):
            act(WAIT_SEND, (here, part), x_sems, label, X)
            act(WAIT_SEND, (here, part), y_sems, label, Y)
            act(WAIT_SEND, (beside, part, 0), xf_sems, label, Y)
            act(WAIT_SEND, (across, part, 1), yf_sems, label, X)
            act(WAIT_RECV, (opposite, part, 0), xf_sems, label, Y)
            act(WAIT_RECV, (opposite, part, 1), yf_sems, label, X)

        guarded(there, action)
        z_sends(label, WAIT_SEND)
    column.arrivals(1)
    column.sends(1, WAIT_SEND)
    column.pass_own(WAIT)
    for copy in kept[2:] + to_core[1:]:
        copy.wait()


def gather_chips(mine, other, halves, out, cot, table, n_exp):
    labels = 2 * n_exp - 1
    any_spec = pl.BlockSpec(memory_space=pl.ANY)
    vmem_spec = pl.BlockSpec(memory_space=pltpu.VMEM)
    pair = lambda count: pltpu.SemaphoreType.DMA((2, 2, count))
    return pl.pallas_call(
        functools.partial(gather_kernel, n_exp),
        in_specs=[vmem_spec] * 9 + [any_spec, any_spec],
        out_specs=[any_spec] * 7,
        out_shape=[
            jax.ShapeDtypeStruct((4, n_exp, 2) + mine.shape, mine.dtype),
            jax.ShapeDtypeStruct((4, n_exp) + out.shape, out.dtype),
        ]
        + [jax.ShapeDtypeStruct((4, 2) + a.shape, a.dtype) for a in halves[:4:2]]
        + [jax.ShapeDtypeStruct((2,) + halves[4].shape, halves[4].dtype)]
        + [jax.ShapeDtypeStruct((n_exp, 2) + a.shape, a.dtype) for a in (cot, table)],
        scratch_shapes=[
            pltpu.SemaphoreType.DMA((5,)),
            pltpu.SemaphoreType.DMA((2, 4)),
            pair(2 * n_exp),
            pair(labels),
            pair(labels),
            pair(labels),
            pair(labels),
            column_sems(2, n_exp),
        ],
        compiler_params=pltpu.CompilerParams(
            collective_id=1, has_side_effects=True, vmem_limit_bytes=32 * MIB
        ),
    )(mine, other, *halves, out, cot, table)


def exchange_kernel(n_exp, first_ref, second_ref, firsts_ref, seconds_ref, sems):
    column = Column(n_exp, (firsts_ref, seconds_ref), sems, (first_ref, second_ref))
    greet(column.z, n_exp, column.ids, (CORE, UP, DOWN))
    column.sends(1, START)
    column.pass_own(START)
    for hop in range(1, n_exp):
        column.arrivals(hop)
        if hop < n_exp - 1:
            column.sends(hop + 1, START)
        column.passes(hop, START)
    column.pass_own(WAIT)
    for hop in range(1, n_exp):
        column.sends(hop, WAIT_SEND)
        column.passes(hop, WAIT)


def exchange_column(tokens, table, n_exp):
    any_spec = pl.BlockSpec(memory_space=pl.ANY)
    return pl.pallas_call(
        functools.partial(exchange_kernel, n_exp),
        in_specs=[any_spec] * 2,
        out_specs=[any_spec] * 2,
        out_shape=[
            jax.ShapeDtypeStruct((n_exp, 2) + a.shape, a.dtype) for a in (tokens, table)
        ],
        scratch_shapes=[column_sems(2, n_exp)],
        compiler_params=pltpu.CompilerParams(collective_id=3, has_side_effects=True),
        cost_estimate=pl.CostEstimate(
            flops=0, bytes_accessed=16 * n_exp * tokens.size, transcendentals=0
        ),
    )(tokens, table)


def scatter_kernel(
    n_exp,
    normed_ref,
    grad_ref,
    kv_grad_ref,
    extra_ref,
    mine_ref,
    theirs_ref,
    turned,
    part,
    from_x,
    from_y,
    second_x,
    second_y,
    total,
    from_z,
    from_core,
    x_sems,
    y_sems,
    x2_sems,
    y2_sems,
    z_sems,
    core_sems,
):
    bf16, f32 = jnp.bfloat16, jnp.float32
    x, y, z, core, ids = neighbours(n_exp)
    barrier = pltpu.get_barrier_semaphore()
    columns = [{EXP: (z + k) % n_exp} for k in range(1, n_exp)]
    for there in [ids[CORE], ids[X], ids[Y]] + columns:
        pl.semaphore_signal(barrier, inc=1, device_id=there, device_id_type=MESH)
    pl.semaphore_wait(barrier, 2 + n_exp)

    def remote(source, target, sems, slot, there):
        return pltpu.make_async_remote_copy(
            src_ref=source,
            dst_ref=target,
            send_sem=sems.at[0, slot],
            recv_sem=sems.at[1, slot],
            device_id=there,
            device_id_type=MESH,
        )

    rows = mine_ref.shape[0]
    q_width, width = grad_ref.shape[1], grad_ref.shape[1] + kv_grad_ref.shape[1]
    turned[...] = normed_ref[...].T
    steps = range(n_exp)

    def first_copies(k):
        return [
            remote(part.at[k, 1 - x, :, 0], from_x.at[k], x_sems, k, ids[X]),
            remote(part.at[k, :, 1 - y, 1], from_y.at[k], y_sems, k, ids[Y]),
        ]

    def second_copies(k):
        return [
            remote(part.at[k, x, 1 - y, 0], second_x.at[k], x2_sems, k, ids[Y]),
            remote(part.at[k, 1 - x, y, 1], second_y.at[k], y2_sems, k, ids[X]),
        ]

    def z_copy(k):
        return remote(
            total.at[k], from_z.at[k], z_sems, k, {EXP: (z + k + 1) % n_exp}
        )

    def produce(k):
        place = (z + k + 1) % n_exp
        blocks = []
        for px in range(2):
            for py in range(2):
                for c in range(2):
                    start = (((py * 2 + c) * 2 + px) * n_exp + place) * rows
                    blocks.append(turned[pl.ds(pl.multiple_of(start, rows), rows), :])
        block = jnp.concatenate(blocks, 0)
        grad = dot_plain(block, grad_ref[...]).astype(bf16)
        kv_grad = dot_plain(block, kv_grad_ref[...]).astype(bf16)
        i = 0
        for px in range(2):
            for py in range(2):
                for c in range(2):
                    part[k, px, py, c, :, :q_width] = grad[i * rows : (i + 1) * rows]
                    part[k, px, py, c, :, q_width:width] = kv_grad[i * rows : (i + 1) * rows]
                    part[k, px, py, c, :, width:] = extra_ref[py, c, px, place]
                    i += 1

    def launch(k):
        for copy in first_copies(k):
            copy.start()

    for k in steps:
        produce(k)
        if k < 2:
            launch(k)

    def second(k):
        along_x, along_y = first_copies(k)
        along_x.wait_recv()
        for py in range(2):
            part[k, x, py, 0] = (part[k, x, py, 0].astype(f32) + from_x[k, py].astype(f32)).astype(bf16)
        along_y.wait_recv()
        for px in range(2):
            part[k, px, y, 1] = (part[k, px, y, 1].astype(f32) + from_y[k, px].astype(f32)).astype(bf16)
        for copy in second_copies(k):
            copy.start()

    def third(k):
        along_y, along_x = second_copies(k)
        along_y.wait_recv()
        total[k, 0] = (part[k, x, y, 0].astype(f32) + second_x[k].astype(f32)).astype(bf16)
        along_x.wait_recv()
        total[k, 1] = (part[k, x, y, 1].astype(f32) + second_y[k].astype(f32)).astype(bf16)
        if k < n_exp - 1:
            z_copy(k).start()

    for k in steps:
        second(k)
        if k + 2 < n_exp:
            launch(k + 2)
        if k:
            third(k - 1)
    third(n_exp - 1)
    result = total[n_exp - 1].astype(f32)
    for k in range(n_exp - 1):
        z_copy(k).wait_recv()
        result = result + from_z[k].astype(f32)
    total[n_exp - 1] = result.astype(bf16)
    to_core = remote(total.at[n_exp - 1, 1 - core], from_core, core_sems, 0, ids[CORE])
    to_core.start()
    for k in steps:
        for copy in first_copies(k) + second_copies(k) + ([z_copy(k)] if k < n_exp - 1 else []):
            copy.wait_send()
    to_core.wait()
    mine_ref[...] = total[n_exp - 1, core].astype(f32)
    theirs_ref[...] = from_core[...].astype(f32)


def dense_grad_scatter(normed, grad, kv_grad, extra, n_exp):
    bf16 = jnp.bfloat16
    rows, model = extra.shape[4], normed.shape[1]
    width = grad.shape[1] + kv_grad.shape[1] + extra.shape[5]
    block = (rows, width)
    vmem = lambda *lead: pltpu.VMEM(lead + block, bf16)
    pair = lambda count: pltpu.SemaphoreType.DMA((2, count))
    spec = pl.BlockSpec(memory_space=pltpu.VMEM)
    return pl.pallas_call(
        functools.partial(scatter_kernel, n_exp),
        in_specs=[spec] * 4,
        out_specs=[spec] * 2,
        out_shape=[jax.ShapeDtypeStruct(block, jnp.float32)] * 2,
        scratch_shapes=[
            pltpu.VMEM((model, normed.shape[0]), bf16),
            vmem(n_exp, 2, 2, 2),
            vmem(n_exp, 2),
            vmem(n_exp, 2),
            vmem(n_exp),
            vmem(n_exp),
            vmem(n_exp, 2),
            vmem(n_exp, 2),
            vmem(),
            pair(n_exp),
            pair(n_exp),
            pair(n_exp),
            pair(n_exp),
            pair(n_exp),
            pair(1),
        ],
        compiler_params=pltpu.CompilerParams(
            collective_id=2, has_side_effects=True, vmem_limit_bytes=60 * MIB
        ),
        cost_estimate=pl.CostEstimate(
            flops=2 * normed.shape[0] * model * width, bytes_accessed=16 * MIB, transcendentals=0
        ),
    )(normed, grad, kv_grad, extra)


def back_kernel(
    n_exp,
    jobs,
    query_grad_ref,
    key_grad_ref,
    value_grad_ref,
    raw_ref,
    w_query_ref,
    w_kv_ref,
    gain_ref,
    cos_ref,
    sin_ref,
    hidden_ref,
    row_gain_ref,
    middle_grad_ref,
    chip_ref,
    into_in_ref,
    kv_grad_ref,
    hidden_grad_ref,
    row_gain_grad_ref,
    gain_grad_ref,
    into_ref,
    kv_send,
    kv_got,
    sib_part,
    own_part,
    part_got,
    x_sems,
    core_sems,
    job_sems,
):
    bf16, f32 = jnp.bfloat16, jnp.float32
    x, _, z, _, ids = neighbours(n_exp)
    tokens, model = hidden_ref.shape
    keys_width = raw_ref.shape[1] // 2
    barrier = pltpu.get_barrier_semaphore()
    slots = sorted({job[2] for job in jobs})
    greeted = [ids[CORE], ids[X]] + [{EXP: xor_chip(z, slot, n_exp)} for slot in slots]
    for there in greeted:
        pl.semaphore_signal(barrier, inc=1, device_id=there, device_id_type=MESH)
    here, there = (pl.ds(pl.multiple_of(i * tokens, tokens), tokens) for i in (x, 1 - x))
    for s in range(2):
        kv_send[s, :, :keys_width] = key_grad_ref[s, there].astype(bf16)
        kv_send[s, :, keys_width:] = value_grad_ref[s, there].astype(bf16)
    pl.semaphore_wait(barrier, len(greeted))
    to_x = pltpu.make_async_remote_copy(
        src_ref=kv_send,
        dst_ref=kv_got,
        send_sem=x_sems.at[0],
        recv_sem=x_sems.at[1],
        device_id=ids[X],
        device_id_type=MESH,
    )
    to_x.start()
    sent = [sent_rows(chip_ref, into_ref, job, job_sems, i, n_exp) for i, job in enumerate(jobs)]
    for copy in sent:
        copy.start()
    tile = 256
    parts = ((1, sib_part), (0, own_part))

    def query_product(s, part):
        rows = query_grad_ref[s * tokens : (s + 1) * tokens]
        for start in range(0, model, tile):
            part[:, start : start + tile] = dot_cols(rows, w_query_ref[start : start + tile])

    for s, part in parts:
        query_product(s, part)
    to_x.wait()
    gain_grad = None
    for s in range(2):
        rows = slice(s * tokens, (s + 1) * tokens)
        for start in range(0, keys_width, HEAD_DIM):
            columns = slice(start, start + HEAD_DIM)
            grad = key_grad_ref[s, here, columns] + kv_got[s, :, columns].astype(f32)
            turned = rotate_rows_back(grad, cos_ref[...], sin_ref[...])
            raw = raw_ref[rows, columns]
            inverse = lax.rsqrt(jnp.mean(raw * raw, axis=-1, keepdims=True) + EPS)
            unit = raw * inverse
            total = jnp.sum(turned * unit, axis=0, keepdims=True)
            gain_grad = total if gain_grad is None else gain_grad + total
            scaled = turned * gain_ref[...]
            kv_grad_ref[rows, columns] = (
                inverse * (scaled - unit * jnp.mean(scaled * unit, axis=-1, keepdims=True))
            ).astype(bf16)
        value_grad = value_grad_ref[s, here] + kv_got[s, :, keys_width:].astype(f32)
        kv_grad_ref[rows, keys_width:] = value_grad.astype(bf16)
    gain_grad_ref[0:1] = gain_grad

    def kv_product(s, part):
        rows = kv_grad_ref[s * tokens : (s + 1) * tokens]
        for start in range(0, model, tile):
            part[:, start : start + tile] += dot_cols(rows, w_kv_ref[start : start + tile])

    kv_product(*parts[0])
    to_core = pltpu.make_async_remote_copy(
        src_ref=sib_part,
        dst_ref=part_got,
        send_sem=core_sems.at[0],
        recv_sem=core_sems.at[1],
        device_id=ids[CORE],
        device_id_type=MESH,
    )
    to_core.start()
    kv_product(*parts[1])
    to_core.wait()
    row_gain_grad_ref[...] = jnp.zeros_like(row_gain_grad_ref)
    count = min(tokens, 64)

    @pl.loop(0, tokens // count)
    def _(i):
        rows = pl.ds(pl.multiple_of(i * count, count), count)
        grad = own_part[rows] + part_got[rows]
        hidden = hidden_ref[rows].astype(f32)
        inverse = lax.rsqrt(jnp.mean(hidden * hidden, axis=-1, keepdims=True) + EPS)
        unit = hidden * inverse
        row_gain_grad_ref[...] += jnp.sum(grad * unit, axis=0, keepdims=True)
        scaled = grad * row_gain_ref[...]
        back = inverse * (scaled - unit * jnp.mean(scaled * unit, axis=-1, keepdims=True))
        hidden_grad_ref[rows] = (middle_grad_ref[rows] + back).astype(bf16)

    for copy in sent:
        copy.wait()


def back_to_input(
    query_grad, key_grad, value_grad, raw, w_query, w_kv, gain, cos, sin, hidden, row_gain, middle_grad,
    chip, into, jobs, n_exp
):
    bf16, f32 = jnp.bfloat16, jnp.float32
    tokens, model = hidden.shape
    total, kv_width = raw.shape
    vmem, any_spec = pl.BlockSpec(memory_space=pltpu.VMEM), pl.BlockSpec(memory_space=pl.ANY)
    return pl.pallas_call(
        functools.partial(back_kernel, n_exp, jobs),
        in_specs=[vmem] * 12 + [any_spec] * 2,
        out_specs=[vmem] * 4 + [any_spec],
        out_shape=[
            jax.ShapeDtypeStruct((total, kv_width), bf16),
            jax.ShapeDtypeStruct((tokens, model), bf16),
            jax.ShapeDtypeStruct((1, model), f32),
            jax.ShapeDtypeStruct((8, HEAD_DIM), f32),
            jax.ShapeDtypeStruct(into.shape, into.dtype),
        ],
        scratch_shapes=[
            pltpu.VMEM((2, tokens, kv_width), bf16),
            pltpu.VMEM((2, tokens, kv_width), bf16),
            pltpu.VMEM((tokens, model), f32),
            pltpu.VMEM((tokens, model), f32),
            pltpu.VMEM((tokens, model), f32),
            pltpu.SemaphoreType.DMA((2,)),
            pltpu.SemaphoreType.DMA((2,)),
            pltpu.SemaphoreType.DMA((2, len(jobs))),
        ],
        input_output_aliases={13: 4},
        compiler_params=pltpu.CompilerParams(
            vmem_limit_bytes=60 * MIB, collective_id=11, has_side_effects=True
        ),
        cost_estimate=pl.CostEstimate(
            flops=2 * total * model * (query_grad.shape[1] + kv_width),
            bytes_accessed=48 * MIB,
            transcendentals=0,
        ),
    )(
        query_grad, key_grad, value_grad, raw, w_query, w_kv, gain, cos, sin, hidden, row_gain,
        middle_grad, chip, into
    )


def out_back_kernel(
    n_exp, jobs, mixed_ref, grad_ref, weight_ref, valid_ref, chip_ref, into_in, weight_grad_ref, mixed_grad_ref, into_ref, sems
):
    bf16 = jnp.bfloat16
    sent = [sent_rows(chip_ref, into_ref, job, sems, i, n_exp) for i, job in enumerate(jobs)]
    step = pl.program_id(0)

    @pl.when(step == 0)
    def _():
        greet_slots(sorted({job[2] for job in jobs}), n_exp)
        for copy in sent:
            copy.start()

    weight_grad_ref[...] = dot_plain(mixed_ref[...].T, grad_ref[...]).astype(bf16)
    mixed_grad = dot_cols(grad_ref[...], weight_ref[...]).astype(bf16)
    mixed_grad_ref[...] = mixed_grad * valid_ref[...].astype(bf16)

    @pl.when(step == pl.num_programs(0) - 1)
    def _():
        for copy in sent:
            copy.wait()


def out_back(mixed, grad, weight, valid, chip, into, jobs, n_exp):
    bf16 = jnp.bfloat16
    total, width = mixed.shape
    model = grad.shape[1]
    block = 2 * HEAD_DIM
    any_spec = pl.BlockSpec(memory_space=pl.ANY)
    columns = pl.BlockSpec((total, block), lambda j: (0, j))
    rows = pl.BlockSpec((block, model), lambda j: (j, 0))
    return pl.pallas_call(
        functools.partial(out_back_kernel, n_exp, jobs),
        grid=(width // block,),
        in_specs=[
            columns,
            pl.BlockSpec(grad.shape, lambda j: (0, 0)),
            rows,
            pl.BlockSpec(valid.shape, lambda j: (0, 0)),
            any_spec,
            any_spec,
        ],
        out_specs=[rows, columns, any_spec],
        out_shape=[
            jax.ShapeDtypeStruct((width, model), bf16),
            jax.ShapeDtypeStruct((total, width), bf16),
            jax.ShapeDtypeStruct(into.shape, bf16),
        ],
        input_output_aliases={5: 2},
        scratch_shapes=[pltpu.SemaphoreType.DMA((2, len(jobs)))],
        compiler_params=pltpu.CompilerParams(
            vmem_limit_bytes=40 * MIB, collective_id=12, has_side_effects=True
        ),
        cost_estimate=pl.CostEstimate(
            flops=4 * total * model * width, bytes_accessed=24 * MIB, transcendentals=0
        ),
    )(mixed, grad, weight, valid, chip, into)


def pick(core, first, second):
    return jnp.where(core == 0, first, second)


def column_halves(weight, core):
    width = weight.shape[1] // KEY_VALUE_HEADS
    parts = [weight[:, i * width : (i + 1) * width] for i in range(KEY_VALUE_HEADS)]
    mine = [pick(core, parts[i], parts[i + 1]) for i in range(0, KEY_VALUE_HEADS, 2)]
    other = [pick(core, parts[i + 1], parts[i]) for i in range(0, KEY_VALUE_HEADS, 2)]
    return mine, other


LOG2E = 1.4426950408889634
MIB = 1 << 20


def rotate_rows(vectors, cosine_table, signed_sine):
    return vectors * cosine_table + pltpu.roll(vectors, HEAD_DIM // 2, 1) * signed_sine


def rotate_rows_back(gradient, cosine_table, signed_sine):
    return gradient * cosine_table - pltpu.roll(gradient, HEAD_DIM // 2, 1) * signed_sine


def dot_cols(first, second):
    return lax.dot_general(
        first, second, (((1,), (1,)), ((), ())), preferred_element_type=jnp.float32
    )


def dot_plain(first, second):
    return jnp.dot(first, second, preferred_element_type=jnp.float32)


def ordered_weight(n_y, weight_ref, ordered_ref):
    n_xz = weight_ref.shape[0] // n_y
    weight = jnp.concatenate(
        [weight_ref[y * n_xz + i, c] for y in range(n_y) for c in range(2) for i in range(n_xz)], 0
    )
    ordered_ref[...] = weight
    return weight


def store_rotated(raw, gain, cos_ref, sin_ref, low_ref):
    tokens = cos_ref.shape[0]
    for h in range(2):
        columns = slice(h * HEAD_DIM, (h + 1) * HEAD_DIM)
        head = raw[:, columns]
        inverse = lax.rsqrt(jnp.mean(head * head, axis=-1, keepdims=True) + EPS)
        scaled = head * inverse * gain
        for s in range(2):
            part = slice(s * tokens, (s + 1) * tokens)
            low_ref[part, columns] = rotate_rows(scaled[part], cos_ref[...], sin_ref[...]).astype(
                jnp.bfloat16
            )


def key_value_kernel(
    n_y,
    own_ref,
    sib_ref,
    row_gain_ref,
    weight_ref,
    gain_ref,
    cos_ref,
    sin_ref,
    raw_ref,
    low_ref,
    ordered_ref,
    normed_ref,
):
    tokens = own_ref.shape[0]

    @pl.when(pl.program_id(0) == 0)
    def _():
        for s, source in enumerate((own_ref, sib_ref)):
            hidden = source[...].astype(jnp.float32)
            inverse = lax.rsqrt(jnp.mean(hidden * hidden, axis=-1, keepdims=True) + EPS)
            normed_ref[s * tokens : (s + 1) * tokens] = (hidden * inverse * row_gain_ref[...]).astype(
                jnp.bfloat16
            )

    raw = dot_plain(normed_ref[...], ordered_weight(n_y, weight_ref, ordered_ref))
    raw_ref[...] = raw

    @pl.when(pl.program_id(0) == 0)
    def _():
        store_rotated(raw, gain_ref[...], cos_ref, sin_ref, low_ref)

    @pl.when(pl.program_id(0) == 1)
    def _():
        low_ref[...] = raw.astype(jnp.bfloat16)


def query_kernel(n_y, n_exp, normed_ref, weight_ref, gain_ref, cos_ref, sin_ref, *refs):
    if n_exp:
        raw_ref, low_ref, ordered_ref, gate_full_ref, up_full_ref, cots_ref, tables_ref = refs[4:11]
        plane = Plane(n_exp, (gate_full_ref, up_full_ref), refs[11])
        column = Column(n_exp, (cots_ref, tables_ref), refs[12])

        @pl.when(pl.program_id(0) == 0)
        def _():
            greet(column.z, n_exp, plane.ids, (CORE, X, Y, UP, DOWN))
            plane.each(START, False)
            column.sends(2, START)
            column.passes(1, START)
    else:
        raw_ref, low_ref, ordered_ref = refs
    raw = dot_plain(normed_ref[...], ordered_weight(n_y, weight_ref, ordered_ref))
    raw_ref[...] = raw
    store_rotated(raw, gain_ref[...], cos_ref, sin_ref, low_ref)
    if n_exp:

        @pl.when(pl.program_id(0) == pl.num_programs(0) - 1)
        def _():
            plane.each(WAIT, False)
            column.arrivals(2)
            column.sends(2, WAIT_SEND)
            column.passes(1, WAIT)


def projection_specs(normed_shape, gathered, first_block, blocks, cos):
    total, model = normed_shape
    n_yxz, _, rows, _ = gathered.shape
    width = 2 * HEAD_DIM
    fixed = lambda j: (0, 0)
    moving = lambda j: (0, j)
    weight = pl.BlockSpec((n_yxz, 2, rows, width), lambda j: (0, 0, 0, j + first_block))
    tail = [pl.BlockSpec((1, HEAD_DIM), fixed), pl.BlockSpec(cos.shape, fixed), pl.BlockSpec(cos.shape, fixed)]
    out_specs = [pl.BlockSpec((total, width), moving)] * 2 + [pl.BlockSpec((model, width), moving)]
    out_shape = [
        jax.ShapeDtypeStruct((total, blocks * width), jnp.float32),
        jax.ShapeDtypeStruct((total, blocks * width), jnp.bfloat16),
        jax.ShapeDtypeStruct((model, blocks * width), jnp.bfloat16),
    ]
    cost = pl.CostEstimate(
        flops=2 * total * model * blocks * width,
        bytes_accessed=total * model * 2 + blocks * width * (model * 4 + total * 6),
        transcendentals=0,
    )
    return weight, tail, out_specs, out_shape, cost


def project_keys(own, sib, row_gain, gathered, first_block, gain, cos, sin, n_y):
    tokens, model = own.shape
    normed_shape = (2 * tokens, model)
    weight, tail, out_specs, out_shape, cost = projection_specs(normed_shape, gathered, first_block, 2, cos)
    fixed = lambda j: (0, 0)
    return pl.pallas_call(
        functools.partial(key_value_kernel, n_y),
        grid=(2,),
        in_specs=[pl.BlockSpec(own.shape, fixed)] * 2
        + [pl.BlockSpec((1, model), fixed), weight]
        + tail,
        out_specs=out_specs + [pl.BlockSpec(normed_shape, fixed)],
        out_shape=out_shape + [jax.ShapeDtypeStruct(normed_shape, jnp.bfloat16)],
        compiler_params=pltpu.CompilerParams(vmem_limit_bytes=56 * MIB),
        cost_estimate=cost,
    )(own, sib, row_gain, gathered, gain, cos, sin)


def project_queries(normed, gathered, blocks, gain, cos, sin, n_y, n_exp, moving):
    weight, tail, out_specs, out_shape, cost = projection_specs(normed.shape, gathered, 0, blocks, cos)
    any_specs = [pl.BlockSpec(memory_space=pl.ANY)] * len(moving)
    return pl.pallas_call(
        functools.partial(query_kernel, n_y, n_exp if moving else 0),
        grid=(blocks,),
        in_specs=[pl.BlockSpec(normed.shape, lambda j: (0, 0)), weight] + tail + any_specs,
        out_specs=out_specs + any_specs,
        out_shape=out_shape + [jax.ShapeDtypeStruct(a.shape, a.dtype) for a in moving],
        scratch_shapes=[plane_sems(2), column_sems(2, n_exp)] if moving else [],
        input_output_aliases={5 + i: 3 + i for i in range(len(moving))},
        compiler_params=pltpu.CompilerParams(
            vmem_limit_bytes=56 * MIB,
            collective_id=4 if moving else None,
            has_side_effects=bool(moving),
        ),
        cost_estimate=cost,
    )(normed, gathered, gain, cos, sin, *moving)


def mask_bias(seg_key, info):
    keys, tokens = seg_key.shape[0], info.shape[1]
    key_pos = lax.broadcasted_iota(jnp.int32, (keys, tokens), 0)
    allowed = (seg_key == info[0:1]) & (key_pos <= info[1:2])
    return jnp.where(allowed, 0.0, MASKED)


def key_tile(keys):
    return min(keys, 256)


def attention_kernel(hops, info_ref, seg_ref, q_ref, k_ref, v_ref, *refs):
    if hops:
        mixed_ref, recip_ref, gate_ref, up_ref, cots_ref, tables_ref = refs[4:10]
        bias_ref, vt_ref, plane_sem, sems = refs[10:]
        column = Column(hops, (cots_ref, tables_ref), sems)
        plane = Plane(hops, (gate_ref, up_ref), plane_sem)
        places = [pl.program_id(i) for i in range(3)]
        ends = [pl.num_programs(i) - 1 for i in range(3)]

        @pl.when((places[0] == 0) & (places[1] == 0) & (places[2] == 0))
        def _():
            greet(column.z, hops, column.ids, (CORE, X, Y, UP, DOWN))
            plane.each(START, True)
            column.sends(hops - 1, START)
            column.passes(hops - 2, START)
    else:
        mixed_ref, recip_ref, bias_ref, vt_ref = refs
    keys = k_ref.shape[1]
    tile = key_tile(keys)

    @pl.when((pl.program_id(1) == 0) & (pl.program_id(2) == 0))
    def _():
        bias_ref[...] = mask_bias(seg_ref[0], info_ref[0])

    @pl.when(pl.program_id(2) == 0)
    def _():
        vt_ref[...] = v_ref[0].astype(jnp.float32).T.astype(jnp.bfloat16)

    queries = q_ref[...]
    total, mixed = None, None
    for start in range(0, keys, tile):
        part = slice(start, start + tile)
        scores = dot_cols(k_ref[0, part], queries) * (HEAD_DIM**-0.5 * LOG2E) + bias_ref[part]
        weights = jnp.exp2(scores)
        tile_total = jnp.sum(weights, axis=0, keepdims=True)
        tile_mixed = dot_plain(vt_ref[:, part], weights.astype(jnp.bfloat16))
        total = tile_total if total is None else total + tile_total
        mixed = tile_mixed if mixed is None else mixed + tile_mixed
    recip = 1.0 / total
    recip_ref[0] = recip
    valid = (info_ref[0, 0:1] > 0).astype(jnp.float32)
    mixed_ref[...] = (mixed * (recip * valid)).T.astype(jnp.bfloat16)
    if hops:

        @pl.when((places[0] == ends[0]) & (places[1] == ends[1]) & (places[2] == ends[2]))
        def _():
            plane.each(WAIT, True)
            column.arrivals(hops - 1)
            column.passes(hops - 1, START)
            column.sends(hops - 1, WAIT_SEND)
            column.passes(hops - 2, WAIT)
            column.passes(hops - 1, WAIT)


def attention_specs(tokens, keys, groups, per_group):
    head = pl.BlockSpec((tokens, HEAD_DIM), lambda s, g, h: (s, g * per_group + h))
    return dict(
        info=pl.BlockSpec((1, 8, tokens), lambda s, g, h: (s, 0, 0)),
        seg=pl.BlockSpec((1, keys, 1), lambda s, g, h: (s, 0, 0)),
        head=head,
        key=pl.BlockSpec((1, keys, HEAD_DIM), lambda s, g, h: (s, 0, g)),
        value=pl.BlockSpec((1, keys, HEAD_DIM), lambda s, g, h: (s, 0, groups + g)),
        recip=pl.BlockSpec((1, 1, tokens), lambda s, g, h: ((s * groups + g) * per_group + h, 0, 0)),
    )


def attend(info, seg_keys, queries, kv_full, groups, per_group, n_exp, moving):
    tokens, keys = info.shape[2], seg_keys.shape[1]
    specs = attention_specs(tokens, keys, groups, per_group)
    steps = 2 * groups * per_group
    return pl.pallas_call(
        functools.partial(attention_kernel, n_exp if moving else 0),
        grid=(2, groups, per_group),
        in_specs=[specs[INFO], specs[SEG], specs[HEAD], specs[KEY], specs[VALUE]]
        + [pl.BlockSpec(memory_space=pl.ANY)] * len(moving),
        out_specs=[specs[HEAD], specs[RECIP]]
        + [pl.BlockSpec(memory_space=pl.ANY)] * len(moving),
        out_shape=[
            jax.ShapeDtypeStruct(queries.shape, jnp.bfloat16),
            jax.ShapeDtypeStruct((steps, 1, tokens), jnp.float32),
        ]
        + [jax.ShapeDtypeStruct(a.shape, a.dtype) for a in moving],
        scratch_shapes=[
            pltpu.VMEM((keys, tokens), jnp.float32),
            pltpu.VMEM((HEAD_DIM, keys), jnp.bfloat16),
        ]
        + ([plane_sems(2), column_sems(2, n_exp)] if moving else []),
        input_output_aliases={5 + i: 2 + i for i in range(len(moving))},
        compiler_params=pltpu.CompilerParams(
            vmem_limit_bytes=48 * MIB,
            collective_id=5 if moving else None,
            has_side_effects=bool(moving),
        ),
        cost_estimate=pl.CostEstimate(
            flops=steps * 8 * tokens * keys * HEAD_DIM,
            bytes_accessed=queries.size * 4 + kv_full.size * 2,
            transcendentals=steps * tokens * keys,
        ),
    )(info, seg_keys, queries, kv_full, kv_full, *moving)


def attention_back_kernel(
    info_ref,
    seg_ref,
    q_ref,
    k_ref,
    v_ref,
    mixed_ref,
    grad_ref,
    recip_ref,
    raw_ref,
    gain_ref,
    cos_ref,
    sin_ref,
    chip_ref,
    into_in_ref,
    raw_grad_ref,
    key_grad_ref,
    value_grad_ref,
    gain_grad_ref,
    into_ref,
    bias_ref,
    kt_ref,
    job_sems,
    *,
    n_exp,
    jobs,
):
    sent = [sent_rows(chip_ref, into_ref, job, job_sems, i, n_exp) for i, job in enumerate(jobs)]
    places = [pl.program_id(i) for i in range(3)]
    ends = [pl.num_programs(i) - 1 for i in range(3)]

    @pl.when((places[0] == 0) & (places[1] == 0) & (places[2] == 0))
    def _():
        greet_slots(sorted({job[2] for job in jobs}), n_exp)
        for copy in sent:
            copy.start()

    keys = k_ref.shape[1]
    tile = key_tile(keys)
    scale = HEAD_DIM**-0.5
    first = (pl.program_id(1) == 0) & (pl.program_id(2) == 0)

    @pl.when(first)
    def _():
        bias_ref[...] = mask_bias(seg_ref[0], info_ref[0])

    @pl.when(first & (pl.program_id(0) == 0))
    def _():
        gain_grad_ref[...] = jnp.zeros_like(gain_grad_ref)

    @pl.when(pl.program_id(2) == 0)
    def _():
        kt_ref[...] = k_ref[0].astype(jnp.float32).T.astype(jnp.bfloat16)
        key_grad_ref[...] = jnp.zeros_like(key_grad_ref)
        value_grad_ref[...] = jnp.zeros_like(value_grad_ref)

    queries, grad = q_ref[...], grad_ref[...]
    recip = recip_ref[0]
    overlap = grad.astype(jnp.float32) * mixed_ref[...].astype(jnp.float32)
    inner = jnp.sum(overlap.T, axis=0, keepdims=True)
    query_grad = None
    for start in range(0, keys, tile):
        part = slice(start, start + tile)
        scores = dot_cols(k_ref[0, part], queries) * (scale * LOG2E) + bias_ref[part]
        probs = jnp.exp2(scores) * recip
        grad_probs = dot_cols(v_ref[0, part], grad)
        grad_scores = (probs * (grad_probs - inner)).astype(jnp.bfloat16)
        value_grad_ref[0, part] += dot_plain(probs.astype(jnp.bfloat16), grad)
        key_grad_ref[0, part] += dot_plain(grad_scores, queries) * scale
        tile_grad = dot_plain(kt_ref[:, part], grad_scores)
        query_grad = tile_grad if query_grad is None else query_grad + tile_grad
    turned = rotate_rows_back((query_grad * scale).T, cos_ref[...], sin_ref[...])
    raw = raw_ref[...]
    inverse = lax.rsqrt(jnp.mean(raw * raw, axis=-1, keepdims=True) + EPS)
    unit = raw * inverse
    gain_grad_ref[0:1] += jnp.sum(turned * unit, axis=0, keepdims=True)
    scaled = turned * gain_ref[...]
    raw_grad_ref[...] = (
        inverse * (scaled - unit * jnp.mean(scaled * unit, axis=-1, keepdims=True))
    ).astype(jnp.bfloat16)

    @pl.when((places[0] == ends[0]) & (places[1] == ends[1]) & (places[2] == ends[2]))
    def _():
        for copy in sent:
            copy.wait()


def attend_back(
    info,
    seg_keys,
    queries,
    kv_full,
    mixed,
    grad_mixed,
    recip,
    raw,
    gain,
    cos,
    sin,
    groups,
    per_group,
    chip,
    into,
    jobs,
    n_exp,
):
    tokens, keys = info.shape[2], seg_keys.shape[1]
    specs = attention_specs(tokens, keys, groups, per_group)
    steps = 2 * groups * per_group
    fixed = lambda s, g, h: (0, 0)
    key_grad = jax.ShapeDtypeStruct((2, keys, groups * HEAD_DIM), jnp.float32)
    return pl.pallas_call(
        functools.partial(attention_back_kernel, n_exp=n_exp, jobs=jobs),
        grid=(2, groups, per_group),
        in_specs=[specs[INFO], specs[SEG], specs[HEAD], specs[KEY], specs[VALUE]]
        + [specs[HEAD], specs[HEAD], specs[RECIP], specs[HEAD]]
        + [pl.BlockSpec(a.shape, fixed) for a in (gain, cos, sin)]
        + [pl.BlockSpec(memory_space=pl.ANY)] * 2,
        out_specs=[specs[HEAD], specs[KEY], specs[KEY], pl.BlockSpec((8, HEAD_DIM), fixed)]
        + [pl.BlockSpec(memory_space=pl.ANY)],
        out_shape=[
            jax.ShapeDtypeStruct(queries.shape, jnp.bfloat16),
            key_grad,
            key_grad,
            jax.ShapeDtypeStruct((8, HEAD_DIM), jnp.float32),
            jax.ShapeDtypeStruct(into.shape, into.dtype),
        ],
        scratch_shapes=[
            pltpu.VMEM((keys, tokens), jnp.float32),
            pltpu.VMEM((HEAD_DIM, keys), jnp.bfloat16),
            pltpu.SemaphoreType.DMA((2, len(jobs))),
        ],
        input_output_aliases={13: 4},
        compiler_params=pltpu.CompilerParams(
            vmem_limit_bytes=48 * MIB, collective_id=6, has_side_effects=True
        ),
        cost_estimate=pl.CostEstimate(
            flops=steps * 20 * tokens * keys * HEAD_DIM,
            bytes_accessed=queries.size * 12 + kv_full.size * 6,
            transcendentals=steps * tokens * keys,
        ),
    )(
        info, seg_keys, queries, kv_full, kv_full, mixed, grad_mixed, recip, raw, gain, cos, sin, chip, into
    )


def moe_kernel(
    n_exp,
    n_y,
    local_experts,
    table_ref,
    own_ref,
    own_cot_ref,
    cots_ref,
    gate_any,
    up_any,
    down_any,
    x_ref,
    val_ref,
    product_ref,
    gate_grad_ref,
    up_grad_ref,
    tokens_ref,
    partial_ref,
    grad_chip_ref,
    out_chip_ref,
    grad_into_ref,
    out_into_ref,
    gate_w,
    up_w,
    down_w,
    token_scr,
    cot_scr,
    held,
    send,
    got,
    weight_sems,
    load_sems,
    token_sems,
    core_sems,
    local_sems,
    grad_sems,
):
    bf16, f32 = jnp.bfloat16, jnp.float32
    column = Column(n_exp, (tokens_ref,), token_sems, (own_ref,))
    z, core = column.z, column.core
    c, q = pl.program_id(0), pl.program_id(1)
    e, s = q // 2, (q % 3 + 1) // 2
    owner = core + s * (1 - 2 * core)
    chip = xor_chip(z, c, n_exp)
    slots, tokens = x_ref.shape[1], token_scr.shape[1]

    def weight_copies(expert):
        for which, (source, target) in enumerate(
            ((gate_any, gate_w), (up_any, up_w), (down_any, down_w))
        ):
            chips, cores, _, depth, _ = source.shape
            n_x = chips // n_y
            for p in range(chips):
                for k in range(cores):
                    start = ((p // n_x * cores + k) * n_x + p % n_x) * depth
                    yield pltpu.make_async_copy(
                        source.at[p, k, expert],
                        target.at[expert, pl.ds(start, depth)],
                        weight_sems.at[which, expert, p * cores + k],
                    )

    def load(which, sources, methods):
        copies = [
            pltpu.make_async_copy(source, scratch.at[which], load_sems.at[which, i])
            for i, (source, scratch) in enumerate(zip(sources, (token_scr, cot_scr)))
        ]
        for method in methods:
            for copy in copies:
                getattr(copy, method)()

    def fetch(i):
        return pltpu.make_async_copy(partial_ref.at[c, i], got.at[i], local_sems.at[i])

    def store(chunk, i):
        target = (grad_chip_ref, out_chip_ref)[i].at[chunk]
        return pltpu.make_async_copy(got.at[i], target, local_sems.at[2 + i])

    other_parts = (tokens_ref.at[chip, 1 - core], cots_ref.at[chip, 1 - core])

    def core_copy(chunk, i):
        return pltpu.make_async_remote_copy(
            src_ref=send.at[i],
            dst_ref=partial_ref.at[chunk, i],
            send_sem=core_sems.at[0, chunk, i],
            recv_sem=core_sems.at[1, chunk, i],
            device_id=column.ids[CORE],
            device_id_type=MESH,
        )

    def grad_copy(chunk):
        return pltpu.make_async_remote_copy(
            src_ref=grad_chip_ref.at[chunk],
            dst_ref=grad_into_ref.at[chunk],
            send_sem=grad_sems.at[0, chunk],
            recv_sem=grad_sems.at[1, chunk],
            device_id={EXP: xor_chip(z, chunk, n_exp)},
            device_id_type=MESH,
        )

    @pl.when((c == 0) & (q == 0))
    def _():
        barrier = pltpu.get_barrier_semaphore()
        greeted = [column.ids[CORE]] + [{EXP: xor_chip(z, k, n_exp)} for k in range(1, n_exp)]
        for there in greeted:
            pl.semaphore_signal(barrier, inc=1, device_id=there, device_id_type=MESH)
        pl.semaphore_wait(barrier, n_exp)
        column.sends(1, START)
        column.pass_own(START)
        for expert in range(2):
            for copy in weight_copies(expert):
                copy.start()
        load(0, (own_ref, own_cot_ref), (START, WAIT))
        for copy in weight_copies(0):
            copy.wait()

    @pl.when((c > 0) & (q == 0))
    def _():
        column.arrivals(c)
        pl.when(c < n_exp - 1)(lambda: column.sends(c + 1, START))
        column.passes(c, START)
        load(0, (tokens_ref.at[chip, core], cots_ref.at[chip, core]), (START,))
        for i in range(2):
            store(c - 1, i).wait()
        pl.when(c == n_exp - 1)(lambda: grad_copy(1).start())
        pl.when(c > 2)(lambda: grad_copy(c - 1).start())
        load(0, (tokens_ref.at[chip, core], cots_ref.at[chip, core]), (WAIT,))

    @pl.when(q == 1)
    def _():
        for copy in column.copies(2, chip, False):
            copy.wait_recv()
        load(1, other_parts, (START, WAIT))

    @pl.when((c == 0) & (q == 2))
    def _():
        for copy in weight_copies(1):
            copy.wait()

    slot_ids = lax.broadcasted_iota(jnp.int32, (slots, tokens), 0).astype(f32)
    expert_rows = table_ref.shape[2] // 2
    first_row = z * local_experts + core * 2

    def hits_of(expert):
        return table_ref[chip, owner, pl.ds(first_row + expert, 1)] == slot_ids

    hits = hits_of(e)
    one_hot = hits.astype(f32).astype(bf16)
    gates = table_ref[chip, owner, pl.ds(expert_rows + first_row + e, 1)]
    gate_row = jnp.sum(jnp.where(hits, gates, 0.0), axis=1, keepdims=True)
    x_rows = dot_plain(one_hot, token_scr[s]).astype(bf16)
    x_ref[0] = x_rows
    grad_val = (gate_row * dot_plain(one_hot, cot_scr[s])).astype(bf16)
    val_ref[0] = grad_val
    gate_act = dot_plain(x_rows, gate_w[e])
    up_act = dot_plain(x_rows, up_w[e])
    sigmoid = 1.0 / (1.0 + jnp.exp(-gate_act))
    silu = gate_act * sigmoid
    product = (silu * up_act).astype(bf16)
    product_ref[0] = product
    grad_product = dot_cols(grad_val, down_w[e])
    grad_gate = (grad_product * up_act * (sigmoid * (1.0 + gate_act * (1.0 - sigmoid)))).astype(bf16)
    grad_up = (grad_product * silu).astype(bf16)
    gate_grad_ref[0] = grad_gate
    up_grad_ref[0] = grad_up
    grad_rows = (dot_cols(grad_gate, gate_w[e]) + dot_cols(grad_up, up_w[e])).astype(bf16)
    weighted = (gate_row * dot_plain(product, down_w[e])).astype(bf16)

    @pl.when(e == 0)
    def _():
        held[s, 0] = grad_rows
        held[s, 1] = weighted

    def combined(i, rows):
        before = hits_of(0).astype(f32).astype(bf16)
        return lax.dot_general(
            jnp.concatenate([before, one_hot], 0),
            jnp.concatenate([held[s, i], rows], 0),
            (((0,), (0,)), ((), ())),
            preferred_element_type=f32,
        )

    @pl.when(q == 2)
    def _():
        for i, rows in enumerate((grad_rows, weighted)):
            pl.when(c > 0)(lambda i=i: core_copy(c - 1, i).wait_send())
            send[i] = combined(i, rows).astype(bf16)
            core_copy(c, i).start()

    @pl.when(q == 3)
    def _():
        for i, rows in enumerate((grad_rows, weighted)):
            own = combined(i, rows)
            core_copy(c, i).wait_recv()
            fetch(i).start()
            fetch(i).wait()
            got[i] = (own + got[i].astype(f32)).astype(bf16)
            store(c, i).start()

    @pl.when((c == n_exp - 1) & (q == 3))
    def _():
        column.pass_own(WAIT_SEND)
        for hop in range(1, n_exp):
            column.sends(hop, WAIT_SEND)
            column.passes(hop, WAIT_SEND)
        for i in range(2):
            core_copy(n_exp - 1, i).wait_send()
            store(n_exp - 1, i).wait()
        for chunk in range(1, n_exp - 1):
            grad_copy(chunk).wait()


def run_experts(tables, own, own_cot, cots, weights, n_y, local_experts, slots, n_exp):
    bf16 = jnp.bfloat16
    tokens, model = own.shape
    ff = weights[0].shape[4]
    pieces = weights[0].shape[0] * weights[0].shape[1]
    any_spec = pl.BlockSpec(memory_space=pl.ANY)
    row_spec = lambda width: pl.BlockSpec(
        (1, slots, width), lambda c, q: (q // 2, 2 * c + (q % 3 + 1) // 2, 0)
    )
    widths = (model, model, ff, ff, ff)
    chip_shape = jax.ShapeDtypeStruct((n_exp, tokens, model), bf16)
    results = pl.pallas_call(
        functools.partial(moe_kernel, n_exp, n_y, local_experts),
        grid=(n_exp, 4),
        in_specs=[pl.BlockSpec(tables.shape, lambda c, q: (0, 0, 0, 0))] + [any_spec] * 6,
        out_specs=[row_spec(width) for width in widths] + [any_spec] * 6,
        out_shape=[jax.ShapeDtypeStruct((2, 2 * n_exp * slots, width), bf16) for width in widths]
        + [
            jax.ShapeDtypeStruct(cots.shape, bf16),
            jax.ShapeDtypeStruct((n_exp, 2, tokens, model), bf16),
            chip_shape,
            chip_shape,
            chip_shape,
            chip_shape,
        ],
        scratch_shapes=[
            pltpu.VMEM((2, model, ff), bf16),
            pltpu.VMEM((2, model, ff), bf16),
            pltpu.VMEM((2, ff, model), bf16),
            pltpu.VMEM((2, tokens, model), bf16),
            pltpu.VMEM((2, tokens, model), bf16),
            pltpu.VMEM((2, 2, slots, model), bf16),
            pltpu.VMEM((2, tokens, model), bf16),
            pltpu.VMEM((2, tokens, model), bf16),
            pltpu.SemaphoreType.DMA((3, 2, pieces)),
            pltpu.SemaphoreType.DMA((2, 2)),
            column_sems(1, n_exp),
            pltpu.SemaphoreType.DMA((2, n_exp, 2)),
            pltpu.SemaphoreType.DMA((4,)),
            pltpu.SemaphoreType.DMA((2, n_exp)),
        ],
        compiler_params=pltpu.CompilerParams(
            vmem_limit_bytes=63 * MIB, collective_id=7, has_side_effects=True
        ),
        cost_estimate=pl.CostEstimate(
            flops=4 * n_exp * (12 * slots * model * ff + 8 * slots * tokens * model),
            bytes_accessed=24 * model * ff + 4 * n_exp * slots * (2 * model + 3 * ff) * 2,
            transcendentals=4 * n_exp * slots * ff,
        ),
    )(tables, own, own_cot, cots, *weights)
    return results[:5], *results[7:]


def weight_grad_kernel(
    n_y,
    n_ctx,
    n_exp,
    merged,
    x_ref,
    val_ref,
    product_ref,
    gg_ref,
    gu_ref,
    chip_ref,
    into_in_ref,
    out_chip_ref,
    *refs,
):
    bf16 = jnp.bfloat16
    results, (into_ref, out_into_ref, pt_ref, ggt_ref, gut_ref, job_sems) = refs[:-6], refs[-6:]
    e, n = pl.program_id(0), pl.program_id(1)
    last, rows = n_exp - 1, chip_ref.shape[1]
    sent = [
        sent_rows(chip_ref, into_ref, (last, last, last, 0, rows), job_sems, 0, n_exp),
        sent_rows(out_chip_ref, out_into_ref, (last, last, 1, 0, rows), job_sems, 1, n_exp),
    ]

    @pl.when((e == 0) & (n == 0))
    def _():
        greet_slots([1, last], n_exp)
        for copy in sent:
            copy.start()

    @pl.when(n == 0)
    def _():
        for source, turned in ((product_ref, pt_ref), (gg_ref, ggt_ref), (gu_ref, gut_ref)):
            turned[...] = source[0].T

    gate, up = (dot_plain(turned[...], x_ref[0]).astype(bf16) for turned in (ggt_ref, gut_ref))
    down = dot_plain(pt_ref[...], val_ref[0]).astype(bf16)
    if merged:
        (result,) = results
        depth = result.shape[-2] // (2 * n_y * n_ctx)
        y, c, x = n // (2 * n_ctx), n // n_ctx % 2, n % n_ctx
        result[y, x, c, 0, 0] = gate
        result[y, x, c, 1, 0] = up
        rows = pl.ds(pl.multiple_of(n * depth, depth), depth)
        for shard in range(2 * n_y * n_ctx):
            place = (shard // (2 * n_ctx), shard % n_ctx, shard // n_ctx % 2, 2, 0, rows)
            result[place] = down[shard * depth : (shard + 1) * depth]
    else:
        for grad, result in zip((gate, up), results):
            depth = result.shape[-1]
            for i in range(result.shape[1]):
                result[0, i, 0, 0] = grad[:, i * depth : (i + 1) * depth]
        depth = results[2].shape[4]
        for shard in range(2 * n_y * n_ctx):
            place = (shard // (2 * n_ctx), shard % n_ctx, shard // n_ctx % 2, 0)
            results[2][place] = down[shard * depth : (shard + 1) * depth]

    @pl.when((e == 1) & (n == pl.num_programs(1) - 1))
    def _():
        for copy in sent:
            copy.wait()


def expert_weight_grads(rows, chip, into, out_chip, n_y, n_ctx, n_exp, merged):
    bf16 = jnp.bfloat16
    x_all, val_all, product_all, gg_all, gu_all = rows
    _, total, model = x_all.shape
    ff = gg_all.shape[2]
    shards = 2 * n_y * n_ctx
    col, depth, down_depth = 256, model // shards, ff // shards
    wide = pl.BlockSpec((1, total, col), lambda e, n: (e, 0, n))
    whole = pl.BlockSpec((1, total, ff), lambda e, n: (e, 0, 0))
    any_spec = pl.BlockSpec(memory_space=pl.ANY)
    if merged:
        out_specs = [
            pl.BlockSpec((n_y, n_ctx, 2, 3, 1, ff, depth), lambda e, n: (0, 0, 0, 0, e, 0, 0))
        ]
        out_shape = [jax.ShapeDtypeStruct((n_y, n_ctx, 2, 3, 2, ff, depth), bf16)]
    else:
        k = col // depth

        def place(e, n):
            shard = n * k
            return (shard // (2 * n_ctx), shard % n_ctx // k, shard // n_ctx % 2, e, 0, 0)

        out_specs = [pl.BlockSpec((1, k, 1, 1, ff, depth), place)] * 2
        out_specs.append(
            pl.BlockSpec((n_y, n_ctx, 2, 1, down_depth, col), lambda e, n: (0, 0, 0, e, 0, n))
        )
        out_shape = [jax.ShapeDtypeStruct((n_y, n_ctx, 2, 2, ff, depth), bf16)] * 2
        out_shape.append(jax.ShapeDtypeStruct((n_y, n_ctx, 2, 2, down_depth, model), bf16))
    *blocks, into, out_into = pl.pallas_call(
        functools.partial(weight_grad_kernel, n_y, n_ctx, n_exp, merged),
        grid=(2, model // col),
        in_specs=[wide, wide, whole, whole, whole] + [any_spec] * 3,
        out_specs=out_specs + [any_spec] * 2,
        out_shape=out_shape + [jax.ShapeDtypeStruct(a.shape, a.dtype) for a in (into, out_chip)],
        scratch_shapes=[pltpu.VMEM((ff, total), bf16)] * 3 + [pltpu.SemaphoreType.DMA((2, 2))],
        input_output_aliases={6: len(out_shape)},
        compiler_params=pltpu.CompilerParams(
            vmem_limit_bytes=63 * MIB, collective_id=8, has_side_effects=True
        ),
        cost_estimate=pl.CostEstimate(
            flops=2 * 6 * total * model * ff,
            bytes_accessed=2 * (2 * total * (2 * model + 3 * ff) + 6 * model * ff),
            transcendentals=0,
        ),
    )(x_all, val_all, product_all, gg_all, gu_all, chip, into, out_chip)
    return blocks, into, out_into


def part_grad_kernel(n_y, n_ctx, n_exp, jobs, wide_ref, *refs):
    bf16 = jnp.bfloat16
    sources, refs = (refs[:2], refs[2:]) if len(refs) == 12 else (refs[:1], refs[1:])
    chip_ref, _, out_chip_ref, _, result, into_ref, out_into_ref = refs[:7]
    turned_refs, job_sems = refs[7:-1], refs[-1]
    e, n = pl.program_id(0), pl.program_id(1)
    pairs = ((chip_ref, into_ref), (out_chip_ref, out_into_ref))
    sent = [
        sent_rows(*pairs[which], job, job_sems, i, n_exp) for i, (which, job) in enumerate(jobs)
    ]

    @pl.when((e == 0) & (n == 0))
    def _():
        greet_slots(sorted({job[2] for _, job in jobs}), n_exp)
        for copy in sent:
            copy.start()

    @pl.when(n == 0)
    def _():
        for source, turned in zip(sources, turned_refs):
            turned[...] = source[0].T

    grads = [dot_plain(turned[...], wide_ref[0]).astype(bf16) for turned in turned_refs]
    shards = 2 * n_y * n_ctx
    depth = result.shape[-2] // shards
    if len(grads) == 2:
        y, c, x = n // (2 * n_ctx), n // n_ctx % 2, n % n_ctx
        for i, grad in enumerate(grads):
            result[y, x, c, i, 0] = grad
    else:
        rows = pl.ds(pl.multiple_of(n * depth, depth), depth)
        for shard in range(shards):
            place = (shard // (2 * n_ctx), shard % n_ctx, shard // n_ctx % 2, 0, 0, rows)
            result[place] = grads[0][shard * depth : (shard + 1) * depth]

    @pl.when((e == 1) & (n == pl.num_programs(1) - 1))
    def _():
        for copy in sent:
            copy.wait()


def part_weight_grads(wide, sources, chip, into, out_chip, out_into, jobs, collective, n_y, n_ctx, n_exp):
    bf16 = jnp.bfloat16
    _, total, model = wide.shape
    ff, kinds, col = sources[0].shape[2], len(sources), 256
    whole = pl.BlockSpec((1, total, ff), lambda e, n: (e, 0, 0))
    any_spec = pl.BlockSpec(memory_space=pl.ANY)
    return pl.pallas_call(
        functools.partial(part_grad_kernel, n_y, n_ctx, n_exp, jobs),
        grid=(2, model // col),
        in_specs=[pl.BlockSpec((1, total, col), lambda e, n: (e, 0, n))]
        + [whole] * kinds
        + [any_spec] * 4,
        out_specs=[
            pl.BlockSpec((n_y, n_ctx, 2, kinds, 1, ff, col), lambda e, n: (0, 0, 0, 0, e, 0, 0))
        ]
        + [any_spec] * 2,
        out_shape=[jax.ShapeDtypeStruct((n_y, n_ctx, 2, kinds, 2, ff, col), bf16)]
        + [jax.ShapeDtypeStruct(a.shape, a.dtype) for a in (into, out_into)],
        scratch_shapes=[pltpu.VMEM((ff, total), bf16)] * kinds
        + [pltpu.SemaphoreType.DMA((2, len(jobs)))],
        input_output_aliases={kinds + 2: 1, kinds + 4: 2},
        compiler_params=pltpu.CompilerParams(
            vmem_limit_bytes=60 * MIB, collective_id=collective, has_side_effects=True
        ),
        cost_estimate=pl.CostEstimate(
            flops=4 * kinds * total * model * ff,
            bytes_accessed=4 * (total * (model + kinds * ff) + kinds * model * ff),
            transcendentals=0,
        ),
    )(wide, *sources, chip, into, out_chip, out_into)


def sum_kernel(plan, value_ref, total_ref, held, arrived, sems):
    partners = [{axis: xor_chip(lax.axis_index(axis), hop, size)} for axis, size, hop in plan]
    barrier = pltpu.get_barrier_semaphore()
    for there in partners:
        pl.semaphore_signal(barrier, inc=1, device_id=there, device_id_type=MESH)
    pl.semaphore_wait(barrier, len(plan))
    held[0] = value_ref[...]
    for i, there in enumerate(partners):
        copy = pltpu.make_async_remote_copy(
            src_ref=held.at[i],
            dst_ref=arrived.at[i],
            send_sem=sems.at[0, i],
            recv_sem=sems.at[1, i],
            device_id=there,
            device_id_type=MESH,
        )
        copy.start()
        copy.wait()
        held[i + 1] = held[i] + arrived[i]
    total_ref[...] = held[len(plan)]


def sum_devices(value, axes):
    plan = [(axis, size, 1 << i) for axis, size in axes for i in range(size.bit_length() - 1)]
    spec = pl.BlockSpec(memory_space=pltpu.VMEM)
    return pl.pallas_call(
        functools.partial(sum_kernel, plan),
        in_specs=[spec],
        out_specs=spec,
        out_shape=jax.ShapeDtypeStruct(value.shape, value.dtype),
        scratch_shapes=[
            pltpu.VMEM((len(plan) + 1,) + value.shape, value.dtype),
            pltpu.VMEM((len(plan),) + value.shape, value.dtype),
            pltpu.SemaphoreType.DMA((2, len(plan))),
        ],
        compiler_params=pltpu.CompilerParams(collective_id=9, has_side_effects=True),
    )(value)


def on_device(
    residual_in,
    segments,
    routes,
    gates,
    attn_gain,
    q_proj,
    key_projection,
    value_projection,
    q_gain,
    k_gain,
    o_proj,
    mlp_gain,
    gate_proj,
    up_proj,
    down_proj,
    out_grad,
):
    bf16, f32 = jnp.bfloat16, jnp.float32
    n_seq, n_ctx, n_exp = lax.axis_size(SEQ), lax.axis_size(CTX), lax.axis_size(EXP)
    n_y = n_seq // 2
    devices = n_seq * n_ctx * n_exp
    core = lax.axis_index(SEQ) % 2
    span_index = lax.axis_index(CTX)
    z_index = lax.axis_index(EXP)
    group_all = [
        [(s * n_ctx + x) * n_exp + z for s in range(c, n_seq, 2) for x in range(n_ctx) for z in range(n_exp)]
        for c in range(2)
    ]
    group_plane = [[s * n_ctx + x for s in range(c, n_seq, 2) for x in range(n_ctx)] for c in range(2)]

    def swap(value):
        return lax.ppermute(value, SEQ, [(i, i ^ 1) for i in range(n_seq)])

    def across(value, step):
        return lax.ppermute(value, EXP, [(i, i ^ step) for i in range(n_exp)])

    token_count = residual_in.shape[1]
    model_width = residual_in.shape[2]
    sequence_length = segments.shape[1]
    route_count = routes.shape[2]
    local_experts = gate_proj.shape[0]
    expert_count = local_experts * n_exp
    half_experts = local_experts // 2
    capacity = token_count * route_count * 9 // (expert_count * 8)
    slots = -(-capacity // 16) * 16
    groups = KEY_VALUE_HEADS // 2
    heads = QUERY_HEADS // 2
    heads_per_group = QUERY_HEADS // KEY_VALUE_HEADS
    score_scale = HEAD_DIM ** (-0.5)
    rows = q_proj.shape[0]
    gain_rows = q_gain.shape[0]
    q_width, kv_width = heads * HEAD_DIM, groups * HEAD_DIM
    width = q_width + 2 * kv_width

    route_ids = routes[0]
    route_hit = route_ids[:, :, None] == jnp.arange(expert_count, dtype=jnp.int32)[None, None, :]
    hit_counts = route_hit.astype(jnp.int32).sum(1)
    earlier = jnp.cumsum(hit_counts, axis=0) - hit_counts
    slot_of = jnp.where(hit_counts > 0, earlier, -1).astype(f32)
    gate_of = jnp.sum(jnp.where(route_hit, gates[0][:, :, None], 0.0), axis=1)
    table = jnp.concatenate([slot_of.T, gate_of.T], 0)
    def gain_block(model_parts, head_parts, dtype):
        lead = model_parts[0].shape[:-1]
        fill = lambda size: jnp.zeros(lead + (1, size), dtype)
        first = jnp.concatenate([p[..., None, :] for p in model_parts] + [fill(128 - 2 * rows)], -1)
        second = jnp.concatenate(
            [p[..., None, :] for p in head_parts] + [fill(128 - 2 * gain_rows)], -1
        )
        return jnp.concatenate([first, second, jnp.zeros(lead + (rows - 2, 128), dtype)], -2)

    extra = gain_block([attn_gain, mlp_gain], [q_gain, k_gain], bf16)
    mine_cols, other_cols = [], []
    for weight in (q_proj, key_projection, value_projection):
        mine, other = column_halves(weight, core)
        mine_cols += mine
        other_cols += other
    mine_block = jnp.concatenate(mine_cols + [extra], 1)
    other_block = jnp.concatenate(other_cols + [extra], 1)
    chips = n_y * n_ctx
    own_links = n_y == 2 and n_ctx == 2 and n_exp == 4
    if own_links:
        halves = []
        for weight in (gate_proj, up_proj, down_proj):
            low, high = weight[:half_experts], weight[half_experts:]
            halves += [pick(core, low, high), pick(core, high, low)]
        w_gathered, w_out, gate_full, up_full, down_pair, cots_all, tables_all = gather_chips(
            mine_block,
            other_block,
            halves,
            o_proj.reshape(2, -1, model_width),
            out_grad[0],
            table,
            n_exp,
        )
        w_out = w_out.reshape(q_width, model_width)
        w_gathered = w_gathered.reshape(chips * n_exp, 2, rows, width + 128)
    else:
        theirs = swap(other_block)
        pair = jnp.stack([pick(core, mine_block, theirs), pick(core, theirs, mine_block)])
        w_gathered = lax.all_gather(
            pair, (SEQ, CTX, EXP), axis=0, tiled=False, axis_index_groups=group_all
        )
        cots_all, tables_all = exchange_column(out_grad[0], table, n_exp)
    w_extra = w_gathered[:, :, :2, width:].reshape(n_y, n_ctx * n_exp, 2, 2, 128)
    w_extra = w_extra.transpose(0, 2, 1, 3, 4).reshape(devices, 2, 128).astype(f32)
    gain_attn = w_extra[:, 0, :rows].reshape(model_width)
    gain_mlp_f = w_extra[:, 0, rows : 2 * rows].reshape(model_width)
    gain_query_f = w_extra[:, 1, :gain_rows].reshape(1, HEAD_DIM)
    gain_key_f = w_extra[:, 1, gain_rows : 2 * gain_rows].reshape(1, HEAD_DIM)

    if not own_links:
        w_out = lax.all_gather(
            o_proj, (SEQ, CTX, EXP), axis=0, tiled=True, axis_index_groups=group_all
        )

    def gather_expert(weight, after):
        if own_links:
            both = weight
        else:
            mine = pick(core, weight[:half_experts], weight[half_experts:])
            theirs = swap(pick(core, weight[half_experts:], weight[:half_experts]))
            both = jnp.stack([pick(core, mine, theirs), pick(core, theirs, mine)])
        both = lax.optimization_barrier((both, after))[0]
        full = lax.all_gather(
            both, (SEQ, CTX), axis=0, tiled=False, axis_index_groups=group_plane
        )
        full = full.reshape((n_y * n_ctx,) + both.shape)
        if own_links:
            return full
        full = full.reshape((n_y, n_ctx) + both.shape).transpose(3, 0, 2, 1, 4, 5)
        return full.reshape(1, 1, half_experts, -1, weight.shape[2])

    hidden = residual_in[0].astype(f32)
    seg_two = jnp.stack([segments[0], swap(segments)[0]])
    seg_here = lax.dynamic_slice_in_dim(seg_two, span_index * token_count, token_count, 1)
    valid_two = (seg_here > 0).astype(f32).reshape(2 * token_count, 1)
    valid_rows = valid_two[:token_count]
    positions = span_index * token_count + jnp.arange(token_count, dtype=jnp.int32)
    cos_one, sin_one = rope_tables(positions)
    half_dim = HEAD_DIM // 2
    signed_sine = jnp.concatenate([-sin_one[:, :half_dim], sin_one[:, half_dim:]], 1)
    info = jnp.zeros((2, 8, token_count), jnp.int32)
    info = info.at[:, 0].set(seg_here).at[:, 1].set(positions[None])
    seg_keys = seg_two[:, :, None]
    inv_attn = lax.rsqrt(jnp.mean(hidden * hidden, axis=-1, keepdims=True) + EPS)
    q_blocks = q_width // (2 * HEAD_DIM)
    kv_raw, kv_low, w_kv, normed_two = project_keys(
        residual_in[0],
        swap(residual_in[0]),
        gain_attn[None],
        w_gathered,
        q_blocks,
        gain_key_f,
        cos_one,
        signed_sine,
        n_y,
    )
    kv_here = kv_low.reshape(2, token_count, 2 * kv_width)
    if n_ctx == 2:
        kv_there = lax.ppermute(kv_here, CTX, [(0, 1), (1, 0)])
        kv_full = jnp.concatenate(
            [pick(span_index, kv_here, kv_there), pick(span_index, kv_there, kv_here)], 1
        )
    else:
        kv_full = lax.all_gather(kv_here, CTX, axis=1, tiled=True)
    moving = (gate_full, up_full, cots_all, tables_all) if own_links else ()
    q_raw, query_rows, w_query, *moving = project_queries(
        normed_two, w_gathered, q_blocks, gain_query_f, cos_one, signed_sine, n_y, n_exp, moving
    )
    mixed_low, recip, *moving = attend(
        info, seg_keys, query_rows, kv_full, groups, heads_per_group, n_exp, moving
    )
    if own_links:
        gate_full, up_full, cots_all, tables_all = moving
    else:
        gate_full, up_full = gather_expert(gate_proj, gain_attn), gather_expert(up_proj, gain_attn)
    down_full = gather_expert(
        down_pair if own_links else down_proj, query_rows if own_links else gain_attn
    )
    tables_all = lax.dynamic_update_slice(
        tables_all, table[None, None], (z_index, core, jnp.int32(0), jnp.int32(0))
    )
    attn_partial = jnp.dot(mixed_low, w_out, preferred_element_type=f32)
    attn_out = attn_partial[:token_count] + swap(attn_partial[token_count:])
    middle = hidden + attn_out
    inv_mlp = lax.rsqrt(jnp.mean(middle * middle, axis=-1, keepdims=True) + EPS)
    normed_mlp = (middle * inv_mlp * gain_mlp_f).astype(bf16)

    rows_all, grad_chip, out_chip, grad_into, out_into = run_experts(
        tables_all,
        normed_mlp,
        out_grad[0],
        cots_all,
        (gate_full, up_full, down_full),
        n_y if own_links else 1,
        local_experts,
        slots,
        n_exp,
    )

    if own_links:
        x_rows, val_rows, product_rows, gate_rows, up_rows = rows_all
        last, first_rows = n_exp - 1, 5 * token_count // 16
        blocks = []
        for i, (wide, sources) in enumerate(
            ((val_rows, (product_rows,)), (x_rows, (gate_rows, up_rows)))
        ):
            span = ((0, first_rows), (first_rows, token_count))[i]
            jobs = [(0, (last, last, last, *span)), (1, (last, last, 1, *span))]
            block, grad_into, out_into = part_weight_grads(
                wide, sources, grad_chip, grad_into, out_chip, out_into, jobs, 13 + i, n_y, n_ctx, n_exp
            )
            blocks.append(block)
    else:
        weight_blocks, grad_into, out_into = expert_weight_grads(
            rows_all, grad_chip, grad_into, out_chip, n_y, n_ctx, n_exp, merged=False
        )
    out_far = (out_chip[2:3].astype(f32) + out_into[3:4].astype(f32)).astype(bf16)

    def scatter_plane(blocks):
        return lax.psum_scatter(
            blocks.reshape((n_y * n_ctx,) + blocks.shape[2:]),
            (SEQ, CTX),
            scatter_dimension=0,
            tiled=True,
            axis_index_groups=group_plane,
        )[0]

    def all_experts(part):
        mine = pick(core, part[0], part[1])
        theirs = swap(pick(core, part[1], part[0]))
        axis = mine.ndim - 3
        both = [pick(core, mine, theirs), pick(core, theirs, mine)]
        return jnp.concatenate(both, axis).astype(f32)

    if own_links:
        parts = []
        for block in blocks:
            part = scatter_plane(block.reshape(n_y, n_ctx, -1, block.shape[-1]))
            parts.append(lax.optimization_barrier(part).reshape(block.shape[2:]))
    else:
        parts = [scatter_plane(weight_blocks[0])]
        for blocks in weight_blocks[1:]:
            blocks, parts[-1] = lax.optimization_barrier((blocks, parts[-1]))
            parts.append(scatter_plane(blocks))

    grad_normed_mlp = grad_chip[0].astype(f32)
    for step in range(1, n_exp):
        grad_normed_mlp = grad_normed_mlp + grad_into[step].astype(f32)
    cotangent = out_grad[0].astype(f32)
    mlp_gain_grad = jnp.sum(grad_normed_mlp * middle * inv_mlp, axis=0)
    grad_middle = cotangent + norm_back(grad_normed_mlp, middle, inv_mlp, gain_mlp_f)
    grad_attn_own = grad_middle.astype(bf16)
    grad_attn = jnp.concatenate([grad_attn_own, swap(grad_attn_own)], 0)
    part_rows = token_count // 4
    out_jobs, back_jobs = [(0, 2, 2, 0, part_rows)], [(0, 2, 2, part_rows, token_count)]
    last_jobs = [(1, 1, 1, 0, token_count)]
    o_grad_part, mixture_gradient, out_into = out_back(
        mixed_low, grad_attn, w_out, valid_two, out_far, out_into, out_jobs, n_exp
    )
    o_grad_plane = scatter_plane(o_grad_part.reshape(n_y, n_ctx, n_exp, -1, model_width))
    grad_q_raw, key_grad, value_grad, q_gain_rows, out_into = attend_back(
        info,
        seg_keys,
        query_rows,
        kv_full,
        mixed_low,
        mixture_gradient,
        recip,
        q_raw,
        gain_query_f,
        cos_one,
        signed_sine,
        groups,
        heads_per_group,
        out_far,
        out_into,
        back_jobs,
        n_exp,
    )
    q_gain_grad = q_gain_rows[0]
    if own_links:
        grad_kv, grad_hidden, attn_gain_grad, k_gain_rows, out_into = back_to_input(
            grad_q_raw,
            key_grad,
            value_grad,
            kv_raw,
            w_query,
            w_kv,
            gain_key_f,
            cos_one,
            signed_sine,
            residual_in[0],
            gain_attn[None],
            grad_middle,
            out_chip,
            out_into,
            last_jobs,
            n_exp,
        )
        k_gain_grad = k_gain_rows[0]
    else:
        kv_grad = jnp.concatenate([key_grad, value_grad], 2)
        query_part = contract_cols(grad_q_raw, w_query)
        kv_grad_here = lax.psum_scatter(
            kv_grad.astype(bf16), CTX, scatter_dimension=1, tiled=True
        ).astype(f32)
        kv_grad_here = kv_grad_here.reshape(2 * token_count, 2 * kv_width)
        cosine_table, sine_values = jnp.concatenate([cos_one] * 2, 0), jnp.concatenate([sin_one] * 2, 0)
        k_raw = kv_raw[:, :kv_width].reshape(-1, groups, HEAD_DIM)
        inv_key = lax.rsqrt(jnp.mean(k_raw * k_raw, axis=-1, keepdims=True) + EPS)
        grad_kn = inverse_rotation(
            kv_grad_here[:, :kv_width].reshape(-1, groups, HEAD_DIM), cosine_table, sine_values
        )
        k_gain_grad = jnp.sum(grad_kn * k_raw * inv_key, axis=(0, 1))
        grad_k_raw = norm_back(grad_kn, k_raw, inv_key, gain_key_f).astype(bf16)
        grad_kv = jnp.concatenate(
            [grad_k_raw.reshape(-1, kv_width), kv_grad_here[:, kv_width:].astype(bf16)], 1
        )
        normed_partial = query_part + contract_cols(grad_kv, w_kv)
        grad_normed = normed_partial[:token_count] + swap(normed_partial[token_count:])
        attn_gain_grad = jnp.sum(grad_normed * hidden * inv_attn, axis=0)
        grad_hidden = grad_middle + norm_back(grad_normed, hidden, inv_attn, gain_attn)

    extra_grad = gain_block(
        [attn_gain_grad.reshape(devices, rows), mlp_gain_grad.reshape(devices, rows)],
        [q_gain_grad.reshape(devices, gain_rows), k_gain_grad.reshape(devices, gain_rows)],
        f32,
    ).astype(bf16)
    if not own_links:
        near = across(out_chip[1], 1)
        out_into = lax.dynamic_update_slice(out_into, near[None], (1, 0, 0))
    expert_out = out_chip[0].astype(f32)
    for step in (1, 2):
        expert_out = expert_out + out_into[step].astype(f32)
    final_out = (middle + expert_out).astype(bf16)
    sums = [
        jnp.sum(value * value * valid_rows, keepdims=True) for value in (hidden, attn_out, expert_out)
    ]
    sums.append(jnp.sum(valid_rows, keepdims=True))
    stats = jnp.pad(jnp.concatenate(sums, 1), ((0, 7), (0, 124)))
    stats = sum_devices(stats, ((SEQ, n_seq), (CTX, n_ctx), (EXP, n_exp)))
    if own_links:
        extra_grad, o_grad_plane, parts, stats, final_out = lax.optimization_barrier(
            (extra_grad, o_grad_plane, parts, stats, final_out)
        )
    o_proj_grad = lax.psum_scatter(o_grad_plane, EXP, scatter_dimension=0, tiled=True)
    o_proj_grad = o_proj_grad[0].astype(f32)
    if own_links:
        grad_mine, grad_theirs = dense_grad_scatter(
            normed_two,
            grad_q_raw,
            grad_kv,
            extra_grad.reshape(n_y, 2, n_ctx, n_exp, rows, 128),
            n_exp,
        )
    else:
        w_grad = jnp.concatenate(
            [
                contract_rows(normed_two, grad_q_raw).astype(bf16),
                contract_rows(normed_two, grad_kv).astype(bf16),
                extra_grad.reshape(model_width, 128),
            ],
            1,
        )
        w_grad = w_grad.reshape(n_y, 2, n_ctx, n_exp, rows, width + 128).transpose(0, 2, 3, 1, 4, 5)
        w_grad = lax.psum_scatter(
            scatter_plane(w_grad), EXP, scatter_dimension=0, tiled=True
        )[0]
        grad_mine = pick(core, w_grad[0], w_grad[1])
        grad_theirs = swap(pick(core, w_grad[1], w_grad[0]))
    rms_stats = jnp.sqrt(stats[0, :3] / (stats[0, 3] * model_width))
    if own_links:
        part = all_experts(jnp.concatenate(parts[::-1], 1))
        gate_grad, up_grad = part[0].transpose(0, 2, 1), part[1].transpose(0, 2, 1)
        depth = part.shape[-1]
        down_grad = part[2].reshape(local_experts, model_width // depth, -1, depth)
        down_grad = down_grad.transpose(0, 2, 1, 3).reshape(local_experts, -1, model_width)
    else:
        gate_grad, up_grad = (all_experts(p).transpose(0, 2, 1) for p in parts[:2])
        down_grad = all_experts(parts[2])
    even = pick(core, grad_mine, grad_theirs).astype(f32)
    odd = pick(core, grad_theirs, grad_mine).astype(f32)

    def columns(start, size):
        step = size // groups
        parts = []
        for g in range(groups):
            parts += [half[:, start + g * step : start + (g + 1) * step] for half in (even, odd)]
        return jnp.concatenate(parts, 1)

    extra_total = even[:, width:] + odd[:, width:]
    return (
        final_out[None],
        grad_hidden.astype(bf16)[None],
        extra_total[0, :rows],
        columns(0, q_width),
        columns(q_width, kv_width),
        columns(q_width + kv_width, kv_width),
        extra_total[1, :gain_rows],
        extra_total[1, gain_rows : 2 * gain_rows],
        o_proj_grad,
        extra_total[0, rows : 2 * rows],
        gate_grad,
        up_grad,
        down_grad,
        rms_stats,
    )


def solution(mesh):
    in_specs = (
        P((SEQ, EXP), CTX, None),
        P((SEQ, EXP), None),
        P((SEQ, EXP), CTX, None),
        P((SEQ, EXP), CTX, None),
        P((SEQ, CTX, EXP)),
        P((SEQ, CTX, EXP), None),
        P((SEQ, CTX, EXP), None),
        P((SEQ, CTX, EXP), None),
        P((SEQ, CTX, EXP)),
        P((SEQ, CTX, EXP)),
        P((SEQ, CTX, EXP), None),
        P((SEQ, CTX, EXP)),
        P(EXP, (SEQ, CTX), None),
        P(EXP, (SEQ, CTX), None),
        P(EXP, (SEQ, CTX), None),
        P((SEQ, EXP), CTX, None),
    )
    out_specs = (
        P((SEQ, EXP), CTX, None),
        P((SEQ, EXP), CTX, None),
        P((SEQ, CTX, EXP)),
        P((SEQ, CTX, EXP), None),
        P((SEQ, CTX, EXP), None),
        P((SEQ, CTX, EXP), None),
        P((SEQ, CTX, EXP)),
        P((SEQ, CTX, EXP)),
        P((SEQ, CTX, EXP), None),
        P((SEQ, CTX, EXP)),
        P(EXP, (SEQ, CTX), None),
        P(EXP, (SEQ, CTX), None),
        P(EXP, (SEQ, CTX), None),
        P(),
    )
    return jax.shard_map(
        on_device, mesh=mesh, in_specs=in_specs, out_specs=out_specs, check_vma=False
    )
```

time: 1820 us -> 1170 us (0.64)
  waiting for transfers between devices: 547 us -> 8.21 us
  Pallas kernels: 821 us -> 1000 us
  starting transfers between devices: 113 us -> 3.34 us
  local copies, waits for them, and re-layouts: 120 us -> 43.8 us
  other arithmetic: 136 us -> 79.8 us
  matrix products: 55.3 us -> 10.6 us
    ppermute x42 -> x6, waiting for transfers between devices: 368 us -> 8.11 us  [the longest x5 8.11 us: swap(): return lax.ppermute(value, SEQ, [(i, i ^ 1) for i in range(n_seq)])]
    pallas_call x10, Pallas kernels: 542 us -> 716 us  [the longest x1 251 us: run_experts(): pl.pallas_call(functools.partial(moe_kernel, n_exp, n_y, local_experts),...]
    unnamed x13 -> x8, waiting for transfers between devices: 127 us -> 0.09 us
    ppermute x42 -> x6, starting transfers between devices: 113 us -> 2.61 us  [the longest x1 1.56 us: on_device(): kv_there = lax.ppermute(kv_here, CTX, [(0, 1), (1, 0)])]
    dot_general x4 -> x0, matrix products: 42.8 us -> none  [the longest x3 29 us: contract_cols(): lax.dot_general(first_op, second_op, (((1,), (1,)), ((), ())), preferred_...]
    reduce_scatter x1, waiting for transfers between devices: 42.3 us -> 0.01 us  [on_device(): lax.psum_scatter(o_grad_plane, EXP, scatter_dimension=0, tiled=True)]
    reshape x7 -> x1, local copies, waits for them, and re-layouts: 39 us -> 2.13 us  [on_device(): down_grad.transpose(0, 2, 1, 3).reshape(local_experts, -1, model_width)]
    scatter x12 -> x0, local copies, waits for them, and re-layouts: 21.5 us -> none  [the longest x1 6.18 us: on_device(): extra_grad.at[:, 0, rows:2 * rows].set(mlp_gain_grad.reshape(devices, rows))]
  transfers between devices with their start and end apart: 51 -> 11, of which waited for: 21 -> 2; matrix products, arithmetic and copies ran while one was open for 15% -> 9% of each run, Pallas kernels for 39% -> 62%
where the time goes in v3:
time: 1170 us
  Pallas kernels  1000 us (85%)
  other arithmetic  79.8 us (7%)
  local copies, waits for them, and re-layouts  43.8 us (4%)
  between operations  15.5 us (1%)
    pallas_call x1, Pallas kernels, run_experts(): pl.pallas_call(functools.partial(moe_kernel, n_exp, n_y, local_experts),...  251 us
    pallas_call x1, Pallas kernels, gather_chips(): pl.pallas_call(functools.partial(gather_kernel, n_exp), in_specs=[vmem_sp...  169 us
    pallas_call x1, Pallas kernels, dense_grad_scatter(): pl.pallas_call(functools.partial(scatter_kernel, n_exp), in_specs=[spec]...  119 us
    pallas_call x2, Pallas kernels, part_weight_grads(): pl.pallas_call(functools.partial(part_grad_kernel, n_y, n_ctx, n_exp, job...  106 us
    pallas_call x1, Pallas kernels, project_queries(): pl.pallas_call(functools.partial(query_kernel, n_y, n_exp if moving else...  90.9 us
    pallas_call x1, Pallas kernels, attend_back(): pl.pallas_call(functools.partial(attention_back_kernel, n_exp=n_exp, jobs...  73.3 us
    pallas_call x1, Pallas kernels, back_to_input(): pl.pallas_call(functools.partial(back_kernel, n_exp, jobs), in_specs=[vme...  72.7 us
    pallas_call x1, Pallas kernels, attend(): pl.pallas_call(functools.partial(attention_kernel, n_exp if moving else 0...  66.7 us
  transfers between devices with their start and end apart: 11, of which 2 were waited for; matrix products, arithmetic and copies ran while one was open for 9% of the time, Pallas kernels for 62%

profile of v3, /device:TPU:0, one launch (start us, length us, event | category | flops | bytes accessed | tf_op | source)
XLA Modules:
  0.0 1165.6 jit_solution(16475014144748612450)
XLA Ops:
  7.9 1.8 select_dynamic-update-slice_fusion.1
  9.7 1.7 select_dynamic-update-slice_fusion
  11.3 1.4 constant_dynamic-update-slice_fusion.9
  12.7 1.4 constant_dynamic-update-slice_fusion.8
  14.8 1.4 constant_dynamic-update-slice_fusion.6
  16.2 1.3 constant_dynamic-update-slice_fusion.1
  17.5 2.4 broadcast_select_fusion.5
  19.9 1.2 broadcast_select_fusion.7
  21.2 1.2 reduce-window.6
  23.6 1.5 broadcast_select_fusion.3
  25.1 1.1 copy-done.6
  26.2 1.1 copy-done.7
  27.4 1.1 copy-done.8
  28.5 1.0 copy-done.18
  29.5 169.3 %shard_map.263 = (bf16[4,4,2,64,2688]{4,3,2,1,0:T(8,128)(2,1)}, bf16[4,4,2,64,2048]{4,3,2,1,0:T(8,128)(2,1)}, bf16[4,2,2,256,768]{4,3,2,1,0:T(8,128)(2,1)S(1)}, ...) custom-call(bf16[64,2688]{1,0:T(8,128)(2,1)} %get-tuple-element.277., ...), custom_call_target="tpu_custom_call" | custom-call | tf_op jit(solution)/shard_map/pallas_call | solution.py:392
  198.9 2.7 copy-done.2
  201.6 2.6 copy-done.3
  205.0 0.8 slice.301
  207.3 1.0 fusion.8
  208.3 0.8 pad_maximum_fusion.4.cos_ref
  209.2 0.9 pad_maximum_fusion.5.sin_ref
  210.0 10.4 shard_map.264
  220.4 1.6 collective-permute-start.2
  223.8 90.9 %shard_map.265 = (f32[1024,2048]{1,0:T(8,128)}, bf16[1024,2048]{1,0:T(8,128)(2,1)}, bf16[2048,2048]{1,0:T(8,128)(2,1)}, bf16[4,2,2,256,768]{4,3,2,1,0:T(8,128)(2...) custom-call(bf16[1024,2048]{1,0:T(8,128)(2,1)} %get-tuple-element.10, ...), custom_call_target="tpu_custom_call", output_to_operand_aliasing={{3}: (5, {}), {4}: (6, {}), {5}: (7, {}), {6}: (8, {})} | custom-call | flops 8589934592 | bytes 33554432 | tf_op jit(solution)/shard_map/pallas_call | solution.py:1017
  315.3 1.4 broadcast_select_fusion.2
  316.9 66.7 %shard_map.266 = (bf16[1024,2048]{1,0:T(8,128)(2,1)}, f32[32,1,512]{2,1,0:T(1,128)S(1)}, bf16[4,2,2,256,768]{4,3,2,1,0:T(8,128)(2,1)}, bf16[4,2,2,256,768]{4,3,2...) custom-call(s32[2,8,512]{2,1,0:T(8,128)S(1)} %scatter.9.info_ref, ...), custom_call_target="tpu_custom_call", output_to_operand_aliasing={{2}: (5, {}), {3}: (6, {}), {4}: (7, {}), {5}: (8, {})} | custom-call | flops 17179869184 | bytes 10485760 | tf_op jit(solution)/shard_map/pallas_call | solution.py:1115
  383.6 10.6 fusion.24
  394.2 2.4 slice.306
  396.6 2.1 copy-done.27
  399.2 7.0 collective-permute-done.3
  406.3 4.8 multiply_reduce_fusion.2
  411.7 1.4 copy-done.24
  413.0 1.7 multiply_convert_fusion.own_ref
  414.8 250.5 %shard_map.267 = (bf16[2,2304,2048]{2,1,0:T(8,128)(2,1)}, bf16[2,2304,2048]{2,1,0:T(8,128)(2,1)}, bf16[2,2304,768]{2,1,0:T(8,128)(2,1)}, bf16[2,2304,768]{2,1,0:...) custom-call(f32[4,2,32,512]{3,2,1,0:T(8,128)} %copy-done.17, ...), custom_call_target="tpu_custom_call" | custom-call | flops 125627793408 | bytes 96731136 | tf_op jit(solution)/shard_map/pallas_call | solution.py:1514
  665.3 35.8 %shard_map.268 = (bf16[2,2,2,1,2,768,256]{6,5,4,3,2,1,0:T(8,128)(2,1)}, bf16[4,512,2048]{2,1,0:T(8,128)(2,1)}, bf16[4,512,2048]{2,1,0:T(8,128)(2,1)}) custom-call(bf16[2,2304,2048]{2,1,0:T(8,128)(2,1)} %get-tuple-element.123.wide_ref, bf16[2,2304,768]{2,1,0:T(8,128)(2,1)} %get-tuple-element.124.refs_0_, ...), custom_call_target="tpu_custom_call", output_to_operand_aliasing={{1}: (3, {}), {2}: (5, {})} | custom-call | flops 14495514624 | bytes 32243712 | tf_op jit(solution)/shard_map/pallas_call | solution.py:1714
  701.2 70.6 %shard_map.269 = (bf16[2,2,2,2,2,768,256]{6,5,4,3,2,1,0:T(8,128)(2,1)}, bf16[4,512,2048]{2,1,0:T(8,128)(2,1)}, bf16[4,512,2048]{2,1,0:T(8,128)(2,1)}) custom-call(bf16[2,2304,2048]{2,1,0:T(8,128)(2,1)} %get-tuple-element.120.wide_ref, bf16[2,2304,768]{2,1,0:T(8,128)(2,1)} %get-tuple-element.121.refs_0_, ...), custom_call_target="tpu_custom_call", output_to_operand_aliasing={{1}: (4, {}), {2}: (6, {})} | custom-call | flops 28991029248 | bytes 45613056 | tf_op jit(solution)/shard_map/pallas_call | solution.py:1714
  772.4 5.9 fusion.6
  778.9 7.3 fusion.16
  786.4 3.1 add_convert_fusion.chip_ref
  789.6 1.1 collective-permute-done.4
  790.7 5.9 pad_maximum_fusion.grad_ref
  796.6 30.0 %shard_map.270 = (bf16[2048,2048]{1,0:T(8,128)(2,1)}, bf16[1024,2048]{1,0:T(8,128)(2,1)S(1)}, bf16[4,512,2048]{2,1,0:T(8,128)(2,1)}) custom-call(bf16[1024,2048]{1,0:T(8,128)(2,1)S(1)} %copy-done.22, bf16[1024,2048]{1,0:T(8,128)(2,1)} %pad_maximum_fusion.grad_ref, bf16[2048,2048]{1,0:T(8,128)(2,1)} %bitcast.172, ...), custom_call_target="tpu_custom_call", output_to_operand_aliasing={{2}: (5, {})} | custom-call | flops 17179869184 | bytes 25165824 | tf_op jit(solution)/shard_map/pallas_call | solution.py:825
  826.7 1.9 copy-done.23
  830.0 73.3 %shard_map.271 = (bf16[1024,2048]{1,0:T(8,128)(2,1)}, f32[2,1024,256]{2,1,0:T(8,128)S(1)}, f32[2,1024,256]{2,1,0:T(8,128)S(1)}, f32[8,128]{1,0:T(8,128)S(1)}, bf16[4,512,2048]{2,1,0:T(8,128)(2,1)}) custom-call(s32[2,8,512]{2,1,0:T(8,128)S(1)} %copy-done.20, s32[2,1024,1]{2,1,0:T(8,128)S(1)} %copy-done.14, ...), custom_call_target="tpu_custom_call", output_to_operand_aliasing={{4}: (13, {})} | custom-call | flops 42949672960 | bytes 31457280 | tf_op jit(solution)/shard_map/pallas_call | solution.py:1257
  903.3 1.3 copy-done.10
  904.7 1.3 copy-done.11
  906.0 72.7 %shard_map.272 = (bf16[1024,512]{1,0:T(8,128)(2,1)}, bf16[512,2048]{1,0:T(8,128)(2,1)}, f32[1,2048]{1,0:T(1,128)}, f32[8,128]{1,0:T(8,128)}, bf16[4,512,2048]{2,1,0:T(8,128)(2,1)}) custom-call(bf16[1024,2048]{1,0:T(8,128)(2,1)} %get-tuple-element.136.query_grad_ref.grad_ref, f32[2,1024,256]{2,1,0:T(8,128)} %copy-done.10, ...), custom_call_target="tpu_custom_call", output_to_operand_aliasing={{4}: (13, {})} | custom-call | flops 10737418240 | bytes 50331648 | tf_op jit(solution)/shard_map/pallas_call | solution.py:758
  978.7 10.5 fusion.1
  989.2 3.3 select_maximum_fusion.value_ref
  992.5 14.7 %shard_map.273 = f32[8,128]{1,0:T(8,128)} custom-call(f32[8,128]{1,0:T(8,128)} %select_maximum_fusion.value_ref), custom_call_target="tpu_custom_call" | custom-call | tf_op jit(solution)/shard_map/pallas_call | solution.py:1765
  1007.7 1.0 maximum_maximum_fusion
  1008.8 2.6 select_bitcast_fusion
  1011.4 119.4 %shard_map.274 = (f32[64,2688]{1,0:T(8,128)}, f32[64,2688]{1,0:T(8,128)}) custom-call(bf16[1024,2048]{1,0:T(8,128)(2,1)} %get-tuple-element.100.normed_ref, bf16[1024,2048]{1,0:T(8,128)(2,1)} %get-tuple-element.136.query_grad_ref.grad_ref, bf16[1024,512]{1,0:T(8,128)(2,1)} %get-tuple-element.152.kv_grad_ref, bf16[2,2,2,4,64,128]{5,4,3,2,1,0:T(8,128)(2,1)} %bitcast.157), custom_call_target="tpu_custom_call" | custom-call | flops 11274289152 | bytes 16777216 | tf_op jit(solution)/shard_map/pallas_call | solution.py:595
  1130.9 1.6 broadcast_select_fusion.10
  1132.5 1.5 slice.299
  1136.0 1.2 sqrt_bitcast_fusion
  1138.5 1.1 pad_maximum_fusion.3
  1139.5 2.9 bitcast_select_fusion.1
  1143.0 2.5 fusion.17
  1145.5 2.1 copy.113
  1147.6 3.5 copy.109
  1151.2 2.4 copy.110
  1153.5 2.1 bitcast_convert_fusion
  1155.6 3.2 copy.148
  (179 shorter events, 15.3 us)
Async XLA Ops:
  7.2 14.0 %copy-start.35 = (s32[1,512,8]{1,2,0:T(8,128)S(1)}, s32[1,512,8]{1,2,0:T(8,128)}, u32[]{:S(2)}) copy-start(s32[1,512,8]{1,2,0:T(8,128)} %param.22) | copy-start | bytes 49156
  7.2 15.5 %copy-start.40 = (f32[1,512,8]{1,2,0:T(8,128)S(1)}, f32[1,512,8]{1,2,0:T(8,128)}, u32[]{:S(2)}) copy-start(f32[1,512,8]{1,2,0:T(8,128)} %param.23) | copy-start | bytes 49156
  7.2 15.7 %copy-start.51 = (bf16[64]{0:T(256)(128)(2,1)S(1)}, bf16[64]{0:T(256)(128)(2,1)}, u32[]{:S(2)}) copy-start(bf16[64]{0:T(256)(128)(2,1)} %param.24) | copy-start | bytes 388
  7.2 15.7 %copy-start.50 = (bf16[64]{0:T(256)(128)(2,1)S(1)}, bf16[64]{0:T(256)(128)(2,1)}, u32[]{:S(2)}) copy-start(bf16[64]{0:T(256)(128)(2,1)} %param.31) | copy-start | bytes 388
  7.2 15.7 %copy-start.49 = (bf16[4]{0:T(256)(128)(2,1)S(1)}, bf16[4]{0:T(256)(128)(2,1)}, u32[]{:S(2)}) copy-start(bf16[4]{0:T(256)(128)(2,1)} %param.28) | copy-start | bytes 28
  7.2 15.7 %copy-start.48 = (bf16[4]{0:T(256)(128)(2,1)S(1)}, bf16[4]{0:T(256)(128)(2,1)}, u32[]{:S(2)}) copy-start(bf16[4]{0:T(256)(128)(2,1)} %param.29) | copy-start | bytes 28
  7.2 407.5 %all-gather.3.cloned.1.call-start = ((), (), s32[]{:S(2)}) async-start(), calls=%async_computation.5 | async-start | bytes 7864320 | tf_op jit(solution)/shard_map/all_gather | solution.py:1903
  7.3 202.7 %collective-permute-start.1 = (bf16[512,2048]{1,0:T(8,128)(2,1)}, bf16[512,2048]{1,0:T(8,128)(2,1)}, u32[]{:S(2)}, u32[]{:S(2)}) collective-permute-start(bf16[512,2048]{1,0:T(8,128)(2,1)} %bitcast.140), channel_id=1, source_target_pairs={{0,8},{8,0},{16,24},{24,16},{1,9},{9,1},{17,25},{25,17},{2,10},{10... | collective-permute-start | bytes 6291464 | tf_op jit(solution)/shard_map/ppermute | solution.py:1811
  7.8 214.8 %collective-permute-start = (s32[1,1024]{1,0:T(1,128)}, s32[1,1024]{1,0:T(1,128)S(1)}, u32[]{:S(2)}, u32[]{:S(2)}) collective-permute-start(s32[1,1024]{1,0:T(1,128)} %param.21), channel_id=1, source_target_pairs={{0,8},{8,0},{16,24},{24,16},{1,9},{9,1},{17,25},{25,17},{2,10},{10... | collective-permute-start | bytes 12296 | tf_op jit(solution)/shard_map/ppermute | solution.py:1811
  7.9 12.0 %copy-start.30 = (bf16[4,256,768]{2,1,0:T(8,128)(2,1)S(1)}, bf16[4,256,768]{2,1,0:T(8,128)(2,1)}, u32[]{:S(2)}) copy-start(bf16[4,256,768]{2,1,0:T(8,128)(2,1)} %param.32) | copy-start | bytes 4718596
  19.9 5.2 copy-start
  22.8 176.0 %copy-start.46 = (bf16[64]{0:T(256)(128)(2,1)}, bf16[64]{0:T(256)(128)(2,1)S(1)}, u32[]{:S(2)}) copy-start(bf16[64]{0:T(256)(128)(2,1)S(1)} %pad.58.clone) | copy-start | bytes 388
  25.1 1.1 copy-start.6
  26.2 1.1 copy-start.7
  27.4 1.1 copy-start.8
  28.5 1.0 copy-start.18
  198.9 2.7 copy-start.2
  201.6 2.6 copy-start.3
  204.2 0.8 copy-start.15
  210.0 12.6 %copy-start.41 = (s32[1,1024]{1,0:T(1,128)S(1)}, s32[1,1024]{1,0:T(1,128)}, u32[]{:S(2)}) copy-start(s32[1,1024]{1,0:T(1,128)} %param.21) | copy-start | bytes 12292
  220.4 94.9 %collective-permute-start.2 = (bf16[2,512,512]{2,1,0:T(8,128)(2,1)}, bf16[2,512,512]{2,1,0:T(8,128)(2,1)}, u32[]{:S(2)}, u32[]{:S(2)}) collective-permute-start(bf16[2,512,512]{2,1,0:T(8,128)(2,1)} %bitcast.155), channel_id=1, source_target_pairs={{0,4},{4,0},{1,5},{5,1},{2,6},{6,2},{3,7},{7,3},{8,12},{12,8},{9,1... | collective-permute-start | bytes 3145736 | tf_op jit(solution)/shard_map/ppermute | solution.py:1939
  223.3 91.4 %copy-start.36 = (s32[2,512]{1,0:T(2,128)}, s32[2,512]{1,0:T(2,128)S(1)}, u32[]{:S(2)}) copy-start(s32[2,512]{1,0:T(2,128)S(1)} %get-tuple-element.222) | copy-start | bytes 12292
  223.7 93.2 %copy-start.13 = (s32[2,1024,1]{2,1,0:T(8,128)}, s32[2,1024,1]{2,1,0:T(8,128)S(1)}, u32[]{:S(2)}) copy-start(s32[2,1024,1]{2,1,0:T(8,128)S(1)} %copy.103.seg_ref) | copy-start | bytes 24580
  223.8 93.1 %copy-start.19 = (s32[2,8,512]{2,1,0:T(8,128)}, s32[2,8,512]{2,1,0:T(8,128)S(1)}, u32[]{:S(2)}) copy-start(s32[2,8,512]{2,1,0:T(8,128)S(1)} %scatter.9.info_ref) | copy-start | bytes 98308
  223.8 91.5 %copy-start.31 = (bf16[1024,512]{1,0:T(8,128)(2,1)S(1)}, bf16[1024,512]{1,0:T(8,128)(2,1)}, u32[]{:S(2)}) copy-start(bf16[1024,512]{1,0:T(8,128)(2,1)} %get-tuple-element.106) | copy-start | bytes 3145732
  314.7 2.2 copy-start.16
  314.7 694.1 %reduce-scatter.15.cloned.1.call-start = ((), (), s32[]{:S(2)}) async-start(), calls=%async_computation.7 | async-start | bytes 7864320
  316.7 66.9 %slice-start = ((s8[8388608]{0:T(1024)(128)(4,1)}), s8[4194304]{0:T(1024)(128)(4,1)S(1)}, s32[]{:S(2)}) async-start(s8[8388608]{0:T(1024)(128)(4,1)} %bitcast.173), calls=%async_computation.9 | async-start | bytes 8388608
  316.8 66.8 %copy-start.12 = (bf16[2,1024,512]{2,1,0:T(8,128)(2,1)}, bf16[2,1024,512]{2,1,0:T(8,128)(2,1)S(1)}, u32[]{:S(2)}) copy-start(bf16[2,1024,512]{2,1,0:T(8,128)(2,1)S(1)} %pad_maximum_fusion.2.k_ref.v_ref) | copy-start | bytes 6291460
  316.9 66.7 %slice-start.1 = ((s8[8388608]{0:T(1024)(128)(4,1)}), s8[4194304]{0:T(1024)(128)(4,1)S(1)}, s32[]{:S(2)}) async-start(s8[8388608]{0:T(1024)(128)(4,1)} %bitcast.173), calls=%async_computation.10 | async-start | bytes 8388608
  394.2 4.5 copy-start.27
  398.8 7.5 collective-permute-start.3
  399.2 12.5 %copy-start.32 = (f32[2048]{0:T(1024)}, f32[2048]{0:T(1024)S(1)}, u32[]{:S(2)}) copy-start(f32[2048]{0:T(1024)S(1)} %mul.125) | copy-start | bytes 24580
  399.2 11.9 %copy-start.17 = (f32[4,2,32,512]{3,2,1,0:T(8,128)}, f32[4,2,32,512]{3,2,1,0:T(8,128)S(1)}, u32[]{:S(2)}) copy-start(f32[4,2,32,512]{3,2,1,0:T(8,128)S(1)} %bitcast_dynamic-update-slice_fusion.table_ref) | copy-start | bytes 1572868
  411.1 2.0 copy-start.24
  411.7 3.1 copy-start.38
  701.1 307.7 %reduce-scatter.17.cloned.1.call-start = ((), (), s32[]{:S(2)}) async-start(), calls=%async_computation.8 | async-start | bytes 15728640
  771.7 0.7 copy-start.33
  771.7 0.7 copy-start.39
  771.8 237.0 %reduce-scatter.13.cloned.1.call-start = ((), (), s32[]{:S(2)}) async-start(), calls=%async_computation.6 | async-start | bytes 10485760
  772.4 5.9 copy-start.1
  772.4 6.5 copy-start.25
  772.4 6.5 copy-start.43
  778.9 7.3 copy-start.37
  786.2 4.5 collective-permute-start.4
  789.6 7.0 copy-start.9
  789.6 7.0 copy-start.22
  826.7 1.9 copy-start.23
  828.6 1.4 copy-start.4
  828.6 1.4 copy-start.5
  828.6 1.4 copy-start.14
  828.6 1.4 copy-start.20
  828.6 1.4 copy-start.21
  828.7 324.9 %reduce-scatter.11.cloned.1.call-start = ((), (), s32[]{:S(2)}) async-start(), calls=%async_computation.4 | async-start | bytes 2621440 | tf_op jit(solution)/shard_map/reduce_scatter | solution.py:2126
  903.3 1.3 copy-start.10
  904.6 1.3 copy-start.11
  906.0 72.7 %copy-start.26 = (bf16[1,512,2048]{2,1,0:T(8,128)(2,1)S(1)}, bf16[1,512,2048]{2,1,0:T(8,128)(2,1)}, u32[]{:S(2)}) copy-start(bf16[1,512,2048]{2,1,0:T(8,128)(2,1)} %param.20) | copy-start | bytes 6291460
  978.7 28.5 %copy-start.44 = (f32[1,2048]{1,0:T(1,128)S(1)}, f32[1,2048]{1,0:T(1,128)}, u32[]{:S(2)}) copy-start(f32[1,2048]{1,0:T(1,128)} %get-tuple-element.143) | copy-start | bytes 24580
  978.7 28.8 %copy-start.45 = (f32[8,128]{1,0:T(8,128)S(1)}, f32[8,128]{1,0:T(8,128)}, u32[]{:S(2)}) copy-start(f32[8,128]{1,0:T(8,128)} %get-tuple-element.145) | copy-start | bytes 12292
  978.7 29.0 %copy-start.34 = (bf16[64,128]{1,0:T(8,128)(2,1)S(1)}, bf16[64,128]{1,0:T(8,128)(2,1)}, u32[]{:S(2)}) copy-start(bf16[64,128]{1,0:T(8,128)(2,1)} %get-tuple-element.283) | copy-start | bytes 49156
  978.7 29.0 %copy-start.47 = (bf16[64]{0:T(256)(128)(2,1)S(1)}, bf16[64]{0:T(256)(128)(2,1)}, u32[]{:S(2)}) copy-start(bf16[64]{0:T(256)(128)(2,1)} %copy-done.46) | copy-start | bytes 388
  1011.3 128.2 %collective-permute-start.5 = (bf16[3,2,768,256]{3,2,1,0:T(8,128)(2,1)S(1)}, bf16[3,2,768,256]{3,2,1,0:T(8,128)(2,1)}, u32[]{:S(2)}, u32[]{:S(2)}) collective-permute-start(bf16[3,2,768,256]{3,2,1,0:T(8,128)(2,1)S(1)} %select_bitcast_fusion), channel_id=1, source_target_pairs={{0,8},{8,0},{16,24},{24,16},{1,9},{9,1},{17,25},{25,17},{2,10},{10... | collective-permute-start | bytes 7077896 | tf_op jit(solution)/shard_map/ppermute | solution.py:1811
  1130.9 8.7 copy-start.28
  1130.9 8.6 copy-start.29
  (1 other events, 0.7 us)
Sparse Core Ops, SparseCore 0:
  314.8 91.4 all-gather.2
  701.2 69.5 reduce-scatter.14
  773.9 120.7 reduce-scatter.16
  897.6 108.8 reduce-scatter.12
  1011.6 42.5 reduce-scatter.10

commit v4 on v3

--- a/solution.py
+++ b/solution.py
@@ -220,6 +220,21 @@
     pl.semaphore_wait(barrier, len(slots))
 
 
+def store_table(routes_ref, gates_ref, table_ref):
+    f32, bf16 = jnp.float32, jnp.bfloat16
+    experts, tokens = table_ref.shape[0] // 2, table_ref.shape[1]
+    expert_ids = lax.broadcasted_iota(jnp.int32, (experts, tokens), 0)
+    hits, gates = jnp.zeros((experts, tokens), f32), jnp.zeros((experts, tokens), f32)
+    for k in range(routes_ref.shape[0]):
+        named = routes_ref[k : k + 1] == expert_ids
+        hits = hits + named.astype(f32)
+        gates = gates + jnp.where(named, gates_ref[k : k + 1], 0.0)
+    row = lax.broadcasted_iota(jnp.int32, (tokens, tokens), 0)
+    before = (row < lax.broadcasted_iota(jnp.int32, (tokens, tokens), 1)).astype(f32).astype(bf16)
+    table_ref[:experts] = jnp.where(hits > 0.0, dot_plain(hits.astype(bf16), before), -1.0)
+    table_ref[experts:] = gates
+
+
 def gather_kernel(
     n_exp,
     mine_ref,
@@ -231,8 +246,9 @@
     down_ref,
     other_down_ref,
     out_ref,
+    routes_ref,
+    gates_ref,
     cot_ref,
-    table_ref,
     full_ref,
     out_full_ref,
     gate_full_ref,
@@ -248,6 +264,9 @@
     xf_sems,
     yf_sems,
     column_sem,
+    first_sems,
+    line_sems,
+    table_ref,
 ):
     column = Column(n_exp, (cots_ref, tables_ref), column_sem, (cot_ref, table_ref))
     x, y, z, core, ids = neighbours(n_exp)
@@ -258,6 +277,8 @@
 
     def act(method, place, sems, slot, name):
         for which, full in enumerate(fulls):
+            if which and len(place) == 2:
+                place = (*place, pl.ds(0, 2))
             part = full.at[place]
             copy = pltpu.make_async_remote_copy(
                 src_ref=part,
@@ -268,6 +289,48 @@
                 device_id_type=MESH,
             )
             getattr(copy, method)()
+
+    def moved(method, place, sems, slot, name):
+        part = out_full_ref.at[place]
+        copy = pltpu.make_async_remote_copy(
+            src_ref=part,
+            dst_ref=part,
+            send_sem=sems.at[(0, *slot)],
+            recv_sem=sems.at[(1, *slot)],
+            device_id=ids[name],
+            device_id_type=MESH,
+        )
+        getattr(copy, method)()
+
+    def first_near(method):
+        for slot, name in enumerate((X, Y)):
+            moved(method, (here, z, pl.ds(2, 2)), first_sems, (slot,), name)
+
+    def first_far(method):
+        moved(method, (beside, z, 2), first_sems, (2,), Y)
+        moved(method, (across, z, 3), first_sems, (3,), X)
+
+    def line(hop, method):
+        for lane, name, part, there in (
+            (0, UP, z - hop + 1, (z >= hop - 1) & (z < n_exp - 1)),
+            (1, DOWN, z + hop - 1, (z + hop - 1 < n_exp) & (z > 0)),
+        ):
+            pl.when(there)(
+                lambda lane=lane, name=name, part=part: moved(
+                    method, (slice(None), part, pl.ds(2, 2)), line_sems, (lane, part), name
+                )
+            )
+
+    def line_arrivals(hop):
+        for lane, name, part, there in (
+            (0, UP, z - hop, z >= hop),
+            (1, DOWN, z + hop, z + hop < n_exp),
+        ):
+            pl.when(there)(
+                lambda lane=lane, name=name, part=part: moved(
+                    WAIT_RECV, (slice(None), part, pl.ds(2, 2)), line_sems, (lane, part), name
+                )
+            )
 
     places = (
         full_ref.at[here, z, core],
@@ -293,6 +356,10 @@
     ]
     for copy in kept + to_core:
         copy.start()
+    store_table(routes_ref, gates_ref, table_ref)
+    kept_table = pltpu.make_async_copy(table_ref, tables_ref.at[z, core], local_sems.at[5])
+    kept_table.start()
+    kept.append(kept_table)
     to_core[0].wait()
     kept[0].wait()
     kept[1].wait()
@@ -352,17 +419,32 @@
 
         guarded(there, action)
 
+    first_near(START)
     spread(0)
     for hop in range(1, n_exp):
         for label in (2 * hop - 1, 2 * hop):
             z_arrival(label)
             spread(label)
+        if hop == 1:
+            first_near(WAIT_RECV)
+            first_far(START)
         if hop == n_exp - 1:
-            column.sends(1, START)
+            first_far(WAIT_RECV)
+            line(1, START)
         for label in (0,) if hop == 1 else (2 * hop - 3, 2 * hop - 2):
             turn(label)
+    line_arrivals(1)
+    line(2, START)
     for label in (2 * n_exp - 3, 2 * n_exp - 2):
         turn(label)
+    for hop in range(2, n_exp):
+        line_arrivals(hop)
+        if hop < n_exp - 1:
+            line(hop + 1, START)
+    first_near(WAIT_SEND)
+    first_far(WAIT_SEND)
+    for hop in range(1, n_exp):
+        line(hop, WAIT_SEND)
     opposite = 2 * (1 - y) + 1 - x
     for label in labels:
         part, there = source(label)
@@ -377,21 +459,19 @@
 
         guarded(there, action)
         z_sends(label, WAIT_SEND)
-    column.arrivals(1)
-    column.sends(1, WAIT_SEND)
     column.pass_own(WAIT)
     for copy in kept[2:] + to_core[1:]:
         copy.wait()
 
 
-def gather_chips(mine, other, halves, out, cot, table, n_exp):
+def gather_chips(mine, other, halves, out, routes, gates, cot, experts, n_exp):
     labels = 2 * n_exp - 1
     any_spec = pl.BlockSpec(memory_space=pl.ANY)
     vmem_spec = pl.BlockSpec(memory_space=pltpu.VMEM)
     pair = lambda count: pltpu.SemaphoreType.DMA((2, 2, count))
     return pl.pallas_call(
         functools.partial(gather_kernel, n_exp),
-        in_specs=[vmem_spec] * 9 + [any_spec, any_spec],
+        in_specs=[vmem_spec] * 11 + [any_spec],
         out_specs=[any_spec] * 7,
         out_shape=[
             jax.ShapeDtypeStruct((4, n_exp, 2) + mine.shape, mine.dtype),
@@ -399,9 +479,12 @@
         ]
         + [jax.ShapeDtypeStruct((4, 2) + a.shape, a.dtype) for a in halves[:4:2]]
         + [jax.ShapeDtypeStruct((2,) + halves[4].shape, halves[4].dtype)]
-        + [jax.ShapeDtypeStruct((n_exp, 2) + a.shape, a.dtype) for a in (cot, table)],
+        + [
+            jax.ShapeDtypeStruct((n_exp, 2) + cot.shape, cot.dtype),
+            jax.ShapeDtypeStruct((n_exp, 2, 2 * experts, cot.shape[0]), jnp.float32),
+        ],
         scratch_shapes=[
-            pltpu.SemaphoreType.DMA((5,)),
+            pltpu.SemaphoreType.DMA((6,)),
             pltpu.SemaphoreType.DMA((2, 4)),
             pair(2 * n_exp),
             pair(labels),
@@ -409,11 +492,14 @@
             pair(labels),
             pair(labels),
             column_sems(2, n_exp),
+            pltpu.SemaphoreType.DMA((2, 4)),
+            pltpu.SemaphoreType.DMA((2, 2, n_exp)),
+            pltpu.VMEM((2 * experts, cot.shape[0]), jnp.float32),
         ],
         compiler_params=pltpu.CompilerParams(
             collective_id=1, has_side_effects=True, vmem_limit_bytes=32 * MIB
         ),
-    )(mine, other, *halves, out, cot, table)
+    )(mine, other, *halves, out, routes, gates, cot)
 
 
 def exchange_kernel(n_exp, first_ref, second_ref, firsts_ref, seconds_ref, sems):
@@ -451,13 +537,14 @@
 
 def scatter_kernel(
     n_exp,
-    normed_ref,
+    turned,
     grad_ref,
     kv_grad_ref,
     extra_ref,
+    stats_ref,
     mine_ref,
     theirs_ref,
-    turned,
+    stats_sum_ref,
     part,
     from_x,
     from_y,
@@ -472,6 +559,9 @@
     y2_sems,
     z_sems,
     core_sems,
+    held,
+    arrived,
+    stat_sems,
 ):
     bf16, f32 = jnp.bfloat16, jnp.float32
     x, y, z, core, ids = neighbours(n_exp)
@@ -491,9 +581,23 @@
             device_id_type=MESH,
         )
 
+    rounds = [ids[CORE], ids[Y], ids[X]]
+    rounds += [{EXP: xor_chip(z, 1 << i, n_exp)} for i in range(n_exp.bit_length() - 1)]
+    held[0] = stats_ref[...]
+
+    def stat_copy(i):
+        return remote(held.at[i], arrived.at[i], stat_sems, i, rounds[i])
+
+    def stat_round(i):
+        if i:
+            stat_copy(i - 1).wait()
+            held[i] = held[i - 1] + arrived[i - 1]
+        if i < len(rounds):
+            stat_copy(i).start()
+
+    stat_round(0)
     rows = mine_ref.shape[0]
     q_width, width = grad_ref.shape[1], grad_ref.shape[1] + kv_grad_ref.shape[1]
-    turned[...] = normed_ref[...].T
     steps = range(n_exp)
 
     def first_copies(k):
@@ -563,12 +667,16 @@
             z_copy(k).start()
 
     for k in steps:
+        stat_round(k + 1)
         second(k)
         if k + 2 < n_exp:
             launch(k + 2)
         if k:
             third(k - 1)
     third(n_exp - 1)
+    for i in range(n_exp + 1, len(rounds) + 1):
+        stat_round(i)
+    stats_sum_ref[...] = held[len(rounds)]
     result = total[n_exp - 1].astype(f32)
     for k in range(n_exp - 1):
         z_copy(k).wait_recv()
@@ -584,9 +692,9 @@
     theirs_ref[...] = from_core[...].astype(f32)
 
 
-def dense_grad_scatter(normed, grad, kv_grad, extra, n_exp):
+def dense_grad_scatter(turned, grad, kv_grad, extra, stats, n_exp):
     bf16 = jnp.bfloat16
-    rows, model = extra.shape[4], normed.shape[1]
+    rows, model = extra.shape[4], turned.shape[0]
     width = grad.shape[1] + kv_grad.shape[1] + extra.shape[5]
     block = (rows, width)
     vmem = lambda *lead: pltpu.VMEM(lead + block, bf16)
@@ -594,11 +702,11 @@
     spec = pl.BlockSpec(memory_space=pltpu.VMEM)
     return pl.pallas_call(
         functools.partial(scatter_kernel, n_exp),
-        in_specs=[spec] * 4,
-        out_specs=[spec] * 2,
-        out_shape=[jax.ShapeDtypeStruct(block, jnp.float32)] * 2,
+        in_specs=[spec] * 5,
+        out_specs=[spec] * 3,
+        out_shape=[jax.ShapeDtypeStruct(block, jnp.float32)] * 2
+        + [jax.ShapeDtypeStruct(stats.shape, stats.dtype)],
         scratch_shapes=[
-            pltpu.VMEM((model, normed.shape[0]), bf16),
             vmem(n_exp, 2, 2, 2),
             vmem(n_exp, 2),
             vmem(n_exp, 2),
@@ -613,14 +721,17 @@
             pair(n_exp),
             pair(n_exp),
             pair(1),
+            pltpu.VMEM((n_exp + 2,) + stats.shape, stats.dtype),
+            pltpu.VMEM((n_exp + 2,) + stats.shape, stats.dtype),
+            pair(n_exp + 2),
         ],
         compiler_params=pltpu.CompilerParams(
             collective_id=2, has_side_effects=True, vmem_limit_bytes=60 * MIB
         ),
         cost_estimate=pl.CostEstimate(
-            flops=2 * normed.shape[0] * model * width, bytes_accessed=16 * MIB, transcendentals=0
+            flops=2 * turned.shape[1] * model * width, bytes_accessed=16 * MIB, transcendentals=0
         ),
-    )(normed, grad, kv_grad, extra)
+    )(turned, grad, kv_grad, extra, stats)
 
 
 def back_kernel(
@@ -748,16 +859,23 @@
 
 
 def back_to_input(
-    query_grad, key_grad, value_grad, raw, w_query, w_kv, gain, cos, sin, hidden, row_gain, middle_grad,
+    query_grad, key_grad, value_grad, raw, weight, gain, cos, sin, hidden, row_gain, middle_grad,
     chip, into, jobs, n_exp
 ):
     bf16, f32 = jnp.bfloat16, jnp.float32
     tokens, model = hidden.shape
-    total, kv_width = raw.shape
+    total, q_width = query_grad.shape
+    kv_width = raw.shape[1] - q_width
+    once = dict(pipeline_mode=pl.Buffered(1))
+    tail = lambda rows: pl.BlockSpec((rows, kv_width), lambda i: (0, q_width // kv_width), **once)
     vmem, any_spec = pl.BlockSpec(memory_space=pltpu.VMEM), pl.BlockSpec(memory_space=pl.ANY)
     return pl.pallas_call(
         functools.partial(back_kernel, n_exp, jobs),
-        in_specs=[vmem] * 12 + [any_spec] * 2,
+        grid=(1,),
+        in_specs=[vmem] * 3
+        + [tail(total), pl.BlockSpec((model, q_width), lambda i: (0, 0), **once), tail(model)]
+        + [vmem] * 6
+        + [any_spec] * 2,
         out_specs=[vmem] * 4 + [any_spec],
         out_shape=[
             jax.ShapeDtypeStruct((total, kv_width), bf16),
@@ -786,20 +904,22 @@
             transcendentals=0,
         ),
     )(
-        query_grad, key_grad, value_grad, raw, w_query, w_kv, gain, cos, sin, hidden, row_gain,
+        query_grad, key_grad, value_grad, raw, weight, weight, gain, cos, sin, hidden, row_gain,
         middle_grad, chip, into
     )
 
 
 def out_back_kernel(
-    n_exp, jobs, mixed_ref, grad_ref, weight_ref, valid_ref, chip_ref, into_in, weight_grad_ref, mixed_grad_ref, into_ref, sems
+    n_exp, jobs, mixed_ref, own_ref, sib_ref, weight_ref, valid_ref, chip_ref, into_in, weight_grad_ref, mixed_grad_ref, into_ref, grad_ref, sems
 ):
     bf16 = jnp.bfloat16
     sent = [sent_rows(chip_ref, into_ref, job, sems, i, n_exp) for i, job in enumerate(jobs)]
-    step = pl.program_id(0)
+    step, tokens = pl.program_id(0), own_ref.shape[0]
 
     @pl.when(step == 0)
     def _():
+        grad_ref[:tokens] = own_ref[...]
+        grad_ref[tokens:] = sib_ref[...]
         greet_slots(sorted({job[2] for job in jobs}), n_exp)
         for copy in sent:
             copy.start()
@@ -814,10 +934,10 @@
             copy.wait()
 
 
-def out_back(mixed, grad, weight, valid, chip, into, jobs, n_exp):
+def out_back(mixed, own, sib, weight, valid, chip, into, jobs, n_exp):
     bf16 = jnp.bfloat16
     total, width = mixed.shape
-    model = grad.shape[1]
+    model = own.shape[1]
     block = 2 * HEAD_DIM
     any_spec = pl.BlockSpec(memory_space=pl.ANY)
     columns = pl.BlockSpec((total, block), lambda j: (0, j))
@@ -827,7 +947,8 @@
         grid=(width // block,),
         in_specs=[
             columns,
-            pl.BlockSpec(grad.shape, lambda j: (0, 0)),
+            pl.BlockSpec(own.shape, lambda j: (0, 0)),
+            pl.BlockSpec(own.shape, lambda j: (0, 0)),
             rows,
             pl.BlockSpec(valid.shape, lambda j: (0, 0)),
             any_spec,
@@ -839,15 +960,15 @@
             jax.ShapeDtypeStruct((total, width), bf16),
             jax.ShapeDtypeStruct(into.shape, bf16),
         ],
-        input_output_aliases={5: 2},
-        scratch_shapes=[pltpu.SemaphoreType.DMA((2, len(jobs)))],
+        input_output_aliases={6: 2},
+        scratch_shapes=[pltpu.VMEM((total, model), bf16), pltpu.SemaphoreType.DMA((2, len(jobs)))],
         compiler_params=pltpu.CompilerParams(
             vmem_limit_bytes=40 * MIB, collective_id=12, has_side_effects=True
         ),
         cost_estimate=pl.CostEstimate(
             flops=4 * total * model * width, bytes_accessed=24 * MIB, transcendentals=0
         ),
-    )(mixed, grad, weight, valid, chip, into)
+    )(mixed, own, sib, weight, valid, chip, into)
 
 
 def pick(core, first, second):
@@ -969,6 +1090,150 @@
             column.arrivals(2)
             column.sends(2, WAIT_SEND)
             column.passes(1, WAIT)
+
+
+def project_kernel(
+    n_y,
+    n_exp,
+    own_ref,
+    sib_ref,
+    row_gain_ref,
+    weight_ref,
+    key_gain_ref,
+    gain_ref,
+    cos_ref,
+    sin_ref,
+    *refs,
+):
+    raw_ref, low_ref, ordered_ref, turned_ref, kv_full_ref = refs[5:10]
+    gate_full_ref, up_full_ref, cots_ref, tables_ref, kv_scr, normed_ref = refs[10:16]
+    plane_sem, column_sem, kv_sems = refs[16:]
+    plane = Plane(n_exp, (gate_full_ref, up_full_ref), plane_sem)
+    column = Column(n_exp, (cots_ref, tables_ref), column_sem)
+    column.own = (refs[0], tables_ref.at[column.z, column.core])
+    j, tokens = pl.program_id(0), own_ref.shape[0]
+    here = kv_full_ref.at[:, pl.ds(pl.multiple_of(column.x * tokens, tokens), tokens)]
+    kv_copies = [
+        pltpu.make_async_remote_copy(
+            src_ref=kv_scr,
+            dst_ref=here,
+            send_sem=kv_sems.at[0],
+            recv_sem=kv_sems.at[1],
+            device_id=column.ids[X],
+            device_id_type=MESH,
+        ),
+        pltpu.make_async_copy(kv_scr, here, kv_sems.at[2]),
+    ]
+
+    @pl.when(j == 0)
+    def _():
+        greet(column.z, n_exp, plane.ids, (CORE, X, Y, UP, DOWN))
+        plane.each(START, False)
+        column.sends(1, START)
+        for s, source in enumerate((own_ref, sib_ref)):
+            hidden = source[...].astype(jnp.float32)
+            inverse = lax.rsqrt(jnp.mean(hidden * hidden, axis=-1, keepdims=True) + EPS)
+            normed_ref[s * tokens : (s + 1) * tokens] = (hidden * inverse * row_gain_ref[...]).astype(
+                jnp.bfloat16
+            )
+
+    @pl.when(j == pl.num_programs(0) // 2)
+    def _():
+        column.arrivals(1)
+        column.sends(2, START)
+        column.passes(1, START)
+
+    raw = dot_plain(normed_ref[...], ordered_weight(n_y, weight_ref, ordered_ref))
+    raw_ref[...] = raw
+
+    @pl.when(j != 1)
+    def _():
+        gain = jnp.where(j == 0, key_gain_ref[...], gain_ref[...])
+        store_rotated(raw, gain, cos_ref, sin_ref, low_ref)
+
+    @pl.when(j == 1)
+    def _():
+        low_ref[...] = raw.astype(jnp.bfloat16)
+        turned_ref[...] = normed_ref[...].T
+
+    for which in range(2):
+
+        @pl.when(j == which)
+        def _(which=which):
+            width = low_ref.shape[1]
+            for s in range(2):
+                kv_scr[s, :, which * width : (which + 1) * width] = low_ref[
+                    s * tokens : (s + 1) * tokens
+                ]
+            if which:
+                for copy in kv_copies:
+                    copy.start()
+
+    @pl.when(j == pl.num_programs(0) - 1)
+    def _():
+        for copy in kv_copies:
+            copy.wait()
+        plane.each(WAIT, False)
+        column.arrivals(2)
+        for hop in (1, 2):
+            column.sends(hop, WAIT_SEND)
+        column.passes(1, WAIT)
+
+
+def project_all(own, sib, row_gain, gathered, blocks, key_gain, gain, cos, sin, cot, n_y, n_exp, moving):
+    bf16 = jnp.bfloat16
+    tokens, model = own.shape
+    total, width = 2 * tokens, 2 * HEAD_DIM
+    n_yxz, _, rows, _ = gathered.shape
+    fixed = lambda j: (0, 0)
+    block = lambda j: jnp.where(j < 2, blocks + j, j - 2)
+    any_specs = [pl.BlockSpec(memory_space=pl.ANY)] * len(moving)
+    columns = pl.BlockSpec((total, width), lambda j: (0, block(j)))
+    return pl.pallas_call(
+        functools.partial(project_kernel, n_y, n_exp),
+        grid=(blocks + 2,),
+        in_specs=[pl.BlockSpec(own.shape, fixed)] * 2
+        + [
+            pl.BlockSpec((1, model), fixed),
+            pl.BlockSpec((n_yxz, 2, rows, width), lambda j: (0, 0, 0, block(j))),
+            pl.BlockSpec((1, HEAD_DIM), fixed),
+            pl.BlockSpec((1, HEAD_DIM), fixed),
+            pl.BlockSpec(cos.shape, fixed),
+            pl.BlockSpec(cos.shape, fixed),
+            pl.BlockSpec(memory_space=pl.ANY),
+        ]
+        + any_specs,
+        out_specs=[
+            columns,
+            columns,
+            pl.BlockSpec((model, width), lambda j: (0, block(j))),
+            pl.BlockSpec((model, total), fixed),
+            pl.BlockSpec(memory_space=pl.ANY),
+        ]
+        + any_specs,
+        out_shape=[
+            jax.ShapeDtypeStruct((total, (blocks + 2) * width), jnp.float32),
+            jax.ShapeDtypeStruct((total, (blocks + 2) * width), bf16),
+            jax.ShapeDtypeStruct((model, (blocks + 2) * width), bf16),
+            jax.ShapeDtypeStruct((model, total), bf16),
+            jax.ShapeDtypeStruct((2, 2 * tokens, 2 * width), bf16),
+        ]
+        + [jax.ShapeDtypeStruct(a.shape, a.dtype) for a in moving],
+        scratch_shapes=[
+            pltpu.VMEM((2, tokens, 2 * width), bf16),
+            pltpu.VMEM((total, model), bf16),
+            plane_sems(2),
+            column_sems(2, n_exp),
+            pltpu.SemaphoreType.DMA((3,)),
+        ],
+        input_output_aliases={9 + i: 5 + i for i in range(len(moving))},
+        compiler_params=pltpu.CompilerParams(
+            vmem_limit_bytes=60 * MIB, collective_id=4, has_side_effects=True
+        ),
+        cost_estimate=pl.CostEstimate(
+            flops=2 * total * model * (blocks + 2) * width, bytes_accessed=64 * MIB, transcendentals=0
+        ),
+    )(own, sib, row_gain, gathered, key_gain, gain, cos, sin, cot, *moving)
 
 
 def projection_specs(normed_shape, gathered, first_block, blocks, cos):
@@ -1120,7 +1385,7 @@
         out_specs=[specs[HEAD], specs[RECIP]]
         + [pl.BlockSpec(memory_space=pl.ANY)] * len(moving),
         out_shape=[
-            jax.ShapeDtypeStruct(queries.shape, jnp.bfloat16),
+            jax.ShapeDtypeStruct((2 * tokens, groups * per_group * HEAD_DIM), jnp.bfloat16),
             jax.ShapeDtypeStruct((steps, 1, tokens), jnp.float32),
         ]
         + [jax.ShapeDtypeStruct(a.shape, a.dtype) for a in moving],
@@ -1264,7 +1529,7 @@
         out_specs=[specs[HEAD], specs[KEY], specs[KEY], pl.BlockSpec((8, HEAD_DIM), fixed)]
         + [pl.BlockSpec(memory_space=pl.ANY)],
         out_shape=[
-            jax.ShapeDtypeStruct(queries.shape, jnp.bfloat16),
+            jax.ShapeDtypeStruct((2 * tokens, groups * per_group * HEAD_DIM), jnp.bfloat16),
             key_grad,
             key_grad,
             jax.ShapeDtypeStruct((8, HEAD_DIM), jnp.float32),
@@ -1866,9 +2131,11 @@
             mine_block,
             other_block,
             halves,
-            o_proj.reshape(2, -1, model_width),
+            o_proj.reshape(4, -1, model_width),
+            routes[0].T,
+            gates[0].T,
             out_grad[0],
-            table,
+            expert_count,
             n_exp,
         )
         w_out = w_out.reshape(q_width, model_width)
@@ -1923,29 +2190,39 @@
     seg_keys = seg_two[:, :, None]
     inv_attn = lax.rsqrt(jnp.mean(hidden * hidden, axis=-1, keepdims=True) + EPS)
     q_blocks = q_width // (2 * HEAD_DIM)
-    kv_raw, kv_low, w_kv, normed_two = project_keys(
-        residual_in[0],
-        swap(residual_in[0]),
-        gain_attn[None],
-        w_gathered,
-        q_blocks,
-        gain_key_f,
-        cos_one,
-        signed_sine,
-        n_y,
-    )
-    kv_here = kv_low.reshape(2, token_count, 2 * kv_width)
-    if n_ctx == 2:
-        kv_there = lax.ppermute(kv_here, CTX, [(0, 1), (1, 0)])
-        kv_full = jnp.concatenate(
-            [pick(span_index, kv_here, kv_there), pick(span_index, kv_there, kv_here)], 1
+    if own_links:
+        q_raw, query_rows, w_query, normed_turned, kv_full, *moving = project_all(
+            residual_in[0],
+            swap(residual_in[0]),
+            gain_attn[None],
+            w_gathered,
+            q_blocks,
+            gain_key_f,
+            gain_query_f,
+            cos_one,
+            signed_sine,
+            out_grad[0],
+            n_y,
+            n_exp,
+            (gate_full, up_full, cots_all, tables_all),
         )
     else:
+        kv_raw, kv_low, w_kv, normed_two = project_keys(
+            residual_in[0],
+            swap(residual_in[0]),
+            gain_attn[None],
+            w_gathered,
+            q_blocks,
+            gain_key_f,
+            cos_one,
+            signed_sine,
+            n_y,
+        )
+        kv_here = kv_low.reshape(2, token_count, 2 * kv_width)
         kv_full = lax.all_gather(kv_here, CTX, axis=1, tiled=True)
-    moving = (gate_full, up_full, cots_all, tables_all) if own_links else ()
-    q_raw, query_rows, w_query, *moving = project_queries(
-        normed_two, w_gathered, q_blocks, gain_query_f, cos_one, signed_sine, n_y, n_exp, moving
-    )
+        q_raw, query_rows, w_query, *moving = project_queries(
+            normed_two, w_gathered, q_blocks, gain_query_f, cos_one, signed_sine, n_y, n_exp, ()
+        )
     mixed_low, recip, *moving = attend(
         info, seg_keys, query_rows, kv_full, groups, heads_per_group, n_exp, moving
     )
@@ -1956,9 +2233,10 @@
     down_full = gather_expert(
         down_pair if own_links else down_proj, query_rows if own_links else gain_attn
     )
-    tables_all = lax.dynamic_update_slice(
-        tables_all, table[None, None], (z_index, core, jnp.int32(0), jnp.int32(0))
-    )
+    if not own_links:
+        tables_all = lax.dynamic_update_slice(
+            tables_all, table[None, None], (z_index, core, jnp.int32(0), jnp.int32(0))
+        )
     attn_partial = jnp.dot(mixed_low, w_out, preferred_element_type=f32)
     attn_out = attn_partial[:token_count] + swap(attn_partial[token_count:])
     middle = hidden + attn_out
@@ -2030,12 +2308,11 @@
     mlp_gain_grad = jnp.sum(grad_normed_mlp * middle * inv_mlp, axis=0)
     grad_middle = cotangent + norm_back(grad_normed_mlp, middle, inv_mlp, gain_mlp_f)
     grad_attn_own = grad_middle.astype(bf16)
-    grad_attn = jnp.concatenate([grad_attn_own, swap(grad_attn_own)], 0)
     part_rows = token_count // 4
     out_jobs, back_jobs = [(0, 2, 2, 0, part_rows)], [(0, 2, 2, part_rows, token_count)]
     last_jobs = [(1, 1, 1, 0, token_count)]
     o_grad_part, mixture_gradient, out_into = out_back(
-        mixed_low, grad_attn, w_out, valid_two, out_far, out_into, out_jobs, n_exp
+        mixed_low, grad_attn_own, swap(grad_attn_own), w_out, valid_two, out_far, out_into, out_jobs, n_exp
     )
     o_grad_plane = scatter_plane(o_grad_part.reshape(n_y, n_ctx, n_exp, -1, model_width))
     grad_q_raw, key_grad, value_grad, q_gain_rows, out_into = attend_back(
@@ -2063,9 +2340,8 @@
             grad_q_raw,
             key_grad,
             value_grad,
-            kv_raw,
+            q_raw,
             w_query,
-            w_kv,
             gain_key_f,
             cos_one,
             signed_sine,
@@ -2118,19 +2394,21 @@
     ]
     sums.append(jnp.sum(valid_rows, keepdims=True))
     stats = jnp.pad(jnp.concatenate(sums, 1), ((0, 7), (0, 124)))
-    stats = sum_devices(stats, ((SEQ, n_seq), (CTX, n_ctx), (EXP, n_exp)))
+    if not own_links:
+        stats = sum_devices(stats, ((SEQ, n_seq), (CTX, n_ctx), (EXP, n_exp)))
     if own_links:
-        extra_grad, o_grad_plane, parts, stats, final_out = lax.optimization_barrier(
+        extra_grad, o_grad_plane, _, stats, final_out = lax.optimization_barrier(
             (extra_grad, o_grad_plane, parts, stats, final_out)
         )
     o_proj_grad = lax.psum_scatter(o_grad_plane, EXP, scatter_dimension=0, tiled=True)
     o_proj_grad = o_proj_grad[0].astype(f32)
     if own_links:
-        grad_mine, grad_theirs = dense_grad_scatter(
-            normed_two,
+        grad_mine, grad_theirs, stats = dense_grad_scatter(
+            normed_turned,
             grad_q_raw,
             grad_kv,
             extra_grad.reshape(n_y, 2, n_ctx, n_exp, rows, 128),
+            stats,
             n_exp,
         )
     else:

time: 1170 us -> 1160 us (level)
  waiting for transfers between devices: 8.21 us -> 22.9 us
  Pallas kernels: 1000 us -> 986 us
  other arithmetic: 79.8 us -> 66.4 us
    unnamed x8, waiting for transfers between devices: 0.09 us -> 14.9 us
    pallas_call x4 -> x2, Pallas kernels: 189 us -> 175 us  [the longest x1 102 us: project_all(): pl.pallas_call(functools.partial(project_kernel, n_y, n_exp), grid=(block...]
    unnamed x113 -> x97, local copies, waits for them, and re-layouts: 29.8 us -> 29.8 us
  transfers between devices with their start and end apart: 11 -> 10, of which waited for: 2 -> 3; matrix products, arithmetic and copies ran while one was open for 9% -> 8% of each run, Pallas kernels for 62% -> 61%
where the time goes in v4:
time: 1160 us; the launch traced here: 1150 us
  Pallas kernels  986 us (85%)
  other arithmetic  66.4 us (6%)
  local copies, waits for them, and re-layouts  43.9 us (4%)
  waiting for transfers between devices  22.9 us (2%)
  between operations  15.3 us (1%)
  matrix products  12.6 us (1%)
    pallas_call x1, Pallas kernels, run_experts(): pl.pallas_call(functools.partial(moe_kernel, n_exp, n_y, local_experts),...  251 us
    pallas_call x1, Pallas kernels, gather_chips(): pl.pallas_call(functools.partial(gather_kernel, n_exp), in_specs=[vmem_sp...  160 us
    pallas_call x1, Pallas kernels, dense_grad_scatter(): pl.pallas_call(functools.partial(scatter_kernel, n_exp), in_specs=[spec]...  120 us
    pallas_call x2, Pallas kernels, part_weight_grads(): pl.pallas_call(functools.partial(part_grad_kernel, n_y, n_ctx, n_exp, job...  106 us
    pallas_call x1, Pallas kernels, project_all(): pl.pallas_call(functools.partial(project_kernel, n_y, n_exp), grid=(block...  102 us
    pallas_call x1, Pallas kernels, attend_back(): pl.pallas_call(functools.partial(attention_back_kernel, n_exp=n_exp, jobs...  73.1 us
    pallas_call x1, Pallas kernels, back_to_input(): pl.pallas_call(functools.partial(back_kernel, n_exp, jobs), grid=(1,), in...  73 us
    pallas_call x1, Pallas kernels, attend(): pl.pallas_call(functools.partial(attention_kernel, n_exp if moving else 0...  69.4 us
  transfers between devices with their start and end apart: 10, of which 3 were waited for; matrix products, arithmetic and copies ran while one was open for 8% of the time, Pallas kernels for 61%

profile of v4, /device:TPU:0, one launch (start us, length us, event | category | flops | bytes accessed | tf_op | source)
XLA Modules:
  0.0 1147.9 jit_solution(12589005880825425984)
XLA Ops:
  7.9 1.2 select_dynamic-update-slice_fusion.1
  9.0 1.0 select_dynamic-update-slice_fusion
  10.1 0.8 constant_dynamic-update-slice_fusion.9
  10.8 0.8 constant_dynamic-update-slice_fusion.8
  11.6 0.8 constant_dynamic-update-slice_fusion.7
  12.3 0.8 constant_dynamic-update-slice_fusion.6
  13.1 0.8 constant_dynamic-update-slice_fusion.1
  13.9 1.6 broadcast_select_fusion.3
  15.8 0.7 constant_dynamic-update-slice_fusion.5
  16.6 159.5 %shard_map.263 = (bf16[4,4,2,64,2688]{4,3,2,1,0:T(8,128)(2,1)}, bf16[4,4,4,32,2048]{4,3,2,1,0:T(8,128)(2,1)}, bf16[4,2,2,256,768]{4,3,2,1,0:T(8,128)(2,1)S(1)}, ...) custom-call(bf16[64,2688]{1,0:T(8,128)(2,1)S(1)} %get-tuple-element., ...), custom_call_target="tpu_custom_call" | custom-call | tf_op jit(solution)/shard_map/pallas_call | solution.py:472
  176.2 2.6 copy-done.2
  178.8 2.6 copy-done.3
  181.4 0.8 copy-done.11
  182.3 0.8 slice.292
  183.2 0.7 broadcast_in_dim_reshape_squeeze.14.row_gain_ref
  185.2 1.0 fusion.8
  186.2 0.8 pad_maximum_fusion.2.cos_ref
  187.1 0.8 pad_maximum_fusion.3.sin_ref
  187.9 1.3 copy-done.27
  189.2 102.0 %shard_map.264 = (f32[1024,2560]{1,0:T(8,128)}, bf16[1024,2560]{1,0:T(8,128)(2,1)}, bf16[2048,2560]{1,0:T(8,128)(2,1)}, bf16[2048,1024]{1,0:T(8,128)(2,1)}, bf16...) custom-call(bf16[512,2048]{1,0:T(8,128)(2,1)} %bitcast.123, ...), custom_call_target="tpu_custom_call", output_to_operand_aliasing={{5}: (9, {}), {6}: (10, {}), {7}: (11, {}), {8}: (12, {})} | custom-call | flops 10737418240 | bytes 67108864 | tf_op jit(solution)/shard_map/pallas_call | solution.py:1192
  291.4 0.7 compare_convert_fusion
  293.4 1.0 copy-done.12
  294.5 1.6 copy-done.20
  296.1 69.4 %shard_map.265 = (bf16[1024,2048]{1,0:T(8,128)(2,1)}, f32[32,1,512]{2,1,0:T(1,128)S(1)}, bf16[4,2,2,256,768]{4,3,2,1,0:T(8,128)(2,1)}, bf16[4,2,2,256,768]{4,3,2...) custom-call(s32[2,8,512]{2,1,0:T(8,128)S(1)} %scatter.9.info_ref, ...), custom_call_target="tpu_custom_call", output_to_operand_aliasing={{2}: (5, {}), {3}: (6, {}), {4}: (7, {}), {5}: (8, {})} | custom-call | flops 17179869184 | bytes 12582912 | tf_op jit(solution)/shard_map/pallas_call | solution.py:1380
  365.5 12.6 %fusion.22 = f32[1024,2048]{1,0:T(8,128)S(1)} fusion(bf16[1024,2048]{1,0:T(8,128)(2,1)} %get-tuple-element.107.mixed_ref, bf16[2048,2048]{1,0:T(8,128)(2,1)} %bitcast.149), kind=kOutput, calls=%fused_computation.104 | convolution fusion | flops 8589934592 | bytes 20971520 | tf_op jit(solution)/shard_map/dot_general | solution.py:2240
  378.2 2.5 slice.297
  380.6 2.1 copy-done.24
  383.1 7.1 collective-permute-done.2
  390.2 4.8 multiply_reduce_fusion.2
  395.7 1.3 copy-done.22
  397.0 1.7 multiply_convert_fusion.own_ref
  398.7 250.8 %shard_map.266 = (bf16[2,2304,2048]{2,1,0:T(8,128)(2,1)}, bf16[2,2304,2048]{2,1,0:T(8,128)(2,1)}, bf16[2,2304,768]{2,1,0:T(8,128)(2,1)}, bf16[2,2304,768]{2,1,0:...) custom-call(f32[4,2,32,512]{3,2,1,0:T(8,128)} %copy-done.13, ...), custom_call_target="tpu_custom_call" | custom-call | flops 125627793408 | bytes 96731136 | tf_op jit(solution)/shard_map/pallas_call | solution.py:1779
  649.5 35.5 %shard_map.267 = (bf16[2,2,2,1,2,768,256]{6,5,4,3,2,1,0:T(8,128)(2,1)}, bf16[4,512,2048]{2,1,0:T(8,128)(2,1)}, bf16[4,512,2048]{2,1,0:T(8,128)(2,1)}) custom-call(bf16[2,2304,2048]{2,1,0:T(8,128)(2,1)} %get-tuple-element.119.wide_ref, bf16[2,2304,768]{2,1,0:T(8,128)(2,1)} %get-tuple-element.120.refs_0_, ...), custom_call_target="tpu_custom_call", output_to_operand_aliasing={{1}: (3, {}), {2}: (5, {})} | custom-call | flops 14495514624 | bytes 32243712 | tf_op jit(solution)/shard_map/pallas_call | solution.py:1979
  685.0 70.9 %shard_map.268 = (bf16[2,2,2,2,2,768,256]{6,5,4,3,2,1,0:T(8,128)(2,1)}, bf16[4,512,2048]{2,1,0:T(8,128)(2,1)}, bf16[4,512,2048]{2,1,0:T(8,128)(2,1)}) custom-call(bf16[2,2304,2048]{2,1,0:T(8,128)(2,1)} %get-tuple-element.116.wide_ref, bf16[2,2304,768]{2,1,0:T(8,128)(2,1)} %get-tuple-element.117.refs_0_, ...), custom_call_target="tpu_custom_call", output_to_operand_aliasing={{1}: (4, {}), {2}: (6, {})} | custom-call | flops 28991029248 | bytes 45613056 | tf_op jit(solution)/shard_map/pallas_call | solution.py:1979
  756.7 5.9 fusion.6
  763.2 7.3 fusion.14
  770.7 3.3 add_convert_fusion.chip_ref
  774.1 0.9 collective-permute-done.3.sib_ref
  775.0 31.0 %shard_map.269 = (bf16[2048,2048]{1,0:T(8,128)(2,1)}, bf16[1024,2048]{1,0:T(8,128)(2,1)S(1)}, bf16[4,512,2048]{2,1,0:T(8,128)(2,1)}) custom-call(bf16[1024,2048]{1,0:T(8,128)(2,1)} %get-tuple-element.107.mixed_ref, bf16[512,2048]{1,0:T(8,128)(2,1)} %get-tuple-element.203.own_ref, ...), custom_call_target="tpu_custom_call", output_to_operand_aliasing={{2}: (6, {})} | custom-call | flops 17179869184 | bytes 25165824 | tf_op jit(solution)/shard_map/pallas_call | solution.py:945
  806.0 1.9 copy-done.21
  809.4 73.1 %shard_map.270 = (bf16[1024,2048]{1,0:T(8,128)(2,1)}, f32[2,1024,256]{2,1,0:T(8,128)S(1)}, f32[2,1024,256]{2,1,0:T(8,128)S(1)}, f32[8,128]{1,0:T(8,128)S(1)}, bf16[4,512,2048]{2,1,0:T(8,128)(2,1)}) custom-call(s32[2,8,512]{2,1,0:T(8,128)S(1)} %copy-done.16, s32[2,1024,1]{2,1,0:T(8,128)S(1)} %copy-done.10, ...), custom_call_target="tpu_custom_call", output_to_operand_aliasing={{4}: (13, {})} | custom-call | flops 42949672960 | bytes 37748736 | tf_op jit(solution)/shard_map/pallas_call | solution.py:1522
  882.5 1.3 copy-done.7
  883.8 1.3 copy-done.8
  885.1 73.0 %shard_map.271 = (bf16[1024,512]{1,0:T(8,128)(2,1)}, bf16[512,2048]{1,0:T(8,128)(2,1)}, f32[1,2048]{1,0:T(1,128)}, f32[8,128]{1,0:T(8,128)}, bf16[4,512,2048]{2,1,0:T(8,128)(2,1)}) custom-call(bf16[1024,2048]{1,0:T(8,128)(2,1)} %get-tuple-element.132.query_grad_ref.grad_ref, f32[2,1024,256]{2,1,0:T(8,128)} %copy-done.7, ...), custom_call_target="tpu_custom_call", output_to_operand_aliasing={{4}: (13, {})} | custom-call | flops 10737418240 | bytes 50331648 | tf_op jit(solution)/shard_map/pallas_call | solution.py:872
  958.1 0.7 convert_reduce_fusion
  959.0 0.7 convert.31
  960.0 11.1 fusion.1
  971.2 3.3 select_maximum_fusion.stats_ref
  974.4 1.0 maximum_maximum_fusion
  975.5 14.8 %reduce-scatter.13.cloned.1.call-done = bf16[1,4,128,2048]{3,2,1,0:T(8,128)(2,1)} async-done(((bf16[4,4,128,2048]{3,2,1,0:T(8,128)(2,1)}), bf16[1,4,128,2048]{3,2,1,0:T(8,128)(2,1)}) %reduce-scatter.13.cloned.1.call-update) | async-done | bytes 2097168
  990.3 2.5 select_bitcast_fusion
  993.0 120.4 %shard_map.272 = (f32[64,2688]{1,0:T(8,128)}, f32[64,2688]{1,0:T(8,128)}, f32[8,128]{1,0:T(8,128)}) custom-call(bf16[2048,1024]{1,0:T(8,128)(2,1)} %get-tuple-element.146.turned, bf16[1024,2048]{1,0:T(8,128)(2,1)} %get-tuple-element.132.query_grad_ref.grad_ref, bf16[1024,512]{1,0:T(8,128)(2,1)} %get-tuple-element.147.kv_grad_ref, ...), custom_call_target="tpu_custom_call" | custom-call | flops 11274289152 | bytes 16777216 | tf_op jit(solution)/shard_map/pallas_call | solution.py:703
  1113.4 1.6 broadcast_select_fusion.8
  1114.9 1.5 slice.291
  1117.1 0.7 pad_maximum_fusion.5
  1118.5 1.2 sqrt_bitcast_fusion
  1120.9 1.1 pad_maximum_fusion.1
  1122.0 2.8 bitcast_select_fusion.1
  1125.5 2.5 fusion.15
  1127.9 2.1 copy.82
  1130.1 3.5 copy.80
  1133.6 2.4 copy.81
  1135.9 2.1 bitcast_convert_fusion
  1138.1 3.2 copy.114
  (145 shorter events, 11.0 us)
Async XLA Ops:
  7.2 8.6 copy-start.45
  7.2 8.6 copy-start.44
  7.2 8.6 copy-start.43
  7.2 8.6 copy-start.42
  7.2 391.5 %all-gather.3.cloned.1.call-start = ((), (), s32[]{:S(2)}) async-start(), calls=%async_computation.5 | async-start | bytes 7864320 | tf_op jit(solution)/shard_map/all_gather | solution.py:2170
  7.3 180.7 %collective-permute-start.1 = (bf16[512,2048]{1,0:T(8,128)(2,1)}, bf16[512,2048]{1,0:T(8,128)(2,1)S(1)}, u32[]{:S(2)}, u32[]{:S(2)}) collective-permute-start(bf16[512,2048]{1,0:T(8,128)(2,1)} %bitcast.122), channel_id=1, source_target_pairs={{0,8},{8,0},{16,24},{24,16},{1,9},{9,1},{17,25},{25,17},{2,10},{10... | collective-permute-start | bytes 6291464 | tf_op jit(solution)/shard_map/ppermute | solution.py:2076
  7.8 283.6 %collective-permute-start = (s32[1,1024]{1,0:T(1,128)}, s32[1,1024]{1,0:T(1,128)S(1)}, u32[]{:S(2)}, u32[]{:S(2)}) collective-permute-start(s32[1,1024]{1,0:T(1,128)} %param.21), channel_id=1, source_target_pairs={{0,8},{8,0},{16,24},{24,16},{1,9},{9,1},{17,25},{25,17},{2,10},{10... | collective-permute-start | bytes 12296 | tf_op jit(solution)/shard_map/ppermute | solution.py:2076
  7.9 7.7 copy-start.28
  7.9 8.6 copy-start.29
  13.9 2.7 copy-start
  13.9 2.7 copy-start.14
  13.9 2.7 copy-start.17
  13.9 2.7 copy-start.18
  15.8 160.4 %copy-start.40 = (bf16[64]{0:T(256)(128)(2,1)}, bf16[64]{0:T(256)(128)(2,1)S(1)}, u32[]{:S(2)}) copy-start(bf16[64]{0:T(256)(128)(2,1)S(1)} %pad.52.clone) | copy-start | bytes 388
  176.2 2.6 copy-start.2
  178.8 2.6 copy-start.3
  181.4 0.8 copy-start.11
  187.9 1.3 copy-start.27
  189.2 102.1 %copy-start.37 = (s32[1,1024]{1,0:T(1,128)S(1)}, s32[1,1024]{1,0:T(1,128)}, u32[]{:S(2)}) copy-start(s32[1,1024]{1,0:T(1,128)} %param.21) | copy-start | bytes 12292
  291.3 684.1 %reduce-scatter.17.cloned.1.call-start = ((), (), s32[]{:S(2)}) async-start(), calls=%async_computation.8 | async-start | bytes 7864320
  292.1 0.6 copy-start.33
  293.0 72.4 %copy-start.9 = (s32[2,1024,1]{2,1,0:T(8,128)}, s32[2,1024,1]{2,1,0:T(8,128)S(1)}, u32[]{:S(2)}) copy-start(s32[2,1024,1]{2,1,0:T(8,128)S(1)} %copy.74.seg_ref) | copy-start | bytes 24580
  293.4 72.0 %copy-start.15 = (s32[2,8,512]{2,1,0:T(8,128)}, s32[2,8,512]{2,1,0:T(8,128)S(1)}, u32[]{:S(2)}) copy-start(s32[2,8,512]{2,1,0:T(8,128)S(1)} %scatter.9.info_ref) | copy-start | bytes 98308
  293.4 1.1 copy-start.12
  294.5 1.6 copy-start.20
  365.5 12.7 %copy-start.13 = (f32[4,2,32,512]{3,2,1,0:T(8,128)}, f32[4,2,32,512]{3,2,1,0:T(8,128)S(1)}, u32[]{:S(2)}) copy-start(f32[4,2,32,512]{3,2,1,0:T(8,128)S(1)} %get-tuple-element.109.table_ref) | copy-start | bytes 1572868
  378.2 4.5 copy-start.24
  382.7 7.5 collective-permute-start.2
  383.1 12.5 %copy-start.30 = (f32[2048]{0:T(1024)}, f32[2048]{0:T(1024)S(1)}, u32[]{:S(2)}) copy-start(f32[2048]{0:T(1024)S(1)} %mul.125) | copy-start | bytes 24580
  395.0 2.0 copy-start.22
  395.7 3.0 copy-start.35
  685.0 290.5 %reduce-scatter.15.cloned.1.call-start = ((), (), s32[]{:S(2)}) async-start(), calls=%async_computation.7 | async-start | bytes 15728640
  756.0 0.7 copy-start.31
  756.0 0.7 copy-start.36
  756.0 234.3 %reduce-scatter.13.cloned.1.call-start = ((), (), s32[]{:S(2)}) async-start(), calls=%async_computation.6 | async-start | bytes 10485760
  756.7 5.9 copy-start.1
  756.7 6.5 copy-start.23
  756.7 6.5 copy-start.39
  763.2 7.3 copy-start.34
  770.5 4.5 collective-permute-start.3
  774.1 31.9 %copy-start.6 = (bf16[1,512,2048]{2,1,0:T(8,128)(2,1)}, bf16[1,512,2048]{2,1,0:T(8,128)(2,1)S(1)}, u32[]{:S(2)}) copy-start(bf16[1,512,2048]{2,1,0:T(8,128)(2,1)S(1)} %add_convert_fusion.chip_ref) | copy-start | bytes 6291460
  806.0 1.9 copy-start.21
  807.9 0.7 copy-start.38
  808.0 1.4 copy-start.4
  808.0 1.4 copy-start.5
  808.0 1.4 copy-start.10
  808.0 1.4 copy-start.16
  808.0 1.4 copy-start.19
  808.0 327.9 %reduce-scatter.11.cloned.1.call-start = ((), (), s32[]{:S(2)}) async-start(), calls=%async_computation.4 | async-start | bytes 2621440 | tf_op jit(solution)/shard_map/reduce_scatter | solution.py:2403
  882.5 1.3 copy-start.7
  883.8 1.3 copy-start.8
  960.0 14.4 %copy-start.32 = (bf16[64,128]{1,0:T(8,128)(2,1)S(1)}, bf16[64,128]{1,0:T(8,128)(2,1)}, u32[]{:S(2)}) copy-start(bf16[64,128]{1,0:T(8,128)(2,1)} %get-tuple-element.261) | copy-start | bytes 49156
  960.0 14.4 %copy-start.41 = (bf16[64]{0:T(256)(128)(2,1)S(1)}, bf16[64]{0:T(256)(128)(2,1)}, u32[]{:S(2)}) copy-start(bf16[64]{0:T(256)(128)(2,1)} %copy-done.40) | copy-start | bytes 388
  992.9 129.1 %collective-permute-start.4 = (bf16[3,2,768,256]{3,2,1,0:T(8,128)(2,1)S(1)}, bf16[3,2,768,256]{3,2,1,0:T(8,128)(2,1)}, u32[]{:S(2)}, u32[]{:S(2)}) collective-permute-start(bf16[3,2,768,256]{3,2,1,0:T(8,128)(2,1)S(1)} %select_bitcast_fusion), channel_id=1, source_target_pairs={{0,8},{8,0},{16,24},{24,16},{1,9},{9,1},{17,25},{25,17},{2,10},{10... | collective-permute-start | bytes 7077896 | tf_op jit(solution)/shard_map/ppermute | solution.py:2076
  1113.3 8.7 copy-start.25
  1113.4 8.7 copy-start.26
Sparse Core Ops, SparseCore 0:
  291.4 94.2 all-gather.2
  685.1 69.5 reduce-scatter.16
  757.8 120.7 reduce-scatter.14
  881.5 108.7 reduce-scatter.12
  993.1 43.9 reduce-scatter.10

commit v5 on v4

--- a/solution.py
+++ b/solution.py
@@ -2397,8 +2397,15 @@
     if not own_links:
         stats = sum_devices(stats, ((SEQ, n_seq), (CTX, n_ctx), (EXP, n_exp)))
     if own_links:
-        extra_grad, o_grad_plane, _, stats, final_out = lax.optimization_barrier(
-            (extra_grad, o_grad_plane, parts, stats, final_out)
+        part = all_experts(jnp.concatenate(parts[::-1], 1))
+        gate_grad, up_grad = part[0].transpose(0, 2, 1), part[1].transpose(0, 2, 1)
+        depth = part.shape[-1]
+        down_grad = part[2].reshape(local_experts, model_width // depth, -1, depth)
+        down_grad = down_grad.transpose(0, 2, 1, 3).reshape(local_experts, -1, model_width)
+        extra_grad, o_grad_plane, gate_grad, up_grad, down_grad, stats, final_out = (
+            lax.optimization_barrier(
+                (extra_grad, o_grad_plane, gate_grad, up_grad, down_grad, stats, final_out)
+            )
         )
     o_proj_grad = lax.psum_scatter(o_grad_plane, EXP, scatter_dimension=0, tiled=True)
     o_proj_grad = o_proj_grad[0].astype(f32)
@@ -2427,13 +2434,7 @@
         grad_mine = pick(core, w_grad[0], w_grad[1])
         grad_theirs = swap(pick(core, w_grad[1], w_grad[0]))
     rms_stats = jnp.sqrt(stats[0, :3] / (stats[0, 3] * model_width))
-    if own_links:
-        part = all_experts(jnp.concatenate(parts[::-1], 1))
-        gate_grad, up_grad = part[0].transpose(0, 2, 1), part[1].transpose(0, 2, 1)
-        depth = part.shape[-1]
-        down_grad = part[2].reshape(local_experts, model_width // depth, -1, depth)
-        down_grad = down_grad.transpose(0, 2, 1, 3).reshape(local_experts, -1, model_width)
-    else:
+    if not own_links:
         gate_grad, up_grad = (all_experts(p).transpose(0, 2, 1) for p in parts[:2])
         down_grad = all_experts(parts[2])
     even = pick(core, grad_mine, grad_theirs).astype(f32)

time: 1160 us -> 1140 us (0.983)
    unnamed x97 -> x101, local copies, waits for them, and re-layouts: 29.8 us -> 28.1 us
  transfers between devices with their start and end apart: 10 -> 10, of which waited for: 3 -> 3; matrix products, arithmetic and copies ran while one was open for 8% -> 9% of each run, Pallas kernels for 61% -> 61%
where the time goes in v5:
time: 1140 us; the launch traced here: 1130 us
  Pallas kernels  983 us (86%)
  other arithmetic  67.1 us (6%)
  local copies, waits for them, and re-layouts  41.8 us (4%)
  between operations  15.4 us (1%)
  matrix products  12.7 us (1%)
  waiting for transfers between devices  12.2 us (1%)
    pallas_call x1, Pallas kernels, run_experts(): pl.pallas_call(functools.partial(moe_kernel, n_exp, n_y, local_experts),...  250 us
    pallas_call x1, Pallas kernels, gather_chips(): pl.pallas_call(functools.partial(gather_kernel, n_exp), in_specs=[vmem_sp...  160 us
    pallas_call x1, Pallas kernels, dense_grad_scatter(): pl.pallas_call(functools.partial(scatter_kernel, n_exp), in_specs=[spec]...  119 us
    pallas_call x2, Pallas kernels, part_weight_grads(): pl.pallas_call(functools.partial(part_grad_kernel, n_y, n_ctx, n_exp, job...  107 us
    pallas_call x1, Pallas kernels, project_all(): pl.pallas_call(functools.partial(project_kernel, n_y, n_exp), grid=(block...  102 us
    pallas_call x1, Pallas kernels, attend_back(): pl.pallas_call(functools.partial(attention_back_kernel, n_exp=n_exp, jobs...  72.8 us
    pallas_call x1, Pallas kernels, back_to_input(): pl.pallas_call(functools.partial(back_kernel, n_exp, jobs), grid=(1,), in...  72.5 us
    pallas_call x1, Pallas kernels, attend(): pl.pallas_call(functools.partial(attention_kernel, n_exp if moving else 0...  69.4 us
  transfers between devices with their start and end apart: 10, of which 3 were waited for; matrix products, arithmetic and copies ran while one was open for 9% of the time, Pallas kernels for 61%

profile of v5, /device:TPU:0, one launch (start us, length us, event | category | flops | bytes accessed | tf_op | source)
XLA Modules:
  0.0 1133.7 jit_solution(11093822197381869896)
XLA Ops:
  7.9 1.2 select_dynamic-update-slice_fusion.1
  9.0 1.0 select_dynamic-update-slice_fusion
  10.1 0.8 constant_dynamic-update-slice_fusion.9
  10.8 0.8 constant_dynamic-update-slice_fusion.8
  11.6 0.8 constant_dynamic-update-slice_fusion.7
  12.3 0.8 constant_dynamic-update-slice_fusion.6
  13.1 0.8 constant_dynamic-update-slice_fusion.1
  13.9 1.6 broadcast_select_fusion.3
  15.8 0.7 constant_dynamic-update-slice_fusion.5
  16.6 159.5 %shard_map.263 = (bf16[4,4,2,64,2688]{4,3,2,1,0:T(8,128)(2,1)}, bf16[4,4,4,32,2048]{4,3,2,1,0:T(8,128)(2,1)}, bf16[4,2,2,256,768]{4,3,2,1,0:T(8,128)(2,1)S(1)}, ...) custom-call(bf16[64,2688]{1,0:T(8,128)(2,1)S(1)} %get-tuple-element., ...), custom_call_target="tpu_custom_call" | custom-call | tf_op jit(solution)/shard_map/pallas_call | solution.py:472
  176.2 2.6 copy-done.2
  178.8 2.6 copy-done.3
  181.4 0.8 copy-done.11
  182.3 0.8 slice.292
  183.2 0.7 broadcast_in_dim_reshape_squeeze.14.row_gain_ref
  185.2 1.0 fusion.8
  186.2 0.8 pad_maximum_fusion.2.cos_ref
  187.1 0.8 pad_maximum_fusion.3.sin_ref
  187.9 1.3 copy-done.28
  189.2 102.1 %shard_map.264 = (f32[1024,2560]{1,0:T(8,128)}, bf16[1024,2560]{1,0:T(8,128)(2,1)}, bf16[2048,2560]{1,0:T(8,128)(2,1)}, bf16[2048,1024]{1,0:T(8,128)(2,1)}, bf16...) custom-call(bf16[512,2048]{1,0:T(8,128)(2,1)} %bitcast.123, ...), custom_call_target="tpu_custom_call", output_to_operand_aliasing={{5}: (9, {}), {6}: (10, {}), {7}: (11, {}), {8}: (12, {})} | custom-call | flops 10737418240 | bytes 67108864 | tf_op jit(solution)/shard_map/pallas_call | solution.py:1192
  291.5 0.7 compare_convert_fusion
  293.4 1.1 copy-done.12
  294.6 1.6 copy-done.20
  296.1 69.4 %shard_map.265 = (bf16[1024,2048]{1,0:T(8,128)(2,1)}, f32[32,1,512]{2,1,0:T(1,128)S(1)}, bf16[4,2,2,256,768]{4,3,2,1,0:T(8,128)(2,1)}, bf16[4,2,2,256,768]{4,3,2...) custom-call(s32[2,8,512]{2,1,0:T(8,128)S(1)} %scatter.9.info_ref, ...), custom_call_target="tpu_custom_call", output_to_operand_aliasing={{2}: (5, {}), {3}: (6, {}), {4}: (7, {}), {5}: (8, {})} | custom-call | flops 17179869184 | bytes 12582912 | tf_op jit(solution)/shard_map/pallas_call | solution.py:1380
  365.5 12.7 %fusion.22 = f32[1024,2048]{1,0:T(8,128)S(1)} fusion(bf16[1024,2048]{1,0:T(8,128)(2,1)} %get-tuple-element.110.mixed_ref, bf16[2048,2048]{1,0:T(8,128)(2,1)} %bitcast.149), kind=kOutput, calls=%fused_computation.104 | convolution fusion | flops 8589934592 | bytes 20971520 | tf_op jit(solution)/shard_map/dot_general | solution.py:2240
  378.2 2.5 slice.297
  380.7 2.1 copy-done.25
  383.2 7.1 collective-permute-done.2
  390.3 4.8 multiply_reduce_fusion.2
  395.7 1.3 copy-done.22
  397.1 1.7 multiply_convert_fusion.own_ref
  398.8 250.5 %shard_map.266 = (bf16[2,2304,2048]{2,1,0:T(8,128)(2,1)}, bf16[2,2304,2048]{2,1,0:T(8,128)(2,1)}, bf16[2,2304,768]{2,1,0:T(8,128)(2,1)}, bf16[2,2304,768]{2,1,0:...) custom-call(f32[4,2,32,512]{3,2,1,0:T(8,128)} %copy-done.13, ...), custom_call_target="tpu_custom_call" | custom-call | flops 125627793408 | bytes 96731136 | tf_op jit(solution)/shard_map/pallas_call | solution.py:1779
  649.3 35.7 %shard_map.267 = (bf16[2,2,2,1,2,768,256]{6,5,4,3,2,1,0:T(8,128)(2,1)}, bf16[4,512,2048]{2,1,0:T(8,128)(2,1)}, bf16[4,512,2048]{2,1,0:T(8,128)(2,1)}) custom-call(bf16[2,2304,2048]{2,1,0:T(8,128)(2,1)} %get-tuple-element.122.wide_ref, bf16[2,2304,768]{2,1,0:T(8,128)(2,1)} %get-tuple-element.123.refs_0_, ...), custom_call_target="tpu_custom_call", output_to_operand_aliasing={{1}: (3, {}), {2}: (5, {})} | custom-call | flops 14495514624 | bytes 32243712 | tf_op jit(solution)/shard_map/pallas_call | solution.py:1979
  685.1 70.9 %shard_map.268 = (bf16[2,2,2,2,2,768,256]{6,5,4,3,2,1,0:T(8,128)(2,1)}, bf16[4,512,2048]{2,1,0:T(8,128)(2,1)}, bf16[4,512,2048]{2,1,0:T(8,128)(2,1)}) custom-call(bf16[2,2304,2048]{2,1,0:T(8,128)(2,1)} %get-tuple-element.119.wide_ref, bf16[2,2304,768]{2,1,0:T(8,128)(2,1)} %get-tuple-element.120.refs_0_, ...), custom_call_target="tpu_custom_call", output_to_operand_aliasing={{1}: (4, {}), {2}: (6, {})} | custom-call | flops 28991029248 | bytes 45613056 | tf_op jit(solution)/shard_map/pallas_call | solution.py:1979
  756.7 5.9 fusion.6
  763.2 7.3 fusion.14
  770.7 3.3 add_convert_fusion.chip_ref
  774.1 0.9 collective-permute-done.3.sib_ref
  775.0 31.0 %shard_map.269 = (bf16[2048,2048]{1,0:T(8,128)(2,1)}, bf16[1024,2048]{1,0:T(8,128)(2,1)S(1)}, bf16[4,512,2048]{2,1,0:T(8,128)(2,1)}) custom-call(bf16[1024,2048]{1,0:T(8,128)(2,1)} %get-tuple-element.110.mixed_ref, bf16[512,2048]{1,0:T(8,128)(2,1)} %get-tuple-element.209.own_ref, ...), custom_call_target="tpu_custom_call", output_to_operand_aliasing={{2}: (6, {})} | custom-call | flops 17179869184 | bytes 25165824 | tf_op jit(solution)/shard_map/pallas_call | solution.py:945
  806.0 1.9 copy-done.21
  809.4 72.8 %shard_map.270 = (bf16[1024,2048]{1,0:T(8,128)(2,1)}, f32[2,1024,256]{2,1,0:T(8,128)S(1)}, f32[2,1024,256]{2,1,0:T(8,128)S(1)}, f32[8,128]{1,0:T(8,128)S(1)}, bf16[4,512,2048]{2,1,0:T(8,128)(2,1)}) custom-call(s32[2,8,512]{2,1,0:T(8,128)S(1)} %copy-done.16, s32[2,1024,1]{2,1,0:T(8,128)S(1)} %copy-done.10, ...), custom_call_target="tpu_custom_call", output_to_operand_aliasing={{4}: (13, {})} | custom-call | flops 42949672960 | bytes 37748736 | tf_op jit(solution)/shard_map/pallas_call | solution.py:1522
  882.2 1.3 copy-done.7
  883.5 1.3 copy-done.8
  884.8 3.7 select_bitcast_fusion
  888.6 72.5 %shard_map.271 = (bf16[1024,512]{1,0:T(8,128)(2,1)}, bf16[512,2048]{1,0:T(8,128)(2,1)}, f32[1,2048]{1,0:T(1,128)}, f32[8,128]{1,0:T(8,128)}, bf16[4,512,2048]{2,1,0:T(8,128)(2,1)}) custom-call(bf16[1024,2048]{1,0:T(8,128)(2,1)} %get-tuple-element.135.query_grad_ref.grad_ref, f32[2,1024,256]{2,1,0:T(8,128)} %copy-done.7, ...), custom_call_target="tpu_custom_call", output_to_operand_aliasing={{4}: (13, {})} | custom-call | flops 10737418240 | bytes 50331648 | tf_op jit(solution)/shard_map/pallas_call | solution.py:872
  961.2 0.7 convert_reduce_fusion
  962.1 0.7 convert.31
  963.1 10.6 fusion.1
  973.7 3.3 select_maximum_fusion.stats_ref
  977.0 1.0 maximum_maximum_fusion
  978.0 2.9 bitcast_select_fusion.1
  981.6 2.5 fusion.15
  984.0 2.1 copy.82
  986.2 4.1 reduce-scatter.13.cloned.1.call-done
  990.3 118.9 %shard_map.272 = (f32[64,2688]{1,0:T(8,128)}, f32[64,2688]{1,0:T(8,128)}, f32[8,128]{1,0:T(8,128)}) custom-call(bf16[2048,1024]{1,0:T(8,128)(2,1)} %get-tuple-element.149.turned, bf16[1024,2048]{1,0:T(8,128)(2,1)} %get-tuple-element.135.query_grad_ref.grad_ref, bf16[1024,512]{1,0:T(8,128)(2,1)} %get-tuple-element.150.kv_grad_ref, ...), custom_call_target="tpu_custom_call" | custom-call | flops 11274289152 | bytes 16777216 | tf_op jit(solution)/shard_map/pallas_call | solution.py:703
  1109.2 1.3 slice.291
  1110.5 3.5 copy.80
  1114.0 2.4 copy.81
  1117.1 1.5 broadcast_select_fusion.8
  1118.6 0.7 pad_maximum_fusion.5
  1120.0 1.2 sqrt_bitcast_fusion
  1122.5 1.1 pad_maximum_fusion.1
  1123.5 2.1 bitcast_convert_fusion
  1125.6 1.3 copy.114
  (149 shorter events, 10.9 us)
Async XLA Ops:
  7.2 8.6 copy-start.47
  7.2 8.6 copy-start.46
  7.2 8.6 copy-start.45
  7.2 8.6 copy-start.44
  7.2 391.6 %all-gather.3.cloned.1.call-start = ((), (), s32[]{:S(2)}) async-start(), calls=%async_computation.5 | async-start | bytes 7864320 | tf_op jit(solution)/shard_map/all_gather | solution.py:2170
  7.3 180.7 %collective-permute-start.1 = (bf16[512,2048]{1,0:T(8,128)(2,1)}, bf16[512,2048]{1,0:T(8,128)(2,1)S(1)}, u32[]{:S(2)}, u32[]{:S(2)}) collective-permute-start(bf16[512,2048]{1,0:T(8,128)(2,1)} %bitcast.122), channel_id=1, source_target_pairs={{0,8},{8,0},{16,24},{24,16},{1,9},{9,1},{17,25},{25,17},{2,10},{10... | collective-permute-start | bytes 6291464 | tf_op jit(solution)/shard_map/ppermute | solution.py:2076
  7.8 283.7 %collective-permute-start = (s32[1,1024]{1,0:T(1,128)}, s32[1,1024]{1,0:T(1,128)S(1)}, u32[]{:S(2)}, u32[]{:S(2)}) collective-permute-start(s32[1,1024]{1,0:T(1,128)} %param.21), channel_id=1, source_target_pairs={{0,8},{8,0},{16,24},{24,16},{1,9},{9,1},{17,25},{25,17},{2,10},{10... | collective-permute-start | bytes 12296 | tf_op jit(solution)/shard_map/ppermute | solution.py:2076
  7.9 7.7 copy-start.30
  7.9 8.6 copy-start.31
  13.9 2.7 copy-start
  13.9 2.7 copy-start.14
  13.9 2.7 copy-start.17
  13.9 2.7 copy-start.18
  15.8 160.4 %copy-start.42 = (bf16[64]{0:T(256)(128)(2,1)}, bf16[64]{0:T(256)(128)(2,1)S(1)}, u32[]{:S(2)}) copy-start(bf16[64]{0:T(256)(128)(2,1)S(1)} %pad.52.clone) | copy-start | bytes 388
  176.2 2.6 copy-start.2
  178.8 2.6 copy-start.3
  181.4 0.8 copy-start.11
  187.9 1.3 copy-start.28
  189.2 102.2 %copy-start.39 = (s32[1,1024]{1,0:T(1,128)S(1)}, s32[1,1024]{1,0:T(1,128)}, u32[]{:S(2)}) copy-start(s32[1,1024]{1,0:T(1,128)} %param.21) | copy-start | bytes 12292
  291.4 593.4 %reduce-scatter.17.cloned.1.call-start = ((), (), s32[]{:S(2)}) async-start(), calls=%async_computation.8 | async-start | bytes 7864320
  292.1 0.6 copy-start.35
  293.1 72.4 %copy-start.9 = (s32[2,1024,1]{2,1,0:T(8,128)}, s32[2,1024,1]{2,1,0:T(8,128)S(1)}, u32[]{:S(2)}) copy-start(s32[2,1024,1]{2,1,0:T(8,128)S(1)} %copy.74.seg_ref) | copy-start | bytes 24580
  293.4 72.1 %copy-start.15 = (s32[2,8,512]{2,1,0:T(8,128)}, s32[2,8,512]{2,1,0:T(8,128)S(1)}, u32[]{:S(2)}) copy-start(s32[2,8,512]{2,1,0:T(8,128)S(1)} %scatter.9.info_ref) | copy-start | bytes 98308
  293.4 1.2 copy-start.12
  294.6 1.6 copy-start.20
  365.5 12.7 %copy-start.13 = (f32[4,2,32,512]{3,2,1,0:T(8,128)}, f32[4,2,32,512]{3,2,1,0:T(8,128)S(1)}, u32[]{:S(2)}) copy-start(f32[4,2,32,512]{3,2,1,0:T(8,128)S(1)} %get-tuple-element.112.table_ref) | copy-start | bytes 1572868
  378.2 4.6 copy-start.25
  382.8 7.5 collective-permute-start.2
  383.2 12.5 %copy-start.32 = (f32[2048]{0:T(1024)}, f32[2048]{0:T(1024)S(1)}, u32[]{:S(2)}) copy-start(f32[2048]{0:T(1024)S(1)} %mul.125) | copy-start | bytes 24580
  395.1 2.0 copy-start.22
  395.7 3.1 copy-start.37
  685.0 199.8 %reduce-scatter.15.cloned.1.call-start = ((), (), s32[]{:S(2)}) async-start(), calls=%async_computation.7 | async-start | bytes 15728640
  756.0 0.7 copy-start.33
  756.0 0.7 copy-start.38
  756.1 234.3 %reduce-scatter.13.cloned.1.call-start = ((), (), s32[]{:S(2)}) async-start(), calls=%async_computation.6 | async-start | bytes 10485760
  756.7 5.9 copy-start.1
  756.7 6.5 copy-start.23
  756.7 6.5 copy-start.41
  763.2 7.3 copy-start.36
  770.5 4.5 collective-permute-start.3
  774.1 31.9 %copy-start.6 = (bf16[1,512,2048]{2,1,0:T(8,128)(2,1)}, bf16[1,512,2048]{2,1,0:T(8,128)(2,1)S(1)}, u32[]{:S(2)}) copy-start(bf16[1,512,2048]{2,1,0:T(8,128)(2,1)S(1)} %add_convert_fusion.chip_ref) | copy-start | bytes 6291460
  806.0 1.9 copy-start.21
  808.0 0.7 copy-start.40
  808.0 1.4 copy-start.4
  808.0 1.4 copy-start.5
  808.0 1.4 copy-start.10
  808.0 1.4 copy-start.16
  808.0 1.4 copy-start.19
  808.0 315.5 %reduce-scatter.11.cloned.1.call-start = ((), (), s32[]{:S(2)}) async-start(), calls=%async_computation.4 | async-start | bytes 2621440 | tf_op jit(solution)/shard_map/reduce_scatter | solution.py:2410
  882.2 1.3 copy-start.7
  883.5 1.3 copy-start.8
  888.5 89.5 %collective-permute-start.4 = (bf16[3,2,768,256]{3,2,1,0:T(8,128)(2,1)}, bf16[3,2,768,256]{3,2,1,0:T(8,128)(2,1)}, u32[]{:S(2)}, u32[]{:S(2)}) collective-permute-start(bf16[3,2,768,256]{3,2,1,0:T(8,128)(2,1)} %select_bitcast_fusion), channel_id=1, source_target_pairs={{0,8},{8,0},{16,24},{24,16},{1,9},{9,1},{17,25},{25,17},{2,10},{10... | collective-permute-start | bytes 7077896 | tf_op jit(solution)/shard_map/ppermute | solution.py:2076
  888.6 74.4 %copy-start.24 = (bf16[1,512,2048]{2,1,0:T(8,128)(2,1)S(1)}, bf16[1,512,2048]{2,1,0:T(8,128)(2,1)}, u32[]{:S(2)}) copy-start(bf16[1,512,2048]{2,1,0:T(8,128)(2,1)} %param.20) | copy-start | bytes 6291460
  963.0 13.9 %copy-start.34 = (bf16[64,128]{1,0:T(8,128)(2,1)S(1)}, bf16[64,128]{1,0:T(8,128)(2,1)}, u32[]{:S(2)}) copy-start(bf16[64,128]{1,0:T(8,128)(2,1)} %get-tuple-element.267) | copy-start | bytes 49156
  963.0 13.9 %copy-start.43 = (bf16[64]{0:T(256)(128)(2,1)S(1)}, bf16[64]{0:T(256)(128)(2,1)}, u32[]{:S(2)}) copy-start(bf16[64]{0:T(256)(128)(2,1)} %copy-done.42) | copy-start | bytes 388
  963.1 14.9 %copy-start.26 = (bf16[1,6144,256]{2,1,0:T(8,128)(2,1)S(1)}, bf16[1,6144,256]{2,1,0:T(8,128)(2,1)}, u32[]{:S(2)}) copy-start(bf16[1,6144,256]{2,1,0:T(8,128)(2,1)} %reduce-scatter.15.cloned.1.call-done) | copy-start | bytes 9437188
  963.1 14.9 %copy-start.27 = (bf16[1,3072,256]{2,1,0:T(8,128)(2,1)S(1)}, bf16[1,3072,256]{2,1,0:T(8,128)(2,1)}, u32[]{:S(2)}) copy-start(bf16[1,3072,256]{2,1,0:T(8,128)(2,1)} %reduce-scatter.17.cloned.1.call-done) | copy-start | bytes 4718596
  1117.0 8.6 copy-start.29
Sparse Core Ops, SparseCore 0:
  291.5 94.2 all-gather.2
  685.2 69.5 reduce-scatter.16
  757.8 120.7 reduce-scatter.14
  881.5 108.7 reduce-scatter.12
  992.6 43.8 reduce-scatter.10

commit v6 on v5

--- a/solution.py
+++ b/solution.py
@@ -2237,8 +2237,8 @@
         tables_all = lax.dynamic_update_slice(
             tables_all, table[None, None], (z_index, core, jnp.int32(0), jnp.int32(0))
         )
-    attn_partial = jnp.dot(mixed_low, w_out, preferred_element_type=f32)
-    attn_out = attn_partial[:token_count] + swap(attn_partial[token_count:])
+    attn_theirs = swap(jnp.dot(mixed_low[token_count:], w_out, preferred_element_type=f32))
+    attn_out = jnp.dot(mixed_low[:token_count], w_out, preferred_element_type=f32) + attn_theirs
     middle = hidden + attn_out
     inv_mlp = lax.rsqrt(jnp.mean(middle * middle, axis=-1, keepdims=True) + EPS)
     normed_mlp = (middle * inv_mlp * gain_mlp_f).astype(bf16)

time: 1140 us -> 1140 us (level)
    dot_general x1 -> x2, matrix products: 12.7 us -> 23.1 us  [the longest x1 12.4 us: on_device(): jnp.dot(mixed_low[:token_count], w_out, preferred_element_type=f32)]
    unnamed x101 -> x99, local copies, waits for them, and re-layouts: 28.1 us -> 25.9 us
  transfers between devices with their start and end apart: 10 -> 10, of which waited for: 3 -> 3; matrix products, arithmetic and copies ran while one was open for 9% -> 9% of each run, Pallas kernels for 61% -> 52%
where the time goes in v6:
time: 1140 us; the launch traced here: 1130 us
  Pallas kernels  981 us (86%)
  other arithmetic  60.7 us (5%)
  local copies, waits for them, and re-layouts  37 us (3%)
  matrix products  23.1 us (2%)
  between operations  15.4 us (1%)
  waiting for transfers between devices  13.9 us (1%)
    pallas_call x1, Pallas kernels, run_experts(): pl.pallas_call(functools.partial(moe_kernel, n_exp, n_y, local_experts),...  250 us
    pallas_call x1, Pallas kernels, gather_chips(): pl.pallas_call(functools.partial(gather_kernel, n_exp), in_specs=[vmem_sp...  160 us
    pallas_call x1, Pallas kernels, dense_grad_scatter(): pl.pallas_call(functools.partial(scatter_kernel, n_exp), in_specs=[spec]...  119 us
    pallas_call x2, Pallas kernels, part_weight_grads(): pl.pallas_call(functools.partial(part_grad_kernel, n_y, n_ctx, n_exp, job...  107 us
    pallas_call x1, Pallas kernels, project_all(): pl.pallas_call(functools.partial(project_kernel, n_y, n_exp), grid=(block...  102 us
    pallas_call x1, Pallas kernels, attend_back(): pl.pallas_call(functools.partial(attention_back_kernel, n_exp=n_exp, jobs...  72.7 us
    pallas_call x1, Pallas kernels, back_to_input(): pl.pallas_call(functools.partial(back_kernel, n_exp, jobs), grid=(1,), in...  72.5 us
    pallas_call x1, Pallas kernels, attend(): pl.pallas_call(functools.partial(attention_kernel, n_exp if moving else 0...  67.5 us
  transfers between devices with their start and end apart: 10, of which 3 were waited for; matrix products, arithmetic and copies ran while one was open for 9% of the time, Pallas kernels for 52%

profile of v6, /device:TPU:0, one launch (start us, length us, event | category | flops | bytes accessed | tf_op | source)
XLA Modules:
  0.0 1132.9 jit_solution(3634349738932891846)
XLA Ops:
  7.9 1.2 select_dynamic-update-slice_fusion.1
  9.0 1.0 select_dynamic-update-slice_fusion
  10.1 0.8 constant_dynamic-update-slice_fusion.9
  10.8 0.8 constant_dynamic-update-slice_fusion.8
  11.6 0.8 constant_dynamic-update-slice_fusion.7
  12.3 0.8 constant_dynamic-update-slice_fusion.6
  13.1 0.8 constant_dynamic-update-slice_fusion.1
  13.9 1.6 broadcast_select_fusion.1
  15.8 0.7 constant_dynamic-update-slice_fusion.5
  16.7 159.5 %shard_map.263 = (bf16[4,4,2,64,2688]{4,3,2,1,0:T(8,128)(2,1)}, bf16[4,4,4,32,2048]{4,3,2,1,0:T(8,128)(2,1)}, bf16[4,2,2,256,768]{4,3,2,1,0:T(8,128)(2,1)S(1)}, ...) custom-call(bf16[64,2688]{1,0:T(8,128)(2,1)S(1)} %get-tuple-element., ...), custom_call_target="tpu_custom_call" | custom-call | tf_op jit(solution)/shard_map/pallas_call | solution.py:472
  176.2 2.7 copy-done.2
  178.8 2.6 copy-done.3
  181.4 0.8 copy-done.11
  182.2 0.8 slice.292
  183.1 1.0 fusion.11
  184.1 0.8 pad_maximum_fusion.2.cos_ref
  185.0 0.8 pad_maximum_fusion.3.sin_ref
  186.0 0.7 broadcast_in_dim_reshape_squeeze.14.row_gain_ref
  187.9 0.7 compare_convert_fusion
  189.7 1.4 copy-done.27
  191.1 102.1 %shard_map.264 = (f32[1024,2560]{1,0:T(8,128)}, bf16[1024,2560]{1,0:T(8,128)(2,1)}, bf16[2048,2560]{1,0:T(8,128)(2,1)}, bf16[2048,1024]{1,0:T(8,128)(2,1)}, bf16...) custom-call(bf16[512,2048]{1,0:T(8,128)(2,1)} %bitcast.123, ...), custom_call_target="tpu_custom_call", output_to_operand_aliasing={{5}: (9, {}), {6}: (10, {}), {7}: (11, {}), {8}: (12, {})} | custom-call | flops 10737418240 | bytes 67108864 | tf_op jit(solution)/shard_map/pallas_call | solution.py:1192
  293.4 1.0 copy-done.12
  294.5 1.6 copy-done.20
  296.1 67.5 %shard_map.265 = (bf16[1024,2048]{1,0:T(8,128)(2,1)}, f32[32,1,512]{2,1,0:T(1,128)S(1)}, bf16[4,2,2,256,768]{4,3,2,1,0:T(8,128)(2,1)}, bf16[4,2,2,256,768]{4,3,2...) custom-call(s32[2,8,512]{2,1,0:T(8,128)S(1)} %scatter.9.info_ref, ...), custom_call_target="tpu_custom_call", output_to_operand_aliasing={{2}: (5, {}), {3}: (6, {}), {4}: (7, {}), {5}: (8, {})} | custom-call | flops 17179869184 | bytes 12582912 | tf_op jit(solution)/shard_map/pallas_call | solution.py:1380
  363.6 10.7 fusion.8
  374.8 7.1 collective-permute-done.2
  381.8 12.4 %multiply_reduce_fusion.2 = (f32[512]{0:T(512)S(1)}, f32[512,2048]{1,0:T(8,128)S(1)}, f32[512,2048]{1,0:T(8,128)}) fusion(bf16[1,512,2048]{2,1,0:T(8,128)(2,1)} %param.20, f32[512,2048]{1,0:T(8,128)} %collective-permute-done.2, bf16[2048,2048]{1,0:T(8,128)(2,1)} %bitcast.150, bf16[1024,2048]{1,0:T(8,128)(2,1)} %get-tuple-element.110.mixed_ref), kind=kOutput, calls=%fused_computation.23 | convolution fusion | flops 4300209664 | bytes 25167872 | tf_op jit(solution)/shard_map/dot_general | solution.py:2241
  394.2 0.7 multiply_multiply_fusion
  394.9 1.3 copy-done.22
  396.2 1.7 multiply_convert_fusion.own_ref
  397.9 250.5 %shard_map.266 = (bf16[2,2304,2048]{2,1,0:T(8,128)(2,1)}, bf16[2,2304,2048]{2,1,0:T(8,128)(2,1)}, bf16[2,2304,768]{2,1,0:T(8,128)(2,1)}, bf16[2,2304,768]{2,1,0:...) custom-call(f32[4,2,32,512]{3,2,1,0:T(8,128)} %copy-done.13, ...), custom_call_target="tpu_custom_call" | custom-call | flops 125627793408 | bytes 96731136 | tf_op jit(solution)/shard_map/pallas_call | solution.py:1779
  648.4 35.8 %shard_map.267 = (bf16[2,2,2,1,2,768,256]{6,5,4,3,2,1,0:T(8,128)(2,1)}, bf16[4,512,2048]{2,1,0:T(8,128)(2,1)}, bf16[4,512,2048]{2,1,0:T(8,128)(2,1)}) custom-call(bf16[2,2304,2048]{2,1,0:T(8,128)(2,1)} %get-tuple-element.122.wide_ref, bf16[2,2304,768]{2,1,0:T(8,128)(2,1)} %get-tuple-element.123.refs_0_, ...), custom_call_target="tpu_custom_call", output_to_operand_aliasing={{1}: (3, {}), {2}: (5, {})} | custom-call | flops 14495514624 | bytes 32243712 | tf_op jit(solution)/shard_map/pallas_call | solution.py:1979
  684.3 70.9 %shard_map.268 = (bf16[2,2,2,2,2,768,256]{6,5,4,3,2,1,0:T(8,128)(2,1)}, bf16[4,512,2048]{2,1,0:T(8,128)(2,1)}, bf16[4,512,2048]{2,1,0:T(8,128)(2,1)}) custom-call(bf16[2,2304,2048]{2,1,0:T(8,128)(2,1)} %get-tuple-element.119.wide_ref, bf16[2,2304,768]{2,1,0:T(8,128)(2,1)} %get-tuple-element.120.refs_0_, ...), custom_call_target="tpu_custom_call", output_to_operand_aliasing={{1}: (4, {}), {2}: (6, {})} | custom-call | flops 28991029248 | bytes 45613056 | tf_op jit(solution)/shard_map/pallas_call | solution.py:1979
  755.9 5.9 fusion.6
  762.4 7.3 fusion.17
  769.9 3.3 add_convert_fusion.chip_ref
  773.3 0.9 collective-permute-done.3.sib_ref
  774.2 31.0 %shard_map.269 = (bf16[2048,2048]{1,0:T(8,128)(2,1)}, bf16[1024,2048]{1,0:T(8,128)(2,1)S(1)}, bf16[4,512,2048]{2,1,0:T(8,128)(2,1)}) custom-call(bf16[1024,2048]{1,0:T(8,128)(2,1)} %get-tuple-element.110.mixed_ref, bf16[512,2048]{1,0:T(8,128)(2,1)} %get-tuple-element.209.own_ref, ...), custom_call_target="tpu_custom_call", output_to_operand_aliasing={{2}: (6, {})} | custom-call | flops 17179869184 | bytes 25165824 | tf_op jit(solution)/shard_map/pallas_call | solution.py:945
  805.2 1.9 copy-done.21
  808.6 72.7 %shard_map.270 = (bf16[1024,2048]{1,0:T(8,128)(2,1)}, f32[2,1024,256]{2,1,0:T(8,128)S(1)}, f32[2,1024,256]{2,1,0:T(8,128)S(1)}, f32[8,128]{1,0:T(8,128)S(1)}, bf16[4,512,2048]{2,1,0:T(8,128)(2,1)}) custom-call(s32[2,8,512]{2,1,0:T(8,128)S(1)} %copy-done.16, s32[2,1024,1]{2,1,0:T(8,128)S(1)} %copy-done.10, ...), custom_call_target="tpu_custom_call", output_to_operand_aliasing={{4}: (13, {})} | custom-call | flops 42949672960 | bytes 37748736 | tf_op jit(solution)/shard_map/pallas_call | solution.py:1522
  881.3 1.3 copy-done.7
  882.6 1.3 copy-done.8
  884.0 3.7 select_bitcast_fusion
  887.8 72.5 %shard_map.271 = (bf16[1024,512]{1,0:T(8,128)(2,1)}, bf16[512,2048]{1,0:T(8,128)(2,1)}, f32[1,2048]{1,0:T(1,128)}, f32[8,128]{1,0:T(8,128)}, bf16[4,512,2048]{2,1,0:T(8,128)(2,1)}) custom-call(bf16[1024,2048]{1,0:T(8,128)(2,1)} %get-tuple-element.135.query_grad_ref.grad_ref, f32[2,1024,256]{2,1,0:T(8,128)} %copy-done.7, ...), custom_call_target="tpu_custom_call", output_to_operand_aliasing={{4}: (13, {})} | custom-call | flops 10737418240 | bytes 50331648 | tf_op jit(solution)/shard_map/pallas_call | solution.py:872
  960.3 0.7 convert_reduce_fusion
  961.2 0.7 convert.31
  962.2 9.0 fusion.1
  971.2 3.3 select_maximum_fusion.stats_ref
  974.4 1.0 maximum_maximum_fusion
  975.5 3.0 bitcast_select_fusion.1
  979.1 2.5 fusion.18
  981.6 2.1 copy.82
  983.7 5.8 reduce-scatter.13.cloned.1.call-done
  989.5 118.9 %shard_map.272 = (f32[64,2688]{1,0:T(8,128)}, f32[64,2688]{1,0:T(8,128)}, f32[8,128]{1,0:T(8,128)}) custom-call(bf16[2048,1024]{1,0:T(8,128)(2,1)} %get-tuple-element.149.turned, bf16[1024,2048]{1,0:T(8,128)(2,1)} %get-tuple-element.135.query_grad_ref.grad_ref, bf16[1024,512]{1,0:T(8,128)(2,1)} %get-tuple-element.150.kv_grad_ref, ...), custom_call_target="tpu_custom_call" | custom-call | flops 11274289152 | bytes 16777216 | tf_op jit(solution)/shard_map/pallas_call | solution.py:703
  1108.4 1.3 slice.291
  1109.7 3.5 copy.80
  1113.2 2.4 copy.81
  1116.3 1.5 broadcast_select_fusion.8
  1117.8 0.7 pad_maximum_fusion.5
  1118.5 0.7 pad_maximum_fusion.4
  1119.2 1.2 sqrt_bitcast_fusion
  1121.7 1.1 pad_maximum_fusion.1
  1122.7 2.1 bitcast_convert_fusion
  1124.8 1.3 copy.114
  (146 shorter events, 9.6 us)
Async XLA Ops:
  7.2 8.6 copy-start.46
  7.2 8.6 copy-start.45
  7.2 8.6 copy-start.44
  7.2 8.6 copy-start.43
  7.2 390.7 %all-gather.3.cloned.1.call-start = ((), (), s32[]{:S(2)}) async-start(), calls=%async_computation.5 | async-start | bytes 7864320 | tf_op jit(solution)/shard_map/all_gather | solution.py:2170
  7.3 182.4 %collective-permute-start.1 = (bf16[512,2048]{1,0:T(8,128)(2,1)}, bf16[512,2048]{1,0:T(8,128)(2,1)S(1)}, u32[]{:S(2)}, u32[]{:S(2)}) collective-permute-start(bf16[512,2048]{1,0:T(8,128)(2,1)} %bitcast.122), channel_id=1, source_target_pairs={{0,8},{8,0},{16,24},{24,16},{1,9},{9,1},{17,25},{25,17},{2,10},{10... | collective-permute-start | bytes 6291464 | tf_op jit(solution)/shard_map/ppermute | solution.py:2076
  7.8 180.1 %collective-permute-start = (s32[1,1024]{1,0:T(1,128)}, s32[1,1024]{1,0:T(1,128)S(1)}, u32[]{:S(2)}, u32[]{:S(2)}) collective-permute-start(s32[1,1024]{1,0:T(1,128)} %param.21), channel_id=1, source_target_pairs={{0,8},{8,0},{16,24},{24,16},{1,9},{9,1},{17,25},{25,17},{2,10},{10... | collective-permute-start | bytes 12296 | tf_op jit(solution)/shard_map/ppermute | solution.py:2076
  7.9 7.7 copy-start.29
  7.9 8.6 copy-start.30
  13.9 2.7 copy-start
  13.9 2.7 copy-start.14
  13.9 2.7 copy-start.17
  13.9 2.7 copy-start.18
  15.8 160.4 %copy-start.41 = (bf16[64]{0:T(256)(128)(2,1)}, bf16[64]{0:T(256)(128)(2,1)S(1)}, u32[]{:S(2)}) copy-start(bf16[64]{0:T(256)(128)(2,1)S(1)} %pad.52.clone) | copy-start | bytes 388
  16.6 171.2 %copy-start.38 = (s32[1,1024]{1,0:T(1,128)S(1)}, s32[1,1024]{1,0:T(1,128)}, u32[]{:S(2)}) copy-start(s32[1,1024]{1,0:T(1,128)} %param.21) | copy-start | bytes 12292
  176.2 2.7 copy-start.2
  178.8 2.6 copy-start.3
  181.4 0.8 copy-start.11
  188.5 0.6 copy-start.34
  189.5 103.9 %copy-start.9 = (s32[2,1024,1]{2,1,0:T(8,128)}, s32[2,1024,1]{2,1,0:T(8,128)S(1)}, u32[]{:S(2)}) copy-start(s32[2,1024,1]{2,1,0:T(8,128)S(1)} %copy.74.seg_ref) | copy-start | bytes 24580
  189.6 103.8 %copy-start.15 = (s32[2,8,512]{2,1,0:T(8,128)}, s32[2,8,512]{2,1,0:T(8,128)S(1)}, u32[]{:S(2)}) copy-start(s32[2,8,512]{2,1,0:T(8,128)S(1)} %scatter.9.info_ref) | copy-start | bytes 98308
  189.6 1.4 copy-start.27
  293.2 590.8 %reduce-scatter.17.cloned.1.call-start = ((), (), s32[]{:S(2)}) async-start(), calls=%async_computation.8 | async-start | bytes 7864320
  293.4 1.0 copy-start.12
  294.5 1.6 copy-start.20
  363.6 10.7 copy-start.13
  374.3 7.5 collective-permute-start.2
  374.8 20.2 %copy-start.31 = (f32[2048]{0:T(1024)}, f32[2048]{0:T(1024)S(1)}, u32[]{:S(2)}) copy-start(f32[2048]{0:T(1024)S(1)} %mul.125) | copy-start | bytes 24580
  394.2 2.0 copy-start.22
  394.9 3.0 copy-start.36
  684.2 199.7 %reduce-scatter.15.cloned.1.call-start = ((), (), s32[]{:S(2)}) async-start(), calls=%async_computation.7 | async-start | bytes 15728640
  755.2 0.7 copy-start.32
  755.2 0.7 copy-start.37
  755.3 234.3 %reduce-scatter.13.cloned.1.call-start = ((), (), s32[]{:S(2)}) async-start(), calls=%async_computation.6 | async-start | bytes 10485760
  755.9 5.9 copy-start.1
  755.9 6.5 copy-start.23
  755.9 6.5 copy-start.40
  762.4 7.3 copy-start.35
  769.7 4.5 collective-permute-start.3
  773.3 31.9 %copy-start.6 = (bf16[1,512,2048]{2,1,0:T(8,128)(2,1)}, bf16[1,512,2048]{2,1,0:T(8,128)(2,1)S(1)}, u32[]{:S(2)}) copy-start(bf16[1,512,2048]{2,1,0:T(8,128)(2,1)S(1)} %add_convert_fusion.chip_ref) | copy-start | bytes 6291460
  805.2 1.9 copy-start.21
  807.2 0.7 copy-start.39
  807.2 1.4 copy-start.4
  807.2 1.4 copy-start.5
  807.2 1.4 copy-start.10
  807.2 1.4 copy-start.16
  807.2 1.4 copy-start.19
  807.2 315.5 %reduce-scatter.11.cloned.1.call-start = ((), (), s32[]{:S(2)}) async-start(), calls=%async_computation.4 | async-start | bytes 2621440 | tf_op jit(solution)/shard_map/reduce_scatter | solution.py:2410
  881.3 1.3 copy-start.7
  882.6 1.3 copy-start.8
  887.7 87.8 %collective-permute-start.4 = (bf16[3,2,768,256]{3,2,1,0:T(8,128)(2,1)}, bf16[3,2,768,256]{3,2,1,0:T(8,128)(2,1)}, u32[]{:S(2)}, u32[]{:S(2)}) collective-permute-start(bf16[3,2,768,256]{3,2,1,0:T(8,128)(2,1)} %select_bitcast_fusion), channel_id=1, source_target_pairs={{0,8},{8,0},{16,24},{24,16},{1,9},{9,1},{17,25},{25,17},{2,10},{10... | collective-permute-start | bytes 7077896 | tf_op jit(solution)/shard_map/ppermute | solution.py:2076
  887.7 74.4 %copy-start.24 = (bf16[1,512,2048]{2,1,0:T(8,128)(2,1)S(1)}, bf16[1,512,2048]{2,1,0:T(8,128)(2,1)}, u32[]{:S(2)}) copy-start(bf16[1,512,2048]{2,1,0:T(8,128)(2,1)} %param.20) | copy-start | bytes 6291460
  962.2 12.3 %copy-start.33 = (bf16[64,128]{1,0:T(8,128)(2,1)S(1)}, bf16[64,128]{1,0:T(8,128)(2,1)}, u32[]{:S(2)}) copy-start(bf16[64,128]{1,0:T(8,128)(2,1)} %get-tuple-element.267) | copy-start | bytes 49156
  962.2 12.3 %copy-start.42 = (bf16[64]{0:T(256)(128)(2,1)S(1)}, bf16[64]{0:T(256)(128)(2,1)}, u32[]{:S(2)}) copy-start(bf16[64]{0:T(256)(128)(2,1)} %copy-done.41) | copy-start | bytes 388
  962.2 13.3 %copy-start.25 = (bf16[1,6144,256]{2,1,0:T(8,128)(2,1)S(1)}, bf16[1,6144,256]{2,1,0:T(8,128)(2,1)}, u32[]{:S(2)}) copy-start(bf16[1,6144,256]{2,1,0:T(8,128)(2,1)} %reduce-scatter.15.cloned.1.call-done) | copy-start | bytes 9437188
  962.2 13.3 %copy-start.26 = (bf16[1,3072,256]{2,1,0:T(8,128)(2,1)S(1)}, bf16[1,3072,256]{2,1,0:T(8,128)(2,1)}, u32[]{:S(2)}) copy-start(bf16[1,3072,256]{2,1,0:T(8,128)(2,1)} %reduce-scatter.17.cloned.1.call-done) | copy-start | bytes 4718596
  1116.2 8.6 copy-start.28
Sparse Core Ops, SparseCore 0:
  293.3 92.3 all-gather.2
  684.4 69.5 reduce-scatter.16
  757.0 120.7 reduce-scatter.14
  880.7 108.7 reduce-scatter.12
  991.8 43.8 reduce-scatter.10
